TPU v7x, 32 devices: a whole 2x2x4 slice. The times are simulated.
32 devices in a mesh: seq: 8 (over z, x), grp: 4 (over y, core).
Axes of the slice: x: 2, y: 2, z: 4, core: 2. Of those that a mesh axis runs over, the one named last changes fastest.
Arguments:
- tokens: bfloat16 [4, 1024, 2048], P('grp', 'seq'), may hold values from -6 to 6
- cotangent: bfloat16 [4, 1024, 2048], P('grp', 'seq'), may hold values from -6 to 6
- lengths: int32 [4, 4], replicated, may hold values from 16 to 912, as said below
- prenorm_gain: float32 [2048], replicated, may hold values from 0.1 to 1.9
- w_query: bfloat16 [2048, 2048], P('seq', 'grp'), may hold values from -0.125 to 0.125
- w_key: bfloat16 [2048, 2048], P('seq', 'grp'), may hold values from -0.125 to 0.125
- w_value: bfloat16 [2048, 2048], P('seq', 'grp'), may hold values from -0.125 to 0.125
- w_gate: bfloat16 [2048, 2048], P('seq', 'grp'), may hold values from -0.125 to 0.125
- rate_weight: bfloat16 [2048, 32], replicated, may hold values from -0.125 to 0.125
- rate_bias: float32 [32], replicated, may hold values from -4 to 4
- init_weight: float32 [32, 64, 64], replicated, may hold values from -0.75 to 0.75
- init_bias: float32 [32, 64], replicated, may hold values from -3 to 3
- inner_gain: float32 [32, 64], replicated, may hold values from 0.1 to 1.9
- inner_bias: float32 [32, 64], replicated, may hold values from -3 to 3
- post_gain: float32 [2048], replicated, may hold values from 0.1 to 1.9
- post_bias: float32 [2048], replicated, may hold values from -2 to 2
- w_out: bfloat16 [2048, 2048], P('grp', 'seq'), may hold values from -0.25 to 0.25
- feedforward_norm_gain: float32 [2048], replicated, may hold values from 0.1 to 1.9
- w_swish: bfloat16 [2048, 5504], P('seq', 'grp'), may hold values from -0.125 to 0.125
- w_up: bfloat16 [2048, 5504], P('seq', 'grp'), may hold values from -0.125 to 0.125
- w_down: bfloat16 [5504, 2048], P('grp', 'seq'), may hold values from -0.15625 to 0.15625
Outputs:
- out_tokens: bfloat16 [4, 1024, 2048], P('grp', 'seq')
- grad_tokens: float32 [4, 1024, 2048], P('grp', 'seq')
- grad_pre_gain: float32 [2048], replicated
- grad_query: float32 [2048, 2048], P('seq', 'grp')
- grad_key: float32 [2048, 2048], P('seq', 'grp')
- grad_value: float32 [2048, 2048], P('seq', 'grp')
- grad_gate: float32 [2048, 2048], P('seq', 'grp')
- grad_rate_weight: float32 [2048, 32], replicated
- grad_rate_bias: float32 [32], replicated
- grad_init_weight: float32 [32, 64, 64], replicated
- grad_init_bias: float32 [32, 64], replicated
- grad_inner_gain: float32 [32, 64], replicated
- grad_inner_bias: float32 [32, 64], replicated
- grad_post_gain: float32 [2048], replicated
- grad_post_bias: float32 [2048], replicated
- grad_out: float32 [2048, 2048], P('grp', 'seq')
- grad_ffn_gain: float32 [2048], replicated
- grad_swish: float32 [2048, 5504], P('seq', 'grp')
- grad_up: float32 [2048, 5504], P('seq', 'grp')
- grad_down: float32 [5504, 2048], P('grp', 'seq')
Inputs may be any that keep to these rules, and one draw needn't show every extreme that they name: `lengths`: lengths are multiples of 16; in each group they leave a padding of at least 16 and under a tenth of 1024 positions at the end; one document of each group, at a place drawn from the seed, covers positions from the first 128 to the last 128 of the stream, and it is the longest.
All inputs are finite; a program needn't handle non-finite values.
Results may differ from a plain program's by a relative error of at most 0.025.
Values may be sent and summed in bfloat16 or wider, within the bound.
No kernel may reach another device: no remote copies, remote signals or barrier semaphores. Data moves between devices by JAX's collectives and lax.ppermute only.
A program may use at most 192 MiB of HBM per device.

v0:
```python
from functools import partial

import jax
import jax.numpy as jnp
from jax import lax
from jax.sharding import PartitionSpec as P

MB = 16


EPS = 1e-06
HIGH = lax.Precision.HIGHEST


def from_behind(block, axis, distance):
    devices = range(lax.axis_size(axis))
    route = [(i - distance, i) for i in devices if i - distance in devices]
    return lax.ppermute(block, axis, route)


def norm_parts(values):
    centred = values - jnp.mean(values, -1, keepdims=True)
    return centred * lax.rsqrt(jnp.mean(centred * centred, -1, keepdims=True) + EPS)


def inner_step(params, carried, inputs):
    init_w, init_b, in_gain, in_shift = params
    state_w, state_b = carried
    queries, key_rows, val_rows, rates, starting = inputs
    state_w = jnp.where(starting[:, None, None, None], init_w[None], state_w)
    state_b = jnp.where(starting[:, None, None], init_b[None], state_b)
    hidden = jnp.einsum("gthf,ghfe->gthe", key_rows, state_w, precision=HIGH) + state_b[:, None]
    centred = hidden - jnp.mean(hidden, -1, keepdims=True)
    inv_std = lax.rsqrt(jnp.mean(centred * centred, -1, keepdims=True) + EPS)
    normalized_rows = centred * inv_std
    err_grad = (normalized_rows * in_gain + in_shift - (val_rows - key_rows)) * in_gain
    grad_hidden = inv_std * (
        err_grad
        - jnp.mean(err_grad, -1, keepdims=True)
        - normalized_rows * jnp.mean(err_grad * normalized_rows, -1, keepdims=True)
    )
    scaled = rates[..., None] * grad_hidden
    lower = (jnp.arange(MB)[:, None] >= jnp.arange(MB)[None, :]).astype(jnp.float32)
    scores = jnp.einsum("gthf,gshf->ghts", queries, key_rows, precision=HIGH)
    mixed = jnp.einsum("ghts,gshf->gthf", (scores + 1.0) * lower, scaled, precision=HIGH)
    updated = (
        jnp.einsum("gthf,ghfe->gthe", queries, state_w, precision=HIGH) + state_b[:, None] - mixed
    )
    result = queries + norm_parts(updated) * in_gain + in_shift
    new_w = state_w - jnp.einsum("gthf,gthe->ghfe", key_rows, scaled, precision=HIGH)
    new_b = state_b - jnp.sum(scaled, 1)
    return ((new_w, new_b), result)


def run_span(state_pair, queries, key_rows, val_rows, rates, starting, params):
    groups = queries.shape[0]
    blocks = queries.shape[1] // MB

    def split_rows(array):
        return jnp.moveaxis(array.reshape((groups, blocks, MB) + array.shape[2:]), 1, 0)

    state_pair, outputs = lax.scan(
        jax.checkpoint(partial(inner_step, params)),
        state_pair,
        (
            split_rows(queries),
            split_rows(key_rows),
            split_rows(val_rows),
            split_rows(rates),
            jnp.moveaxis(starting, 1, 0),
        ),
    )
    return (state_pair, jnp.moveaxis(outputs, 0, 1).reshape(queries.shape))


def rows_dot(left, right):
    return jnp.dot(left, right, preferred_element_type=jnp.float32)


def trans_dot(left, right):
    return lax.dot_general(
        left, right, (((0,), (0,)), ((), ())), preferred_element_type=jnp.float32
    )


def back_dot(left, right):
    return lax.dot_general(
        left, right, (((1,), (1,)), ((), ())), preferred_element_type=jnp.float32
    )


def fetch(w_query, w_key, w_value, w_gate, w_out, w_swish, w_up, w_down):
    return (
        lax.all_gather(w_query, "seq", axis=0, tiled=True),
        lax.all_gather(w_key, "seq", axis=0, tiled=True),
        lax.all_gather(w_value, "seq", axis=0, tiled=True),
        lax.all_gather(w_gate, "seq", axis=0, tiled=True),
        lax.all_gather(w_out, "seq", axis=1, tiled=True),
        lax.all_gather(w_swish, "seq", axis=0, tiled=True),
        lax.all_gather(w_up, "seq", axis=0, tiled=True),
        lax.all_gather(w_down, "seq", axis=1, tiled=True),
    )


def pass_state(state_w, state_b, offset):
    return (
        from_behind(state_w.astype(jnp.bfloat16), "seq", offset).astype(state_w.dtype),
        from_behind(state_b.astype(jnp.bfloat16), "seq", offset).astype(state_b.dtype),
    )


def forward_chain(queries, key_rows, val_rows, rates, starting, params, pieces):
    groups, _, head_count, head_dim = queries.shape
    per_piece = groups // pieces
    seq_index = lax.axis_index("seq")
    turns = lax.axis_size("seq") + pieces - 1
    start_state = (
        jnp.zeros((per_piece, head_count, head_dim, head_dim), jnp.float32),
        jnp.zeros((per_piece, head_count, head_dim), jnp.float32),
        jnp.zeros(queries.shape, jnp.float32),
        jnp.zeros((groups, head_count, head_dim, head_dim), jnp.float32),
        jnp.zeros((groups, head_count, head_dim), jnp.float32),
    )

    def forward_one_turn(turn_no, carried):
        arrived_w, arrived_b = pass_state(carried[0], carried[1], 1)
        piece_no = turn_no - seq_index

        def forward_do_work(state_in):
            results, kept_w, kept_b = (state_in[2], state_in[3], state_in[4])

            def cut_piece(array):
                return array

            (new_w, new_b), piece_out = run_span(
                (arrived_w, arrived_b),
                cut_piece(queries),
                cut_piece(key_rows),
                cut_piece(val_rows),
                cut_piece(rates),
                cut_piece(starting),
                params,
            )
            results = piece_out
            kept_w = arrived_w
            kept_b = arrived_b
            return (new_w, new_b, results, kept_w, kept_b)

        def forward_no_work(state_in):
            return state_in

        return lax.cond(
            (piece_no >= 0) & (piece_no < pieces), forward_do_work, forward_no_work, carried
        )

    finished = lax.fori_loop(0, turns, forward_one_turn, start_state)
    return (finished[2], finished[3], finished[4])


def backward_chain(
    queries, key_rows, val_rows, rates, starting, params, kept_w, kept_b, grad_inner, pieces
):
    groups, _, head_count, head_dim = queries.shape
    per_piece = groups // pieces
    last_index = lax.axis_size("seq") - 1 - lax.axis_index("seq")
    turns = lax.axis_size("seq") + pieces - 1
    zero_params = tuple((jnp.zeros_like(item) for item in params))
    start_state = (
        jnp.zeros((per_piece, head_count, head_dim, head_dim), jnp.float32),
        jnp.zeros((per_piece, head_count, head_dim), jnp.float32),
        jnp.zeros(queries.shape, jnp.float32),
        jnp.zeros(queries.shape, jnp.float32),
        jnp.zeros(queries.shape, jnp.float32),
        jnp.zeros(rates.shape, jnp.float32),
        zero_params,
    )

    def backward_one_turn(turn_no, carried):
        arrived_w, arrived_b = pass_state(carried[0], carried[1], -1)
        piece_no = turn_no - last_index

        def backward_do_work(state_in):
            grad_q, grad_k, grad_v, grad_r, grad_p = (
                state_in[2],
                state_in[3],
                state_in[4],
                state_in[5],
                state_in[6],
            )

            def cut_piece(array):
                return array

            piece_starts = cut_piece(starting)

            def span_map(state_pair, q_part, k_part, v_part, r_part, p_part):
                return run_span(state_pair, q_part, k_part, v_part, r_part, piece_starts, p_part)

            _, pull_back = jax.vjp(
                span_map,
                (cut_piece(kept_w), cut_piece(kept_b)),
                cut_piece(queries),
                cut_piece(key_rows),
                cut_piece(val_rows),
                cut_piece(rates),
                params,
            )
            state_grad, piece_q, piece_k, piece_v, piece_r, piece_p = pull_back(
                ((arrived_w, arrived_b), cut_piece(grad_inner))
            )
            grad_q = piece_q
            grad_k = piece_k
            grad_v = piece_v
            grad_r = piece_r
            grad_p = jax.tree.map(jnp.add, grad_p, piece_p)
            return (state_grad[0], state_grad[1], grad_q, grad_k, grad_v, grad_r, grad_p)

        def backward_no_work(state_in):
            return state_in

        return lax.cond(
            (piece_no >= 0) & (piece_no < pieces), backward_do_work, backward_no_work, carried
        )

    finished = lax.fori_loop(0, turns, backward_one_turn, start_state)
    return (finished[2], finished[3], finished[4], finished[5], finished[6])


def body(
    tokens,
    cotangent,
    lengths,
    prenorm_gain,
    w_query,
    w_key,
    w_value,
    w_gate,
    rate_weight,
    rate_bias,
    init_weight,
    init_bias,
    inner_gain,
    inner_bias,
    post_gain,
    post_bias,
    w_out,
    feedforward_norm_gain,
    w_swish,
    w_up,
    w_down,
):
    seq_index = lax.axis_index("seq")
    grp_index = lax.axis_index("grp")
    groups = lax.axis_size("grp")
    rows_tok = tokens.shape[1]
    width = tokens.shape[2]
    head_dim = init_weight.shape[1]
    local_heads = init_weight.shape[0] // groups
    features = local_heads * head_dim
    blocks = rows_tok // MB
    all_rows = groups * rows_tok
    pieces = 1
    positions = seq_index * rows_tok + jnp.arange(rows_tok, dtype=jnp.int32)
    ends = jnp.cumsum(lengths, axis=1)
    starts = ends - lengths
    live_rows = (positions[None, :] < ends[:, -1:]).astype(jnp.float32).reshape(all_rows, 1)
    block_pos = seq_index * rows_tok + jnp.arange(blocks, dtype=jnp.int32) * MB
    starting = jnp.any(block_pos[None, :, None] == starts[:, None, :], -1)
    mats = fetch(w_query, w_key, w_value, w_gate, w_out, w_swish, w_up, w_down)
    document_rows = tokens[0].astype(jnp.float32)
    first_inverse_norm = lax.rsqrt(jnp.mean(document_rows * document_rows, -1, keepdims=True) + EPS)
    first_unit_rows = document_rows * first_inverse_norm
    normalized_rows = (first_unit_rows * prenorm_gain).astype(jnp.bfloat16)
    rows_all = lax.all_gather(normalized_rows[None], "grp", axis=0, tiled=True).reshape(
        all_rows, width
    )
    queries = rows_dot(rows_all, mats[0]).astype(jnp.bfloat16)
    key_rows = rows_dot(rows_all, mats[1]).astype(jnp.bfloat16)
    val_rows = rows_dot(rows_all, mats[2]).astype(jnp.bfloat16)
    gate_pre = rows_dot(rows_all, mats[3])
    rate_cols = lax.dynamic_slice_in_dim(rate_weight, grp_index * local_heads, local_heads, 1)
    rate_shift = lax.dynamic_slice_in_dim(rate_bias, grp_index * local_heads, local_heads, 0)
    logits = rows_dot(rows_all, rate_cols) + rate_shift
    rate_sig = jax.nn.sigmoid(logits)
    rates = rate_sig / head_dim * live_rows
    params = tuple(
        (
            lax.dynamic_slice_in_dim(item, grp_index * local_heads, local_heads, 0)
            for item in (init_weight, init_bias, inner_gain, inner_bias)
        )
    )
    shape_four = (groups, rows_tok, local_heads, head_dim)
    q_four = queries.astype(jnp.float32).reshape(shape_four)
    k_four = key_rows.astype(jnp.float32).reshape(shape_four)
    v_four = val_rows.astype(jnp.float32).reshape(shape_four)
    r_three = rates.reshape(groups, rows_tok, local_heads)
    inner_out, kept_w, kept_b = forward_chain(
        q_four, k_four, v_four, r_three, starting, params, pieces
    )
    inner = inner_out.reshape(all_rows, features)
    row_sums = lax.psum((jnp.sum(inner, -1), jnp.sum(inner * inner, -1)), "grp")
    mean_o = row_sums[0] / width
    inv_o = lax.rsqrt(row_sums[1] / width - mean_o * mean_o + EPS)
    o_hat = (inner - mean_o[:, None]) * inv_o[:, None]
    post_g = lax.dynamic_slice_in_dim(post_gain, grp_index * features, features, 0)
    post_b = lax.dynamic_slice_in_dim(post_bias, grp_index * features, features, 0)
    post = o_hat * post_g + post_b
    gelu_val, gelu_pull = jax.vjp(jax.nn.gelu, gate_pre)
    gated = (gelu_val * post).astype(jnp.bfloat16)
    mix_part = rows_dot(gated, mats[4]).reshape(groups, rows_tok, width)
    mixing = lax.psum_scatter(mix_part, "grp", scatter_dimension=0, tiled=True)[0]
    residual_stream = document_rows + mixing
    second_inverse_norm = lax.rsqrt(
        jnp.mean(residual_stream * residual_stream, -1, keepdims=True) + EPS
    )
    second_unit_rows = residual_stream * second_inverse_norm
    feedforward_input = (second_unit_rows * feedforward_norm_gain).astype(jnp.bfloat16)
    ffn_rows = lax.all_gather(feedforward_input[None], "grp", axis=0, tiled=True).reshape(
        all_rows, width
    )
    act_a = rows_dot(ffn_rows, mats[5])
    act_u = rows_dot(ffn_rows, mats[6])
    sig_a = jax.nn.sigmoid(act_a)
    hidden = (act_a * sig_a * act_u).astype(jnp.bfloat16)
    ffn_part = rows_dot(hidden, mats[7]).reshape(groups, rows_tok, width)
    ffn_out = lax.psum_scatter(
        ffn_part.astype(jnp.bfloat16), "grp", scatter_dimension=0, tiled=True
    ).astype(jnp.float32)[0]
    out_tokens = (residual_stream + ffn_out).astype(jnp.bfloat16)[None]
    mats = fetch(w_query, w_key, w_value, w_gate, w_out, w_swish, w_up, w_down)
    grad_own = cotangent[0]
    grad_rows = lax.all_gather(grad_own[None], "grp", axis=0, tiled=True).reshape(all_rows, width)
    d_hidden = back_dot(grad_rows, mats[7])
    g_down = trans_dot(hidden, grad_rows)
    d_a = (d_hidden * act_u * sig_a * (1.0 + act_a * (1.0 - sig_a))).astype(jnp.bfloat16)
    d_u = (d_hidden * act_a * sig_a).astype(jnp.bfloat16)
    g_swish = trans_dot(ffn_rows, d_a)
    g_up = trans_dot(ffn_rows, d_u)
    d_ffn_part = (back_dot(d_a, mats[5]) + back_dot(d_u, mats[6])).reshape(groups, rows_tok, width)
    feedforward_gradient = lax.psum_scatter(
        d_ffn_part.astype(jnp.bfloat16), "grp", scatter_dimension=0, tiled=True
    ).astype(jnp.float32)[0]
    second_scaled_rows = feedforward_gradient * feedforward_norm_gain
    feedforward_gain_gradient = jnp.sum(feedforward_gradient * second_unit_rows, 0)
    d_resid = grad_own.astype(jnp.float32) + second_inverse_norm * (
        second_scaled_rows
        - second_unit_rows * jnp.mean(second_scaled_rows * second_unit_rows, -1, keepdims=True)
    )
    d_mix = lax.all_gather(d_resid.astype(jnp.bfloat16)[None], "grp", axis=0, tiled=True).reshape(
        all_rows, width
    )
    d_gated = back_dot(d_mix, mats[4])
    g_out = trans_dot(gated, d_mix)
    d_post = d_gated * gelu_val
    d_gate_pre = gelu_pull(d_gated * post)[0].astype(jnp.bfloat16)
    g_post_gain = jnp.sum(d_post * o_hat, 0)
    g_post_bias = jnp.sum(d_post, 0)
    d_ohat = d_post * post_g
    back_sums = lax.psum((jnp.sum(d_ohat, -1), jnp.sum(d_ohat * o_hat, -1)), "grp")
    d_inner = inv_o[:, None] * (
        d_ohat - back_sums[0][:, None] / width - o_hat * back_sums[1][:, None] / width
    )
    grad_q, grad_k, grad_v, grad_r, grad_p = backward_chain(
        q_four,
        k_four,
        v_four,
        r_three,
        starting,
        params,
        kept_w,
        kept_b,
        d_inner.reshape(shape_four),
        pieces,
    )
    d_queries = grad_q.reshape(all_rows, features).astype(jnp.bfloat16)
    d_keys = grad_k.reshape(all_rows, features).astype(jnp.bfloat16)
    d_values = grad_v.reshape(all_rows, features).astype(jnp.bfloat16)
    d_logits = (
        grad_r.reshape(all_rows, local_heads) * live_rows * rate_sig * (1.0 - rate_sig) / head_dim
    ).astype(jnp.bfloat16)
    g_query = trans_dot(rows_all, d_queries)
    g_key = trans_dot(rows_all, d_keys)
    g_value = trans_dot(rows_all, d_values)
    g_gate = trans_dot(rows_all, d_gate_pre)
    g_rate_cols = trans_dot(rows_all, d_logits)
    g_rate_shift = jnp.sum(d_logits.astype(jnp.float32), 0)
    d_rows = (
        back_dot(d_queries, mats[0])
        + back_dot(d_keys, mats[1])
        + back_dot(d_values, mats[2])
        + back_dot(d_gate_pre, mats[3])
        + back_dot(d_logits, rate_cols)
    )
    normalized_gradient = lax.psum_scatter(
        d_rows.reshape(groups, rows_tok, width).astype(jnp.bfloat16),
        "grp",
        scatter_dimension=0,
        tiled=True,
    ).astype(jnp.float32)[0]
    first_scaled_rows = normalized_gradient * prenorm_gain
    prenorm_gain_gradient = jnp.sum(normalized_gradient * first_unit_rows, 0)
    grad_tokens = (
        d_resid
        + first_inverse_norm
        * (
            first_scaled_rows
            - first_unit_rows * jnp.mean(first_scaled_rows * first_unit_rows, -1, keepdims=True)
        )
    )[None]
    big_grads = (
        lax.psum_scatter(
            g_query.astype(jnp.bfloat16), "seq", scatter_dimension=0, tiled=True
        ).astype(jnp.float32),
        lax.psum_scatter(g_key.astype(jnp.bfloat16), "seq", scatter_dimension=0, tiled=True).astype(
            jnp.float32
        ),
        lax.psum_scatter(
            g_value.astype(jnp.bfloat16), "seq", scatter_dimension=0, tiled=True
        ).astype(jnp.float32),
        lax.psum_scatter(
            g_gate.astype(jnp.bfloat16), "seq", scatter_dimension=0, tiled=True
        ).astype(jnp.float32),
        lax.psum_scatter(g_out.astype(jnp.bfloat16), "seq", scatter_dimension=1, tiled=True).astype(
            jnp.float32
        ),
        lax.psum_scatter(
            g_swish.astype(jnp.bfloat16), "seq", scatter_dimension=0, tiled=True
        ).astype(jnp.float32),
        lax.psum_scatter(g_up.astype(jnp.bfloat16), "seq", scatter_dimension=0, tiled=True).astype(
            jnp.float32
        ),
        lax.psum_scatter(
            g_down.astype(jnp.bfloat16), "seq", scatter_dimension=1, tiled=True
        ).astype(jnp.float32),
    )

    def place_heads(whole, local_part, axis_no):
        return lax.dynamic_update_slice_in_dim(
            jnp.zeros(whole, jnp.float32),
            local_part,
            grp_index * local_part.shape[axis_no],
            axis_no,
        )

    small = lax.psum(
        (
            prenorm_gain_gradient,
            place_heads(rate_weight.shape, g_rate_cols, 1),
            place_heads(rate_bias.shape, g_rate_shift, 0),
            place_heads(init_weight.shape, grad_p[0], 0),
            place_heads(init_bias.shape, grad_p[1], 0),
            place_heads(inner_gain.shape, grad_p[2], 0),
            place_heads(inner_bias.shape, grad_p[3], 0),
            place_heads(post_gain.shape, g_post_gain, 0),
            place_heads(post_bias.shape, g_post_bias, 0),
            feedforward_gain_gradient,
        ),
        ("seq", "grp"),
    )
    return (
        out_tokens,
        grad_tokens,
        small[0],
        big_grads[0],
        big_grads[1],
        big_grads[2],
        big_grads[3],
        small[1],
        small[2],
        small[3],
        small[4],
        small[5],
        small[6],
        small[7],
        small[8],
        big_grads[4],
        small[9],
        big_grads[5],
        big_grads[6],
        big_grads[7],
    )


def solution(mesh):
    placed = (
        P("grp", "seq", None),
        P("grp", "seq", None),
        P(),
        P(),
        P("seq", "grp"),
        P("seq", "grp"),
        P("seq", "grp"),
        P("seq", "grp"),
        P(),
        P(),
        P(),
        P(),
        P(),
        P(),
        P(),
        P(),
        P("grp", "seq"),
        P(),
        P("seq", "grp"),
        P("seq", "grp"),
        P("grp", "seq"),
    )
    return jax.shard_map(
        body,
        mesh=mesh,
        in_specs=placed,
        out_specs=(
            P("grp", "seq", None),
            P("grp", "seq", None),
            P(),
            P("seq", "grp"),
            P("seq", "grp"),
            P("seq", "grp"),
            P("seq", "grp"),
            P(),
            P(),
            P(),
            P(),
            P(),
            P(),
            P(),
            P(),
            P("grp", "seq"),
            P(),
            P("seq", "grp"),
            P("seq", "grp"),
            P("grp", "seq"),
        ),
        check_vma=False,
    )
```

profile of v0, /device:TPU:0, one launch (start us, length us, event | category | flops | bytes accessed | tf_op | source)
XLA Modules:
  0.0 5244.6 jit_solution(1486586548015015550)
XLA Ops:
  19.2 17.4 all-gather.13.cloned.1.call-done
  39.6 48.4 all-gather.21.cloned.1.call-done
  91.9 46.1 all-gather.19.cloned.1.call-done
  141.8 45.9 all-gather.17.cloned.1.call-done
  194.6 843.3 %while.117 = (s32[]{:T(128)}, f32[4,8,64,64]{3,2,1,0:T(8,128)}, f32[4,8,64]{2,1,0:T(8,128)}, f32[4,128,8,64]{3,2,1,0:T(8,128)S(1)}, f32[4,8,64,64]{3,2,1,0:T(8,1...) while((s32[]{:T(128)}, f32[4,8,64,64]{3,2,1,0:T(8,128)}, ...), condition=%wide.region_15.16_spmd, body=%wide.region_3.15_spmd.sunk | while | flops 90007048 | bytes 24077120 | solution.py:156
  203.6 7.4 collective-permute-done.3
  212.1 144.7 %conditional.4 = ((f32[4,8,64,64]{3,2,1,0:T(8,128)}, f32[4,8,64]{2,1,0:T(8,128)}, f32[4,128,8,64]{3,2,1,0:T(8,128)S(1)}, f32[4,8,64,64]{3,2,1,0:T(8,128)}, f32[4,8,64]{2,1,0:T(8,128)S(1)})) conditional(s32[]{:T(128)} %convert_element_type.467, (f32[4,8,64,64]{3,2,1,0:T(8,128)}, f32[4,8,64]{2,1,0:T(8,128)}, f32[4,128,8,64]{3,2,1,0:T(8,128)S(1)}, ...), branch_computations={%region_4.4_spmd, %region_5.14_spmd} | conditional | flops 89740800 | bytes 21414300 | solution.py:152
  222.3 132.0 %while.116 = (s32[]{:T(128)}, f32[4,8,64,64]{3,2,1,0:T(8,128)}, f32[4,8,64]{2,1,0:T(8,128)}, f32[8,4,16,8,64]{4,2,3,1,0:T(8,128)}, pred[8,4]{1,0:T(8,128)(4,1)},...) while((s32[]{:T(128)}, f32[4,8,64,64]{3,2,1,0:T(8,128)}, ...), condition=%wide.region_14.13_spmd, body=%wide.region_6.12_spmd.sunk | while | flops 89740800 | bytes 6635709 | solution.py:62
  362.3 8.1 collective-permute-done.3
  373.0 149.8 %collective-permute-start.2 = (bf16[4,8,64,64]{3,2,1,0:T(8,128)(2,1)S(1)}, bf16[4,8,64,64]{3,2,1,0:T(8,128)(2,1)}, u32[]{:S(2)}, u32[]{:S(2)}) collective-permute-start(bf16[4,8,64,64]{3,2,1,0:T(8,128)(2,1)S(1)} %convert_element_type.468), channel_id=1, source_target_pairs={{0,4},{4,8},{8,12},{12,16},{16,20},{20,24},{24,28},{1,5},{5,9},{9,... | collective-permute-start | bytes 786440 | tf_op jit(solution)/shard_map/while/body/eval_jaxpr/ppermute | solution.py:18
  524.8 7.3 collective-permute-done.3
  540.5 146.8 %collective-permute-start.3 = (bf16[4,8,64]{2,1,0:T(8,128)(2,1)S(1)}, bf16[4,8,64]{2,1,0:T(8,128)(2,1)S(1)}, u32[]{:S(2)}, u32[]{:S(2)}) collective-permute-start(bf16[4,8,64]{2,1,0:T(8,128)(2,1)S(1)} %convert_element_type.470), channel_id=1, source_target_pairs={{0,4},{4,8},{8,12},{12,16},{16,20},{20,24},{24,28},{1,5},{5,9},{9,... | collective-permute-start | bytes 12296 | tf_op jit(solution)/shard_map/while/body/eval_jaxpr/ppermute | solution.py:18
  691.2 8.3 collective-permute-start.2
  709.9 145.4 %collective-permute-start.2 = (bf16[4,8,64,64]{3,2,1,0:T(8,128)(2,1)S(1)}, bf16[4,8,64,64]{3,2,1,0:T(8,128)(2,1)}, u32[]{:S(2)}, u32[]{:S(2)}) collective-permute-start(bf16[4,8,64,64]{3,2,1,0:T(8,128)(2,1)S(1)} %convert_element_type.468), channel_id=1, source_target_pairs={{0,4},{4,8},{8,12},{12,16},{16,20},{20,24},{24,28},{1,5},{5,9},{9,... | collective-permute-start | bytes 786440 | tf_op jit(solution)/shard_map/while/body/eval_jaxpr/ppermute | solution.py:18
  873.6 145.2 %collective-permute-start.3 = (bf16[4,8,64]{2,1,0:T(8,128)(2,1)S(1)}, bf16[4,8,64]{2,1,0:T(8,128)(2,1)S(1)}, u32[]{:S(2)}, u32[]{:S(2)}) collective-permute-start(bf16[4,8,64]{2,1,0:T(8,128)(2,1)S(1)} %convert_element_type.470), channel_id=1, source_target_pairs={{0,4},{4,8},{8,12},{12,16},{16,20},{20,24},{24,28},{1,5},{5,9},{9,... | collective-permute-start | bytes 12296 | tf_op jit(solution)/shard_map/while/body/eval_jaxpr/ppermute | solution.py:18
  1056.7 482.0 %reduce-scatter.13.cloned.1.call-done = f32[1,128,2048]{2,1,0:T(8,128)} async-done(((f32[4,128,2048]{2,1,0:T(8,128)}), f32[1,128,2048]{2,1,0:T(8,128)}) %reduce-scatter.13.cloned.1.call-update) | async-done | bytes 1048592 | tf_op jit(solution)/shard_map/reduce_scatter | solution.py:311
  1543.5 89.3 %all-gather.29.cloned.1.call-done = bf16[2048,1376]{0,1:T(8,128)(2,1)} async-done(((bf16[256,1376]{0,1:T(8,128)(2,1)}), bf16[2048,1376]{0,1:T(8,128)(2,1)}) %all-gather.29.cloned.1.call-update) | async-done | bytes 5636112 | tf_op jit(solution)/shard_map/all_gather | solution.py:100
  1632.9 23.0 all-gather.25.cloned.1.call-done
  1655.9 7.9 fusion.155
  1663.9 86.2 %all-gather.27.cloned.1.call-done = bf16[2048,1376]{0,1:T(8,128)(2,1)} async-done(((bf16[256,1376]{0,1:T(8,128)(2,1)}), bf16[2048,1376]{0,1:T(8,128)(2,1)}) %all-gather.27.cloned.1.call-update) | async-done | bytes 5636112 | tf_op jit(solution)/shard_map/all_gather | solution.py:99
  1750.0 8.0 fusion.154
  1758.0 14.5 all-gather.33.cloned.1.call-done
  1772.5 94.1 %all-gather.31.cloned.1.call-done = bf16[1376,2048]{1,0:T(8,128)(2,1)} async-done(((bf16[1376,256]{1,0:T(8,128)(2,1)}), bf16[1376,2048]{1,0:T(8,128)(2,1)}) %all-gather.31.cloned.1.call-update) | async-done | bytes 5636112 | tf_op jit(solution)/shard_map/all_gather | solution.py:101
  1866.6 10.4 multiply_convert_fusion
  1880.8 7.2 add_convert_fusion.1
  1888.1 29.7 reduce-scatter.17.cloned.1.call-done
  1921.4 7.5 convolution_convert_fusion.2
  1967.8 2694.3 %while.118 = (s32[]{:T(128)}, f32[4,8,64,64]{3,2,1,0:T(8,128)}, f32[4,8,64]{2,1,0:T(8,128)S(1)}, bf16[4,128,8,64]{3,2,1,0:T(8,128)(2,1)}, bf16[4,128,8,64]{3,2,1...) while((s32[]{:T(128)}, f32[4,8,64,64]{3,2,1,0:T(8,128)}, ...), condition=%wide.region_64.65_spmd, body=%wide.region_29.64_spmd.sunk | while | flops 296375296 | bytes 53189296 | solution.py:225
  1990.1 16.9 collective-permute-done.1
  2011.1 26.9 collective-permute-done.1
  2042.1 17.6 collective-permute-done.1
  2063.8 10.8 collective-permute-done.1
  2078.8 30.8 collective-permute-done.1
  2113.7 32.0 collective-permute-done.1
  2149.8 22.8 collective-permute-done.1
  2176.8 2156.5 %collective-permute-done.1 = bf16[4,8,64]{2,1,0:T(8,128)(2,1)S(1)} collective-permute-done((bf16[4,8,64]{2,1,0:T(8,128)(2,1)S(1)}, bf16[4,8,64]{2,1,0:T(8,128)(2,1)S(1)}, u32[]{:S(2)}, u32[]{:S(2)}) %collective-permute-start.1) | collective-permute-done | bytes 4128 | tf_op jit(solution)/shard_map/while/body/eval_jaxpr/ppermute | solution.py:18
  4333.4 320.4 %conditional.5 = ((f32[4,8,64,64]{3,2,1,0:T(8,128)}, f32[4,8,64]{2,1,0:T(8,128)S(1)}, bf16[4,128,8,64]{3,2,1,0:T(8,128)(2,1)}, bf16[4,128,8,64]{3,2,1,0:T(8,128)...) conditional(s32[]{:T(128)} %convert_element_type.472, ...), branch_computations={%region_30.30_spmd, %region_31.63_spmd} | conditional | flops 296109056 | bytes 50526320 | solution.py:221
  4352.8 77.0 %while.114 = (s32[]{:T(128)}, f32[4,8,64,64]{3,2,1,0:T(8,128)S(1)}, f32[4,8,64]{2,1,0:T(8,128)S(1)}, f32[8,4,8,64,64]{4,3,2,1,0:T(8,128)}, f32[8,4,8,64]{3,2,1,0...) while((s32[]{:T(128)}, f32[4,8,64,64]{3,2,1,0:T(8,128)S(1)}, ...), condition=%wide.region_38.37_spmd.clone, body=%wide.region_32.36_spmd.clone.sunk | while | flops 51712512 | bytes 5396673 | solution.py:62
  4432.6 214.9 %while.115 = (s32[]{:T(128)}, f32[8,64,64]{2,1,0:T(8,128)S(1)}, f32[8,64]{1,0:T(8,128)S(1)}, f32[8,64]{1,0:T(8,128)S(1)}, f32[8,64]{1,0:T(8,128)S(1)}, /*index=5...) while((s32[]{:T(128)}, f32[8,64,64]{2,1,0:T(8,128)S(1)}, ...), condition=%wide.region_63.62_spmd.clone, body=%wide.region_39.61_spmd.clone.sunk | while | flops 244362240 | bytes 18879824 | solution.py:62
  4703.9 7.3 convolution_convert_fusion.8
  4724.5 38.9 all-reduce
  4763.4 16.2 reduce-scatter.29.cloned.1.call-done
  4781.3 69.1 %reduce-scatter.25.cloned.1.call-done = bf16[256,512]{1,0:T(8,128)(2,1)} async-done(((bf16[2048,512]{1,0:T(8,128)(2,1)}), bf16[256,512]{1,0:T(8,128)(2,1)}) %reduce-scatter.25.cloned.1.call-update) | async-done | bytes 262160 | tf_op jit(solution)/shard_map/reduce_scatter | solution.py:417
  4852.2 68.8 %reduce-scatter.23.cloned.1.call-done = bf16[256,512]{1,0:T(8,128)(2,1)} async-done(((bf16[2048,512]{1,0:T(8,128)(2,1)}), bf16[256,512]{1,0:T(8,128)(2,1)}) %reduce-scatter.23.cloned.1.call-update) | async-done | bytes 262160 | tf_op jit(solution)/shard_map/reduce_scatter | solution.py:414
  4922.8 68.9 %reduce-scatter.21.cloned.1.call-done = bf16[256,512]{1,0:T(8,128)(2,1)} async-done(((bf16[2048,512]{1,0:T(8,128)(2,1)}), bf16[256,512]{1,0:T(8,128)(2,1)}) %reduce-scatter.21.cloned.1.call-update) | async-done | bytes 262160 | tf_op jit(solution)/shard_map/reduce_scatter | solution.py:411
  4993.5 69.0 %reduce-scatter.27.cloned.1.call-done = bf16[256,512]{1,0:T(8,128)(2,1)} async-done(((bf16[2048,512]{1,0:T(8,128)(2,1)}), bf16[256,512]{1,0:T(8,128)(2,1)}) %reduce-scatter.27.cloned.1.call-update) | async-done | bytes 262160 | tf_op jit(solution)/shard_map/reduce_scatter | solution.py:420
  5064.3 31.2 reduce-scatter.15.cloned.1.call-done
  5098.9 134.9 %all-reduce.6.cloned.1.call-done = (f32[2048,32]{0,1:T(8,128)}, f32[32,64,64]{2,1,0:T(8,128)}) async-done(((f32[2048,32]{0,1:T(8,128)}, f32[32,64,64]{2,1,0:T(8,128)}), (f32[2048,32]{0,1:T(8,128)}, f32[32,64,64]{2,1,0:T(8,128)})) %all-reduce.6.cloned.1.call-update) | async-done | bytes 786448 | tf_op jit(solution)/shard_map/psum | solution.py:445
  (1173 shorter events, 742.6 us)
Async XLA Ops:
  7.2 29.4 all-gather.13.cloned.1.call-start
  11.2 76.9 %all-gather.21.cloned.1.call-start = ((), (), s32[]{:S(2)}) async-start(), calls=%async_computation.16 | async-start | bytes 2359296 | tf_op jit(solution)/shard_map/all_gather | solution.py:96
  11.9 126.1 %all-gather.19.cloned.1.call-start = ((), (), s32[]{:S(2)}) async-start(), calls=%async_computation.15 | async-start | bytes 2359296 | tf_op jit(solution)/shard_map/all_gather | solution.py:95
  12.6 175.1 %all-gather.17.cloned.1.call-start = ((), (), s32[]{:S(2)}) async-start(), calls=%async_computation.14 | async-start | bytes 2359296 | tf_op jit(solution)/shard_map/all_gather | solution.py:94
  13.2 1032.8 %all-gather.15.cloned.1.call-start = ((), (), s32[]{:S(2)}) async-start(), calls=%async_computation.13 | async-start | bytes 2359296 | tf_op jit(solution)/shard_map/all_gather | solution.py:97
  13.8 1036.9 %all-gather.23.cloned.1.call-start = ((), (), s32[]{:S(2)}) async-start(), calls=%async_computation.17 | async-start | bytes 2359296 | tf_op jit(solution)/shard_map/all_gather | solution.py:98
  14.4 1524.2 %reduce-scatter.13.cloned.1.call-start = ((), (), s32[]{:S(2)}) async-start(), calls=%async_computation.18 | async-start | bytes 5242880 | tf_op jit(solution)/shard_map/reduce_scatter | solution.py:311
  196.1 14.9 collective-permute-start.2
  373.0 159.1 %collective-permute-start.2 = (bf16[4,8,64,64]{3,2,1,0:T(8,128)(2,1)S(1)}, bf16[4,8,64,64]{3,2,1,0:T(8,128)(2,1)}, u32[]{:S(2)}, u32[]{:S(2)}) collective-permute-start(bf16[4,8,64,64]{3,2,1,0:T(8,128)(2,1)S(1)} %convert_element_type.468), channel_id=1, source_target_pairs={{0,4},{4,8},{8,12},{12,16},{16,20},{20,24},{24,28},{1,5},{5,9},{9,... | collective-permute-start | bytes 786440 | tf_op jit(solution)/shard_map/while/body/eval_jaxpr/ppermute | solution.py:18
  534.6 154.2 %collective-permute-start.2 = (bf16[4,8,64,64]{3,2,1,0:T(8,128)(2,1)S(1)}, bf16[4,8,64,64]{3,2,1,0:T(8,128)(2,1)}, u32[]{:S(2)}, u32[]{:S(2)}) collective-permute-start(bf16[4,8,64,64]{3,2,1,0:T(8,128)(2,1)S(1)} %convert_element_type.468), channel_id=1, source_target_pairs={{0,4},{4,8},{8,12},{12,16},{16,20},{20,24},{24,28},{1,5},{5,9},{9,... | collective-permute-start | bytes 786440 | tf_op jit(solution)/shard_map/while/body/eval_jaxpr/ppermute | solution.py:18
  540.5 148.2 %collective-permute-start.3 = (bf16[4,8,64]{2,1,0:T(8,128)(2,1)S(1)}, bf16[4,8,64]{2,1,0:T(8,128)(2,1)S(1)}, u32[]{:S(2)}, u32[]{:S(2)}) collective-permute-start(bf16[4,8,64]{2,1,0:T(8,128)(2,1)S(1)} %convert_element_type.470), channel_id=1, source_target_pairs={{0,4},{4,8},{8,12},{12,16},{16,20},{20,24},{24,28},{1,5},{5,9},{9,... | collective-permute-start | bytes 12296 | tf_op jit(solution)/shard_map/while/body/eval_jaxpr/ppermute | solution.py:18
  691.2 16.2 collective-permute-start.2
  709.9 153.6 %collective-permute-start.2 = (bf16[4,8,64,64]{3,2,1,0:T(8,128)(2,1)S(1)}, bf16[4,8,64,64]{3,2,1,0:T(8,128)(2,1)}, u32[]{:S(2)}, u32[]{:S(2)}) collective-permute-start(bf16[4,8,64,64]{3,2,1,0:T(8,128)(2,1)S(1)} %convert_element_type.468), channel_id=1, source_target_pairs={{0,4},{4,8},{8,12},{12,16},{16,20},{20,24},{24,28},{1,5},{5,9},{9,... | collective-permute-start | bytes 786440 | tf_op jit(solution)/shard_map/while/body/eval_jaxpr/ppermute | solution.py:18
  866.1 154.2 %collective-permute-start.2 = (bf16[4,8,64,64]{3,2,1,0:T(8,128)(2,1)S(1)}, bf16[4,8,64,64]{3,2,1,0:T(8,128)(2,1)}, u32[]{:S(2)}, u32[]{:S(2)}) collective-permute-start(bf16[4,8,64,64]{3,2,1,0:T(8,128)(2,1)S(1)} %convert_element_type.468), channel_id=1, source_target_pairs={{0,4},{4,8},{8,12},{12,16},{16,20},{20,24},{24,28},{1,5},{5,9},{9,... | collective-permute-start | bytes 786440 | tf_op jit(solution)/shard_map/while/body/eval_jaxpr/ppermute | solution.py:18
  873.6 146.6 %collective-permute-start.3 = (bf16[4,8,64]{2,1,0:T(8,128)(2,1)S(1)}, bf16[4,8,64]{2,1,0:T(8,128)(2,1)S(1)}, u32[]{:S(2)}, u32[]{:S(2)}) collective-permute-start(bf16[4,8,64]{2,1,0:T(8,128)(2,1)S(1)} %convert_element_type.470), channel_id=1, source_target_pairs={{0,4},{4,8},{8,12},{12,16},{16,20},{20,24},{24,28},{1,5},{5,9},{9,... | collective-permute-start | bytes 12296 | tf_op jit(solution)/shard_map/while/body/eval_jaxpr/ppermute | solution.py:18
  1022.7 14.0 collective-permute-start.2
  1055.9 577.0 %all-gather.29.cloned.1.call-start = ((), (), s32[]{:S(2)}) async-start(), calls=%async_computation.21 | async-start | bytes 6340608 | tf_op jit(solution)/shard_map/all_gather | solution.py:100
  1056.6 599.3 %all-gather.25.cloned.1.call-start = ((), (), s32[]{:S(2)}) async-start(), calls=%async_computation.19 | async-start | bytes 2621440 | tf_op jit(solution)/shard_map/all_gather | solution.py:318
  1541.2 208.8 %all-gather.27.cloned.1.call-start = ((), (), s32[]{:S(2)}) async-start(), calls=%async_computation.20 | async-start | bytes 6340608 | tf_op jit(solution)/shard_map/all_gather | solution.py:99
  1541.8 230.7 %all-gather.33.cloned.1.call-start = ((), (), s32[]{:S(2)}) async-start(), calls=%async_computation.24 | async-start | bytes 2621440 | tf_op jit(solution)/shard_map/all_gather | solution.py:332
  1542.5 324.1 %all-gather.31.cloned.1.call-start = ((), (), s32[]{:S(2)}) async-start(), calls=%async_computation.22 | async-start | bytes 6340608 | tf_op jit(solution)/shard_map/all_gather | solution.py:101
  1543.1 374.7 %reduce-scatter.17.cloned.1.call-start = ((), (), s32[]{:S(2)}) async-start(), calls=%async_computation.25 | async-start | bytes 2621440 | tf_op jit(solution)/shard_map/reduce_scatter | solution.py:340
  1888.1 63.2 %all-gather.35.cloned.1.call-start = ((), (), s32[]{:S(2)}) async-start(), calls=%async_computation.26 | async-start | bytes 2621440 | tf_op jit(solution)/shard_map/all_gather | solution.py:349
  1921.3 2794.6 %reduce-scatter.35.cloned.1.call-start = ((), (), s32[]{:S(2)}) async-start(), calls=%async_computation.35 | async-start | bytes 6340608 | tf_op jit(solution)/shard_map/reduce_scatter | solution.py:432
  1928.9 2789.3 %reduce-scatter.33.cloned.1.call-start = ((), (), s32[]{:S(2)}) async-start(), calls=%async_computation.34 | async-start | bytes 6340608 | tf_op jit(solution)/shard_map/reduce_scatter | solution.py:429
  1936.9 2783.7 %reduce-scatter.31.cloned.1.call-start = ((), (), s32[]{:S(2)}) async-start(), calls=%async_computation.33 | async-start | bytes 6340608 | tf_op jit(solution)/shard_map/reduce_scatter | solution.py:426
  1944.8 2778.1 %reduce-scatter.19.cloned.1.call-start = ((), (), s32[]{:S(2)}) async-start(), calls=%async_computation.27 | async-start | bytes 2621440 | tf_op jit(solution)/shard_map/reduce_scatter | solution.py:394
  1987.5 19.5 collective-permute-start
  1988.8 18.2 collective-permute-start.1
  2008.5 29.5 collective-permute-start
  2009.8 28.2 collective-permute-start.1
  2039.5 20.2 collective-permute-start
  2040.8 18.9 collective-permute-start.1
  2076.1 33.4 collective-permute-start
  2077.4 32.1 collective-permute-start.1
  2111.1 34.7 collective-permute-start
  2112.4 33.3 collective-permute-start.1
  2147.2 25.5 collective-permute-start
  2148.5 24.1 collective-permute-start.1
  2174.1 2159.1 %collective-permute-start = (bf16[4,8,64,64]{3,2,1,0:T(8,128)(2,1)S(1)}, bf16[4,8,64,64]{3,2,1,0:T(8,128)(2,1)S(1)}, u32[]{:S(2)}, u32[]{:S(2)}) collective-permute-start(bf16[4,8,64,64]{3,2,1,0:T(8,128)(2,1)S(1)} %convert_element_type.473), channel_id=1, source_target_pairs={{4,0},{8,4},{12,8},{16,12},{20,16},{24,20},{28,24},{5,1},{9,5},{13... | collective-permute-start | bytes 786440 | tf_op jit(solution)/shard_map/while/body/eval_jaxpr/ppermute | solution.py:18
  2175.4 2157.8 %collective-permute-start.1 = (bf16[4,8,64]{2,1,0:T(8,128)(2,1)S(1)}, bf16[4,8,64]{2,1,0:T(8,128)(2,1)S(1)}, u32[]{:S(2)}, u32[]{:S(2)}) collective-permute-start(bf16[4,8,64]{2,1,0:T(8,128)(2,1)S(1)} %convert_element_type.475), channel_id=1, source_target_pairs={{4,0},{8,4},{12,8},{16,12},{20,16},{24,20},{28,24},{5,1},{9,5},{13... | collective-permute-start | bytes 12296 | tf_op jit(solution)/shard_map/while/body/eval_jaxpr/ppermute | solution.py:18
  4679.9 99.6 %reduce-scatter.29.cloned.1.call-start = ((), (), s32[]{:S(2)}) async-start(), calls=%async_computation.32 | async-start | bytes 2359296 | tf_op jit(solution)/shard_map/reduce_scatter | solution.py:423
  4685.2 165.2 %reduce-scatter.25.cloned.1.call-start = ((), (), s32[]{:S(2)}) async-start(), calls=%async_computation.30 | async-start | bytes 2359296 | tf_op jit(solution)/shard_map/reduce_scatter | solution.py:417
  4689.5 231.5 %reduce-scatter.23.cloned.1.call-start = ((), (), s32[]{:S(2)}) async-start(), calls=%async_computation.29 | async-start | bytes 2359296 | tf_op jit(solution)/shard_map/reduce_scatter | solution.py:414
  4693.8 298.0 %reduce-scatter.21.cloned.1.call-start = ((), (), s32[]{:S(2)}) async-start(), calls=%async_computation.28 | async-start | bytes 2359296 | tf_op jit(solution)/shard_map/reduce_scatter | solution.py:411
  4698.1 364.4 %reduce-scatter.27.cloned.1.call-start = ((), (), s32[]{:S(2)}) async-start(), calls=%async_computation.31 | async-start | bytes 2359296 | tf_op jit(solution)/shard_map/reduce_scatter | solution.py:420
  4702.6 392.9 %reduce-scatter.15.cloned.1.call-start = ((), (), s32[]{:S(2)}) async-start(), calls=%async_computation.23 | async-start | bytes 2621440 | tf_op jit(solution)/shard_map/reduce_scatter | solution.py:326
  4711.3 522.6 %all-reduce.6.cloned.1.call-start = ((), (), s32[]{:S(2)}) async-start(), calls=%async_computation.36 | async-start | bytes 2621440 | tf_op jit(solution)/shard_map/psum | solution.py:445
  (66 other events, 4053.4 us)
Sparse Core Ops, SparseCore 0:
  11.3 25.2 all-gather.12
  38.7 49.2 all-gather.20
  90.2 47.7 all-gather.18
  140.0 47.7 all-gather.16
  189.8 55.7 all-gather.14
  247.4 59.7 all-gather.22
  1056.0 482.6 reduce-scatter.12
  1540.9 91.9 all-gather.28
  1635.1 20.7 all-gather.24
  1658.0 91.9 all-gather.26
  1751.7 20.7 all-gather.32
  1774.6 91.9 all-gather.30
  1888.2 29.5 reduce-scatter.16
  1921.4 22.5 all-gather.34
  1947.6 136.8 reduce-scatter.34
  2088.0 125.2 reduce-scatter.32
  2216.8 108.4 reduce-scatter.30
  4680.0 27.2 reduce-scatter.18
  4711.3 68.1 reduce-scatter.28
  4783.3 67.0 reduce-scatter.24
  4854.4 66.6 reduce-scatter.22
  4925.0 66.7 reduce-scatter.20
  4995.7 66.7 reduce-scatter.26
  5065.0 30.3 reduce-scatter.14
  5102.2 131.5 all-reduce.5
where the time goes:
time: 5260 us; the launch traced here: 5240 us
  waiting for transfers between devices  3790 us (72%)
  starting transfers between devices  664 us (13%)
  matrix products  399 us (8%)
  other arithmetic  160 us (3%)
  local copies, waits for them, and re-layouts  137 us (3%)
    ppermute x32, waiting for transfers between devices, from_behind(): return lax.ppermute(block, axis, route)  2350 us
    ppermute x32, starting transfers between devices, from_behind(): return lax.ppermute(block, axis, route)  662 us
    reduce_scatter x1, waiting for transfers between devices, body(): lax.psum_scatter(mix_part, 'grp', scatter_dimension=0, tiled=True)[0]  482 us
    psum x1, waiting for transfers between devices, body(): lax.psum((prenorm_gain_gradient, place_heads(rate_weight.shape, g_rate_co...  135 us
  transfers between devices with their start and end apart: 57, of which 34 were waited for; matrix products, arithmetic and copies ran while one was open for 12% of the time, Pallas kernels for 0%

commit v1 on v0

v1 whole, which is shorter than its diff:
```python
from functools import partial

import jax
import jax.numpy as jnp
from jax import lax
from jax.experimental import pallas as pl
from jax.experimental.pallas import tpu as pltpu
from jax.sharding import PartitionSpec as P

MB = 16
EPS = 1e-06
F32 = jnp.float32
BF16 = jnp.bfloat16


def mm(left, right):
    return jnp.dot(left, right, preferred_element_type=F32)


def mm_nt(left, right):
    return lax.dot_general(left, right, (((1,), (1,)), ((), ())), preferred_element_type=F32)


def split_two(value):
    high = value.astype(BF16)
    return high, (value - high.astype(F32)).astype(BF16)


def mean_rows(value):
    return jnp.mean(value, axis=0, keepdims=True)


def chunk_rows(ref_value, heads, lanes):
    tokens = ref_value.shape[1]
    parts = [
        ref_value[h, m * MB : (m + 1) * MB, lanes[0] : lanes[1]]
        for m in range(tokens // MB)
        for h in range(heads)
    ]
    return jnp.concatenate(parts, axis=0)


def chunk_masks(info, heads, count):
    step = MB * heads
    row = lax.broadcasted_iota(jnp.int32, (count, count), 0)
    col = lax.broadcasted_iota(jnp.int32, (count, count), 1)
    columns = jnp.transpose(info)
    same = ((row % step) // MB == (col % step) // MB) & (columns[:, 1:2] == info[1:2, :])
    return row // step, col // step, row % MB, col % MB, same, columns


def augment(rows, heads, head_dim, wide):
    count = rows.shape[0]
    near = lax.broadcasted_iota(jnp.int32, (head_dim, wide), 0)
    far = lax.broadcasted_iota(jnp.int32, (head_dim, wide), 1)
    tile = (far % head_dim == near).astype(BF16)
    lane = lax.broadcasted_iota(jnp.int32, (count, wide), 1)
    own = (lax.broadcasted_iota(jnp.int32, (count, wide), 0) % (MB * heads)) // MB
    return jnp.where(lane // head_dim == own, mm(rows, tile), 0.0)


def one_hot_heads(count, heads):
    lane = lax.broadcasted_iota(jnp.int32, (count, 128), 1)
    own = (lax.broadcasted_iota(jnp.int32, (count, 128), 0) % (MB * heads)) // MB
    return (lane == own).astype(BF16)


def forward_kernel(
    heads, x_ref, info_ref, gb_ref, init_ref, out_ref, n_ref, r_ref, nb_ref, stat_ref, w_ref, state
):
    head_dim = gb_ref.shape[1]
    tokens = x_ref.shape[1]
    count = heads * tokens
    full = init_ref.shape[1]
    wide = full - 128

    @pl.when(pl.program_id(0) == 0)
    def _():
        state[...] = init_ref[...]

    carried = state[...]
    w_ref[0] = carried
    info = info_ref[...]
    x = x_ref[...]
    q_rows = chunk_rows(x, heads, (0, head_dim))
    k_rows = chunk_rows(x, heads, (head_dim, 2 * head_dim))
    v_rows = chunk_rows(x, heads, (2 * head_dim, 3 * head_dim))
    g_rows = chunk_rows(x, heads, (3 * head_dim, 4 * head_dim))
    q_t = jnp.transpose(q_rows.astype(F32))
    target_t = jnp.transpose(v_rows.astype(F32) - k_rows.astype(F32))
    mb_row, mb_col, t_row, t_col, same, columns = chunk_masks(info, heads, count)
    gram = jnp.where(same & (mb_row < mb_col), mm_nt(k_rows, k_rows) + 1.0, 0.0).astype(BF16)
    cross = jnp.where(
        same & ((mb_row < mb_col) | ((mb_row == mb_col) & (t_row <= t_col))),
        mm_nt(k_rows, q_rows) + 1.0,
        0.0,
    ).astype(BF16)
    hot = one_hot_heads(count, heads)
    k_aug = jnp.concatenate([augment(k_rows, heads, head_dim, wide).astype(BF16), hot], axis=1)
    q_aug = jnp.concatenate([augment(q_rows, heads, head_dim, wide).astype(BF16), hot], axis=1)
    init = init_ref[...]
    stacked = jnp.concatenate(split_two(carried) + split_two(init), axis=0)
    fresh = info[2:3, :] > 0.5

    def through_state(rows):
        both = mm_nt(stacked, rows)
        return jnp.where(
            fresh,
            both[2 * head_dim : 3 * head_dim] + both[3 * head_dim :],
            both[:head_dim] + both[head_dim : 2 * head_dim],
        )

    z_start = through_state(k_aug)
    gain = gb_ref[0]
    shift = gb_ref[1]
    repeats = count // 128
    inner = 128 // (MB * heads)
    done = []
    for p in range(repeats):
        cols = slice(p * 128, (p + 1) * 128)
        z_base = z_start[:, cols]
        if p:
            z_base = z_base - mm(jnp.concatenate(done, axis=1), gram[: p * 128, cols])
        target = target_t[:, cols]
        rate = info[0:1, cols]
        z = z_base
        for step in range(inner):
            if step:
                z = z_base - mm(scaled.astype(BF16), gram[cols, cols])
            centred = z - mean_rows(z)
            inv = lax.rsqrt(mean_rows(centred * centred) + EPS)
            n = centred * inv
            err = (n * gain + shift - target) * gain
            scaled = (rate * inv) * (err - mean_rows(err) - n * mean_rows(err * n))
        done.append(scaled.astype(BF16))
        n_ref[:, cols] = n
        r_ref[:, cols] = scaled
        stat_ref[0:1, cols] = inv
    r_bf = jnp.concatenate(done, axis=1)
    z_bar = through_state(q_aug) - mm(r_bf, cross)
    centred = z_bar - mean_rows(z_bar)
    inv = lax.rsqrt(mean_rows(centred * centred) + EPS)
    nb = centred * inv
    nb_ref[...] = nb
    stat_ref[1:2, :] = inv
    wide_gain = jnp.concatenate([gain] * repeats, axis=1)
    wide_shift = jnp.concatenate([shift] * repeats, axis=1)
    out_rows = jnp.transpose(q_t + nb * wide_gain + wide_shift)
    packed = jnp.concatenate([out_rows.astype(BF16), g_rows], axis=1)
    for m in range(tokens // MB):
        for h in range(heads):
            at = (m * heads + h) * MB
            out_ref[0, h, m * MB : (m + 1) * MB, :] = packed[at : at + MB]
    base = jnp.where(info[4:5, 0:1] > 0.5, init, carried)
    state[...] = base - mm((r_ref[...] * info[3:4, :]).astype(BF16), k_aug)


def backward_kernel(
    heads,
    x_ref,
    d_ref,
    info_ref,
    gb_ref,
    init_ref,
    n_ref,
    r_ref,
    nb_ref,
    stat_ref,
    w_ref,
    dx_ref,
    dr_ref,
    dgb_ref,
    dinit_ref,
    state,
):
    head_dim = gb_ref.shape[1]
    tokens = x_ref.shape[1]
    count = heads * tokens
    full = init_ref.shape[1]
    wide = full - 128

    @pl.when(pl.program_id(0) == 0)
    def _():
        state[...] = jnp.zeros_like(state)
        dgb_ref[...] = jnp.zeros_like(dgb_ref)
        dinit_ref[...] = jnp.zeros_like(dinit_ref)

    d_end = state[...]
    carried = w_ref[0]
    init = init_ref[...]
    info = info_ref[...]
    x = x_ref[...]
    d_in = d_ref[0]
    q_rows = chunk_rows(x, heads, (0, head_dim))
    k_rows = chunk_rows(x, heads, (head_dim, 2 * head_dim))
    v_rows = chunk_rows(x, heads, (2 * head_dim, 3 * head_dim))
    d_rows = chunk_rows(d_in, heads, (0, head_dim))
    dg_rows = chunk_rows(d_in, heads, (head_dim, 2 * head_dim))
    target_t = jnp.transpose(v_rows.astype(F32) - k_rows.astype(F32))
    d_t = jnp.transpose(d_rows.astype(F32))
    mb_row, mb_col, t_row, t_col, same, columns = chunk_masks(info, heads, count)
    earlier = same & (mb_row < mb_col)
    later = same & (mb_row > mb_col)
    up_to = same & ((mb_row < mb_col) | ((mb_row == mb_col) & (t_row <= t_col)))
    from_on = same & ((mb_row > mb_col) | ((mb_row == mb_col) & (t_row >= t_col)))
    gram = jnp.where(later, mm_nt(k_rows, k_rows) + 1.0, 0.0).astype(BF16)
    cross = jnp.where(from_on, mm_nt(q_rows, k_rows) + 1.0, 0.0).astype(BF16)
    hot = one_hot_heads(count, heads)
    k_aug = jnp.concatenate([augment(k_rows, heads, head_dim, wide).astype(BF16), hot], axis=1)
    q_aug = jnp.concatenate([augment(q_rows, heads, head_dim, wide).astype(BF16), hot], axis=1)
    gain = gb_ref[0]
    shift = gb_ref[1]
    repeats = count // 128
    inner = 128 // (MB * heads)
    wide_gain = jnp.concatenate([gain] * repeats, axis=1)
    nb = nb_ref[...]
    inv_b = stat_ref[1:2, :]
    d_nb = d_t * wide_gain
    d_zbar = inv_b * (d_nb - mean_rows(d_nb) - nb * mean_rows(d_nb * nb))
    scaled_t = r_ref[...]
    last = info[3:4, :]
    dr_base = -mm(d_zbar.astype(BF16), cross) - last * mm_nt(d_end.astype(BF16), k_aug)
    gain_sum = jnp.zeros((head_dim, 128), F32)
    shift_sum = jnp.zeros((head_dim, 128), F32)
    for p in range(repeats):
        cols = slice(p * 128, (p + 1) * 128)
        gain_sum = gain_sum + d_t[:, cols] * nb[:, cols]
        shift_sum = shift_sum + d_t[:, cols]
    done = []
    errs = []
    for p in reversed(range(repeats)):
        cols = slice(p * 128, (p + 1) * 128)
        base = dr_base[:, cols]
        if done:
            base = base - mm(jnp.concatenate(done, axis=1), gram[(p + 1) * 128 :, cols])
        n = n_ref[:, cols]
        inv = stat_ref[0:1, cols]
        rate = info[0:1, cols]
        miss = n * gain + shift - target_t[:, cols]
        err = miss * gain
        along = mean_rows(err * n)
        plain = inv * (err - mean_rows(err) - n * along)
        gain2 = gain * gain
        d_scaled = base
        for step in range(inner):
            if step:
                d_scaled = base - mm(d_z.astype(BF16), gram[cols, cols])
            g = rate * d_scaled
            g_n = mean_rows(g * n)
            d_err = inv * (g - mean_rows(g) - n * g_n)
            d_n = d_err * gain2 - inv * (g * along + err * g_n)
            d_z = inv * (d_n - mean_rows(d_n) - n * (mean_rows(d_n * n) + mean_rows(g * plain)))
        done.insert(0, d_z.astype(BF16))
        errs.insert(0, d_err * gain)
        dr_ref[0:1, cols] = jnp.sum(d_scaled * plain, axis=0, keepdims=True)
        gain_sum = gain_sum + d_err * (miss + gain * n)
        shift_sum = shift_sum + d_err * gain
    dgb_ref[0] += gain_sum
    dgb_ref[1] += shift_sum
    dz_bf = jnp.concatenate(done, axis=1)
    d_z = dz_bf.astype(F32)
    d_errg = jnp.concatenate(errs, axis=1)
    turned = jnp.transpose(jnp.concatenate([d_zbar, scaled_t, d_z, d_errg], axis=0))
    zb_rows = turned[:, :head_dim].astype(BF16)
    r_rows = turned[:, head_dim : 2 * head_dim].astype(BF16)
    z_rows = turned[:, 2 * head_dim : 3 * head_dim].astype(BF16)
    e_rows = turned[:, 3 * head_dim :]
    d_cross = jnp.where(from_on, -mm_nt(zb_rows, r_rows), 0.0).astype(BF16)
    d_cross_t = jnp.where(up_to, -mm_nt(r_rows, zb_rows), 0.0).astype(BF16)
    d_gram = (
        jnp.where(later, -mm_nt(z_rows, r_rows), 0.0)
        + jnp.where(earlier, -mm_nt(r_rows, z_rows), 0.0)
    ).astype(BF16)
    is_init = columns[:, 2:3] > 0.5
    is_last = columns[:, 3:4] > 0.5

    def stack_heads(weight):
        parts = [weight[:, h * head_dim : (h + 1) * head_dim] for h in range(heads)]
        pad = wide - heads * head_dim
        if pad:
            parts.append(jnp.zeros((pad, head_dim), F32))
        return jnp.concatenate(parts, axis=0).astype(BF16)

    w_both = jnp.concatenate([stack_heads(carried), stack_heads(init)], axis=0)
    d_stack = stack_heads(d_end)

    def by_state(rows):
        own = augment(rows, heads, head_dim, wide)
        return jnp.concatenate(
            [jnp.where(is_init, 0.0, own), jnp.where(is_init, own, 0.0)], axis=1
        ).astype(BF16)

    dq = d_rows.astype(F32) + mm(d_cross, k_rows) + mm(by_state(zb_rows), w_both)
    r_own = jnp.where(is_last, augment(r_rows, heads, head_dim, wide), 0.0).astype(BF16)
    dk = (
        e_rows
        + mm(d_gram, k_rows)
        + mm(d_cross_t, q_rows)
        + mm(by_state(z_rows), w_both)
        - mm(r_own, d_stack)
    )
    packed = jnp.concatenate(
        [dq.astype(BF16), dk.astype(BF16), (-e_rows).astype(BF16), dg_rows], axis=1
    )
    for m in range(tokens // MB):
        for h in range(heads):
            at = (m * heads + h) * MB
            dx_ref[h, m * MB : (m + 1) * MB, :] = packed[at : at + MB]
    row_init = info[2:3, :] > 0.5
    zb_two = jnp.concatenate(
        [jnp.where(row_init, 0.0, d_zbar), jnp.where(row_init, d_zbar, 0.0)], axis=0
    ).astype(BF16)
    z_two = jnp.concatenate(
        [jnp.where(row_init, 0.0, d_z), jnp.where(row_init, d_z, 0.0)], axis=0
    ).astype(BF16)
    d_both = mm(zb_two, q_aug) + mm(z_two, k_aug)
    fresh = info[4:5, 0:1] > 0.5
    state[...] = d_both[:head_dim] + jnp.where(fresh, 0.0, d_end)
    dinit_ref[...] += d_both[head_dim:] + jnp.where(fresh, d_end, 0.0)


def chain_specs(heads, tokens, head_dim, full, at):
    count = heads * tokens
    return dict(
        x=pl.BlockSpec((heads, tokens, 4 * head_dim), lambda i: (0, at(i), 0)),
        pair=pl.BlockSpec((1, heads, tokens, 2 * head_dim), lambda i: (at(i), 0, 0, 0)),
        info=pl.BlockSpec((8, count), lambda i: (0, at(i))),
        gb=pl.BlockSpec((2, head_dim, 128), lambda i: (0, 0, 0)),
        init=pl.BlockSpec((head_dim, full), lambda i: (0, 0)),
        tall=pl.BlockSpec((head_dim, count), lambda i: (0, at(i))),
        weight=pl.BlockSpec((1, head_dim, full), lambda i: (at(i), 0, 0)),
    )


def chain_forward(x4, info, gb, init, tokens):
    heads, total, packed = x4.shape
    head_dim = packed // 4
    chunks = total // tokens
    full = init.shape[1]
    s = chain_specs(heads, tokens, head_dim, full, lambda i: i)
    tall = jax.ShapeDtypeStruct((head_dim, heads * total), F32)
    return pl.pallas_call(
        partial(forward_kernel, heads),
        grid=(chunks,),
        in_specs=[s["x"], s["info"], s["gb"], s["init"]],
        out_specs=[s["pair"], s["tall"], s["tall"], s["tall"], s["info"], s["weight"]],
        out_shape=[
            jax.ShapeDtypeStruct((chunks, heads, tokens, 2 * head_dim), BF16),
            tall,
            tall,
            tall,
            jax.ShapeDtypeStruct((8, heads * total), F32),
            jax.ShapeDtypeStruct((chunks, head_dim, full), F32),
        ],
        scratch_shapes=[pltpu.VMEM((head_dim, full), F32)],
        compiler_params=pltpu.CompilerParams(
            dimension_semantics=("arbitrary",), vmem_limit_bytes=32 * 1024 * 1024
        ),
        cost_estimate=pl.CostEstimate(
            flops=40_000_000_000, bytes_accessed=16_000_000, transcendentals=0
        ),
        name="chain_forward",
    )(x4, info, gb, init)


def chain_backward(x4, d_pair, info, gb, init, kept, tokens):
    heads, total, packed = x4.shape
    head_dim = packed // 4
    chunks = total // tokens
    full = init.shape[1]
    s = chain_specs(heads, tokens, head_dim, full, lambda i: chunks - 1 - i)
    return pl.pallas_call(
        partial(backward_kernel, heads),
        grid=(chunks,),
        in_specs=[
            s["x"],
            s["pair"],
            s["info"],
            s["gb"],
            s["init"],
            s["tall"],
            s["tall"],
            s["tall"],
            s["info"],
            s["weight"],
        ],
        out_specs=[s["x"], s["info"], s["gb"], s["init"]],
        out_shape=[
            jax.ShapeDtypeStruct(x4.shape, BF16),
            jax.ShapeDtypeStruct((8, heads * total), F32),
            jax.ShapeDtypeStruct(gb.shape, F32),
            jax.ShapeDtypeStruct(init.shape, F32),
        ],
        scratch_shapes=[pltpu.VMEM((head_dim, full), F32)],
        compiler_params=pltpu.CompilerParams(
            dimension_semantics=("arbitrary",), vmem_limit_bytes=40 * 1024 * 1024
        ),
        cost_estimate=pl.CostEstimate(
            flops=80_000_000_000, bytes_accessed=20_000_000, transcendentals=0
        ),
        name="chain_backward",
    )(x4, d_pair, info, gb, init, *kept)


def chain_setup(starting, rates, init_weight, init_bias, inner_gain, inner_bias, blocks):
    heads, head_dim, _ = init_weight.shape
    count = starting.shape[0]
    doc = jnp.cumsum(starting.astype(jnp.int32))
    by_chunk = doc.reshape(-1, blocks)
    before = jnp.concatenate([jnp.zeros((1,), jnp.int32), by_chunk[:-1, -1]])
    use_init = by_chunk > before[:, None]
    in_last = by_chunk == by_chunk[:, -1:]
    fresh = jnp.broadcast_to(use_init[:, -1:], use_init.shape)
    spread = jnp.stack(
        [by_chunk, use_init.astype(jnp.int32), in_last.astype(jnp.int32), fresh.astype(jnp.int32)]
    ).astype(F32).reshape(4, count)
    spread = jnp.broadcast_to(spread[:, :, None], (4, count, heads * MB)).reshape(4, -1)
    rate_row = jnp.swapaxes(rates.reshape(count, MB, heads), 1, 2).reshape(1, -1)
    info = jnp.concatenate([rate_row, spread, jnp.zeros((3, rate_row.shape[1]), F32)], axis=0)
    reps = 128 // (MB * heads)

    def pattern(item):
        row = jnp.broadcast_to(item.T[:, None, :, None], (head_dim, reps, heads, MB))
        return row.reshape(head_dim, 128)

    gb = jnp.stack([pattern(inner_gain), pattern(inner_bias)])
    wide = max(128, heads * head_dim)
    w_t = jnp.transpose(init_weight, (2, 0, 1)).reshape(head_dim, heads * head_dim)
    init = jnp.concatenate(
        [
            jnp.pad(w_t, ((0, 0), (0, wide - heads * head_dim))),
            jnp.pad(init_bias.T, ((0, 0), (0, 128 - heads))),
        ],
        axis=1,
    )
    return info, gb, init


def chain_param_grads(dgb, dinit, heads):
    head_dim = dinit.shape[0]
    wide = dinit.shape[1] - 128
    d_w = dinit[:, : heads * head_dim].reshape(head_dim, heads, head_dim).transpose(1, 2, 0)
    d_b = dinit[:, wide : wide + heads].T
    both = jnp.sum(dgb.reshape(2, head_dim, -1, heads, MB), axis=(2, 4))
    return d_w, d_b, both[0].T, both[1].T


def trans_dot(left, right):
    return lax.dot_general(
        left, right, (((0,), (0,)), ((), ())), preferred_element_type=jnp.float32
    )


class HeadPlan:
    def __init__(self, heads, seq, grp):
        self.seq, self.grp, self.heads = seq, grp, heads
        self.local = heads // seq
        self.mixed = (heads // grp) % seq == 0
        self.each = (heads // grp) // seq if self.mixed else 0

    def pick(self, item, seq_index):
        rest = item.shape[1:]
        if self.mixed:
            item = item.reshape((self.grp, self.seq, self.each) + rest)
            item = lax.dynamic_index_in_dim(item, seq_index, 1, keepdims=False)
            return item.reshape((self.local,) + rest)
        return lax.dynamic_slice_in_dim(item, seq_index * self.local, self.local, 0)

    def order(self, item):
        rest = item.shape[2:]
        if self.mixed:
            item = item.reshape((self.seq, self.grp, self.each) + rest)
            item = jnp.swapaxes(item, 0, 1)
        return item.reshape((self.heads,) + rest)


def gather_heads(plan, mats, head_dim):
    rows = mats[0].shape[0]
    count = len(mats)
    if plan.mixed:
        block = jnp.stack(
            [m.reshape(rows, plan.seq, plan.each, head_dim) for m in mats], axis=3
        )
        block = block.transpose(1, 2, 0, 3, 4).reshape(plan.seq, plan.each, rows, -1)
        block = lax.all_to_all(block, "seq", 0, 0, tiled=True)
        block = jnp.swapaxes(block, 0, 1).reshape(plan.each, plan.seq * rows, -1)
        return lax.all_gather(block, "grp", axis=0, tiled=True)
    block = lax.all_gather(jnp.stack(mats), "grp", axis=2, tiled=True)
    block = block.reshape(count, rows, plan.seq, plan.local, head_dim)
    block = block.transpose(2, 3, 1, 0, 4).reshape(plan.seq, plan.local, rows, -1)
    block = lax.all_to_all(block, "seq", 0, 0, tiled=True)
    return jnp.swapaxes(block, 0, 1).reshape(plan.local, plan.seq * rows, -1)


def scatter_heads(plan, grads, count):
    local, all_rows, packed = grads.shape
    rows = all_rows // plan.seq
    head_dim = packed // count
    if plan.mixed:
        grads = lax.psum_scatter(grads, "grp", scatter_dimension=0, tiled=True)
        block = jnp.swapaxes(grads.reshape(plan.each, plan.seq, rows, packed), 0, 1)
        block = lax.all_to_all(block, "seq", 0, 0, tiled=True)
        block = block.reshape(plan.seq * plan.each, rows, count, head_dim)
        out = block.transpose(2, 1, 0, 3).reshape(count, rows, -1)
    else:
        block = jnp.swapaxes(grads.reshape(local, plan.seq, rows, packed), 0, 1)
        block = lax.all_to_all(block, "seq", 0, 0, tiled=True)
        block = block.reshape(plan.heads, rows, count, head_dim)
        block = block.transpose(2, 1, 0, 3).reshape(count, rows, -1)
        out = lax.psum_scatter(block, "grp", scatter_dimension=2, tiled=True)
    return out.astype(jnp.float32)


def to_owner(plan, pair):
    got = lax.all_to_all(pair, "seq", 0, 0, tiled=True)
    tokens, packed = got.shape[2:]
    got = plan.order(got.reshape(plan.seq, plan.local, tokens, 2, packed // 2))
    return got.transpose(2, 1, 0, 3).reshape(2, tokens, -1)


def from_owner(plan, first, second, head_dim):
    tokens = first.shape[0]
    both = jnp.stack([first, second], axis=1).reshape(tokens, 2, plan.heads, head_dim)
    both = both.transpose(2, 0, 1, 3).reshape(plan.heads, tokens, 2 * head_dim)
    if plan.mixed:
        both = both.reshape(plan.grp, plan.seq, plan.each, tokens, 2 * head_dim)
        both = jnp.swapaxes(both, 0, 1)
    both = both.reshape(plan.seq, plan.local, tokens, 2 * head_dim)
    return lax.all_to_all(both, "seq", 0, 0, tiled=True)


def body(
    tokens,
    cotangent,
    lengths,
    prenorm_gain,
    w_query,
    w_key,
    w_value,
    w_gate,
    rate_weight,
    rate_bias,
    init_weight,
    init_bias,
    inner_gain,
    inner_bias,
    post_gain,
    post_bias,
    w_out,
    feedforward_norm_gain,
    w_swish,
    w_up,
    w_down,
):
    seq_index = lax.axis_index("seq")
    grp_index = lax.axis_index("grp")
    groups = lax.axis_size("grp")
    seq = lax.axis_size("seq")
    rows_tok = tokens.shape[1]
    width = tokens.shape[2]
    heads, head_dim, _ = init_weight.shape
    plan = HeadPlan(heads, seq, groups)
    local = plan.local
    stream = rows_tok * seq
    all_rows = groups * rows_tok

    stream_rows = lax.all_gather(tokens[0], "seq", axis=0, tiled=True).astype(F32)
    w_heads = gather_heads(plan, (w_query, w_key, w_value, w_gate), head_dim)
    m_out = lax.all_gather(w_out, "seq", axis=1, tiled=True)
    m_swish = lax.all_gather(w_swish, "seq", axis=0, tiled=True)
    m_up = lax.all_gather(w_up, "seq", axis=0, tiled=True)
    m_down = lax.all_gather(w_down, "seq", axis=1, tiled=True)
    grad_own = cotangent[0]
    grad_rows = lax.all_gather(grad_own, "grp", axis=0, tiled=True)

    own_lengths = lax.dynamic_index_in_dim(lengths, grp_index, 0, keepdims=False)
    ends = jnp.cumsum(own_lengths)
    starts = ends - own_lengths
    live = (jnp.arange(stream, dtype=jnp.int32) < ends[-1]).astype(F32)[:, None]
    block_pos = jnp.arange(stream // MB, dtype=jnp.int32) * MB
    starting = jnp.any(block_pos[:, None] == starts[None, :], -1)

    inv_first = lax.rsqrt(jnp.mean(stream_rows * stream_rows, -1, keepdims=True) + EPS)
    unit_all = stream_rows * inv_first
    normed = (unit_all * prenorm_gain).astype(BF16)
    x4 = lax.dot_general(
        normed, w_heads, (((1,), (1,)), ((), ())), preferred_element_type=F32
    ).astype(BF16)
    x4 = x4.transpose(1, 0, 2)
    rate_cols = plan.pick(rate_weight.T, seq_index).T
    logits = mm(normed, rate_cols) + plan.pick(rate_bias, seq_index)
    rate_sig = jax.nn.sigmoid(logits)
    rates = rate_sig / head_dim * live
    own_params = [
        plan.pick(item, seq_index) for item in (init_weight, init_bias, inner_gain, inner_bias)
    ]
    info, gb, init = chain_setup(starting, rates, *own_params, rows_tok // MB)
    pair, *kept = chain_forward(x4, info, gb, init, rows_tok)
    inner, gate_pre = to_owner(plan, pair).astype(F32)

    mean_o = jnp.mean(inner, -1, keepdims=True)
    inv_o = lax.rsqrt(jnp.mean(inner * inner, -1, keepdims=True) - mean_o * mean_o + EPS)
    o_hat = (inner - mean_o) * inv_o
    post = o_hat * post_gain + post_bias
    gelu_val, gelu_pull = jax.vjp(jax.nn.gelu, gate_pre)
    gated_own = (gelu_val * post).astype(BF16)
    gated = lax.all_to_all(gated_own, "grp", 1, 0, tiled=True)
    mix_part = mm(gated, m_out).astype(BF16)
    mixing = lax.psum_scatter(mix_part, "grp", scatter_dimension=0, tiled=True).astype(F32)
    own_rows = tokens[0].astype(F32)
    resid = own_rows + mixing
    inv_second = lax.rsqrt(jnp.mean(resid * resid, -1, keepdims=True) + EPS)
    unit_second = resid * inv_second
    ffn_in = (unit_second * feedforward_norm_gain).astype(BF16)
    ffn_rows = lax.all_gather(ffn_in, "grp", axis=0, tiled=True)
    act_a = mm(ffn_rows, m_swish)
    act_u = mm(ffn_rows, m_up)
    sig_a = jax.nn.sigmoid(act_a)
    hidden = (act_a * sig_a * act_u).astype(BF16)
    ffn_out = lax.psum_scatter(
        mm(hidden, m_down).astype(BF16), "grp", scatter_dimension=0, tiled=True
    ).astype(F32)
    out_tokens = (resid + ffn_out).astype(BF16)[None]

    d_hidden = mm_nt(grad_rows, m_down)
    g_down = trans_dot(hidden, grad_rows).astype(BF16)
    d_a = (d_hidden * act_u * sig_a * (1.0 + act_a * (1.0 - sig_a))).astype(BF16)
    d_u = (d_hidden * act_a * sig_a).astype(BF16)
    d_ffn_part = (mm_nt(d_a, m_swish) + mm_nt(d_u, m_up)).astype(BF16)
    d_ffn = lax.psum_scatter(d_ffn_part, "grp", scatter_dimension=0, tiled=True).astype(F32)
    g_swish = trans_dot(ffn_rows, d_a).astype(BF16)
    g_up = trans_dot(ffn_rows, d_u).astype(BF16)
    second_scaled = d_ffn * feedforward_norm_gain
    g_ffn_gain = jnp.sum(d_ffn * unit_second, 0)
    d_resid = grad_own.astype(F32) + inv_second * (
        second_scaled - unit_second * jnp.mean(second_scaled * unit_second, -1, keepdims=True)
    )
    d_mix = lax.all_gather(d_resid.astype(BF16), "grp", axis=0, tiled=True)
    d_gated_cols = mm_nt(d_mix, m_out).astype(BF16)
    g_out = trans_dot(gated, d_mix).astype(BF16)
    d_gated = lax.all_to_all(d_gated_cols, "grp", 0, 1, tiled=True).astype(F32)
    d_post = d_gated * gelu_val
    d_gate_pre = gelu_pull(d_gated * post)[0].astype(BF16)
    g_post_gain = jnp.sum(d_post * o_hat, 0)
    g_post_bias = jnp.sum(d_post, 0)
    d_ohat = d_post * post_gain
    d_inner = inv_o * (
        d_ohat
        - jnp.mean(d_ohat, -1, keepdims=True)
        - o_hat * jnp.mean(d_ohat * o_hat, -1, keepdims=True)
    )
    d_pair = from_owner(plan, d_inner.astype(BF16), d_gate_pre, head_dim)
    d_x4, d_rate_rows, d_gb, d_init = chain_backward(x4, d_pair, info, gb, init, kept, rows_tok)
    d_rates = d_rate_rows[0].reshape(stream // MB, local, MB).swapaxes(1, 2).reshape(stream, local)
    d_logits = (d_rates * live * rate_sig * (1.0 - rate_sig) / head_dim).astype(BF16)
    d_normed_part = lax.dot_general(
        d_x4, w_heads, (((0, 2), (0, 2)), ((), ())), preferred_element_type=F32
    ) + mm_nt(d_logits, rate_cols)
    g_pre_gain = jnp.sum(d_normed_part * unit_all, 0)
    d_normed = lax.psum_scatter(
        d_normed_part.astype(BF16), "seq", scatter_dimension=0, tiled=True
    ).astype(F32)
    own_inv = lax.rsqrt(jnp.mean(own_rows * own_rows, -1, keepdims=True) + EPS)
    own_unit = own_rows * own_inv
    first_scaled = d_normed * prenorm_gain
    grad_tokens = (
        d_resid
        + own_inv
        * (first_scaled - own_unit * jnp.mean(first_scaled * own_unit, -1, keepdims=True))
    )[None]
    g_heads = lax.dot_general(
        normed, d_x4, (((0,), (1,)), ((), ())), preferred_element_type=F32
    ).astype(BF16)
    g_heads = scatter_heads(plan, g_heads.transpose(1, 0, 2), 4)
    g_rate_cols = trans_dot(normed, d_logits)
    g_rate_shift = jnp.sum(d_logits.astype(F32), 0)
    head_grads = chain_param_grads(d_gb, d_init, local)
    packed = jnp.concatenate(
        [item.reshape(local, -1) for item in head_grads]
        + [g_rate_cols.T, g_rate_shift[:, None]],
        axis=1,
    )
    packed = jnp.pad(packed, ((0, 0), (0, -packed.shape[1] % 128)))
    packed = plan.order(lax.all_gather(lax.psum(packed, "grp"), "seq", axis=0))
    sizes = (head_dim * head_dim, head_dim, head_dim, head_dim, width, 1)
    small = []
    offset = 0
    for size in sizes:
        small.append(packed[:, offset : offset + size])
        offset += size
    wide = lax.psum((g_post_gain, g_post_bias, g_ffn_gain), ("seq", "grp"))
    g_pre_gain = lax.psum(g_pre_gain, ("seq", "grp"))
    scatter = partial(lax.psum_scatter, axis_name="seq", tiled=True)
    return (
        out_tokens,
        grad_tokens,
        g_pre_gain,
        g_heads[0],
        g_heads[1],
        g_heads[2],
        g_heads[3],
        small[4].T,
        small[5][:, 0],
        small[0].reshape(heads, head_dim, head_dim),
        small[1],
        small[2],
        small[3],
        wide[0],
        wide[1],
        scatter(g_out, scatter_dimension=1).astype(F32),
        wide[2],
        scatter(g_swish, scatter_dimension=0).astype(F32),
        scatter(g_up, scatter_dimension=0).astype(F32),
        scatter(g_down, scatter_dimension=1).astype(F32),
    )


def solution(mesh):
    whole = P()
    rows = P("grp", "seq", None)
    wide = P("seq", "grp")
    tall = P("grp", "seq")
    return jax.shard_map(
        body,
        mesh=mesh,
        in_specs=(rows, rows, whole, whole, wide, wide, wide, wide)
        + (whole,) * 8
        + (tall, whole, wide, wide, tall),
        out_specs=(rows, rows, whole, wide, wide, wide, wide)
        + (whole,) * 8
        + (tall, whole, wide, wide, tall),
        check_vma=False,
    )
```

time: 5260 us -> 1440 us (0.27)
  waiting for transfers between devices: 3790 us -> 952 us
  starting transfers between devices: 664 us -> 15.3 us
  matrix products: 399 us -> 111 us
  blocking collectives: 50.8 us -> 207 us
  other arithmetic: 160 us -> 33.4 us
  local copies, waits for them, and re-layouts: 137 us -> 43 us
  Pallas kernels: 0 us -> 54.3 us
    ppermute x32 -> x0, waiting for transfers between devices: 2350 us -> none  [from_behind(): return lax.ppermute(block, axis, route)]
    ppermute x32 -> x0, starting transfers between devices: 662 us -> none  [from_behind(): return lax.ppermute(block, axis, route)]
    reduce_scatter x12 -> x9, waiting for transfers between devices: 835 us -> 512 us  [the longest x1 109 us: body(): scatter(g_down, scatter_dimension=1).astype(F32)]
    dot_general x186 -> x13, matrix products: 355 us -> 79.2 us  [the longest x5 29.1 us: mm(): return jnp.dot(left, right, preferred_element_type=F32)]
    psum x1, waiting for transfers between devices: 135 us -> 0.01 us  [body(): packed = plan.order(lax.all_gather(lax.psum(packed, 'grp'), 'seq', axis=0))]
    all_to_all x0 -> x3, blocking collectives: none -> 92.9 us  [the longest x1 49.7 us: gather_heads(): block = lax.all_to_all(block, 'seq', 0, 0, tiled=True)]
    all_gather x0 -> x1, blocking collectives: none -> 74.1 us  [body(): packed = plan.order(lax.all_gather(lax.psum(packed, 'grp'), 'seq', axis=0))]
    all_gather x12 -> x9, waiting for transfers between devices: 465 us -> 392 us  [the longest x1 94.3 us: body(): m_down = lax.all_gather(w_down, 'seq', axis=1, tiled=True)]
  transfers between devices with their start and end apart: 57 -> 22, of which waited for: 34 -> 18; matrix products, arithmetic and copies ran while one was open for 12% -> 8% of each run, Pallas kernels for 0% -> 2%
where the time goes in v1:
time: 1440 us; the launch traced here: 1430 us
  waiting for transfers between devices  952 us (66%)
  blocking collectives  207 us (14%)
  matrix products  111 us (8%)
  Pallas kernels  54.3 us (4%)
  local copies, waits for them, and re-layouts  43 us (3%)
  other arithmetic  33.4 us (2%)
  starting transfers between devices  15.3 us (1%)
  between operations  15.3 us (1%)
    reduce_scatter x1, waiting for transfers between devices, body(): scatter(g_down, scatter_dimension=1).astype(F32)  109 us
    reduce_scatter x1, waiting for transfers between devices, body(): scatter(g_up, scatter_dimension=0).astype(F32)  109 us
    all_gather x1, waiting for transfers between devices, body(): m_down = lax.all_gather(w_down, 'seq', axis=1, tiled=True)  94.3 us
    reduce_scatter x1, waiting for transfers between devices, body(): lax.psum_scatter(d_normed_part.astype(BF16), 'seq', scatter_dimension=0,...  88.7 us
    all_gather x1, waiting for transfers between devices, body(): m_swish = lax.all_gather(w_swish, 'seq', axis=0, tiled=True)  88.4 us
    all_gather x1, waiting for transfers between devices, body(): m_up = lax.all_gather(w_up, 'seq', axis=0, tiled=True)  86.3 us
    all_gather x1, blocking collectives, body(): packed = plan.order(lax.all_gather(lax.psum(packed, 'grp'), 'seq', axis=0))  74.1 us
    reduce_scatter x1, waiting for transfers between devices, body(): scatter(g_out, scatter_dimension=1).astype(F32)  69.2 us
  transfers between devices with their start and end apart: 22, of which 18 were waited for; matrix products, arithmetic and copies ran while one was open for 8% of the time, Pallas kernels for 2%

profile of v1, /device:TPU:0, one launch (start us, length us, event | category | flops | bytes accessed | tf_op | source)
XLA Modules:
  0.0 1431.2 jit_solution(18011128849007978654)
XLA Ops:
  12.6 49.7 %all_to_all.49 = bf16[8,1,256,256]{2,3,1,0:T(8,128)(2,1)S(1)} all-to-all(bf16[8,1,256,256]{2,3,1,0:T(8,128)(2,1)S(1)} %bitcast.275), channel_id=1, replica_groups=mesh['seq'=8,'grp'=4] {'seq'}, dimensions={0} | all-to-all | bytes 2097152 | tf_op jit(solution)/shard_map/all_to_all | solution.py:485
  71.1 33.8 %all-gather.26.cloned.1.call-done = bf16[1,1024,2048]{2,1,0:T(8,128)(2,1)} async-done(((bf16[1,128,2048]{2,1,0:T(8,128)(2,1)}), bf16[1,1024,2048]{2,1,0:T(8,128)(2,1)}) %all-gather.26.cloned.1.call-update) | async-done | bytes 4194320 | tf_op jit(solution)/shard_map/all_gather | solution.py:567
  105.0 3.2 fusion.4
  110.7 28.9 %all-gather.12.cloned.1.call-done = bf16[4,2048,256]{2,1,0:T(8,128)(2,1)} async-done(((bf16[1,2048,256]{2,1,0:T(8,128)(2,1)}), bf16[4,2048,256]{2,1,0:T(8,128)(2,1)}) %all-gather.12.cloned.1.call-update) | async-done | bytes 4194320 | tf_op jit(solution)/shard_map/all_gather | solution.py:487
  139.6 8.0 convert_bitcast_fusion.2.x_ref
  147.6 21.8 %chain_forward.1 = (bf16[8,4,128,128]{3,2,1,0:T(8,128)(2,1)}, f32[64,4096]{1,0:T(8,128)S(1)}, f32[64,4096]{1,0:T(8,128)S(1)}, f32[64,4096]{1,0:T(8,128)S(1)}, f3...) custom-call(bf16[4,1024,256]{2,1,0:T(8,128)(2,1)S(1)} %convert_bitcast_fusion.2.x_ref, ...), custom_call_target="tpu_custom_call" | custom-call | flops 40000000000 | bytes 16000000 | tf_op jit(solution)/shard_map/chain_forward/pallas_call | solution.py:342
  172.5 5.5 all-to-all-start.1
  178.0 35.4 %all-to-all-done.1 = bf16[8,4,128,128]{3,2,1,0:T(8,128)(2,1)S(1)} async-done(((bf16[8,4,128,128]{3,2,1,0:T(8,128)(2,1)}), bf16[8,4,128,128]{3,2,1,0:T(8,128)(2,1)S(1)}, u32[]{:S(2)}, u32[]{:S(2)}) %all-to-all-start.1) | async-done | bytes 1048608 | tf_op jit(solution)/shard_map/all_to_all | solution.py:515
  218.2 12.1 all_to_all.50
  232.3 4.2 convolution_convert_fusion.4
  237.2 28.6 %reduce-scatter.10.cloned.1.call-done = bf16[128,2048]{1,0:T(8,128)(2,1)} async-done(((bf16[512,2048]{1,0:T(8,128)(2,1)}), bf16[128,2048]{1,0:T(8,128)(2,1)}) %reduce-scatter.10.cloned.1.call-update) | async-done | bytes 524304 | tf_op jit(solution)/shard_map/reduce_scatter | solution.py:609
  271.4 88.4 %all-gather.18.cloned.1.call-done = bf16[2048,1376]{0,1:T(8,128)(2,1)} async-done(((bf16[256,1376]{0,1:T(8,128)(2,1)}), bf16[2048,1376]{0,1:T(8,128)(2,1)}) %all-gather.18.cloned.1.call-update) | async-done | bytes 5636112 | tf_op jit(solution)/shard_map/all_gather | solution.py:570
  359.9 22.9 %all-gather.16.cloned.1.call-done = bf16[512,2048]{1,0:T(8,128)(2,1)} async-done(((bf16[128,2048]{1,0:T(8,128)(2,1)}), bf16[512,2048]{1,0:T(8,128)(2,1)}) %all-gather.16.cloned.1.call-update) | async-done | bytes 2097168 | tf_op jit(solution)/shard_map/all_gather | solution.py:615
  382.7 7.9 fusion.73
  390.7 86.3 %all-gather.20.cloned.1.call-done = bf16[2048,1376]{0,1:T(8,128)(2,1)} async-done(((bf16[256,1376]{0,1:T(8,128)(2,1)}), bf16[2048,1376]{0,1:T(8,128)(2,1)}) %all-gather.20.cloned.1.call-update) | async-done | bytes 5636112 | tf_op jit(solution)/shard_map/all_gather | solution.py:571
  477.0 7.9 fusion.74
  484.9 14.6 %all-gather.28.cloned.1.call-done = bf16[1,512,2048]{2,1,0:T(8,128)(2,1)} async-done(((bf16[1,128,2048]{2,1,0:T(8,128)(2,1)}), bf16[1,512,2048]{2,1,0:T(8,128)(2,1)}) %all-gather.28.cloned.1.call-update) | async-done | bytes 2097168 | tf_op jit(solution)/shard_map/all_gather | solution.py:574
  499.5 94.3 %all-gather.22.cloned.1.call-done = bf16[1376,2048]{1,0:T(8,128)(2,1)} async-done(((bf16[1376,256]{1,0:T(8,128)(2,1)}), bf16[1376,2048]{1,0:T(8,128)(2,1)}) %all-gather.22.cloned.1.call-update) | async-done | bytes 5636112 | tf_op jit(solution)/shard_map/all_gather | solution.py:572
  593.7 10.3 multiply_convert_fusion
  604.0 7.1 fusion.75
  611.1 4.8 add_convert_fusion
  616.0 29.7 %reduce-scatter.14.cloned.1.call-done = bf16[128,2048]{1,0:T(8,128)(2,1)} async-done(((bf16[512,2048]{1,0:T(8,128)(2,1)}), bf16[128,2048]{1,0:T(8,128)(2,1)}) %reduce-scatter.14.cloned.1.call-update) | async-done | bytes 524304 | tf_op jit(solution)/shard_map/reduce_scatter | solution.py:630
  650.2 22.7 %all-gather.24.cloned.1.call-done = bf16[512,2048]{1,0:T(8,128)(2,1)} async-done(((bf16[128,2048]{1,0:T(8,128)(2,1)}), bf16[512,2048]{1,0:T(8,128)(2,1)}) %all-gather.24.cloned.1.call-update) | async-done | bytes 2097168 | tf_op jit(solution)/shard_map/all_gather | solution.py:638
  672.9 3.5 convolution_convert_fusion.6
  677.4 4.3 all-to-all-start.3
  681.9 8.7 all-to-all-done.3
  690.6 2.8 multiply_reduce_fusion
  696.8 31.1 %all_to_all.51.d_ref = bf16[8,4,128,128]{3,2,1,0:T(8,128)(2,1)S(1)} all-to-all(bf16[8,4,128,128]{3,2,1,0:T(8,128)(2,1)S(1)} %bitcast.277), channel_id=1, replica_groups=mesh['seq'=8,'grp'=4] {'seq'}, dimensions={0} | all-to-all | bytes 2097152 | tf_op jit(solution)/shard_map/all_to_all | solution.py:529
  734.0 32.4 %chain_backward.1 = (bf16[4,1024,256]{2,1,0:T(8,128)(2,1)S(1)}, f32[8,4096]{1,0:T(8,128)S(1)}, f32[2,64,128]{2,1,0:T(8,128)S(1)}, f32[64,384]{1,0:T(8,128)S(1)}) custom-call(bf16[4,1024,256]{2,1,0:T(8,128)(2,1)S(1)} %copy-done.3, bf16[8,4,128,128]{3,2,1,0:T(8,128)(2,1)S(1)} %all_to_all.51.d_ref, f32[8,4096]{1,0:T(8,128)S(1)} %maximum_maximum_fusion.info_ref, ...), custom_call_target="tpu_custom_call" | custom-call | flops 80000000000 | bytes 20000000 | tf_op jit(solution)/shard_map/chain_backward/pallas_call | solution.py:372
  766.5 6.5 convert_bitcast_fusion
  774.8 3.7 fusion.67
  779.3 8.2 convolution_convert_fusion.1
  787.8 7.6 convolution_convert_fusion
  795.5 7.5 convolution_convert_fusion.2
  804.1 4.3 convolution_convert_fusion.3
  810.7 8.7 fusion.3
  820.7 7.2 convolution_convert_fusion.5
  828.1 39.9 %all-reduce.2 = (f32[2048]{0:T(1024)}, f32[2048]{0:T(1024)}, f32[2048]{0:T(1024)}, f32[2048]{0:T(1024)}) all-reduce(f32[2048]{0:T(1024)S(1)} %get-tuple-element.155, f32[2048]{0:T(1024)S(1)} %bitcast.306, f32[2048]{0:T(1024)S(1)} %bitcast.307, f32[2048]{0:T(1024)S(1)} %copy-done.36), channel_id=1, replica_groups=mesh['seq'=8,'grp'=4] {'seq','grp'}, use_global_device_ids=true, to_apply=%region_17.18 | all-reduce | flops 8192 | bytes 65536 | tf_op jit(solution)/shard_map/psum | solution.py:692
  870.2 4.5 all-to-all-start.5
  874.7 74.1 %all_gather.43 = f32[8,4,6400]{2,1,0:T(4,128)S(1)} all-gather(f32[1,4,6400]{2,1,0:T(4,128)} %all-reduce.5.cloned.1.call-done), channel_id=1, replica_groups=mesh['seq'=8,'grp'=4] {'seq'}, dimensions={0}, use_global_device_ids=true | all-gather | bytes 921600 | tf_op jit(solution)/shard_map/all_gather | solution.py:684
  952.7 44.5 %reduce-scatter.22.cloned.1.call-done = bf16[256,1376]{0,1:T(8,128)(2,1)} async-done(((bf16[2048,1376]{0,1:T(8,128)(2,1)}), bf16[256,1376]{0,1:T(8,128)(2,1)}) %reduce-scatter.22.cloned.1.call-update) | async-done | bytes 704528 | tf_op jit(solution)/shard_map/reduce_scatter | solution.py:712
  997.1 2.3 convert_element_type.291
  999.5 109.4 %reduce-scatter.24.cloned.1.call-done = bf16[256,1376]{0,1:T(8,128)(2,1)} async-done(((bf16[2048,1376]{0,1:T(8,128)(2,1)}), bf16[256,1376]{0,1:T(8,128)(2,1)}) %reduce-scatter.24.cloned.1.call-update) | async-done | bytes 704528 | tf_op jit(solution)/shard_map/reduce_scatter | solution.py:713
  1111.2 109.5 %reduce-scatter.26.cloned.1.call-done = bf16[1376,256]{1,0:T(8,128)(2,1)} async-done(((bf16[1376,2048]{1,0:T(8,128)(2,1)}), bf16[1376,256]{1,0:T(8,128)(2,1)}) %reduce-scatter.26.cloned.1.call-update) | async-done | bytes 704528 | tf_op jit(solution)/shard_map/reduce_scatter | solution.py:714
  1223.0 69.2 %reduce-scatter.20.cloned.1.call-done = bf16[512,256]{1,0:T(8,128)(2,1)} async-done(((bf16[512,2048]{1,0:T(8,128)(2,1)}), bf16[512,256]{1,0:T(8,128)(2,1)}) %reduce-scatter.20.cloned.1.call-update) | async-done | bytes 262160 | tf_op jit(solution)/shard_map/reduce_scatter | solution.py:710
  1294.0 88.7 %reduce-scatter.16.cloned.1.call-done = bf16[128,2048]{1,0:T(8,128)(2,1)} async-done(((bf16[1024,2048]{1,0:T(8,128)(2,1)}), bf16[128,2048]{1,0:T(8,128)(2,1)}) %reduce-scatter.16.cloned.1.call-update) | async-done | bytes 524304 | tf_op jit(solution)/shard_map/reduce_scatter | solution.py:660
  1384.1 32.6 %reduce-scatter.12.cloned.1.call-done = bf16[128,2048]{1,0:T(8,128)(2,1)} async-done(((bf16[512,2048]{1,0:T(8,128)(2,1)}), bf16[128,2048]{1,0:T(8,128)(2,1)}) %reduce-scatter.12.cloned.1.call-update) | async-done | bytes 524304 | tf_op jit(solution)/shard_map/reduce_scatter | solution.py:620
  1416.7 3.2 fusion.28
  (264 shorter events, 73.3 us)
Async XLA Ops:
  7.2 63.5 %copy-start = (f32[32,64,64]{2,1,0:T(8,128)S(1)}, f32[32,64,64]{2,1,0:T(8,128)}, u32[]{:S(2)}) copy-start(f32[32,64,64]{2,1,0:T(8,128)} %param.31) | copy-start | bytes 1572868
  7.2 97.7 %all-gather.26.cloned.1.call-start = ((), (), s32[]{:S(2)}) async-start(), calls=%async_computation.32 | async-start | bytes 4718592 | tf_op jit(solution)/shard_map/all_gather | solution.py:567
  7.9 131.6 %all-gather.12.cloned.1.call-start = ((), (), s32[]{:S(2)}) async-start(), calls=%async_computation.15 | async-start | bytes 5242880 | tf_op jit(solution)/shard_map/all_gather | solution.py:487
  12.6 51.8 %copy-start.48 = (s32[4,4]{1,0:T(4,128)S(1)}, s32[4,4]{1,0:T(4,128)}, u32[]{:S(2)}) copy-start(s32[4,4]{1,0:T(4,128)} %param.23) | copy-start | bytes 196
  12.6 54.1 %copy-start.47 = (f32[32]{0:T(128)S(1)}, f32[32]{0:T(128)}, u32[]{:S(2)}) copy-start(f32[32]{0:T(128)} %param.30) | copy-start | bytes 388
  63.6 167.9 %all-gather.14.cloned.1.call-start = ((), (), s32[]{:S(2)}) async-start(), calls=%async_computation.16 | async-start | bytes 2359296 | tf_op jit(solution)/shard_map/all_gather | solution.py:569
  67.9 40.3 %copy-start.32 = (bf16[4,1,1,2048]{3,1,0,2:T(2,128)(2,1)}, bf16[4,1,1,2048]{3,1,0,2:T(2,128)(2,1)S(1)}, u32[]{:S(2)}) copy-start(bf16[4,1,1,2048]{3,1,0,2:T(2,128)(2,1)S(1)} %constant_dynamic-slice_fusion.5) | copy-start | bytes 49156
  69.7 38.5 %copy-start.34 = (f32[2048]{0:T(1024)S(1)}, f32[2048]{0:T(1024)}, u32[]{:S(2)}) copy-start(f32[2048]{0:T(1024)} %param.24) | copy-start | bytes 24580
  108.4 31.2 %copy-start.42 = (f32[1024]{0:T(1024)}, f32[1024]{0:T(1024)S(1)}, u32[]{:S(2)}) copy-start(f32[1024]{0:T(1024)S(1)} %add_rsqrt_fusion) | copy-start | bytes 12292
  147.6 21.9 %copy-start.2 = (bf16[4,1024,256]{2,1,0:T(8,128)(2,1)}, bf16[4,1024,256]{2,1,0:T(8,128)(2,1)S(1)}, u32[]{:S(2)}) copy-start(bf16[4,1024,256]{2,1,0:T(8,128)(2,1)S(1)} %convert_bitcast_fusion.2.x_ref) | copy-start | bytes 6291460
  147.6 30.4 %copy-start.38 = (f32[2048]{0:T(1024)S(1)}, f32[2048]{0:T(1024)}, u32[]{:S(2)}) copy-start(f32[2048]{0:T(1024)} %param.36) | copy-start | bytes 24580
  147.6 30.4 %copy-start.37 = (f32[2048]{0:T(1024)S(1)}, f32[2048]{0:T(1024)}, u32[]{:S(2)}) copy-start(f32[2048]{0:T(1024)} %param.35) | copy-start | bytes 24580
  172.5 44.4 %copy-start.10 = (f32[8,4096]{1,0:T(8,128)}, f32[8,4096]{1,0:T(8,128)S(1)}, u32[]{:S(2)}) copy-start(f32[8,4096]{1,0:T(8,128)S(1)} %get-tuple-element.34.stat_ref) | copy-start | bytes 393220
  172.5 41.0 %all-to-all-start.1 = ((bf16[8,4,128,128]{3,2,1,0:T(8,128)(2,1)}), bf16[8,4,128,128]{3,2,1,0:T(8,128)(2,1)S(1)}, u32[]{:S(2)}, u32[]{:S(2)}) async-start(bf16[8,4,128,128]{3,2,1,0:T(8,128)(2,1)} %get-tuple-element.30), calls=%async_computation.1 | async-start | bytes 2097152 | tf_op jit(solution)/shard_map/all_to_all | solution.py:515
  178.0 87.8 %reduce-scatter.10.cloned.1.call-start = ((), (), s32[]{:S(2)}) async-start(), calls=%async_computation.17 | async-start | bytes 2621440 | tf_op jit(solution)/shard_map/reduce_scatter | solution.py:609
  236.5 29.2 %copy-start.12 = (bf16[1,128,2048]{2,1,0:T(8,128)(2,1)S(1)}, bf16[1,128,2048]{2,1,0:T(8,128)(2,1)}, u32[]{:S(2)}) copy-start(bf16[1,128,2048]{2,1,0:T(8,128)(2,1)} %param.21) | copy-start | bytes 1572868
  236.5 30.5 %copy-start.30 = (f32[2048]{0:T(1024)S(1)}, f32[2048]{0:T(1024)}, u32[]{:S(2)}) copy-start(f32[2048]{0:T(1024)} %param.38) | copy-start | bytes 24580
  236.6 123.3 %all-gather.18.cloned.1.call-start = ((), (), s32[]{:S(2)}) async-start(), calls=%async_computation.19 | async-start | bytes 6340608 | tf_op jit(solution)/shard_map/all_gather | solution.py:570
  237.1 145.6 %all-gather.16.cloned.1.call-start = ((), (), s32[]{:S(2)}) async-start(), calls=%async_computation.18 | async-start | bytes 2621440 | tf_op jit(solution)/shard_map/all_gather | solution.py:615
  267.1 380.8 %copy-start.40 = (f32[128]{0:T(128)}, f32[128]{0:T(128)S(1)}, u32[]{:S(2)}) copy-start(f32[128]{0:T(128)S(1)} %add_rsqrt_fusion.2) | copy-start | bytes 1540
  269.1 207.9 %all-gather.20.cloned.1.call-start = ((), (), s32[]{:S(2)}) async-start(), calls=%async_computation.20 | async-start | bytes 6340608 | tf_op jit(solution)/shard_map/all_gather | solution.py:571
  269.9 229.6 %all-gather.28.cloned.1.call-start = ((), (), s32[]{:S(2)}) async-start(), calls=%async_computation.33 | async-start | bytes 2621440 | tf_op jit(solution)/shard_map/all_gather | solution.py:574
  270.6 323.1 %all-gather.22.cloned.1.call-start = ((), (), s32[]{:S(2)}) async-start(), calls=%async_computation.21 | async-start | bytes 6340608 | tf_op jit(solution)/shard_map/all_gather | solution.py:572
  271.4 374.3 %reduce-scatter.14.cloned.1.call-start = ((), (), s32[]{:S(2)}) async-start(), calls=%async_computation.23 | async-start | bytes 2621440 | tf_op jit(solution)/shard_map/reduce_scatter | solution.py:630
  611.1 34.6 %copy-start.16 = (bf16[128,2048]{1,0:T(8,128)(2,1)S(1)}, bf16[128,2048]{1,0:T(8,128)(2,1)}, u32[]{:S(2)}) copy-start(bf16[128,2048]{1,0:T(8,128)(2,1)} %reduce-scatter.10.cloned.1.call-done) | copy-start | bytes 1572868
  615.9 32.0 %copy-start.22 = (bf16[1,128,2048]{2,1,0:T(8,128)(2,1)S(1)}, bf16[1,128,2048]{2,1,0:T(8,128)(2,1)}, u32[]{:S(2)}) copy-start(bf16[1,128,2048]{2,1,0:T(8,128)(2,1)} %param.22) | copy-start | bytes 1572868
  615.9 57.0 %all-gather.24.cloned.1.call-start = ((), (), s32[]{:S(2)}) async-start(), calls=%async_computation.24 | async-start | bytes 2621440 | tf_op jit(solution)/shard_map/all_gather | solution.py:638
  647.9 28.6 %copy-start.44 = (f32[128]{0:T(128)}, f32[128]{0:T(128)S(1)}, u32[]{:S(2)}) copy-start(f32[128]{0:T(128)S(1)} %broadcast_multiply_fusion.4) | copy-start | bytes 1540
  677.4 13.2 all-to-all-start.3
  681.7 186.2 %reduce-scatter.18.cloned.1.call-start = ((), (), s32[]{:S(2)}) async-start(), calls=%async_computation.26 | async-start | bytes 5242880 | tf_op jit(solution)/shard_map/reduce_scatter | solution.py:500
  734.0 32.5 %copy-start.25 = (bf16[1,1024,2048]{2,1,0:T(8,128)(2,1)S(1)}, bf16[1,1024,2048]{2,1,0:T(8,128)(2,1)}, u32[]{:S(2)}) copy-start(bf16[1,1024,2048]{2,1,0:T(8,128)(2,1)} %all-gather.26.cloned.1.call-done) | copy-start | bytes 12582916
  734.0 32.5 %copy-start.35 = (f32[2048]{0:T(1024)S(1)}, f32[2048]{0:T(1024)}, u32[]{:S(2)}) copy-start(f32[2048]{0:T(1024)} %param.24) | copy-start | bytes 24580
  734.0 32.5 %copy-start.43 = (f32[1024]{0:T(1024)S(1)}, f32[1024]{0:T(1024)}, u32[]{:S(2)}) copy-start(f32[1024]{0:T(1024)} %copy-done.42) | copy-start | bytes 12292
  773.1 101.7 %all-reduce.5.cloned.1.call-start = ((), (), s32[]{:S(2)}) async-start(), calls=%async_computation.27 | async-start | bytes 204800 | tf_op jit(solution)/shard_map/psum | solution.py:684
  779.3 217.9 %reduce-scatter.22.cloned.1.call-start = ((), (), s32[]{:S(2)}) async-start(), calls=%async_computation.29 | async-start | bytes 6340608 | tf_op jit(solution)/shard_map/reduce_scatter | solution.py:712
  787.5 321.4 %reduce-scatter.24.cloned.1.call-start = ((), (), s32[]{:S(2)}) async-start(), calls=%async_computation.30 | async-start | bytes 6340608 | tf_op jit(solution)/shard_map/reduce_scatter | solution.py:713
  795.4 425.3 %reduce-scatter.26.cloned.1.call-start = ((), (), s32[]{:S(2)}) async-start(), calls=%async_computation.31 | async-start | bytes 6340608 | tf_op jit(solution)/shard_map/reduce_scatter | solution.py:714
  803.1 489.2 %reduce-scatter.20.cloned.1.call-start = ((), (), s32[]{:S(2)}) async-start(), calls=%async_computation.28 | async-start | bytes 2359296 | tf_op jit(solution)/shard_map/reduce_scatter | solution.py:710
  808.4 574.3 %reduce-scatter.16.cloned.1.call-start = ((), (), s32[]{:S(2)}) async-start(), calls=%async_computation.25 | async-start | bytes 4718592 | tf_op jit(solution)/shard_map/reduce_scatter | solution.py:660
  819.4 597.2 %reduce-scatter.12.cloned.1.call-start = ((), (), s32[]{:S(2)}) async-start(), calls=%async_computation.22 | async-start | bytes 2621440 | tf_op jit(solution)/shard_map/reduce_scatter | solution.py:620
  870.2 549.7 %all-to-all-start.5 = ((bf16[8,1,256,256]{2,3,1,0:T(8,128)(2,1)}), bf16[8,1,256,256]{2,3,1,0:T(8,128)(2,1)S(1)}, u32[]{:S(2)}, u32[]{:S(2)}) async-start(bf16[8,1,256,256]{2,3,1,0:T(8,128)(2,1)} %copy.214), calls=%async_computation.10 | async-start | bytes 2097152 | tf_op jit(solution)/shard_map/all_to_all | solution.py:502
  999.4 383.3 %copy-start.13 = (bf16[1,128,2048]{2,1,0:T(8,128)(2,1)S(1)}, bf16[1,128,2048]{2,1,0:T(8,128)(2,1)}, u32[]{:S(2)}) copy-start(bf16[1,128,2048]{2,1,0:T(8,128)(2,1)} %param.21) | copy-start | bytes 1572868
  999.4 417.2 %copy-start.17 = (bf16[128,2048]{1,0:T(8,128)(2,1)S(1)}, bf16[128,2048]{1,0:T(8,128)(2,1)}, u32[]{:S(2)}) copy-start(bf16[128,2048]{1,0:T(8,128)(2,1)} %reduce-scatter.10.cloned.1.call-done) | copy-start | bytes 1572868
  999.4 417.2 %copy-start.21 = (bf16[128,2048]{1,0:T(8,128)(2,1)S(1)}, bf16[128,2048]{1,0:T(8,128)(2,1)}, u32[]{:S(2)}) copy-start(bf16[128,2048]{1,0:T(8,128)(2,1)} %reduce-scatter.14.cloned.1.call-done) | copy-start | bytes 1572868
  999.4 417.2 %copy-start.23 = (bf16[1,128,2048]{2,1,0:T(8,128)(2,1)S(1)}, bf16[1,128,2048]{2,1,0:T(8,128)(2,1)}, u32[]{:S(2)}) copy-start(bf16[1,128,2048]{2,1,0:T(8,128)(2,1)} %param.22) | copy-start | bytes 1572868
  999.4 417.2 %copy-start.31 = (f32[2048]{0:T(1024)S(1)}, f32[2048]{0:T(1024)}, u32[]{:S(2)}) copy-start(f32[2048]{0:T(1024)} %param.38) | copy-start | bytes 24580
  999.5 417.2 %copy-start.41 = (f32[128]{0:T(128)S(1)}, f32[128]{0:T(128)}, u32[]{:S(2)}) copy-start(f32[128]{0:T(128)} %copy-done.40) | copy-start | bytes 1540
  999.5 417.2 %copy-start.45 = (f32[128]{0:T(128)S(1)}, f32[128]{0:T(128)}, u32[]{:S(2)}) copy-start(f32[128]{0:T(128)} %copy-done.44) | copy-start | bytes 1540
  (25 other events, 112.2 us)
Sparse Core Ops, SparseCore 0:
  10.2 94.7 all-gather.25
  107.1 32.4 all-gather.11
  141.6 67.7 all-gather.13
  236.7 29.0 reduce-scatter.9
  267.8 91.9 all-gather.17
  361.9 20.7 all-gather.15
  385.0 91.9 all-gather.19
  478.6 20.7 all-gather.27
  501.7 91.9 all-gather.21
  616.0 29.6 reduce-scatter.13
  650.3 22.5 all-gather.23
  773.2 42.6 reduce-scatter.17
  818.9 29.4 all-reduce.4
  851.9 145.1 reduce-scatter.21
  1000.6 108.2 reduce-scatter.23
  1112.4 108.2 reduce-scatter.25
  1224.1 68.0 reduce-scatter.19
  1295.7 86.9 reduce-scatter.15
  1385.4 31.1 reduce-scatter.11

commit v2 on v1

--- a/solution.py
+++ b/solution.py
@@ -66,7 +66,7 @@
 
 
 def forward_kernel(
-    heads, x_ref, info_ref, gb_ref, init_ref, out_ref, n_ref, r_ref, nb_ref, stat_ref, w_ref, state
+    heads, idx_ref, x_ref, info_ref, gb_ref, init_ref, out_ref, n_ref, r_ref, nb_ref, stat_ref, w_ref, state
 ):
     head_dim = gb_ref.shape[1]
     tokens = x_ref.shape[1]
@@ -85,7 +85,6 @@
     q_rows = chunk_rows(x, heads, (0, head_dim))
     k_rows = chunk_rows(x, heads, (head_dim, 2 * head_dim))
     v_rows = chunk_rows(x, heads, (2 * head_dim, 3 * head_dim))
-    g_rows = chunk_rows(x, heads, (3 * head_dim, 4 * head_dim))
     q_t = jnp.transpose(q_rows.astype(F32))
     target_t = jnp.transpose(v_rows.astype(F32) - k_rows.astype(F32))
     mb_row, mb_col, t_row, t_col, same, columns = chunk_masks(info, heads, count)
@@ -146,17 +145,19 @@
     wide_gain = jnp.concatenate([gain] * repeats, axis=1)
     wide_shift = jnp.concatenate([shift] * repeats, axis=1)
     out_rows = jnp.transpose(q_t + nb * wide_gain + wide_shift)
-    packed = jnp.concatenate([out_rows.astype(BF16), g_rows], axis=1)
     for m in range(tokens // MB):
         for h in range(heads):
             at = (m * heads + h) * MB
-            out_ref[0, h, m * MB : (m + 1) * MB, :] = packed[at : at + MB]
+            out_ref[m * MB : (m + 1) * MB, h * head_dim : (h + 1) * head_dim] = out_rows[
+                at : at + MB
+            ]
     base = jnp.where(info[4:5, 0:1] > 0.5, init, carried)
     state[...] = base - mm((r_ref[...] * info[3:4, :]).astype(BF16), k_aug)
 
 
 def backward_kernel(
     heads,
+    idx_ref,
     x_ref,
     d_ref,
     info_ref,
@@ -190,14 +191,17 @@
     init = init_ref[...]
     info = info_ref[...]
     x = x_ref[...]
-    d_in = d_ref[0]
+    d_in = d_ref[...]
     q_rows = chunk_rows(x, heads, (0, head_dim))
     k_rows = chunk_rows(x, heads, (head_dim, 2 * head_dim))
     v_rows = chunk_rows(x, heads, (2 * head_dim, 3 * head_dim))
-    d_rows = chunk_rows(d_in, heads, (0, head_dim))
-    dg_rows = chunk_rows(d_in, heads, (head_dim, 2 * head_dim))
+    d_heads = [d_in[:, h * head_dim : (h + 1) * head_dim] for h in range(heads)]
+    d_rows = jnp.concatenate(
+        [d_heads[h][m * MB : (m + 1) * MB] for m in range(tokens // MB) for h in range(heads)],
+        axis=0,
+    )
     target_t = jnp.transpose(v_rows.astype(F32) - k_rows.astype(F32))
-    d_t = jnp.transpose(d_rows.astype(F32))
+    d_t = jnp.transpose(d_rows)
     mb_row, mb_col, t_row, t_col, same, columns = chunk_masks(info, heads, count)
     earlier = same & (mb_row < mb_col)
     later = same & (mb_row > mb_col)
@@ -290,7 +294,7 @@
             [jnp.where(is_init, 0.0, own), jnp.where(is_init, own, 0.0)], axis=1
         ).astype(BF16)
 
-    dq = d_rows.astype(F32) + mm(d_cross, k_rows) + mm(by_state(zb_rows), w_both)
+    dq = d_rows + mm(d_cross, k_rows) + mm(by_state(zb_rows), w_both)
     r_own = jnp.where(is_last, augment(r_rows, heads, head_dim, wide), 0.0).astype(BF16)
     dk = (
         e_rows
@@ -299,9 +303,7 @@
         + mm(by_state(z_rows), w_both)
         - mm(r_own, d_stack)
     )
-    packed = jnp.concatenate(
-        [dq.astype(BF16), dk.astype(BF16), (-e_rows).astype(BF16), dg_rows], axis=1
-    )
+    packed = jnp.concatenate([dq.astype(BF16), dk.astype(BF16), (-e_rows).astype(BF16)], axis=1)
     for m in range(tokens // MB):
         for h in range(heads):
             at = (m * heads + h) * MB
@@ -322,101 +324,115 @@
 def chain_specs(heads, tokens, head_dim, full, at):
     count = heads * tokens
     return dict(
-        x=pl.BlockSpec((heads, tokens, 4 * head_dim), lambda i: (0, at(i), 0)),
-        pair=pl.BlockSpec((1, heads, tokens, 2 * head_dim), lambda i: (at(i), 0, 0, 0)),
-        info=pl.BlockSpec((8, count), lambda i: (0, at(i))),
-        gb=pl.BlockSpec((2, head_dim, 128), lambda i: (0, 0, 0)),
-        init=pl.BlockSpec((head_dim, full), lambda i: (0, 0)),
-        tall=pl.BlockSpec((head_dim, count), lambda i: (0, at(i))),
-        weight=pl.BlockSpec((1, head_dim, full), lambda i: (at(i), 0, 0)),
-    )
-
-
-def chain_forward(x4, info, gb, init, tokens):
-    heads, total, packed = x4.shape
-    head_dim = packed // 4
+        x=pl.BlockSpec((heads, tokens, 3 * head_dim), lambda i, idx: (0, idx[at(i)], 0)),
+        rows=pl.BlockSpec((tokens, heads * head_dim), lambda i, idx: (idx[at(i)], 0)),
+        info=pl.BlockSpec((8, count), lambda i, idx: (0, idx[at(i)])),
+        gb=pl.BlockSpec((2, head_dim, 128), lambda i, idx: (0, 0, 0)),
+        init=pl.BlockSpec((head_dim, full), lambda i, idx: (0, 0)),
+        tall=pl.BlockSpec((head_dim, count), lambda i, idx: (0, at(i))),
+        stat=pl.BlockSpec((8, count), lambda i, idx: (0, at(i))),
+        weight=pl.BlockSpec((1, head_dim, full), lambda i, idx: (at(i), 0, 0)),
+    )
+
+
+def chain_forward(idx, x3, info, gb, init, tokens):
+    heads, total, packed = x3.shape
+    head_dim = packed // 3
     chunks = total // tokens
     full = init.shape[1]
     s = chain_specs(heads, tokens, head_dim, full, lambda i: i)
     tall = jax.ShapeDtypeStruct((head_dim, heads * total), F32)
     return pl.pallas_call(
         partial(forward_kernel, heads),
-        grid=(chunks,),
-        in_specs=[s["x"], s["info"], s["gb"], s["init"]],
-        out_specs=[s["pair"], s["tall"], s["tall"], s["tall"], s["info"], s["weight"]],
+        grid_spec=pltpu.PrefetchScalarGridSpec(
+            num_scalar_prefetch=1,
+            grid=(chunks,),
+            in_specs=[s["x"], s["info"], s["gb"], s["init"]],
+            out_specs=[s["rows"], s["tall"], s["tall"], s["tall"], s["stat"], s["weight"]],
+            scratch_shapes=[pltpu.VMEM((head_dim, full), F32)],
+        ),
         out_shape=[
-            jax.ShapeDtypeStruct((chunks, heads, tokens, 2 * head_dim), BF16),
+            jax.ShapeDtypeStruct((total, heads * head_dim), F32),
             tall,
             tall,
             tall,
             jax.ShapeDtypeStruct((8, heads * total), F32),
             jax.ShapeDtypeStruct((chunks, head_dim, full), F32),
         ],
-        scratch_shapes=[pltpu.VMEM((head_dim, full), F32)],
         compiler_params=pltpu.CompilerParams(
             dimension_semantics=("arbitrary",), vmem_limit_bytes=32 * 1024 * 1024
         ),
         cost_estimate=pl.CostEstimate(
-            flops=40_000_000_000, bytes_accessed=16_000_000, transcendentals=0
+            flops=20_000_000_000, bytes_accessed=16_000_000, transcendentals=0
         ),
         name="chain_forward",
-    )(x4, info, gb, init)
-
-
-def chain_backward(x4, d_pair, info, gb, init, kept, tokens):
-    heads, total, packed = x4.shape
-    head_dim = packed // 4
+    )(idx, x3, info, gb, init)
+
+
+def chain_backward(idx, x3, d_inner, info, gb, init, kept, tokens):
+    heads, total, packed = x3.shape
+    head_dim = packed // 3
     chunks = total // tokens
     full = init.shape[1]
     s = chain_specs(heads, tokens, head_dim, full, lambda i: chunks - 1 - i)
     return pl.pallas_call(
         partial(backward_kernel, heads),
-        grid=(chunks,),
-        in_specs=[
-            s["x"],
-            s["pair"],
-            s["info"],
-            s["gb"],
-            s["init"],
-            s["tall"],
-            s["tall"],
-            s["tall"],
-            s["info"],
-            s["weight"],
-        ],
-        out_specs=[s["x"], s["info"], s["gb"], s["init"]],
+        grid_spec=pltpu.PrefetchScalarGridSpec(
+            num_scalar_prefetch=1,
+            grid=(chunks,),
+            in_specs=[
+                s["x"],
+                s["rows"],
+                s["info"],
+                s["gb"],
+                s["init"],
+                s["tall"],
+                s["tall"],
+                s["tall"],
+                s["stat"],
+                s["weight"],
+            ],
+            out_specs=[s["x"], s["info"], s["gb"], s["init"]],
+            scratch_shapes=[pltpu.VMEM((head_dim, full), F32)],
+        ),
         out_shape=[
-            jax.ShapeDtypeStruct(x4.shape, BF16),
+            jax.ShapeDtypeStruct(x3.shape, BF16),
             jax.ShapeDtypeStruct((8, heads * total), F32),
             jax.ShapeDtypeStruct(gb.shape, F32),
             jax.ShapeDtypeStruct(init.shape, F32),
         ],
-        scratch_shapes=[pltpu.VMEM((head_dim, full), F32)],
         compiler_params=pltpu.CompilerParams(
             dimension_semantics=("arbitrary",), vmem_limit_bytes=40 * 1024 * 1024
         ),
         cost_estimate=pl.CostEstimate(
-            flops=80_000_000_000, bytes_accessed=20_000_000, transcendentals=0
+            flops=30_000_000_000, bytes_accessed=20_000_000, transcendentals=0
         ),
         name="chain_backward",
-    )(x4, d_pair, info, gb, init, *kept)
-
-
-def chain_setup(starting, rates, init_weight, init_bias, inner_gain, inner_bias, blocks):
+    )(idx, x3, d_inner, info, gb, init, *kept)
+
+
+def chain_info(starts, chunk_start, rates, heads, tokens):
+    blocks = tokens // MB
+    chunks = chunk_start.shape[0]
+
+    def begun(limit):
+        return jnp.sum((starts < limit[..., None]).astype(jnp.int32), -1)
+
+    at = chunk_start[:, None] + jnp.arange(blocks, dtype=jnp.int32) * MB
+    doc = begun(at + 1)
+    before = begun(chunk_start)[:, None]
+    end = begun(chunk_start + tokens)[:, None]
+    fresh = jnp.broadcast_to(end > before, doc.shape)
+    spread = jnp.stack(
+        [item.astype(F32) for item in (doc, doc > before, doc == end, fresh)]
+    ).reshape(4, chunks * blocks, 1)
+    spread = jnp.broadcast_to(spread, (4, chunks * blocks, heads * MB)).reshape(4, -1)
+    rate_row = jnp.swapaxes(rates.reshape(-1, MB, heads), 1, 2).reshape(1, -1)
+    return jnp.concatenate([rate_row, spread, jnp.zeros((3, rate_row.shape[1]), F32)], axis=0)
+
+
+def chain_params(init_weight, init_bias, inner_gain, inner_bias):
     heads, head_dim, _ = init_weight.shape
-    count = starting.shape[0]
-    doc = jnp.cumsum(starting.astype(jnp.int32))
-    by_chunk = doc.reshape(-1, blocks)
-    before = jnp.concatenate([jnp.zeros((1,), jnp.int32), by_chunk[:-1, -1]])
-    use_init = by_chunk > before[:, None]
-    in_last = by_chunk == by_chunk[:, -1:]
-    fresh = jnp.broadcast_to(use_init[:, -1:], use_init.shape)
-    spread = jnp.stack(
-        [by_chunk, use_init.astype(jnp.int32), in_last.astype(jnp.int32), fresh.astype(jnp.int32)]
-    ).astype(F32).reshape(4, count)
-    spread = jnp.broadcast_to(spread[:, :, None], (4, count, heads * MB)).reshape(4, -1)
-    rate_row = jnp.swapaxes(rates.reshape(count, MB, heads), 1, 2).reshape(1, -1)
-    info = jnp.concatenate([rate_row, spread, jnp.zeros((3, rate_row.shape[1]), F32)], axis=0)
     reps = 128 // (MB * heads)
 
     def pattern(item):
@@ -433,7 +449,7 @@
         ],
         axis=1,
     )
-    return info, gb, init
+    return gb, init
 
 
 def chain_param_grads(dgb, dinit, heads):
@@ -451,6 +467,97 @@
     )
 
 
+def tie(*values):
+    return lax.optimization_barrier(values)
+
+
+def ring_pairs(size, step):
+    order = list(range(0, size, 2)) + list(range(size - 1, 0, -2))
+    return [(order[i], order[(i + step) % size]) for i in range(size)]
+
+
+def ring_place(size, index):
+    return jnp.where(index % 2 == 0, index // 2, size - (index + 1) // 2)
+
+
+def ring_member(size, place):
+    return jnp.where(place < size // 2, 2 * place, 2 * (size - place) - 1)
+
+
+def slot_steps(size):
+    steps = [0]
+    for s in range(1, size // 2):
+        steps += [-s, s]
+    return steps + [-(size // 2)]
+
+
+def ring_gather(block, size):
+    arrived = [(block,)]
+    ahead = back = block
+    for s in range(1, size // 2 + 1):
+        ahead = lax.ppermute(ahead, "seq", ring_pairs(size, 1))
+        if s < size // 2:
+            back = lax.ppermute(back, "seq", ring_pairs(size, -1))
+            ahead, back = tie(ahead, back)
+            arrived.append((ahead, back))
+        else:
+            arrived.append((ahead,))
+    return arrived
+
+
+def ring_scatter(part, size):
+    half = size // 2
+    ahead, back = part(half).astype(BF16), part(1 - half).astype(BF16)
+    for s in range(1, half + 1):
+        ahead, back = tie(ahead, back)
+        ahead = lax.ppermute(ahead, "seq", ring_pairs(size, 1)).astype(F32)
+        if s < half:
+            back = lax.ppermute(back, "seq", ring_pairs(size, -1)).astype(F32)
+            ahead = (ahead + part(half - s)).astype(BF16)
+            if s < half - 1:
+                back = (back + part(1 - half + s)).astype(BF16)
+    return part(0) + ahead + back
+
+
+def pairwise_sum(value, axis, size):
+    bit = 1
+    while bit < size:
+        value = value + lax.ppermute(value, axis, [(i, i ^ bit) for i in range(size)])
+        bit *= 2
+    return value
+
+
+def swap(value, bit):
+    return lax.ppermute(value, "grp", [(i, i ^ bit) for i in range(4)])
+
+
+def grp_gather(value):
+    if lax.axis_size("grp") != 4:
+        return lax.all_gather(value, "grp", axis=0)
+    index = lax.axis_index("grp")
+    across = swap(value, 2)
+    beside = swap(value, 1)
+    corner = swap(across, 1)
+    out = jnp.zeros((4,) + value.shape, value.dtype)
+    for k, block in enumerate((value, beside, across, corner)):
+        out = lax.dynamic_update_index_in_dim(out, block, index ^ k, 0)
+    return out
+
+
+def grp_scatter(value):
+    if lax.axis_size("grp") != 4:
+        return lax.psum_scatter(value.astype(BF16), "grp", scatter_dimension=0, tiled=False)
+    index = lax.axis_index("grp")
+
+    def block(k):
+        return lax.dynamic_index_in_dim(value, index ^ k, 0, keepdims=False)
+
+    corner = swap(block(3).astype(BF16), 1).astype(F32)
+    across = swap((corner + block(2)).astype(BF16), 2).astype(F32)
+    beside = swap(block(1).astype(BF16), 1).astype(F32)
+    return (block(0) + beside + across).astype(BF16)
+
+
 class HeadPlan:
     def __init__(self, heads, seq, grp):
         self.seq, self.grp, self.heads = seq, grp, heads
@@ -474,59 +581,39 @@
         return item.reshape((self.heads,) + rest)
 
 
-def gather_heads(plan, mats, head_dim):
-    rows = mats[0].shape[0]
+def exchange(block):
+    return lax.all_to_all(block, "seq", 0, 0, tiled=True)
+
+
+def gather_heads(plan, mats, head_dim, gather):
+    cols = mats[0].shape[1]
     count = len(mats)
+    seq = plan.seq
     if plan.mixed:
-        block = jnp.stack(
-            [m.reshape(rows, plan.seq, plan.each, head_dim) for m in mats], axis=3
-        )
-        block = block.transpose(1, 2, 0, 3, 4).reshape(plan.seq, plan.each, rows, -1)
-        block = lax.all_to_all(block, "seq", 0, 0, tiled=True)
-        block = jnp.swapaxes(block, 0, 1).reshape(plan.each, plan.seq * rows, -1)
-        return lax.all_gather(block, "grp", axis=0, tiled=True)
-    block = lax.all_gather(jnp.stack(mats), "grp", axis=2, tiled=True)
-    block = block.reshape(count, rows, plan.seq, plan.local, head_dim)
-    block = block.transpose(2, 3, 1, 0, 4).reshape(plan.seq, plan.local, rows, -1)
-    block = lax.all_to_all(block, "seq", 0, 0, tiled=True)
-    return jnp.swapaxes(block, 0, 1).reshape(plan.local, plan.seq * rows, -1)
-
-
-def scatter_heads(plan, grads, count):
-    local, all_rows, packed = grads.shape
-    rows = all_rows // plan.seq
+        block = jnp.stack([m.reshape(seq, plan.each, head_dim, cols) for m in mats], axis=2)
+        block = exchange(block.reshape(seq, -1, cols))
+        block = block.transpose(1, 0, 2).reshape(plan.each, count * head_dim, seq * cols)
+        return gather(block).reshape(plan.local, count * head_dim, seq * cols)
+    block = lax.all_gather(jnp.stack(mats), "grp", axis=1, tiled=True)
+    block = block.reshape(count, seq, plan.local, head_dim, cols).transpose(1, 2, 0, 3, 4)
+    block = exchange(block.reshape(seq, -1, cols))
+    return block.transpose(1, 0, 2).reshape(plan.local, count * head_dim, seq * cols)
+
+
+def scatter_heads(plan, grads, count, scatter):
+    local, packed, width = grads.shape
+    seq = plan.seq
+    cols = width // seq
     head_dim = packed // count
     if plan.mixed:
-        grads = lax.psum_scatter(grads, "grp", scatter_dimension=0, tiled=True)
-        block = jnp.swapaxes(grads.reshape(plan.each, plan.seq, rows, packed), 0, 1)
-        block = lax.all_to_all(block, "seq", 0, 0, tiled=True)
-        block = block.reshape(plan.seq * plan.each, rows, count, head_dim)
-        out = block.transpose(2, 1, 0, 3).reshape(count, rows, -1)
-    else:
-        block = jnp.swapaxes(grads.reshape(local, plan.seq, rows, packed), 0, 1)
-        block = lax.all_to_all(block, "seq", 0, 0, tiled=True)
-        block = block.reshape(plan.heads, rows, count, head_dim)
-        block = block.transpose(2, 1, 0, 3).reshape(count, rows, -1)
-        out = lax.psum_scatter(block, "grp", scatter_dimension=2, tiled=True)
-    return out.astype(jnp.float32)
-
-
-def to_owner(plan, pair):
-    got = lax.all_to_all(pair, "seq", 0, 0, tiled=True)
-    tokens, packed = got.shape[2:]
-    got = plan.order(got.reshape(plan.seq, plan.local, tokens, 2, packed // 2))
-    return got.transpose(2, 1, 0, 3).reshape(2, tokens, -1)
-
-
-def from_owner(plan, first, second, head_dim):
-    tokens = first.shape[0]
-    both = jnp.stack([first, second], axis=1).reshape(tokens, 2, plan.heads, head_dim)
-    both = both.transpose(2, 0, 1, 3).reshape(plan.heads, tokens, 2 * head_dim)
-    if plan.mixed:
-        both = both.reshape(plan.grp, plan.seq, plan.each, tokens, 2 * head_dim)
-        both = jnp.swapaxes(both, 0, 1)
-    both = both.reshape(plan.seq, plan.local, tokens, 2 * head_dim)
-    return lax.all_to_all(both, "seq", 0, 0, tiled=True)
+        block = scatter(grads.reshape(plan.grp, plan.each * packed, width))
+        block = block.reshape(-1, seq, cols).transpose(1, 0, 2)
+        block = exchange(block).reshape(seq, plan.each, count, head_dim, cols)
+        return block.transpose(2, 0, 1, 3, 4).reshape(count, -1, cols).astype(F32)
+    block = grads.astype(BF16).reshape(local * packed, seq, cols).transpose(1, 0, 2)
+    block = exchange(block).reshape(seq, local, count, head_dim, cols)
+    block = block.transpose(2, 0, 1, 3, 4).reshape(count, -1, cols)
+    return lax.psum_scatter(block, "grp", scatter_dimension=1, tiled=True).astype(F32)
 
 
 def body(
@@ -561,105 +648,163 @@
     heads, head_dim, _ = init_weight.shape
     plan = HeadPlan(heads, seq, groups)
     local = plan.local
+    features = local * head_dim
     stream = rows_tok * seq
-    all_rows = groups * rows_tok
-
-    stream_rows = lax.all_gather(tokens[0], "seq", axis=0, tiled=True).astype(F32)
-    w_heads = gather_heads(plan, (w_query, w_key, w_value, w_gate), head_dim)
-    m_out = lax.all_gather(w_out, "seq", axis=1, tiled=True)
-    m_swish = lax.all_gather(w_swish, "seq", axis=0, tiled=True)
-    m_up = lax.all_gather(w_up, "seq", axis=0, tiled=True)
-    m_down = lax.all_gather(w_down, "seq", axis=1, tiled=True)
-    grad_own = cotangent[0]
-    grad_rows = lax.all_gather(grad_own, "grp", axis=0, tiled=True)
+    far = partial(lax.all_gather, axis_name="grp", axis=0)
+    steps = slot_steps(seq)
+    place = ring_place(seq, seq_index)
+    member_of_slot = ring_member(seq, (place + jnp.array(steps, jnp.int32)) % seq)
+    apart = (ring_place(seq, jnp.arange(seq, dtype=jnp.int32)) - place) % seq
+    slot_of_member = jnp.where(apart >= seq // 2, 2 * (seq - apart) - 1, 2 * apart)
+    slot_of_member = jnp.where(apart == 0, 0, slot_of_member)
+    to_slots = (member_of_slot[:, None] == jnp.arange(seq)[None, :]).astype(F32)
+
+    def in_slots(stat):
+        cut = stat.reshape(-1, seq, rows_tok)
+        out = jnp.einsum("sm,kmt->kst", to_slots, cut, precision=lax.Precision.HIGHEST)
+        return out.reshape(-1, stream)
+
+    def in_order(stat):
+        cut = stat.reshape(-1, seq, rows_tok)
+        out = jnp.einsum("sm,kst->kmt", to_slots, cut, precision=lax.Precision.HIGHEST)
+        return out.reshape(-1, stream)
+
+    def by_distance(rows):
+        cut = rows.reshape(seq, rows_tok, width)
+        return lambda k: cut[steps.index(k if k < seq // 2 else k - seq)]
+
+    w_proj = gather_heads(plan, (w_query.T, w_key.T, w_value.T), head_dim, grp_gather)
+    token_steps = ring_gather(tokens[0], seq)
+    stream_rows = jnp.concatenate(sum(token_steps, ()), axis=0).astype(F32)
+    w_side = gather_heads(plan, (w_gate.T, w_out), head_dim, grp_gather)
+    grad_own, _ = tie(cotangent[0], token_steps[-1][0])
+    grad_steps = ring_gather(grad_own, seq)
+    share = w_down.shape[0] // seq
+    padded = share + -share % MB
+
+    def cut_hidden(mat):
+        cut = mat.reshape(seq, share, mat.shape[1])
+        return jnp.pad(cut, ((0, 0), (0, padded - share), (0, 0)))
+
+    ffn_block = jnp.concatenate([cut_hidden(m) for m in (w_swish.T, w_up.T, w_down)], axis=1)
+    ffn_block, _ = tie(ffn_block, token_steps[-1][0])
+    ffn_block = exchange(ffn_block).transpose(1, 0, 2).reshape(3 * padded, width)
+    ffn_all = far(ffn_block).reshape(groups, 3, padded, width)
+    m_swish, m_up, m_down = (ffn_all[:, i].reshape(groups * padded, width) for i in range(3))
+    m_gate = w_side[:, :head_dim].reshape(features, width)
+    m_out = w_side[:, head_dim:].reshape(features, width)
 
     own_lengths = lax.dynamic_index_in_dim(lengths, grp_index, 0, keepdims=False)
     ends = jnp.cumsum(own_lengths)
     starts = ends - own_lengths
-    live = (jnp.arange(stream, dtype=jnp.int32) < ends[-1]).astype(F32)[:, None]
-    block_pos = jnp.arange(stream // MB, dtype=jnp.int32) * MB
-    starting = jnp.any(block_pos[:, None] == starts[None, :], -1)
+    chunk_start = member_of_slot * rows_tok
+    positions = (chunk_start[:, None] + jnp.arange(rows_tok, dtype=jnp.int32)).reshape(stream, 1)
+    live = (positions < ends[-1]).astype(F32)
 
     inv_first = lax.rsqrt(jnp.mean(stream_rows * stream_rows, -1, keepdims=True) + EPS)
     unit_all = stream_rows * inv_first
     normed = (unit_all * prenorm_gain).astype(BF16)
-    x4 = lax.dot_general(
-        normed, w_heads, (((1,), (1,)), ((), ())), preferred_element_type=F32
-    ).astype(BF16)
-    x4 = x4.transpose(1, 0, 2)
-    rate_cols = plan.pick(rate_weight.T, seq_index).T
-    logits = mm(normed, rate_cols) + plan.pick(rate_bias, seq_index)
+    x3 = jnp.stack([mm_nt(normed, w_proj[h]).astype(BF16) for h in range(local)])
+    gate_pre = mm_nt(normed, m_gate)
+    rate_rows = plan.pick(rate_weight.T, seq_index)
+    logits = mm_nt(normed, rate_rows) + plan.pick(rate_bias, seq_index)
     rate_sig = jax.nn.sigmoid(logits)
     rates = rate_sig / head_dim * live
-    own_params = [
-        plan.pick(item, seq_index) for item in (init_weight, init_bias, inner_gain, inner_bias)
-    ]
-    info, gb, init = chain_setup(starting, rates, *own_params, rows_tok // MB)
-    pair, *kept = chain_forward(x4, info, gb, init, rows_tok)
-    inner, gate_pre = to_owner(plan, pair).astype(F32)
-
-    mean_o = jnp.mean(inner, -1, keepdims=True)
-    inv_o = lax.rsqrt(jnp.mean(inner * inner, -1, keepdims=True) - mean_o * mean_o + EPS)
+    gb, init = chain_params(
+        *(plan.pick(item, seq_index) for item in (init_weight, init_bias, inner_gain, inner_bias))
+    )
+    info = chain_info(starts, chunk_start, rates, local, rows_tok)
+    inner, *kept = chain_forward(slot_of_member, x3, info, gb, init, rows_tok)
+
+    sums = jnp.stack([jnp.sum(inner, -1), jnp.sum(inner * inner, -1)])
+    sums = in_slots(pairwise_sum(in_order(sums), "seq", seq)) / width
+    mean_o = sums[0][:, None]
+    inv_o = lax.rsqrt(sums[1][:, None] - mean_o * mean_o + EPS)
     o_hat = (inner - mean_o) * inv_o
-    post = o_hat * post_gain + post_bias
+    post_g = plan.pick(post_gain.reshape(heads, head_dim), seq_index).reshape(features)
+    post_b = plan.pick(post_bias.reshape(heads, head_dim), seq_index).reshape(features)
+    post = o_hat * post_g + post_b
     gelu_val, gelu_pull = jax.vjp(jax.nn.gelu, gate_pre)
-    gated_own = (gelu_val * post).astype(BF16)
-    gated = lax.all_to_all(gated_own, "grp", 1, 0, tiled=True)
-    mix_part = mm(gated, m_out).astype(BF16)
-    mixing = lax.psum_scatter(mix_part, "grp", scatter_dimension=0, tiled=True).astype(F32)
+    gated = (gelu_val * post).astype(BF16)
+    mixing = ring_scatter(by_distance(mm(gated, m_out)), seq)
     own_rows = tokens[0].astype(F32)
     resid = own_rows + mixing
     inv_second = lax.rsqrt(jnp.mean(resid * resid, -1, keepdims=True) + EPS)
     unit_second = resid * inv_second
     ffn_in = (unit_second * feedforward_norm_gain).astype(BF16)
-    ffn_rows = lax.all_gather(ffn_in, "grp", axis=0, tiled=True)
-    act_a = mm(ffn_rows, m_swish)
-    act_u = mm(ffn_rows, m_up)
-    sig_a = jax.nn.sigmoid(act_a)
-    hidden = (act_a * sig_a * act_u).astype(BF16)
-    ffn_out = lax.psum_scatter(
-        mm(hidden, m_down).astype(BF16), "grp", scatter_dimension=0, tiled=True
-    ).astype(F32)
+
+    kept_ffn = []
+    for arrived, grads in zip(ring_gather(ffn_in, seq), grad_steps):
+        rows = jnp.concatenate(arrived, axis=0)
+        grad = jnp.concatenate(grads, axis=0)
+        act_a = mm_nt(rows, m_swish)
+        act_u = mm_nt(rows, m_up)
+        sig_a = jax.nn.sigmoid(act_a)
+        hidden = (act_a * sig_a * act_u).astype(BF16)
+        d_hidden = mm_nt(grad, m_down)
+        d_a = (d_hidden * act_u * sig_a * (1.0 + act_a * (1.0 - sig_a))).astype(BF16)
+        d_u = (d_hidden * act_a * sig_a).astype(BF16)
+        d_in = mm(d_a, m_swish) + mm(d_u, m_up)
+        kept_ffn.append((rows, grad, hidden, d_a, d_u, d_in))
+    ffn_rows, grad_rows, hidden, d_a, d_u, d_in = (
+        jnp.concatenate(items, axis=0) for items in zip(*kept_ffn)
+    )
+    d_ffn = ring_scatter(by_distance(d_in), seq)
+    g_ffn = jnp.stack(
+        [
+            trans_dot(left, right).astype(BF16).reshape(groups, padded, width)
+            for left, right in ((d_a, ffn_rows), (d_u, ffn_rows), (hidden, grad_rows))
+        ],
+        axis=1,
+    ).reshape(groups, 3 * padded, width)
+    g_ffn = lax.psum_scatter(g_ffn, "grp", scatter_dimension=0, tiled=False)
+    g_ffn = exchange(g_ffn.reshape(3 * padded, seq, -1).transpose(1, 0, 2))
+    g_ffn = g_ffn.reshape(seq, 3, padded, -1)[:, :, :share].transpose(1, 0, 2, 3)
+    g_ffn = g_ffn.reshape(3, seq * share, -1).astype(F32)
+    ffn_part = mm(hidden, m_down).astype(BF16).reshape(seq, rows_tok, width)
+    ffn_part = jnp.take(ffn_part, slot_of_member, axis=0)
+    ffn_out = lax.psum_scatter(ffn_part, "seq", scatter_dimension=0, tiled=False).astype(F32)
     out_tokens = (resid + ffn_out).astype(BF16)[None]
 
-    d_hidden = mm_nt(grad_rows, m_down)
-    g_down = trans_dot(hidden, grad_rows).astype(BF16)
-    d_a = (d_hidden * act_u * sig_a * (1.0 + act_a * (1.0 - sig_a))).astype(BF16)
-    d_u = (d_hidden * act_a * sig_a).astype(BF16)
-    d_ffn_part = (mm_nt(d_a, m_swish) + mm_nt(d_u, m_up)).astype(BF16)
-    d_ffn = lax.psum_scatter(d_ffn_part, "grp", scatter_dimension=0, tiled=True).astype(F32)
-    g_swish = trans_dot(ffn_rows, d_a).astype(BF16)
-    g_up = trans_dot(ffn_rows, d_u).astype(BF16)
     second_scaled = d_ffn * feedforward_norm_gain
     g_ffn_gain = jnp.sum(d_ffn * unit_second, 0)
     d_resid = grad_own.astype(F32) + inv_second * (
         second_scaled - unit_second * jnp.mean(second_scaled * unit_second, -1, keepdims=True)
     )
-    d_mix = lax.all_gather(d_resid.astype(BF16), "grp", axis=0, tiled=True)
-    d_gated_cols = mm_nt(d_mix, m_out).astype(BF16)
-    g_out = trans_dot(gated, d_mix).astype(BF16)
-    d_gated = lax.all_to_all(d_gated_cols, "grp", 0, 1, tiled=True).astype(F32)
+    mix_steps = ring_gather(d_resid.astype(BF16), seq)
+    d_mix = jnp.concatenate(sum(mix_steps, ()), axis=0)
+    d_gated = jnp.concatenate(
+        [mm_nt(jnp.concatenate(arrived, axis=0), m_out) for arrived in mix_steps], axis=0
+    )
     d_post = d_gated * gelu_val
     d_gate_pre = gelu_pull(d_gated * post)[0].astype(BF16)
     g_post_gain = jnp.sum(d_post * o_hat, 0)
     g_post_bias = jnp.sum(d_post, 0)
-    d_ohat = d_post * post_gain
-    d_inner = inv_o * (
-        d_ohat
-        - jnp.mean(d_ohat, -1, keepdims=True)
-        - o_hat * jnp.mean(d_ohat * o_hat, -1, keepdims=True)
-    )
-    d_pair = from_owner(plan, d_inner.astype(BF16), d_gate_pre, head_dim)
-    d_x4, d_rate_rows, d_gb, d_init = chain_backward(x4, d_pair, info, gb, init, kept, rows_tok)
+    d_ohat = d_post * post_g
+    sums = jnp.stack([jnp.sum(d_ohat, -1), jnp.sum(d_ohat * o_hat, -1)])
+    sums = in_slots(pairwise_sum(in_order(sums), "seq", seq)) / width
+    d_inner = inv_o * (d_ohat - sums[0][:, None] - o_hat * sums[1][:, None])
+    g_side = jnp.concatenate(
+        [
+            trans_dot(d_gate_pre, normed).astype(BF16).reshape(local, head_dim, width),
+            trans_dot(gated, d_mix).astype(BF16).reshape(local, head_dim, width),
+        ],
+        axis=1,
+    )
+    far_sum = partial(lax.psum_scatter, axis_name="grp", scatter_dimension=0, tiled=False)
+    g_side = scatter_heads(plan, g_side, 2, far_sum)
+    d_x3, d_rate_rows, d_gb, d_init = chain_backward(
+        slot_of_member, x3, d_inner, info, gb, init, kept, rows_tok
+    )
     d_rates = d_rate_rows[0].reshape(stream // MB, local, MB).swapaxes(1, 2).reshape(stream, local)
     d_logits = (d_rates * live * rate_sig * (1.0 - rate_sig) / head_dim).astype(BF16)
-    d_normed_part = lax.dot_general(
-        d_x4, w_heads, (((0, 2), (0, 2)), ((), ())), preferred_element_type=F32
-    ) + mm_nt(d_logits, rate_cols)
+    d_normed_part = mm(d_gate_pre, m_gate) + mm(d_logits, rate_rows)
+    for h in range(local):
+        d_normed_part = d_normed_part + mm(d_x3[h], w_proj[h])
+    d_normed = ring_scatter(by_distance(d_normed_part), seq)
     g_pre_gain = jnp.sum(d_normed_part * unit_all, 0)
-    d_normed = lax.psum_scatter(
-        d_normed_part.astype(BF16), "seq", scatter_dimension=0, tiled=True
-    ).astype(F32)
+    g_proj = jnp.stack([trans_dot(d_x3[h], normed) for h in range(local)])
+    g_proj = scatter_heads(plan, g_proj, 3, grp_scatter)
     own_inv = lax.rsqrt(jnp.mean(own_rows * own_rows, -1, keepdims=True) + EPS)
     own_unit = own_rows * own_inv
     first_scaled = d_normed * prenorm_gain
@@ -668,50 +813,48 @@
         + own_inv
         * (first_scaled - own_unit * jnp.mean(first_scaled * own_unit, -1, keepdims=True))
     )[None]
-    g_heads = lax.dot_general(
-        normed, d_x4, (((0,), (1,)), ((), ())), preferred_element_type=F32
-    ).astype(BF16)
-    g_heads = scatter_heads(plan, g_heads.transpose(1, 0, 2), 4)
-    g_rate_cols = trans_dot(normed, d_logits)
+
+    g_rate_cols = trans_dot(d_logits, normed)
     g_rate_shift = jnp.sum(d_logits.astype(F32), 0)
-    head_grads = chain_param_grads(d_gb, d_init, local)
-    packed = jnp.concatenate(
-        [item.reshape(local, -1) for item in head_grads]
-        + [g_rate_cols.T, g_rate_shift[:, None]],
-        axis=1,
-    )
-    packed = jnp.pad(packed, ((0, 0), (0, -packed.shape[1] % 128)))
-    packed = plan.order(lax.all_gather(lax.psum(packed, "grp"), "seq", axis=0))
-    sizes = (head_dim * head_dim, head_dim, head_dim, head_dim, width, 1)
+    parts = [item.reshape(local, -1) for item in chain_param_grads(d_gb, d_init, local)]
+    parts += [item.reshape(local, head_dim) for item in (g_post_gain, g_post_bias)]
+    parts += [g_rate_cols, g_rate_shift[:, None]]
+    sizes = [item.shape[1] for item in parts]
+    packed = jnp.concatenate(parts, axis=1)
+    packed = jnp.pad(packed, ((0, 0), (0, -packed.shape[1] % 1024)))
+    flat = jnp.concatenate([packed.reshape(-1), g_pre_gain, g_ffn_gain]).reshape(-1, 1024)
+    flat = pairwise_sum(flat, "grp", groups)
+    count = packed.size // 1024
+    gains = pairwise_sum(flat[count:], "seq", seq).reshape(2, width)
+    blocks = jnp.stack(sum(ring_gather(flat[:count], seq), ()))
+    blocks = jnp.take(blocks, slot_of_member, axis=0)
+    packed = plan.order(blocks.reshape(seq, local, -1))
     small = []
     offset = 0
     for size in sizes:
         small.append(packed[:, offset : offset + size])
         offset += size
-    wide = lax.psum((g_post_gain, g_post_bias, g_ffn_gain), ("seq", "grp"))
-    g_pre_gain = lax.psum(g_pre_gain, ("seq", "grp"))
-    scatter = partial(lax.psum_scatter, axis_name="seq", tiled=True)
     return (
         out_tokens,
         grad_tokens,
-        g_pre_gain,
-        g_heads[0],
-        g_heads[1],
-        g_heads[2],
-        g_heads[3],
-        small[4].T,
-        small[5][:, 0],
+        gains[0],
+        g_proj[0].T,
+        g_proj[1].T,
+        g_proj[2].T,
+        g_side[0].T,
+        small[6].T,
+        small[7][:, 0],
         small[0].reshape(heads, head_dim, head_dim),
         small[1],
         small[2],
         small[3],
-        wide[0],
-        wide[1],
-        scatter(g_out, scatter_dimension=1).astype(F32),
-        wide[2],
-        scatter(g_swish, scatter_dimension=0).astype(F32),
-        scatter(g_up, scatter_dimension=0).astype(F32),
-        scatter(g_down, scatter_dimension=1).astype(F32),
+        small[4].reshape(width),
+        small[5].reshape(width),
+        g_side[1],
+        gains[1],
+        g_ffn[0].T,
+        g_ffn[1].T,
+        g_ffn[2],
     )
 
 

time: 1440 us -> 889 us (0.62)
  the two profiles are of different devices: /device:TPU:0 before, /device:TPU:14 now
where the time goes in v2:
time: 889 us; the launch traced here: 881 us
  waiting for transfers between devices  339 us (38%)
  matrix products  155 us (17%)
  local copies, waits for them, and re-layouts  134 us (15%)
  starting transfers between devices  126 us (14%)
  Pallas kernels  55.5 us (6%)
  other arithmetic  54.4 us (6%)
  between operations  16.5 us (2%)
    ppermute x12, waiting for transfers between devices, ring_scatter(): ahead = lax.ppermute(ahead, 'seq', ring_pairs(size, 1)).astype(F32)  115 us
    ppermute x20, waiting for transfers between devices, ring_gather(): ahead = lax.ppermute(ahead, 'seq', ring_pairs(size, 1))  107 us
    dot_general x18, matrix products, mm(): return jnp.dot(left, right, preferred_element_type=F32)  66.9 us
    unnamed x235, local copies, waits for them, and re-layouts  50.9 us
    dot_general x26, matrix products, mm_nt(): lax.dot_general(left, right, (((1,), (1,)), ((), ())), preferred_element_...  49.5 us
    all_to_all x6, starting transfers between devices, exchange(): return lax.all_to_all(block, 'seq', 0, 0, tiled=True)  46 us
    dot_general x10, matrix products, trans_dot(): lax.dot_general(left, right, (((0,), (0,)), ((), ())), preferred_element_...  37.8 us
    pallas_call x1, Pallas kernels, chain_backward(): pl.pallas_call(partial(backward_kernel, heads), grid_spec=pltpu.PrefetchS...  33.4 us
  transfers between devices with their start and end apart: 86, of which 44 were waited for; matrix products, arithmetic and copies ran while one was open for 33% of the time, Pallas kernels for 6%

profile of v2, /device:TPU:14, one launch (start us, length us, event | category | flops | bytes accessed | tf_op | source)
XLA Modules:
  0.0 880.9 jit_solution(12052751597623185993)
XLA Ops:
  12.3 6.2 all-to-all-start
  31.8 7.0 all-to-all-start.1
  50.0 17.6 %collective-permute-done.2 = bf16[128,2048]{1,0:T(8,128)(2,1)} collective-permute-done((bf16[128,2048]{1,0:T(8,128)(2,1)}, bf16[128,2048]{1,0:T(8,128)(2,1)}, u32[]{:S(2)}, u32[]{:S(2)}) %collective-permute-start.2) | collective-permute-done | bytes 524320 | tf_op jit(solution)/shard_map/ppermute | solution.py:498
  87.3 6.6 collective-permute-done.6
  93.9 5.5 all-to-all-start.2
  131.5 11.9 %all-to-all-done.2 = bf16[8,528,256]{2,1,0:T(8,128)(2,1)} async-done(((bf16[8,528,256]{2,1,0:T(8,128)(2,1)}), bf16[8,528,256]{2,1,0:T(8,128)(2,1)}, u32[]{:S(2)}, u32[]{:S(2)}) %all-to-all-start.2) | async-done | bytes 2162720 | tf_op jit(solution)/shard_map/all_to_all | solution.py:585
  152.8 22.1 %chain_forward.1 = (f32[1024,256]{1,0:T(8,128)S(1)}, f32[64,4096]{1,0:T(8,128)S(1)}, f32[64,4096]{1,0:T(8,128)S(1)}, f32[64,4096]{1,0:T(8,128)S(1)}, f32[8,4096]{1,0:T(8,128)S(1)}, /*index=5*/f32[8,64,384]{2,1,0:T(8,128)S(1)}) custom-call(s32[8]{0:T(128)S(1)} %get-tuple-element.375.idx_ref, bf16[4,1024,192]{2,1,0:T(8,128)(2,1)S(1)} %pad_maximum_fusion.2.x_ref, ...), custom_call_target="tpu_custom_call" | custom-call | flops 20000000000 | bytes 16000000 | tf_op jit(solution)/shard_map/chain_forward/pallas_call | solution.py:345
  191.4 4.7 multiply_convert_fusion.1
  199.6 9.6 %collective-permute-done.16 = bf16[128,2048]{1,0:T(8,128)(2,1)S(1)} collective-permute-done((bf16[128,2048]{1,0:T(8,128)(2,1)S(1)}, bf16[128,2048]{1,0:T(8,128)(2,1)S(1)}, u32[]{:S(2)}, u32[]{:S(2)}) %collective-permute-start.16) | collective-permute-done | bytes 524320 | tf_op jit(solution)/shard_map/ppermute | solution.py:513
  212.0 8.3 collective-permute-done.18
  226.8 10.3 %collective-permute-done.20 = bf16[128,2048]{1,0:T(8,128)(2,1)S(1)} collective-permute-done((bf16[128,2048]{1,0:T(8,128)(2,1)S(1)}, bf16[128,2048]{1,0:T(8,128)(2,1)S(1)}, u32[]{:S(2)}, u32[]{:S(2)}) %collective-permute-start.20) | collective-permute-done | bytes 524320 | tf_op jit(solution)/shard_map/ppermute | solution.py:513
  240.2 5.8 collective-permute-done.31
  250.9 8.8 collective-permute-done.22
  263.7 7.1 collective-permute-done.32
  275.9 6.2 collective-permute-done.23
  284.6 8.9 %collective-permute-done.34 = bf16[128,2048]{1,0:T(8,128)(2,1)} collective-permute-done((bf16[128,2048]{1,0:T(8,128)(2,1)S(1)}, bf16[128,2048]{1,0:T(8,128)(2,1)}, u32[]{:S(2)}, u32[]{:S(2)}) %collective-permute-start.34) | collective-permute-done | bytes 524320 | tf_op jit(solution)/shard_map/ppermute | solution.py:498
  296.8 7.7 collective-permute-done.25
  310.0 14.1 %collective-permute-done.27 = bf16[128,2048]{1,0:T(8,128)(2,1)} collective-permute-done((bf16[128,2048]{1,0:T(8,128)(2,1)S(1)}, bf16[128,2048]{1,0:T(8,128)(2,1)}, u32[]{:S(2)}, u32[]{:S(2)}) %collective-permute-start.27) | collective-permute-done | bytes 524320 | tf_op jit(solution)/shard_map/ppermute | solution.py:498
  364.7 10.4 %collective-permute-done.37 = bf16[128,2048]{1,0:T(8,128)(2,1)S(1)} collective-permute-done((bf16[128,2048]{1,0:T(8,128)(2,1)S(1)}, bf16[128,2048]{1,0:T(8,128)(2,1)S(1)}, u32[]{:S(2)}, u32[]{:S(2)}) %collective-permute-start.37) | collective-permute-done | bytes 524320 | tf_op jit(solution)/shard_map/ppermute | solution.py:513
  379.4 10.3 %collective-permute-done.39 = bf16[128,2048]{1,0:T(8,128)(2,1)S(1)} collective-permute-done((bf16[128,2048]{1,0:T(8,128)(2,1)S(1)}, bf16[128,2048]{1,0:T(8,128)(2,1)S(1)}, u32[]{:S(2)}, u32[]{:S(2)}) %collective-permute-start.39) | collective-permute-done | bytes 524320 | tf_op jit(solution)/shard_map/ppermute | solution.py:513
  392.6 11.0 %collective-permute-done.41 = bf16[128,2048]{1,0:T(8,128)(2,1)S(1)} collective-permute-done((bf16[128,2048]{1,0:T(8,128)(2,1)S(1)}, bf16[128,2048]{1,0:T(8,128)(2,1)S(1)}, u32[]{:S(2)}, u32[]{:S(2)}) %collective-permute-start.41) | collective-permute-done | bytes 524320 | tf_op jit(solution)/shard_map/ppermute | solution.py:513
  406.4 11.3 %collective-permute-done.43 = bf16[128,2048]{1,0:T(8,128)(2,1)S(1)} collective-permute-done((bf16[128,2048]{1,0:T(8,128)(2,1)S(1)}, bf16[128,2048]{1,0:T(8,128)(2,1)S(1)}, u32[]{:S(2)}, u32[]{:S(2)}) %collective-permute-start.43) | collective-permute-done | bytes 524320 | tf_op jit(solution)/shard_map/ppermute | solution.py:513
  424.2 9.5 %collective-permute-done.45 = bf16[128,2048]{1,0:T(8,128)(2,1)S(1)} collective-permute-done((bf16[128,2048]{1,0:T(8,128)(2,1)S(1)}, bf16[128,2048]{1,0:T(8,128)(2,1)S(1)}, u32[]{:S(2)}, u32[]{:S(2)}) %collective-permute-start.45) | collective-permute-done | bytes 524320 | tf_op jit(solution)/shard_map/ppermute | solution.py:500
  436.3 11.0 %collective-permute-done.46 = bf16[128,2048]{1,0:T(8,128)(2,1)S(1)} collective-permute-done((bf16[128,2048]{1,0:T(8,128)(2,1)S(1)}, bf16[128,2048]{1,0:T(8,128)(2,1)S(1)}, u32[]{:S(2)}, u32[]{:S(2)}) %collective-permute-start.46) | collective-permute-done | bytes 524320 | tf_op jit(solution)/shard_map/ppermute | solution.py:498
  450.3 9.6 %collective-permute-done.48 = bf16[128,2048]{1,0:T(8,128)(2,1)S(1)} collective-permute-done((bf16[128,2048]{1,0:T(8,128)(2,1)S(1)}, bf16[128,2048]{1,0:T(8,128)(2,1)S(1)}, u32[]{:S(2)}, u32[]{:S(2)}) %collective-permute-start.48) | collective-permute-done | bytes 524320 | tf_op jit(solution)/shard_map/ppermute | solution.py:498
  460.8 8.3 collective-permute-done.50
  488.0 4.7 pad_maximum_fusion.3
  492.9 5.9 convolution_convert_fusion.2
  498.8 6.1 convolution_convert_fusion.3
  521.3 7.8 convolution_convert_fusion
  529.2 5.1 gather_fusion
  537.1 6.5 fusion.183
  551.2 33.4 %chain_backward.1 = (bf16[4,1024,192]{2,1,0:T(8,128)(2,1)S(1)}, f32[8,4096]{1,0:T(8,128)S(1)}, f32[2,64,128]{2,1,0:T(8,128)S(1)}, f32[64,384]{1,0:T(8,128)S(1)}) custom-call(s32[8]{0:T(128)S(1)} %get-tuple-element.375.idx_ref, bf16[4,1024,192]{2,1,0:T(8,128)(2,1)S(1)} %copy-done.3, f32[1024,256]{1,0:T(8,128)S(1)} %subtract_multiply_fusion.d_ref, ...), custom_call_target="tpu_custom_call" | custom-call | flops 30000001024 | bytes 20000000 | tf_op jit(solution)/shard_map/chain_backward/pallas_call | solution.py:378
  593.3 5.8 fusion.84
  599.1 5.7 fusion.83
  604.8 5.7 fusion.82
  610.5 21.1 %fusion.3 = (f32[2048]{0:T(1024)S(1)}, bf16[1024,2048]{1,0:T(8,128)(2,1)}, f32[1024,2048]{1,0:T(8,128)}) fusion(bf16[1024,2048]{1,0:T(8,128)(2,1)} %constant_dynamic-update-slice_fusion, f32[1024]{0:T(1024)S(1)} %copy-done.73, bf16[4,192,2048]{2,1,0:T(8,128)(2,1)} %constant_dynamic-update-slice_fusion.56, bf16[4,1024,192]{2,1,0:T(8,128)(2,1)S(1)} %get-tuple-element.135, ...), kind=kOutput, calls=%fused_computation.8 | convolution fusion | flops 826275840 | bytes 60043264 | tf_op jit(solution)/shard_map/dot_general | solution.py:17
  665.0 24.4 %collective-permute-done.65 = f32[4,1024]{1,0:T(4,128)S(1)} collective-permute-done((f32[4,1024]{1,0:T(4,128)S(1)}, f32[4,1024]{1,0:T(4,128)S(1)}, u32[]{:S(2)}, u32[]{:S(2)}) %collective-permute-start.65) | collective-permute-done | bytes 16416 | tf_op jit(solution)/shard_map/ppermute | solution.py:525
  691.9 5.7 collective-permute-done.69
  704.2 11.9 %all-to-all-start.3 = ((bf16[8,192,256]{2,1,0:T(8,128)(2,1)}), bf16[8,192,256]{2,1,0:T(8,128)(2,1)S(1)}, u32[]{:S(2)}, u32[]{:S(2)}) async-start(bf16[8,192,256]{2,1,0:T(8,128)(2,1)} %bitcast.423), calls=%async_computation.4 | async-start | bytes 1572864 | tf_op jit(solution)/shard_map/all_to_all | solution.py:585
  717.0 9.3 %collective-permute-done.72 = f32[28,1024]{1,0:T(8,128)} collective-permute-done((f32[28,1024]{1,0:T(8,128)}, f32[28,1024]{1,0:T(8,128)}, u32[]{:S(2)}, u32[]{:S(2)}) %collective-permute-start.72) | collective-permute-done | bytes 114720 | tf_op jit(solution)/shard_map/ppermute | solution.py:500
  737.4 5.4 collective-permute-done.74
  742.8 7.5 all-to-all-start.4
  751.6 13.8 %collective-permute-done.57 = bf16[128,2048]{1,0:T(8,128)(2,1)} collective-permute-done((bf16[128,2048]{1,0:T(8,128)(2,1)}, bf16[128,2048]{1,0:T(8,128)(2,1)}, u32[]{:S(2)}, u32[]{:S(2)}) %collective-permute-start.57) | collective-permute-done | bytes 524320 | tf_op jit(solution)/shard_map/ppermute | solution.py:515
  775.4 5.5 all-to-all-done.4
  780.9 7.9 all-to-all-start.5
  793.1 14.7 %collective-permute-done.59 = bf16[128,2048]{1,0:T(8,128)(2,1)} collective-permute-done((bf16[128,2048]{1,0:T(8,128)(2,1)S(1)}, bf16[128,2048]{1,0:T(8,128)(2,1)}, u32[]{:S(2)}, u32[]{:S(2)}) %collective-permute-start.59) | collective-permute-done | bytes 524320 | tf_op jit(solution)/shard_map/ppermute | solution.py:515
  812.3 35.3 %collective-permute-done.60 = bf16[128,2048]{1,0:T(8,128)(2,1)S(1)} collective-permute-done((bf16[128,2048]{1,0:T(8,128)(2,1)S(1)}, bf16[128,2048]{1,0:T(8,128)(2,1)S(1)}, u32[]{:S(2)}, u32[]{:S(2)}) %collective-permute-start.60) | collective-permute-done | bytes 524320 | tf_op jit(solution)/shard_map/ppermute | solution.py:513
  (611 shorter events, 365.6 us)
Async XLA Ops:
  7.3 32.3 %collective-permute-start = (bf16[128,2048]{1,0:T(8,128)(2,1)}, bf16[128,2048]{1,0:T(8,128)(2,1)}, u32[]{:S(2)}, u32[]{:S(2)}) collective-permute-start(bf16[128,2048]{1,0:T(8,128)(2,1)} %bitcast.465), channel_id=1, source_target_pairs={{0,8},{8,16},{16,24},{24,28},{28,20},{20,12},{12,4},{4,0},{1,9},{9... | collective-permute-start | bytes 1572872 | tf_op jit(solution)/shard_map/ppermute | solution.py:498
  7.8 31.8 %collective-permute-start.1 = (bf16[128,2048]{1,0:T(8,128)(2,1)}, bf16[128,2048]{1,0:T(8,128)(2,1)}, u32[]{:S(2)}, u32[]{:S(2)}) collective-permute-start(bf16[128,2048]{1,0:T(8,128)(2,1)} %bitcast.466), channel_id=1, source_target_pairs={{0,4},{8,0},{16,8},{24,16},{28,24},{20,28},{12,20},{4,12},{1,5},{9... | collective-permute-start | bytes 1572872 | tf_op jit(solution)/shard_map/ppermute | solution.py:500
  12.3 19.5 %all-to-all-start = ((bf16[8,128,256]{2,1,0:T(8,128)(2,1)}), bf16[8,128,256]{2,1,0:T(8,128)(2,1)}, u32[]{:S(2)}, u32[]{:S(2)}) async-start(bf16[8,128,256]{2,1,0:T(8,128)(2,1)} %bitcast.4), calls=%async_computation | async-start | bytes 1048576 | tf_op jit(solution)/shard_map/all_to_all | solution.py:585
  31.8 41.6 %all-to-all-start.1 = ((bf16[8,192,256]{2,1,0:T(8,128)(2,1)}), bf16[8,192,256]{2,1,0:T(8,128)(2,1)S(1)}, u32[]{:S(2)}, u32[]{:S(2)}) async-start(bf16[8,192,256]{2,1,0:T(8,128)(2,1)} %bitcast.14), calls=%async_computation.1 | async-start | bytes 1572864 | tf_op jit(solution)/shard_map/all_to_all | solution.py:585
  39.5 28.1 %collective-permute-start.2 = (bf16[128,2048]{1,0:T(8,128)(2,1)}, bf16[128,2048]{1,0:T(8,128)(2,1)}, u32[]{:S(2)}, u32[]{:S(2)}) collective-permute-start(bf16[128,2048]{1,0:T(8,128)(2,1)} %collective-permute-done), channel_id=1, source_target_pairs={{0,8},{8,16},{16,24},{24,28},{28,20},{20,12},{12,4},{4,0},{1,9},{9... | collective-permute-start | bytes 1572872 | tf_op jit(solution)/shard_map/ppermute | solution.py:498
  40.1 27.5 %collective-permute-start.3 = (bf16[128,2048]{1,0:T(8,128)(2,1)}, bf16[128,2048]{1,0:T(8,128)(2,1)}, u32[]{:S(2)}, u32[]{:S(2)}) collective-permute-start(bf16[128,2048]{1,0:T(8,128)(2,1)} %collective-permute-done.1), channel_id=1, source_target_pairs={{0,4},{8,0},{16,8},{24,16},{28,24},{20,28},{12,20},{4,12},{1,5},{9... | collective-permute-start | bytes 1572872 | tf_op jit(solution)/shard_map/ppermute | solution.py:500
  47.0 34.4 %collective-permute-start.8 = (bf16[1,128,2048]{1,2,0:T(8,128)(2,1)S(1)}, bf16[1,128,2048]{1,2,0:T(8,128)(2,1)}, u32[]{:S(2)}, u32[]{:S(2)}) collective-permute-start(bf16[1,128,2048]{1,2,0:T(8,128)(2,1)S(1)} %bitcast.488), channel_id=1, source_target_pairs={{0,2},{1,3},{2,0},{3,1},{4,6},{5,7},{6,4},{7,5},{8,10},{9,11},{10,... | collective-permute-start | bytes 1572872 | tf_op jit(solution)/shard_map/ppermute | solution.py:531
  47.5 30.4 %collective-permute-start.7 = (bf16[1,128,2048]{1,2,0:T(8,128)(2,1)S(1)}, bf16[1,128,2048]{1,2,0:T(8,128)(2,1)}, u32[]{:S(2)}, u32[]{:S(2)}) collective-permute-start(bf16[1,128,2048]{1,2,0:T(8,128)(2,1)S(1)} %bitcast.489), channel_id=1, source_target_pairs={{0,1},{1,0},{2,3},{3,2},{4,5},{5,4},{6,7},{7,6},{8,9},{9,8},{10,11... | collective-permute-start | bytes 1572872 | tf_op jit(solution)/shard_map/ppermute | solution.py:531
  74.2 38.4 %collective-permute-start.11 = (bf16[1,192,2048]{2,1,0:T(8,128)(2,1)S(1)}, bf16[1,192,2048]{2,1,0:T(8,128)(2,1)S(1)}, u32[]{:S(2)}, u32[]{:S(2)}) collective-permute-start(bf16[1,192,2048]{2,1,0:T(8,128)(2,1)S(1)} %reshape.753), channel_id=1, source_target_pairs={{0,2},{1,3},{2,0},{3,1},{4,6},{5,7},{6,4},{7,5},{8,10},{9,11},{10,... | collective-permute-start | bytes 2359304 | tf_op jit(solution)/shard_map/ppermute | solution.py:531
  77.9 34.9 %collective-permute-start.10 = (bf16[1,192,2048]{2,1,0:T(8,128)(2,1)S(1)}, bf16[1,192,2048]{2,1,0:T(8,128)(2,1)}, u32[]{:S(2)}, u32[]{:S(2)}) collective-permute-start(bf16[1,192,2048]{2,1,0:T(8,128)(2,1)S(1)} %reshape.753), channel_id=1, source_target_pairs={{0,1},{1,0},{2,3},{3,2},{4,5},{5,4},{6,7},{7,6},{8,9},{9,8},{10,11... | collective-permute-start | bytes 2359304 | tf_op jit(solution)/shard_map/ppermute | solution.py:531
  83.4 95.1 %collective-permute-start.9 = (bf16[1,128,2048]{1,2,0:T(8,128)(2,1)}, bf16[1,128,2048]{1,2,0:T(8,128)(2,1)}, u32[]{:S(2)}, u32[]{:S(2)}) collective-permute-start(bf16[1,128,2048]{1,2,0:T(8,128)(2,1)} %collective-permute-done.8), channel_id=1, source_target_pairs={{0,1},{1,0},{2,3},{3,2},{4,5},{5,4},{6,7},{7,6},{8,9},{9,8},{10,11... | collective-permute-start | bytes 1572872 | tf_op jit(solution)/shard_map/ppermute | solution.py:531
  93.9 49.6 %all-to-all-start.2 = ((bf16[8,528,256]{2,1,0:T(8,128)(2,1)}), bf16[8,528,256]{2,1,0:T(8,128)(2,1)}, u32[]{:S(2)}, u32[]{:S(2)}) async-start(bf16[8,528,256]{2,1,0:T(8,128)(2,1)} %fusion.11), calls=%async_computation.2 | async-start | bytes 4325376 | tf_op jit(solution)/shard_map/all_to_all | solution.py:585
  99.4 230.4 %all-gather.2.cloned.1.call-start = ((), (), s32[]{:S(2)}) async-start(), calls=%async_computation.9 | async-start | bytes 10813440 | tf_op jit(solution)/shard_map/all_gather | solution.py:692
  151.8 591.1 %reduce-scatter.6.cloned.1.call-start = ((), (), s32[]{:S(2)}) async-start(), calls=%async_computation.11 | async-start | bytes 2621440 | tf_op jit(solution)/shard_map/reduce_scatter | solution.py:609
  222.2 14.9 %collective-permute-start.20 = (bf16[128,2048]{1,0:T(8,128)(2,1)S(1)}, bf16[128,2048]{1,0:T(8,128)(2,1)S(1)}, u32[]{:S(2)}, u32[]{:S(2)}) collective-permute-start(bf16[128,2048]{1,0:T(8,128)(2,1)S(1)} %get-tuple-element.97), channel_id=1, source_target_pairs={{0,8},{8,16},{16,24},{24,28},{28,20},{20,12},{12,4},{4,0},{1,9},{9... | collective-permute-start | bytes 1572872 | tf_op jit(solution)/shard_map/ppermute | solution.py:513
  224.8 21.3 %collective-permute-start.31 = (bf16[128,2048]{1,0:T(8,128)(2,1)S(1)}, bf16[128,2048]{1,0:T(8,128)(2,1)S(1)}, u32[]{:S(2)}, u32[]{:S(2)}) collective-permute-start(bf16[128,2048]{1,0:T(8,128)(2,1)S(1)} %bitcast.468), channel_id=1, source_target_pairs={{0,4},{8,0},{16,8},{24,16},{28,24},{20,28},{12,20},{4,12},{1,5},{9... | collective-permute-start | bytes 1572872 | tf_op jit(solution)/shard_map/ppermute | solution.py:500
  225.4 23.0 %collective-permute-start.30 = (bf16[128,2048]{1,0:T(8,128)(2,1)S(1)}, bf16[128,2048]{1,0:T(8,128)(2,1)S(1)}, u32[]{:S(2)}, u32[]{:S(2)}) collective-permute-start(bf16[128,2048]{1,0:T(8,128)(2,1)S(1)} %bitcast.469), channel_id=1, source_target_pairs={{0,8},{8,16},{16,24},{24,28},{28,20},{20,12},{12,4},{4,0},{1,9},{9... | collective-permute-start | bytes 1572872 | tf_op jit(solution)/shard_map/ppermute | solution.py:498
  239.3 20.4 %collective-permute-start.22 = (bf16[128,2048]{1,0:T(8,128)(2,1)S(1)}, bf16[128,2048]{1,0:T(8,128)(2,1)S(1)}, u32[]{:S(2)}, u32[]{:S(2)}) collective-permute-start(bf16[128,2048]{1,0:T(8,128)(2,1)S(1)} %fusion.52), channel_id=1, source_target_pairs={{0,8},{8,16},{16,24},{24,28},{28,20},{20,12},{12,4},{4,0},{1,9},{9... | collective-permute-start | bytes 1572872 | tf_op jit(solution)/shard_map/ppermute | solution.py:513
  248.4 22.5 %collective-permute-start.32 = (bf16[128,2048]{1,0:T(8,128)(2,1)S(1)}, bf16[128,2048]{1,0:T(8,128)(2,1)S(1)}, u32[]{:S(2)}, u32[]{:S(2)}) collective-permute-start(bf16[128,2048]{1,0:T(8,128)(2,1)S(1)} %collective-permute-done.30), channel_id=1, source_target_pairs={{0,8},{8,16},{16,24},{24,28},{28,20},{20,12},{12,4},{4,0},{1,9},{9... | collective-permute-start | bytes 1572872 | tf_op jit(solution)/shard_map/ppermute | solution.py:498
  250.9 20.0 %collective-permute-start.33 = (bf16[128,2048]{1,0:T(8,128)(2,1)S(1)}, bf16[128,2048]{1,0:T(8,128)(2,1)S(1)}, u32[]{:S(2)}, u32[]{:S(2)}) collective-permute-start(bf16[128,2048]{1,0:T(8,128)(2,1)S(1)} %collective-permute-done.31), channel_id=1, source_target_pairs={{0,4},{8,0},{16,8},{24,16},{28,24},{20,28},{12,20},{4,12},{1,5},{9... | collective-permute-start | bytes 1572872 | tf_op jit(solution)/shard_map/ppermute | solution.py:500
  262.3 19.8 %collective-permute-start.23 = (bf16[128,2048]{1,0:T(8,128)(2,1)S(1)}, bf16[128,2048]{1,0:T(8,128)(2,1)S(1)}, u32[]{:S(2)}, u32[]{:S(2)}) collective-permute-start(bf16[128,2048]{1,0:T(8,128)(2,1)S(1)} %get-tuple-element.273), channel_id=1, source_target_pairs={{0,8},{8,16},{16,24},{24,28},{28,20},{20,12},{12,4},{4,0},{1,9},{9... | collective-permute-start | bytes 1572872 | tf_op jit(solution)/shard_map/ppermute | solution.py:498
  270.9 22.6 %collective-permute-start.34 = (bf16[128,2048]{1,0:T(8,128)(2,1)S(1)}, bf16[128,2048]{1,0:T(8,128)(2,1)}, u32[]{:S(2)}, u32[]{:S(2)}) collective-permute-start(bf16[128,2048]{1,0:T(8,128)(2,1)S(1)} %collective-permute-done.32), channel_id=1, source_target_pairs={{0,8},{8,16},{16,24},{24,28},{28,20},{20,12},{12,4},{4,0},{1,9},{9... | collective-permute-start | bytes 1572872 | tf_op jit(solution)/shard_map/ppermute | solution.py:498
  273.4 20.1 %collective-permute-start.35 = (bf16[128,2048]{1,0:T(8,128)(2,1)S(1)}, bf16[128,2048]{1,0:T(8,128)(2,1)S(1)}, u32[]{:S(2)}, u32[]{:S(2)}) collective-permute-start(bf16[128,2048]{1,0:T(8,128)(2,1)S(1)} %collective-permute-done.33), channel_id=1, source_target_pairs={{0,4},{8,0},{16,8},{24,16},{28,24},{20,28},{12,20},{4,12},{1,5},{9... | collective-permute-start | bytes 1572872 | tf_op jit(solution)/shard_map/ppermute | solution.py:500
  282.1 22.5 %collective-permute-start.25 = (bf16[128,2048]{1,0:T(8,128)(2,1)S(1)}, bf16[128,2048]{1,0:T(8,128)(2,1)S(1)}, u32[]{:S(2)}, u32[]{:S(2)}) collective-permute-start(bf16[128,2048]{1,0:T(8,128)(2,1)S(1)} %collective-permute-done.23), channel_id=1, source_target_pairs={{0,8},{8,16},{16,24},{24,28},{28,20},{20,12},{12,4},{4,0},{1,9},{9... | collective-permute-start | bytes 1572872 | tf_op jit(solution)/shard_map/ppermute | solution.py:498
  284.6 20.0 %collective-permute-start.26 = (bf16[128,2048]{1,0:T(8,128)(2,1)S(1)}, bf16[128,2048]{1,0:T(8,128)(2,1)S(1)}, u32[]{:S(2)}, u32[]{:S(2)}) collective-permute-start(bf16[128,2048]{1,0:T(8,128)(2,1)S(1)} %collective-permute-done.24), channel_id=1, source_target_pairs={{0,4},{8,0},{16,8},{24,16},{28,24},{20,28},{12,20},{4,12},{1,5},{9... | collective-permute-start | bytes 1572872 | tf_op jit(solution)/shard_map/ppermute | solution.py:500
  293.5 54.8 %collective-permute-start.36 = (bf16[128,2048]{1,0:T(8,128)(2,1)}, bf16[128,2048]{1,0:T(8,128)(2,1)}, u32[]{:S(2)}, u32[]{:S(2)}) collective-permute-start(bf16[128,2048]{1,0:T(8,128)(2,1)} %collective-permute-done.34), channel_id=1, source_target_pairs={{0,8},{8,16},{16,24},{24,28},{28,20},{20,12},{12,4},{4,0},{1,9},{9... | collective-permute-start | bytes 1572872 | tf_op jit(solution)/shard_map/ppermute | solution.py:498
  304.6 19.5 %collective-permute-start.27 = (bf16[128,2048]{1,0:T(8,128)(2,1)S(1)}, bf16[128,2048]{1,0:T(8,128)(2,1)}, u32[]{:S(2)}, u32[]{:S(2)}) collective-permute-start(bf16[128,2048]{1,0:T(8,128)(2,1)S(1)} %collective-permute-done.25), channel_id=1, source_target_pairs={{0,8},{8,16},{16,24},{24,28},{28,20},{20,12},{12,4},{4,0},{1,9},{9... | collective-permute-start | bytes 1572872 | tf_op jit(solution)/shard_map/ppermute | solution.py:498
  307.0 17.0 %collective-permute-start.28 = (bf16[128,2048]{1,0:T(8,128)(2,1)S(1)}, bf16[128,2048]{1,0:T(8,128)(2,1)S(1)}, u32[]{:S(2)}, u32[]{:S(2)}) collective-permute-start(bf16[128,2048]{1,0:T(8,128)(2,1)S(1)} %collective-permute-done.26), channel_id=1, source_target_pairs={{0,4},{8,0},{16,8},{24,16},{28,24},{20,28},{12,20},{4,12},{1,5},{9... | collective-permute-start | bytes 1572872 | tf_op jit(solution)/shard_map/ppermute | solution.py:500
  324.1 28.8 %collective-permute-start.29 = (bf16[128,2048]{1,0:T(8,128)(2,1)}, bf16[128,2048]{1,0:T(8,128)(2,1)}, u32[]{:S(2)}, u32[]{:S(2)}) collective-permute-start(bf16[128,2048]{1,0:T(8,128)(2,1)} %collective-permute-done.27), channel_id=1, source_target_pairs={{0,8},{8,16},{16,24},{24,28},{28,20},{20,12},{12,4},{4,0},{1,9},{9... | collective-permute-start | bytes 1572872 | tf_op jit(solution)/shard_map/ppermute | solution.py:498
  492.8 278.5 %reduce-scatter.8.cloned.1.call-start = ((), (), s32[]{:S(2)}) async-start(), calls=%async_computation.12 | async-start | bytes 10813440 | tf_op jit(solution)/shard_map/reduce_scatter | solution.py:760
  515.6 341.4 %reduce-scatter.4.cloned.1.call-start = ((), (), s32[]{:S(2)}) async-start(), calls=%async_computation.10 | async-start | bytes 4718592 | tf_op jit(solution)/shard_map/reduce_scatter | solution.py:766
  654.0 47.5 %collective-permute-start.66 = (bf16[192,2048]{1,0:T(8,128)(2,1)S(1)}, bf16[192,2048]{1,0:T(8,128)(2,1)S(1)}, u32[]{:S(2)}, u32[]{:S(2)}) collective-permute-start(bf16[192,2048]{1,0:T(8,128)(2,1)S(1)} %get-tuple-element.307), channel_id=1, source_target_pairs={{0,1},{1,0},{2,3},{3,2},{4,5},{5,4},{6,7},{7,6},{8,9},{9,8},{10,11... | collective-permute-start | bytes 2359304 | tf_op jit(solution)/shard_map/ppermute | solution.py:531
  657.0 44.5 %collective-permute-start.68 = (bf16[192,2048]{1,0:T(8,128)(2,1)S(1)}, bf16[192,2048]{1,0:T(8,128)(2,1)S(1)}, u32[]{:S(2)}, u32[]{:S(2)}) collective-permute-start(bf16[192,2048]{1,0:T(8,128)(2,1)S(1)} %fusion.12), channel_id=1, source_target_pairs={{0,2},{1,3},{2,0},{3,1},{4,6},{5,7},{6,4},{7,5},{8,10},{9,11},{10,... | collective-permute-start | bytes 2359304 | tf_op jit(solution)/shard_map/ppermute | solution.py:531
  661.1 70.7 %collective-permute-start.54 = (bf16[128,2048]{1,0:T(8,128)(2,1)}, bf16[128,2048]{1,0:T(8,128)(2,1)}, u32[]{:S(2)}, u32[]{:S(2)}) collective-permute-start(bf16[128,2048]{1,0:T(8,128)(2,1)} %get-tuple-element.136), channel_id=1, source_target_pairs={{0,8},{8,16},{16,24},{24,28},{28,20},{20,12},{12,4},{4,0},{1,9},{9... | collective-permute-start | bytes 1572872 | tf_op jit(solution)/shard_map/ppermute | solution.py:513
  661.7 27.6 %collective-permute-start.65 = (f32[4,1024]{1,0:T(4,128)S(1)}, f32[4,1024]{1,0:T(4,128)S(1)}, u32[]{:S(2)}, u32[]{:S(2)}) collective-permute-start(f32[4,1024]{1,0:T(4,128)S(1)} %add.547), channel_id=1, source_target_pairs={{0,16},{4,20},{8,24},{12,28},{16,0},{20,4},{24,8},{28,12},{1,17},{... | collective-permute-start | bytes 49160 | tf_op jit(solution)/shard_map/ppermute | solution.py:525
  664.9 32.7 %collective-permute-start.69 = (f32[28,1024]{1,0:T(8,128)S(1)}, f32[28,1024]{1,0:T(8,128)}, u32[]{:S(2)}, u32[]{:S(2)}) collective-permute-start(f32[28,1024]{1,0:T(8,128)S(1)} %bitcast.504), channel_id=1, source_target_pairs={{0,8},{8,16},{16,24},{24,28},{28,20},{20,12},{12,4},{4,0},{1,9},{9... | collective-permute-start | bytes 344072 | tf_op jit(solution)/shard_map/ppermute | solution.py:498
  697.6 34.2 %collective-permute-start.55 = (bf16[128,2048]{1,0:T(8,128)(2,1)}, bf16[128,2048]{1,0:T(8,128)(2,1)}, u32[]{:S(2)}, u32[]{:S(2)}) collective-permute-start(bf16[128,2048]{1,0:T(8,128)(2,1)} %get-tuple-element.137), channel_id=1, source_target_pairs={{0,4},{8,0},{16,8},{24,16},{28,24},{20,28},{12,20},{4,12},{1,5},{9... | collective-permute-start | bytes 1572872 | tf_op jit(solution)/shard_map/ppermute | solution.py:515
  697.6 19.4 %collective-permute-start.71 = (f32[28,1024]{1,0:T(8,128)}, f32[28,1024]{1,0:T(8,128)S(1)}, u32[]{:S(2)}, u32[]{:S(2)}) collective-permute-start(f32[28,1024]{1,0:T(8,128)} %collective-permute-done.69), channel_id=1, source_target_pairs={{0,8},{8,16},{16,24},{24,28},{28,20},{20,12},{12,4},{4,0},{1,9},{9... | collective-permute-start | bytes 344072 | tf_op jit(solution)/shard_map/ppermute | solution.py:498
  701.5 24.9 %collective-permute-start.72 = (f32[28,1024]{1,0:T(8,128)}, f32[28,1024]{1,0:T(8,128)}, u32[]{:S(2)}, u32[]{:S(2)}) collective-permute-start(f32[28,1024]{1,0:T(8,128)} %collective-permute-done.70), channel_id=1, source_target_pairs={{0,4},{8,0},{16,8},{24,16},{28,24},{20,28},{12,20},{4,12},{1,5},{9... | collective-permute-start | bytes 344072 | tf_op jit(solution)/shard_map/ppermute | solution.py:500
  704.2 38.5 %all-to-all-start.3 = ((bf16[8,192,256]{2,1,0:T(8,128)(2,1)}), bf16[8,192,256]{2,1,0:T(8,128)(2,1)S(1)}, u32[]{:S(2)}, u32[]{:S(2)}) async-start(bf16[8,192,256]{2,1,0:T(8,128)(2,1)} %bitcast.423), calls=%async_computation.4 | async-start | bytes 1572864 | tf_op jit(solution)/shard_map/all_to_all | solution.py:585
  726.4 16.4 %collective-permute-start.74 = (f32[28,1024]{1,0:T(8,128)}, f32[28,1024]{1,0:T(8,128)S(1)}, u32[]{:S(2)}, u32[]{:S(2)}) collective-permute-start(f32[28,1024]{1,0:T(8,128)} %collective-permute-done.72), channel_id=1, source_target_pairs={{0,4},{8,0},{16,8},{24,16},{28,24},{20,28},{12,20},{4,12},{1,5},{9... | collective-permute-start | bytes 344072 | tf_op jit(solution)/shard_map/ppermute | solution.py:500
  734.9 16.7 %collective-permute-start.56 = (bf16[128,2048]{1,0:T(8,128)(2,1)}, bf16[128,2048]{1,0:T(8,128)(2,1)}, u32[]{:S(2)}, u32[]{:S(2)}) collective-permute-start(bf16[128,2048]{1,0:T(8,128)(2,1)} %get-tuple-element.138), channel_id=1, source_target_pairs={{0,8},{8,16},{16,24},{24,28},{28,20},{20,12},{12,4},{4,0},{1,9},{9... | collective-permute-start | bytes 1572872 | tf_op jit(solution)/shard_map/ppermute | solution.py:513
  734.9 30.4 %collective-permute-start.57 = (bf16[128,2048]{1,0:T(8,128)(2,1)}, bf16[128,2048]{1,0:T(8,128)(2,1)}, u32[]{:S(2)}, u32[]{:S(2)}) collective-permute-start(bf16[128,2048]{1,0:T(8,128)(2,1)} %get-tuple-element.139), channel_id=1, source_target_pairs={{0,4},{8,0},{16,8},{24,16},{28,24},{20,28},{12,20},{4,12},{1,5},{9... | collective-permute-start | bytes 1572872 | tf_op jit(solution)/shard_map/ppermute | solution.py:515
  742.8 38.0 %all-to-all-start.4 = ((bf16[8,128,256]{1,2,0:T(8,128)(2,1)}), bf16[8,128,256]{1,2,0:T(8,128)(2,1)S(1)}, u32[]{:S(2)}, u32[]{:S(2)}) async-start(bf16[8,128,256]{1,2,0:T(8,128)(2,1)} %bitcast.507), calls=%async_computation.6 | async-start | bytes 1048576 | tf_op jit(solution)/shard_map/all_to_all | solution.py:585
  768.2 40.7 %collective-permute-start.58 = (bf16[128,2048]{1,0:T(8,128)(2,1)}, bf16[128,2048]{1,0:T(8,128)(2,1)}, u32[]{:S(2)}, u32[]{:S(2)}) collective-permute-start(bf16[128,2048]{1,0:T(8,128)(2,1)} %get-tuple-element.140), channel_id=1, source_target_pairs={{0,8},{8,16},{16,24},{24,28},{28,20},{20,12},{12,4},{4,0},{1,9},{9... | collective-permute-start | bytes 1572872 | tf_op jit(solution)/shard_map/ppermute | solution.py:513
  768.2 39.5 %collective-permute-start.59 = (bf16[128,2048]{1,0:T(8,128)(2,1)S(1)}, bf16[128,2048]{1,0:T(8,128)(2,1)}, u32[]{:S(2)}, u32[]{:S(2)}) collective-permute-start(bf16[128,2048]{1,0:T(8,128)(2,1)S(1)} %get-tuple-element.141), channel_id=1, source_target_pairs={{0,4},{8,0},{16,8},{24,16},{28,24},{20,28},{12,20},{4,12},{1,5},{9... | collective-permute-start | bytes 1572872 | tf_op jit(solution)/shard_map/ppermute | solution.py:515
  780.9 82.8 %all-to-all-start.5 = ((bf16[8,528,256]{2,1,0:T(8,128)(2,1)}), bf16[8,528,256]{2,1,0:T(8,128)(2,1)}, u32[]{:S(2)}, u32[]{:S(2)}) async-start(bf16[8,528,256]{2,1,0:T(8,128)(2,1)} %bitcast.420), calls=%async_computation.8 | async-start | bytes 4325376 | tf_op jit(solution)/shard_map/all_to_all | solution.py:585
  810.5 37.1 %collective-permute-start.60 = (bf16[128,2048]{1,0:T(8,128)(2,1)S(1)}, bf16[128,2048]{1,0:T(8,128)(2,1)S(1)}, u32[]{:S(2)}, u32[]{:S(2)}) collective-permute-start(bf16[128,2048]{1,0:T(8,128)(2,1)S(1)} %fusion.40), channel_id=1, source_target_pairs={{0,8},{8,16},{16,24},{24,28},{28,20},{20,12},{12,4},{4,0},{1,9},{9... | collective-permute-start | bytes 1572872 | tf_op jit(solution)/shard_map/ppermute | solution.py:513
  (131 other events, 2207.0 us)
Sparse Core Ops, SparseCore 0:
  151.9 61.8 all-gather.1
  492.9 30.4 reduce-scatter.5
  526.2 73.3 reduce-scatter.7
  654.1 131.6 reduce-scatter.3

commit v3 on v2

--- a/solution.py
+++ b/solution.py
@@ -30,13 +30,16 @@
     return jnp.mean(value, axis=0, keepdims=True)
 
 
-def chunk_rows(ref_value, heads, lanes):
-    tokens = ref_value.shape[1]
-    parts = [
-        ref_value[h, m * MB : (m + 1) * MB, lanes[0] : lanes[1]]
-        for m in range(tokens // MB)
-        for h in range(heads)
-    ]
+def chunk_rows(value, heads, start, lanes, size):
+    tokens = value.shape[0]
+    cuts = [value[:, lanes * h + start : lanes * h + start + size] for h in range(heads)]
+    parts = [cut[m * MB : (m + 1) * MB] for m in range(tokens // MB) for cut in cuts]
+    return jnp.concatenate(parts, axis=0)
+
+
+def head_rows(rows, heads, h):
+    step = MB * heads
+    parts = [rows[m * step + h * MB : m * step + (h + 1) * MB] for m in range(rows.shape[0] // step)]
     return jnp.concatenate(parts, axis=0)
 
 
@@ -69,7 +72,7 @@
     heads, idx_ref, x_ref, info_ref, gb_ref, init_ref, out_ref, n_ref, r_ref, nb_ref, stat_ref, w_ref, state
 ):
     head_dim = gb_ref.shape[1]
-    tokens = x_ref.shape[1]
+    tokens = x_ref.shape[0]
     count = heads * tokens
     full = init_ref.shape[1]
     wide = full - 128
@@ -82,9 +85,9 @@
     w_ref[0] = carried
     info = info_ref[...]
     x = x_ref[...]
-    q_rows = chunk_rows(x, heads, (0, head_dim))
-    k_rows = chunk_rows(x, heads, (head_dim, 2 * head_dim))
-    v_rows = chunk_rows(x, heads, (2 * head_dim, 3 * head_dim))
+    q_rows = chunk_rows(x, heads, 0, 3 * head_dim, head_dim)
+    k_rows = chunk_rows(x, heads, head_dim, 3 * head_dim, head_dim)
+    v_rows = chunk_rows(x, heads, 2 * head_dim, 3 * head_dim, head_dim)
     q_t = jnp.transpose(q_rows.astype(F32))
     target_t = jnp.transpose(v_rows.astype(F32) - k_rows.astype(F32))
     mb_row, mb_col, t_row, t_col, same, columns = chunk_masks(info, heads, count)
@@ -144,13 +147,12 @@
     stat_ref[1:2, :] = inv
     wide_gain = jnp.concatenate([gain] * repeats, axis=1)
     wide_shift = jnp.concatenate([shift] * repeats, axis=1)
-    out_rows = jnp.transpose(q_t + nb * wide_gain + wide_shift)
-    for m in range(tokens // MB):
-        for h in range(heads):
-            at = (m * heads + h) * MB
-            out_ref[m * MB : (m + 1) * MB, h * head_dim : (h + 1) * head_dim] = out_rows[
-                at : at + MB
-            ]
+    out_t = q_t + nb * wide_gain + wide_shift
+    stat_ref[2:3, :] = jnp.sum(out_t, axis=0, keepdims=True)
+    stat_ref[3:4, :] = jnp.sum(out_t * out_t, axis=0, keepdims=True)
+    out_rows = jnp.transpose(out_t)
+    for h in range(heads):
+        out_ref[:, h * head_dim : (h + 1) * head_dim] = head_rows(out_rows, heads, h)
     base = jnp.where(info[4:5, 0:1] > 0.5, init, carried)
     state[...] = base - mm((r_ref[...] * info[3:4, :]).astype(BF16), k_aug)
 
@@ -160,6 +162,7 @@
     idx_ref,
     x_ref,
     d_ref,
+    gate_ref,
     info_ref,
     gb_ref,
     init_ref,
@@ -169,13 +172,12 @@
     stat_ref,
     w_ref,
     dx_ref,
-    dr_ref,
     dgb_ref,
     dinit_ref,
     state,
 ):
     head_dim = gb_ref.shape[1]
-    tokens = x_ref.shape[1]
+    tokens = x_ref.shape[0]
     count = heads * tokens
     full = init_ref.shape[1]
     wide = full - 128
@@ -191,15 +193,10 @@
     init = init_ref[...]
     info = info_ref[...]
     x = x_ref[...]
-    d_in = d_ref[...]
-    q_rows = chunk_rows(x, heads, (0, head_dim))
-    k_rows = chunk_rows(x, heads, (head_dim, 2 * head_dim))
-    v_rows = chunk_rows(x, heads, (2 * head_dim, 3 * head_dim))
-    d_heads = [d_in[:, h * head_dim : (h + 1) * head_dim] for h in range(heads)]
-    d_rows = jnp.concatenate(
-        [d_heads[h][m * MB : (m + 1) * MB] for m in range(tokens // MB) for h in range(heads)],
-        axis=0,
-    )
+    q_rows = chunk_rows(x, heads, 0, 3 * head_dim, head_dim)
+    k_rows = chunk_rows(x, heads, head_dim, 3 * head_dim, head_dim)
+    v_rows = chunk_rows(x, heads, 2 * head_dim, 3 * head_dim, head_dim)
+    d_rows = chunk_rows(d_ref[...], heads, 0, head_dim, head_dim)
     target_t = jnp.transpose(v_rows.astype(F32) - k_rows.astype(F32))
     d_t = jnp.transpose(d_rows)
     mb_row, mb_col, t_row, t_col, same, columns = chunk_masks(info, heads, count)
@@ -232,6 +229,7 @@
         shift_sum = shift_sum + d_t[:, cols]
     done = []
     errs = []
+    d_rates = []
     for p in reversed(range(repeats)):
         cols = slice(p * 128, (p + 1) * 128)
         base = dr_base[:, cols]
@@ -256,7 +254,7 @@
             d_z = inv * (d_n - mean_rows(d_n) - n * (mean_rows(d_n * n) + mean_rows(g * plain)))
         done.insert(0, d_z.astype(BF16))
         errs.insert(0, d_err * gain)
-        dr_ref[0:1, cols] = jnp.sum(d_scaled * plain, axis=0, keepdims=True)
+        d_rates.insert(0, jnp.sum(d_scaled * plain, axis=0, keepdims=True))
         gain_sum = gain_sum + d_err * (miss + gain * n)
         shift_sum = shift_sum + d_err * gain
     dgb_ref[0] += gain_sum
@@ -304,10 +302,16 @@
         - mm(r_own, d_stack)
     )
     packed = jnp.concatenate([dq.astype(BF16), dk.astype(BF16), (-e_rows).astype(BF16)], axis=1)
-    for m in range(tokens // MB):
-        for h in range(heads):
-            at = (m * heads + h) * MB
-            dx_ref[h, m * MB : (m + 1) * MB, :] = packed[at : at + MB]
+    each = 3 * head_dim
+    d_logits = jnp.concatenate(d_rates, axis=1) * info[5:6, :]
+    turned = jnp.transpose(jnp.concatenate([d_logits, jnp.zeros((7, count), F32)], axis=0))
+    lane = lax.broadcasted_iota(jnp.int32, (tokens, 128), 1)
+    logit_rows = jnp.zeros((tokens, 128), F32)
+    for h in range(heads):
+        dx_ref[:, h * each : (h + 1) * each] = head_rows(packed, heads, h)
+        logit_rows = jnp.where(lane == h, head_rows(turned, heads, h)[:, 0:1], logit_rows)
+    dx_ref[:, heads * each : heads * each + 128] = logit_rows.astype(BF16)
+    dx_ref[:, heads * each + 128 :] = gate_ref[...]
     row_init = info[2:3, :] > 0.5
     zb_two = jnp.concatenate(
         [jnp.where(row_init, 0.0, d_zbar), jnp.where(row_init, d_zbar, 0.0)], axis=0
@@ -324,7 +328,8 @@
 def chain_specs(heads, tokens, head_dim, full, at):
     count = heads * tokens
     return dict(
-        x=pl.BlockSpec((heads, tokens, 3 * head_dim), lambda i, idx: (0, idx[at(i)], 0)),
+        x=pl.BlockSpec((tokens, heads * 3 * head_dim), lambda i, idx: (idx[at(i)], 0)),
+        dx=pl.BlockSpec((tokens, heads * 4 * head_dim + 128), lambda i, idx: (idx[at(i)], 0)),
         rows=pl.BlockSpec((tokens, heads * head_dim), lambda i, idx: (idx[at(i)], 0)),
         info=pl.BlockSpec((8, count), lambda i, idx: (0, idx[at(i)])),
         gb=pl.BlockSpec((2, head_dim, 128), lambda i, idx: (0, 0, 0)),
@@ -336,8 +341,9 @@
 
 
 def chain_forward(idx, x3, info, gb, init, tokens):
-    heads, total, packed = x3.shape
-    head_dim = packed // 3
+    total = x3.shape[0]
+    head_dim = gb.shape[1]
+    heads = x3.shape[1] // (3 * head_dim)
     chunks = total // tokens
     full = init.shape[1]
     s = chain_specs(heads, tokens, head_dim, full, lambda i: i)
@@ -363,15 +369,16 @@
             dimension_semantics=("arbitrary",), vmem_limit_bytes=32 * 1024 * 1024
         ),
         cost_estimate=pl.CostEstimate(
-            flops=20_000_000_000, bytes_accessed=16_000_000, transcendentals=0
+            flops=1, bytes_accessed=1, transcendentals=0
         ),
         name="chain_forward",
     )(idx, x3, info, gb, init)
 
 
-def chain_backward(idx, x3, d_inner, info, gb, init, kept, tokens):
-    heads, total, packed = x3.shape
-    head_dim = packed // 3
+def chain_backward(idx, x3, d_inner, d_gate, info, gb, init, kept, tokens):
+    total = x3.shape[0]
+    head_dim = gb.shape[1]
+    heads = x3.shape[1] // (3 * head_dim)
     chunks = total // tokens
     full = init.shape[1]
     s = chain_specs(heads, tokens, head_dim, full, lambda i: chunks - 1 - i)
@@ -383,6 +390,7 @@
             in_specs=[
                 s["x"],
                 s["rows"],
+                s["rows"],
                 s["info"],
                 s["gb"],
                 s["init"],
@@ -392,12 +400,11 @@
                 s["stat"],
                 s["weight"],
             ],
-            out_specs=[s["x"], s["info"], s["gb"], s["init"]],
+            out_specs=[s["dx"], s["gb"], s["init"]],
             scratch_shapes=[pltpu.VMEM((head_dim, full), F32)],
         ),
         out_shape=[
-            jax.ShapeDtypeStruct(x3.shape, BF16),
-            jax.ShapeDtypeStruct((8, heads * total), F32),
+            jax.ShapeDtypeStruct((total, heads * 4 * head_dim + 128), BF16),
             jax.ShapeDtypeStruct(gb.shape, F32),
             jax.ShapeDtypeStruct(init.shape, F32),
         ],
@@ -405,13 +412,13 @@
             dimension_semantics=("arbitrary",), vmem_limit_bytes=40 * 1024 * 1024
         ),
         cost_estimate=pl.CostEstimate(
-            flops=30_000_000_000, bytes_accessed=20_000_000, transcendentals=0
+            flops=1, bytes_accessed=1, transcendentals=0
         ),
         name="chain_backward",
-    )(idx, x3, d_inner, info, gb, init, *kept)
-
-
-def chain_info(starts, chunk_start, rates, heads, tokens):
+    )(idx, x3, d_inner, d_gate, info, gb, init, *kept)
+
+
+def chain_info(starts, chunk_start, rates, factors, heads, tokens):
     blocks = tokens // MB
     chunks = chunk_start.shape[0]
 
@@ -427,8 +434,12 @@
         [item.astype(F32) for item in (doc, doc > before, doc == end, fresh)]
     ).reshape(4, chunks * blocks, 1)
     spread = jnp.broadcast_to(spread, (4, chunks * blocks, heads * MB)).reshape(4, -1)
-    rate_row = jnp.swapaxes(rates.reshape(-1, MB, heads), 1, 2).reshape(1, -1)
-    return jnp.concatenate([rate_row, spread, jnp.zeros((3, rate_row.shape[1]), F32)], axis=0)
+
+    def as_row(item):
+        return jnp.swapaxes(item.reshape(-1, MB, heads), 1, 2).reshape(1, -1)
+
+    rows = [as_row(rates), spread, as_row(factors)]
+    return jnp.concatenate(rows + [jnp.zeros((2, spread.shape[1]), F32)], axis=0)
 
 
 def chain_params(init_weight, init_bias, inner_gain, inner_bias):
@@ -461,14 +472,252 @@
     return d_w, d_b, both[0].T, both[1].T
 
 
+def cut_kernel(turned, share, padded, *refs):
+    mats, out_ref, held = refs[: len(turned)], refs[-2], refs[-1]
+    for i, mat in enumerate(mats):
+        value = mat[...].astype(F32)
+        held[...] = jnp.transpose(value) if turned[i] else value
+        for s in range(out_ref.shape[0]):
+            out_ref[s, i * padded : i * padded + share] = held[
+                s * share : (s + 1) * share
+            ].astype(BF16)
+            if padded > share:
+                out_ref[s, i * padded + share : (i + 1) * padded] = jnp.zeros(
+                    (padded - share, out_ref.shape[2]), BF16
+                )
+
+
+def cut_features(seq, mats, turned):
+    features = mats[0].shape[1] if turned[0] else mats[0].shape[0]
+    cols = mats[0].shape[0] if turned[0] else mats[0].shape[1]
+    share = features // seq
+    padded = share + -share % MB
+    return pl.pallas_call(
+        partial(cut_kernel, turned, share, padded),
+        out_shape=jax.ShapeDtypeStruct((seq, len(mats) * padded, cols), BF16),
+        scratch_shapes=[pltpu.VMEM((features, cols), F32)],
+        compiler_params=pltpu.CompilerParams(vmem_limit_bytes=24 * 1024 * 1024),
+        cost_estimate=pl.CostEstimate(flops=1, bytes_accessed=1, transcendentals=0),
+        name="cut_features",
+    )(*mats)
+
+
+def join_kernel(turned, share, padded, in_ref, *refs):
+    outs, held = refs[:-1], refs[-1]
+    for i, out in enumerate(outs):
+        for s in range(in_ref.shape[0]):
+            held[s * share : (s + 1) * share] = in_ref[
+                s, i * padded : i * padded + share
+            ].astype(F32)
+        out[...] = jnp.transpose(held[...]) if turned[i] else held[...]
+
+
+def join_features(block, features, turned):
+    seq, rows, cols = block.shape
+    shapes = [(cols, features) if turn else (features, cols) for turn in turned]
+    return pl.pallas_call(
+        partial(join_kernel, turned, features // seq, rows // len(turned)),
+        out_shape=[jax.ShapeDtypeStruct(shape, F32) for shape in shapes],
+        scratch_shapes=[pltpu.VMEM((features, cols), F32)],
+        compiler_params=pltpu.CompilerParams(vmem_limit_bytes=24 * 1024 * 1024),
+        cost_estimate=pl.CostEstimate(flops=1, bytes_accessed=1, transcendentals=0),
+        name="join_features",
+    )(block)
+
+
+def ffn_kernel(count, parts, kept, member_ref, *refs):
+    rows_refs = refs[:count]
+    grad_refs = refs[count : 2 * count]
+    weights = refs[2 * count : 2 * count + parts]
+    outs = refs[2 * count + parts + kept :]
+    (x_ref, g_ref, at_ref, ut_ref, ht_ref, y_ref, d_ref, a_t, u_t, h_t, y_all, d_all) = outs
+    step = pl.program_id(0)
+    size = rows_refs[0].shape[0]
+
+    @pl.when(step == 0)
+    def _():
+        padded = weights[0].shape[0] // 3
+        swish, up, down = (
+            jnp.concatenate([w[i * padded : (i + 1) * padded] for w in weights], axis=0)
+            for i in range(3)
+        )
+        rows = jnp.concatenate([ref[...] for ref in rows_refs], axis=0)
+        grad = jnp.concatenate([ref[0] for ref in grad_refs], axis=0)
+        act_a = mm_nt(rows, swish)
+        act_u = mm_nt(rows, up)
+        d_hidden = mm_nt(grad, down)
+        sig = jax.nn.sigmoid(act_a)
+        gate = act_a * sig
+        hidden = gate * act_u
+        d_a = d_hidden * act_u * sig * (1.0 + act_a * (1.0 - sig))
+        d_u = d_hidden * gate
+        d_all[...] = (mm(d_a.astype(BF16), swish) + mm(d_u.astype(BF16), up)).astype(BF16)
+        y_all[...] = mm(hidden.astype(BF16), down).astype(BF16)
+        fill = -hidden.shape[1] % 128
+        for out, value in ((a_t, d_a), (u_t, d_u), (h_t, hidden)):
+            if fill:
+                value = jnp.concatenate([value, jnp.zeros((value.shape[0], fill), F32)], axis=1)
+            out[...] = jnp.transpose(value)[: out.shape[0]].astype(BF16)
+
+    for i in range(count):
+
+        @pl.when(step == i)
+        def _(i=i):
+            part = slice(i * size, (i + 1) * size)
+            x_ref[...] = rows_refs[i][...]
+            g_ref[...] = grad_refs[i][0]
+            at_ref[...] = a_t[:, part]
+            ut_ref[...] = u_t[:, part]
+            ht_ref[...] = h_t[:, part]
+            y_ref[0] = y_all[part]
+            d_ref[...] = d_all[part]
+
+
+def ffn_step(members, slot, rows, grad_all, weights, kept):
+    count = len(rows)
+    size, width = rows[0].shape
+    seq = grad_all.shape[0]
+    total = seq * size
+    features = sum(w.shape[0] for w in weights) // 3
+    whole = pl.BlockSpec(memory_space=pltpu.VMEM)
+
+    def grad_spec(i):
+        return pl.BlockSpec((1, size, width), lambda s, member: (member[i], 0, 0))
+
+    row_spec = pl.BlockSpec((size, width), lambda s, member: (slot + s, 0))
+    turned_spec = pl.BlockSpec((features, size), lambda s, member: (0, slot + s))
+    turned = jax.ShapeDtypeStruct((features, total), BF16)
+    tall = jax.ShapeDtypeStruct((total, width), BF16)
+    first = 1 + 2 * count + len(weights)
+    out = pl.pallas_call(
+        partial(ffn_kernel, count, len(weights), len(kept)),
+        grid_spec=pltpu.PrefetchScalarGridSpec(
+            num_scalar_prefetch=1,
+            grid=(count,),
+            in_specs=[whole] * count
+            + [grad_spec(i) for i in range(count)]
+            + [whole] * len(weights)
+            + [pl.BlockSpec(memory_space=pl.ANY)] * len(kept),
+            out_specs=[row_spec, row_spec]
+            + [turned_spec] * 3
+            + [
+                pl.BlockSpec((1, size, width), lambda s, member: (member[s], 0, 0)),
+                pl.BlockSpec((size, width), lambda s, member: (s, 0)),
+            ],
+            scratch_shapes=[pltpu.VMEM((features, count * size), BF16)] * 3
+            + [pltpu.VMEM((count * size, width), BF16)] * 2,
+        ),
+        out_shape=[tall, tall, turned, turned, turned]
+        + [
+            jax.ShapeDtypeStruct((seq, size, width), BF16),
+            jax.ShapeDtypeStruct((count * size, width), BF16),
+        ],
+        input_output_aliases={first + i: i for i in range(len(kept))},
+        compiler_params=pltpu.CompilerParams(
+            dimension_semantics=("arbitrary",), vmem_limit_bytes=48 * 1024 * 1024
+        ),
+        cost_estimate=pl.CostEstimate(
+            flops=12_000_000_000, bytes_accessed=1, transcendentals=0
+        ),
+        name="ffn_step",
+    )(members, *rows, *([grad_all] * count), *weights, *kept)
+    return out[:-1], out[-1]
+
+
+def ffn_grad_kernel(parts, at_ref, ut_ref, ht_ref, x_ref, g_ref, *outs):
+    x = x_ref[...]
+    g = g_ref[...]
+    padded = at_ref.shape[0] // parts
+    for i, out in enumerate(outs):
+        own = slice(i * padded, (i + 1) * padded)
+        out[:padded] = mm(at_ref[own], x).astype(BF16)
+        out[padded : 2 * padded] = mm(ut_ref[own], x).astype(BF16)
+        out[2 * padded :] = mm(ht_ref[own], g).astype(BF16)
+
+
+def ffn_grads(parts, kept):
+    x, g, a_t, u_t, h_t = kept
+    total, width = x.shape
+    features = a_t.shape[0]
+    wide = pl.BlockSpec((total, 256), lambda i: (0, i))
+    whole = pl.BlockSpec((features, total), lambda i: (0, 0))
+    rows = 3 * features // parts
+    return pl.pallas_call(
+        partial(ffn_grad_kernel, parts),
+        grid=(width // 256,),
+        in_specs=[whole] * 3 + [wide] * 2,
+        out_specs=[pl.BlockSpec((rows, 256), lambda i: (0, i))] * parts,
+        out_shape=[jax.ShapeDtypeStruct((rows, width), BF16)] * parts,
+        compiler_params=pltpu.CompilerParams(
+            dimension_semantics=("arbitrary",), vmem_limit_bytes=40 * 1024 * 1024
+        ),
+        cost_estimate=pl.CostEstimate(
+            flops=12_000_000_000, bytes_accessed=1, transcendentals=0
+        ),
+        name="ffn_grads",
+    )(a_t, u_t, h_t, x, g)
+
+
+def proj_grad_kernel(heads, head_dim, d_ref, x_ref, w_ref, *refs):
+    outs, rate_ref, gain_ref, turned = refs[:heads], refs[heads], refs[heads + 1], refs[heads + 2]
+    each = 3 * head_dim
+
+    @pl.when(pl.program_id(0) == 0)
+    def _():
+        turned[...] = jnp.transpose(d_ref[...].astype(F32)).astype(BF16)
+
+    grad = mm(turned[...], x_ref[...])
+    gain_ref[...] = jnp.broadcast_to(
+        jnp.sum(grad * w_ref[...].astype(F32), axis=0, keepdims=True), gain_ref.shape
+    )
+    gate = heads * each + 128
+    for h, out in enumerate(outs):
+        out[:each] = grad[h * each : (h + 1) * each].astype(BF16)
+        out[each:] = grad[gate + h * head_dim : gate + (h + 1) * head_dim].astype(BF16)
+    rate_ref[...] = grad[heads * each : heads * each + 8]
+
+
+def proj_grads(d_x, normed, weight, heads, head_dim):
+    total, packed = d_x.shape
+    width = normed.shape[1]
+
+    def wide(rows):
+        return pl.BlockSpec((rows, 256), lambda i: (0, i))
+
+    return pl.pallas_call(
+        partial(proj_grad_kernel, heads, head_dim),
+        grid=(width // 256,),
+        in_specs=[pl.BlockSpec((total, packed), lambda i: (0, 0)), wide(total), wide(packed)],
+        out_specs=[wide(4 * head_dim)] * heads + [wide(8)] * 2,
+        out_shape=[jax.ShapeDtypeStruct((4 * head_dim, width), BF16)] * heads
+        + [jax.ShapeDtypeStruct((8, width), F32)] * 2,
+        scratch_shapes=[pltpu.VMEM((packed, total), BF16)],
+        compiler_params=pltpu.CompilerParams(
+            dimension_semantics=("arbitrary",), vmem_limit_bytes=40 * 1024 * 1024
+        ),
+        cost_estimate=pl.CostEstimate(
+            flops=9_000_000_000, bytes_accessed=1, transcendentals=0
+        ),
+        name="proj_grads",
+    )(d_x, normed, weight)
+
+
 def trans_dot(left, right):
     return lax.dot_general(
         left, right, (((0,), (0,)), ((), ())), preferred_element_type=jnp.float32
     )
 
 
-def tie(*values):
-    return lax.optimization_barrier(values)
+def after(value, *first):
+    anywhere = pl.BlockSpec(memory_space=pl.ANY)
+    return pl.pallas_call(
+        lambda *refs: None,
+        out_shape=jax.ShapeDtypeStruct(value.shape, value.dtype),
+        in_specs=[anywhere] * (1 + len(first)),
+        out_specs=anywhere,
+        input_output_aliases={0: 0},
+        name="after",
+    )(value, *first)
 
 
 def ring_pairs(size, step):
@@ -485,38 +734,50 @@
 
 
 def slot_steps(size):
-    steps = [0]
+    steps = [0, -(size // 2)]
     for s in range(1, size // 2):
         steps += [-s, s]
-    return steps + [-(size // 2)]
-
-
-def ring_gather(block, size):
+    return steps
+
+
+def by_slots(arrived):
+    return [arrived[0], arrived[-1]] + list(arrived[1:-1])
+
+
+def ring_gather(block, size, work=None):
     arrived = [(block,)]
     ahead = back = block
     for s in range(1, size // 2 + 1):
+        done = work(s - 1, arrived[-1]) if work else []
         ahead = lax.ppermute(ahead, "seq", ring_pairs(size, 1))
+        if done:
+            ahead = after(ahead, *done)
         if s < size // 2:
             back = lax.ppermute(back, "seq", ring_pairs(size, -1))
-            ahead, back = tie(ahead, back)
             arrived.append((ahead, back))
         else:
             arrived.append((ahead,))
+    if work:
+        work(size // 2, arrived[-1])
     return arrived
 
 
-def ring_scatter(part, size):
+def ring_scatter(part, size, work=()):
     half = size // 2
     ahead, back = part(half).astype(BF16), part(1 - half).astype(BF16)
     for s in range(1, half + 1):
-        ahead, back = tie(ahead, back)
-        ahead = lax.ppermute(ahead, "seq", ring_pairs(size, 1)).astype(F32)
+        done = work[s - 1](ahead) if s <= len(work) else []
+        ahead = lax.ppermute(ahead, "seq", ring_pairs(size, 1))
         if s < half:
-            back = lax.ppermute(back, "seq", ring_pairs(size, -1)).astype(F32)
+            back = lax.ppermute(back, "seq", ring_pairs(size, -1))
+        if done:
+            ahead = after(ahead, *done)
+        ahead = ahead.astype(F32)
+        if s < half:
             ahead = (ahead + part(half - s)).astype(BF16)
             if s < half - 1:
-                back = (back + part(1 - half + s)).astype(BF16)
-    return part(0) + ahead + back
+                back = (back.astype(F32) + part(1 - half + s)).astype(BF16)
+    return part(0).astype(F32) + ahead + back.astype(F32)
 
 
 def pairwise_sum(value, axis, size):
@@ -531,31 +792,46 @@
     return lax.ppermute(value, "grp", [(i, i ^ bit) for i in range(4)])
 
 
-def grp_gather(value):
+def near(index, k):
+    return index ^ k if lax.axis_size("grp") == 4 else k
+
+
+def start_gather(value):
     if lax.axis_size("grp") != 4:
-        return lax.all_gather(value, "grp", axis=0)
-    index = lax.axis_index("grp")
-    across = swap(value, 2)
-    beside = swap(value, 1)
-    corner = swap(across, 1)
-    out = jnp.zeros((4,) + value.shape, value.dtype)
-    for k, block in enumerate((value, beside, across, corner)):
-        out = lax.dynamic_update_index_in_dim(out, block, index ^ k, 0)
-    return out
-
-
-def grp_scatter(value):
+        whole = lax.all_gather(value, "grp", axis=0)
+        return [whole[k] for k in range(whole.shape[0])]
+    return [value, swap(value, 1), swap(value, 2)]
+
+
+def end_gather(parts):
     if lax.axis_size("grp") != 4:
-        return lax.psum_scatter(value.astype(BF16), "grp", scatter_dimension=0, tiled=False)
-    index = lax.axis_index("grp")
-
-    def block(k):
-        return lax.dynamic_index_in_dim(value, index ^ k, 0, keepdims=False)
-
-    corner = swap(block(3).astype(BF16), 1).astype(F32)
-    across = swap((corner + block(2)).astype(BF16), 2).astype(F32)
+        return parts
+    return parts + [swap(parts[2], 1)]
+
+
+def start_scatter(block):
+    if lax.axis_size("grp") != 4:
+        whole = jnp.stack([block(k) for k in range(lax.axis_size("grp"))]).astype(BF16)
+        return lax.psum_scatter(whole, "grp", scatter_dimension=0, tiled=False)
+    return swap(block(3).astype(BF16), 1)
+
+
+def cross_scatter(block, corner):
+    if lax.axis_size("grp") != 4:
+        return corner
+    return swap((corner.astype(F32) + block(2)).astype(BF16), 2)
+
+
+def end_scatter(block, across):
+    if lax.axis_size("grp") != 4:
+        return across
     beside = swap(block(1).astype(BF16), 1).astype(F32)
-    return (block(0) + beside + across).astype(BF16)
+    return (block(0) + beside + across.astype(F32)).astype(BF16)
+
+
+def in_turn(blocks, order):
+    picked = [lax.dynamic_index_in_dim(blocks, order[i], 0) for i in range(blocks.shape[0])]
+    return jnp.concatenate(picked, axis=0)
 
 
 class HeadPlan:
@@ -565,13 +841,23 @@
         self.mixed = (heads // grp) % seq == 0
         self.each = (heads // grp) // seq if self.mixed else 0
 
-    def pick(self, item, seq_index):
+    def pick(self, item, seq_index, grp_index):
         rest = item.shape[1:]
         if self.mixed:
             item = item.reshape((self.grp, self.seq, self.each) + rest)
             item = lax.dynamic_index_in_dim(item, seq_index, 1, keepdims=False)
-            return item.reshape((self.local,) + rest)
+            return self.turn(item.reshape((self.local,) + rest), grp_index)
         return lax.dynamic_slice_in_dim(item, seq_index * self.local, self.local, 0)
+
+    def turn(self, item, grp_index):
+        if not self.mixed:
+            return item
+        item = item.reshape((self.grp, self.each) + item.shape[1:])
+        parts = [
+            lax.dynamic_index_in_dim(item, near(grp_index, k), 0, keepdims=False)
+            for k in range(self.grp)
+        ]
+        return jnp.concatenate(parts, axis=0)
 
     def order(self, item):
         rest = item.shape[2:]
@@ -585,35 +871,53 @@
     return lax.all_to_all(block, "seq", 0, 0, tiled=True)
 
 
-def gather_heads(plan, mats, head_dim, gather):
-    cols = mats[0].shape[1]
+def cut_heads(plan, mats, turned, head_dim):
     count = len(mats)
     seq = plan.seq
+    if plan.each == 1:
+        return cut_features(seq, mats, turned)
+    mats = [m.T if turn else m for m, turn in zip(mats, turned)]
+    cols = mats[0].shape[1]
     if plan.mixed:
         block = jnp.stack([m.reshape(seq, plan.each, head_dim, cols) for m in mats], axis=2)
-        block = exchange(block.reshape(seq, -1, cols))
-        block = block.transpose(1, 0, 2).reshape(plan.each, count * head_dim, seq * cols)
-        return gather(block).reshape(plan.local, count * head_dim, seq * cols)
-    block = lax.all_gather(jnp.stack(mats), "grp", axis=1, tiled=True)
-    block = block.reshape(count, seq, plan.local, head_dim, cols).transpose(1, 2, 0, 3, 4)
-    block = exchange(block.reshape(seq, -1, cols))
-    return block.transpose(1, 0, 2).reshape(plan.local, count * head_dim, seq * cols)
-
-
-def scatter_heads(plan, grads, count, scatter):
-    local, packed, width = grads.shape
+    else:
+        block = lax.all_gather(jnp.stack(mats), "grp", axis=1, tiled=True)
+        block = block.reshape(count, seq, plan.local, head_dim, cols).transpose(1, 2, 0, 3, 4)
+    return block.reshape(seq, -1, cols)
+
+
+def gather_heads(plan, block, count, head_dim):
+    seq, _, cols = block.shape
+    block = block.transpose(1, 0, 2).reshape(-1, seq * cols)
+    parts = end_gather(start_gather(block)) if plan.mixed else [block]
+    size = count * head_dim
+    return [part[i : i + size] for part in parts for i in range(0, part.shape[0], size)]
+
+
+def heads_block(plan, grads):
+    each = plan.each
+    return lambda k: jnp.concatenate(grads[k * each : (k + 1) * each], axis=0)
+
+
+def scatter_heads(plan, grads, block, count):
+    packed, width = grads[0].shape
     seq = plan.seq
     cols = width // seq
     head_dim = packed // count
     if plan.mixed:
-        block = scatter(grads.reshape(plan.grp, plan.each * packed, width))
-        block = block.reshape(-1, seq, cols).transpose(1, 0, 2)
-        block = exchange(block).reshape(seq, plan.each, count, head_dim, cols)
-        return block.transpose(2, 0, 1, 3, 4).reshape(count, -1, cols).astype(F32)
-    block = grads.astype(BF16).reshape(local * packed, seq, cols).transpose(1, 0, 2)
-    block = exchange(block).reshape(seq, local, count, head_dim, cols)
+        each = plan.each
+        block = exchange(block.reshape(-1, seq, cols).transpose(1, 0, 2))
+        if each == 1:
+            return join_features(block, seq * head_dim, (True,) * count)
+        block = block.reshape(seq, each, count, head_dim, cols)
+        block = block.transpose(2, 0, 1, 3, 4).reshape(count, -1, cols).astype(F32)
+        return [part.T for part in block]
+    block = jnp.concatenate(grads, axis=0).astype(BF16)
+    block = block.reshape(-1, seq, cols).transpose(1, 0, 2)
+    block = exchange(block).reshape(seq, plan.local, count, head_dim, cols)
     block = block.transpose(2, 0, 1, 3, 4).reshape(count, -1, cols)
-    return lax.psum_scatter(block, "grp", scatter_dimension=1, tiled=True).astype(F32)
+    block = lax.psum_scatter(block, "grp", scatter_dimension=1, tiled=True).astype(F32)
+    return [part.T for part in block]
 
 
 def body(
@@ -650,13 +954,12 @@
     local = plan.local
     features = local * head_dim
     stream = rows_tok * seq
-    far = partial(lax.all_gather, axis_name="grp", axis=0)
     steps = slot_steps(seq)
     place = ring_place(seq, seq_index)
     member_of_slot = ring_member(seq, (place + jnp.array(steps, jnp.int32)) % seq)
     apart = (ring_place(seq, jnp.arange(seq, dtype=jnp.int32)) - place) % seq
-    slot_of_member = jnp.where(apart >= seq // 2, 2 * (seq - apart) - 1, 2 * apart)
-    slot_of_member = jnp.where(apart == 0, 0, slot_of_member)
+    slot_of_member = jnp.where(apart > seq // 2, 2 * (seq - apart), 2 * apart + 1)
+    slot_of_member = jnp.where(apart == 0, 0, jnp.where(apart == seq // 2, 1, slot_of_member))
     to_slots = (member_of_slot[:, None] == jnp.arange(seq)[None, :]).astype(F32)
 
     def in_slots(stat):
@@ -669,30 +972,16 @@
         out = jnp.einsum("sm,kst->kmt", to_slots, cut, precision=lax.Precision.HIGHEST)
         return out.reshape(-1, stream)
 
+    def pick(item):
+        return plan.pick(item, seq_index, grp_index)
+
     def by_distance(rows):
-        cut = rows.reshape(seq, rows_tok, width)
-        return lambda k: cut[steps.index(k if k < seq // 2 else k - seq)]
-
-    w_proj = gather_heads(plan, (w_query.T, w_key.T, w_value.T), head_dim, grp_gather)
-    token_steps = ring_gather(tokens[0], seq)
-    stream_rows = jnp.concatenate(sum(token_steps, ()), axis=0).astype(F32)
-    w_side = gather_heads(plan, (w_gate.T, w_out), head_dim, grp_gather)
-    grad_own, _ = tie(cotangent[0], token_steps[-1][0])
-    grad_steps = ring_gather(grad_own, seq)
-    share = w_down.shape[0] // seq
-    padded = share + -share % MB
-
-    def cut_hidden(mat):
-        cut = mat.reshape(seq, share, mat.shape[1])
-        return jnp.pad(cut, ((0, 0), (0, padded - share), (0, 0)))
-
-    ffn_block = jnp.concatenate([cut_hidden(m) for m in (w_swish.T, w_up.T, w_down)], axis=1)
-    ffn_block, _ = tie(ffn_block, token_steps[-1][0])
-    ffn_block = exchange(ffn_block).transpose(1, 0, 2).reshape(3 * padded, width)
-    ffn_all = far(ffn_block).reshape(groups, 3, padded, width)
-    m_swish, m_up, m_down = (ffn_all[:, i].reshape(groups * padded, width) for i in range(3))
-    m_gate = w_side[:, :head_dim].reshape(features, width)
-    m_out = w_side[:, head_dim:].reshape(features, width)
+        return lambda k: lax.slice_in_dim(
+            rows, at_slot(k) * rows_tok, (at_slot(k) + 1) * rows_tok, axis=0
+        )
+
+    def at_slot(k):
+        return steps.index(k if k < seq // 2 else k - seq)
 
     own_lengths = lax.dynamic_index_in_dim(lengths, grp_index, 0, keepdims=False)
     ends = jnp.cumsum(own_lengths)
@@ -701,81 +990,125 @@
     positions = (chunk_start[:, None] + jnp.arange(rows_tok, dtype=jnp.int32)).reshape(stream, 1)
     live = (positions < ends[-1]).astype(F32)
 
-    inv_first = lax.rsqrt(jnp.mean(stream_rows * stream_rows, -1, keepdims=True) + EPS)
-    unit_all = stream_rows * inv_first
-    normed = (unit_all * prenorm_gain).astype(BF16)
-    x3 = jnp.stack([mm_nt(normed, w_proj[h]).astype(BF16) for h in range(local)])
-    gate_pre = mm_nt(normed, m_gate)
-    rate_rows = plan.pick(rate_weight.T, seq_index)
-    logits = mm_nt(normed, rate_rows) + plan.pick(rate_bias, seq_index)
+    proj_block = exchange(
+        cut_heads(plan, (w_query, w_key, w_value), (True, True, True), head_dim)
+    )
+    padded = w_down.shape[0] // seq
+    padded += -padded % MB
+    token_steps = ring_gather(tokens[0], seq)
+    last_tokens = token_steps[-1][0]
+    rate_rows = jnp.pad(pick(rate_weight.T), ((0, 128 - local), (0, 0)))
+    w_proj = jnp.concatenate(gather_heads(plan, proj_block, 3, head_dim) + [rate_rows], axis=0)
+    packed = w_proj.shape[0] - 128
+    side_block = cut_heads(plan, (w_gate, w_out), (True, False), head_dim)
+    side_block = exchange(after(side_block, last_tokens))
+    ffn_block = cut_features(seq, (w_swish, w_up, w_down), (True, True, False))
+    ffn_block = exchange(after(ffn_block, last_tokens))
+    grad_own = cotangent[0]
+    grad_all = lax.all_gather(after(grad_own, ffn_block), "seq", axis=0)
+
+    kept_first = []
+    for arrived in token_steps:
+        rows = jnp.concatenate(arrived, axis=0).astype(F32)
+        inv = lax.rsqrt(jnp.mean(rows * rows, -1, keepdims=True) + EPS)
+        unit_gain = (rows * inv * prenorm_gain).astype(BF16)
+        out = mm_nt(unit_gain, w_proj)
+        kept_first.append((unit_gain, out[:, :packed].astype(BF16), out[:, packed:]))
+    normed, x3, logits = (
+        jnp.concatenate(items, axis=0) for items in zip(*by_slots(kept_first))
+    )
+    logits = logits[:, :local] + pick(rate_bias)
     rate_sig = jax.nn.sigmoid(logits)
     rates = rate_sig / head_dim * live
-    gb, init = chain_params(
-        *(plan.pick(item, seq_index) for item in (init_weight, init_bias, inner_gain, inner_bias))
-    )
-    info = chain_info(starts, chunk_start, rates, local, rows_tok)
+    factors = live * rate_sig * (1.0 - rate_sig) / head_dim
+    gb, init = chain_params(*(pick(i) for i in (init_weight, init_bias, inner_gain, inner_bias)))
+    info = chain_info(starts, chunk_start, rates, factors, local, rows_tok)
     inner, *kept = chain_forward(slot_of_member, x3, info, gb, init, rows_tok)
-
-    sums = jnp.stack([jnp.sum(inner, -1), jnp.sum(inner * inner, -1)])
-    sums = in_slots(pairwise_sum(in_order(sums), "seq", seq)) / width
+    kept_stat = after(kept[3], side_block, ffn_block)
+
+    sides = gather_heads(plan, side_block, 2, head_dim)
+    m_gate = jnp.concatenate([side[:head_dim] for side in sides], axis=0)
+    m_out = jnp.concatenate([side[head_dim:] for side in sides], axis=0)
+    gate_pre = mm_nt(normed, m_gate)
+    ffn_block = ffn_block.transpose(1, 0, 2).reshape(3 * padded, width)
+    ffn_parts = start_gather(ffn_block)
+
+    sums = jnp.sum(kept_stat[2:4].reshape(2, stream // MB, local, MB), axis=2).reshape(2, stream)
+    sums = in_slots(pairwise_sum(sums, "seq", seq)) / width
     mean_o = sums[0][:, None]
     inv_o = lax.rsqrt(sums[1][:, None] - mean_o * mean_o + EPS)
     o_hat = (inner - mean_o) * inv_o
-    post_g = plan.pick(post_gain.reshape(heads, head_dim), seq_index).reshape(features)
-    post_b = plan.pick(post_bias.reshape(heads, head_dim), seq_index).reshape(features)
+    post_g = pick(post_gain.reshape(heads, head_dim)).reshape(features)
+    post_b = pick(post_bias.reshape(heads, head_dim)).reshape(features)
     post = o_hat * post_g + post_b
     gelu_val, gelu_pull = jax.vjp(jax.nn.gelu, gate_pre)
     gated = (gelu_val * post).astype(BF16)
-    mixing = ring_scatter(by_distance(mm(gated, m_out)), seq)
+    ffn = {}
+
+    mixing = ring_scatter(
+        by_distance(mm(gated, m_out).astype(BF16)),
+        seq,
+        [lambda since: [], lambda since: [], lambda since: [], lambda since: ffn_parts[2:3]],
+    )
+    ffn["parts"] = end_gather(ffn_parts)
     own_rows = tokens[0].astype(F32)
     resid = own_rows + mixing
     inv_second = lax.rsqrt(jnp.mean(resid * resid, -1, keepdims=True) + EPS)
     unit_second = resid * inv_second
     ffn_in = (unit_second * feedforward_norm_gain).astype(BF16)
 
-    kept_ffn = []
-    for arrived, grads in zip(ring_gather(ffn_in, seq), grad_steps):
-        rows = jnp.concatenate(arrived, axis=0)
-        grad = jnp.concatenate(grads, axis=0)
-        act_a = mm_nt(rows, m_swish)
-        act_u = mm_nt(rows, m_up)
-        sig_a = jax.nn.sigmoid(act_a)
-        hidden = (act_a * sig_a * act_u).astype(BF16)
-        d_hidden = mm_nt(grad, m_down)
-        d_a = (d_hidden * act_u * sig_a * (1.0 + act_a * (1.0 - sig_a))).astype(BF16)
-        d_u = (d_hidden * act_a * sig_a).astype(BF16)
-        d_in = mm(d_a, m_swish) + mm(d_u, m_up)
-        kept_ffn.append((rows, grad, hidden, d_a, d_u, d_in))
-    ffn_rows, grad_rows, hidden, d_a, d_u, d_in = (
-        jnp.concatenate(items, axis=0) for items in zip(*kept_ffn)
-    )
-    d_ffn = ring_scatter(by_distance(d_in), seq)
-    g_ffn = jnp.stack(
-        [
-            trans_dot(left, right).astype(BF16).reshape(groups, padded, width)
-            for left, right in ((d_a, ffn_rows), (d_u, ffn_rows), (hidden, grad_rows))
-        ],
-        axis=1,
-    ).reshape(groups, 3 * padded, width)
-    g_ffn = lax.psum_scatter(g_ffn, "grp", scatter_dimension=0, tiled=False)
-    g_ffn = exchange(g_ffn.reshape(3 * padded, seq, -1).transpose(1, 0, 2))
-    g_ffn = g_ffn.reshape(seq, 3, padded, -1)[:, :, :share].transpose(1, 0, 2, 3)
-    g_ffn = g_ffn.reshape(3, seq * share, -1).astype(F32)
-    ffn_part = mm(hidden, m_down).astype(BF16).reshape(seq, rows_tok, width)
-    ffn_part = jnp.take(ffn_part, slot_of_member, axis=0)
-    ffn_out = lax.psum_scatter(ffn_part, "seq", scatter_dimension=0, tiled=False).astype(F32)
-    out_tokens = (resid + ffn_out).astype(BF16)[None]
-
+    got = {"kept": ()}
+    d_parts = {}
+
+    def step_work(s, arrived):
+        slot = 2 * s if s < seq // 2 else 1
+        members = lax.slice_in_dim(member_of_slot, slot, slot + len(arrived))
+        got["kept"], d_in = ffn_step(
+            members, slot, arrived, grad_all, ffn["parts"], got["kept"]
+        )
+        for i in range(len(arrived)):
+            d_parts[steps[slot + i]] = d_in[i * rows_tok : (i + 1) * rows_tok]
+        return [d_in]
+
+    ring_gather(ffn_in, seq, step_work)
+    kept_ffn = got["kept"]
+
+    def ffn_work(since):
+        rows, *others = kept_ffn[:5]
+        got["ffn"] = ffn_grads(groups, [after(rows, since)] + others)
+        return got["ffn"][:1]
+
+    def ffn_corner(since):
+        got["corner"] = start_scatter(ffn_grad)
+        got["across"] = cross_scatter(ffn_grad, got["corner"])
+        return [got["corner"]]
+
+    def ffn_grad(k):
+        return got["ffn"][k]
+
+    d_ffn = ring_scatter(
+        lambda k: d_parts[k if k < seq // 2 else k - seq], seq, [ffn_work, ffn_corner]
+    )
+    ffn_out = lax.psum_scatter(
+        after(kept_ffn[5], d_ffn), "seq", scatter_dimension=0, tiled=False
+    )
+    out_tokens = (resid + ffn_out.astype(F32)).astype(BF16)[None]
     second_scaled = d_ffn * feedforward_norm_gain
     g_ffn_gain = jnp.sum(d_ffn * unit_second, 0)
     d_resid = grad_own.astype(F32) + inv_second * (
         second_scaled - unit_second * jnp.mean(second_scaled * unit_second, -1, keepdims=True)
     )
     mix_steps = ring_gather(d_resid.astype(BF16), seq)
-    d_mix = jnp.concatenate(sum(mix_steps, ()), axis=0)
-    d_gated = jnp.concatenate(
-        [mm_nt(jnp.concatenate(arrived, axis=0), m_out) for arrived in mix_steps], axis=0
-    )
+    g_ffn = end_scatter(ffn_grad, got["across"])
+    g_ffn = after(g_ffn.reshape(3 * padded, seq, -1).transpose(1, 0, 2), mix_steps[-1][0])
+    d_gated = []
+    g_out = 0.0
+    for s, arrived in enumerate(mix_steps):
+        rows = jnp.concatenate(arrived, axis=0)
+        first = (2 * s if s < seq // 2 else 1) * rows_tok
+        d_gated.append(mm_nt(rows, m_out))
+        g_out = g_out + trans_dot(gated[first : first + rows.shape[0]], rows)
+    d_gated = jnp.concatenate(by_slots(d_gated), axis=0)
     d_post = d_gated * gelu_val
     d_gate_pre = gelu_pull(d_gated * post)[0].astype(BF16)
     g_post_gain = jnp.sum(d_post * o_hat, 0)
@@ -783,28 +1116,40 @@
     d_ohat = d_post * post_g
     sums = jnp.stack([jnp.sum(d_ohat, -1), jnp.sum(d_ohat * o_hat, -1)])
     sums = in_slots(pairwise_sum(in_order(sums), "seq", seq)) / width
+    g_ffn = exchange(after(g_ffn, sums))
     d_inner = inv_o * (d_ohat - sums[0][:, None] - o_hat * sums[1][:, None])
-    g_side = jnp.concatenate(
-        [
-            trans_dot(d_gate_pre, normed).astype(BF16).reshape(local, head_dim, width),
-            trans_dot(gated, d_mix).astype(BF16).reshape(local, head_dim, width),
-        ],
-        axis=1,
-    )
-    far_sum = partial(lax.psum_scatter, axis_name="grp", scatter_dimension=0, tiled=False)
-    g_side = scatter_heads(plan, g_side, 2, far_sum)
-    d_x3, d_rate_rows, d_gb, d_init = chain_backward(
-        slot_of_member, x3, d_inner, info, gb, init, kept, rows_tok
-    )
-    d_rates = d_rate_rows[0].reshape(stream // MB, local, MB).swapaxes(1, 2).reshape(stream, local)
-    d_logits = (d_rates * live * rate_sig * (1.0 - rate_sig) / head_dim).astype(BF16)
-    d_normed_part = mm(d_gate_pre, m_gate) + mm(d_logits, rate_rows)
-    for h in range(local):
-        d_normed_part = d_normed_part + mm(d_x3[h], w_proj[h])
-    d_normed = ring_scatter(by_distance(d_normed_part), seq)
-    g_pre_gain = jnp.sum(d_normed_part * unit_all, 0)
-    g_proj = jnp.stack([trans_dot(d_x3[h], normed) for h in range(local)])
-    g_proj = scatter_heads(plan, g_proj, 3, grp_scatter)
+    g_out = g_out.astype(BF16).reshape(local, head_dim, width)
+    if plan.mixed:
+        g_out = plan.turn(g_out, grp_index).reshape(groups, plan.each * head_dim, width)
+        g_out = lax.psum_scatter(g_out, "grp", scatter_dimension=0, tiled=False)
+        g_out = g_out.reshape(plan.each, head_dim, width)
+    d_x, d_gb, d_init = chain_backward(
+        slot_of_member, x3, d_inner, d_gate_pre, info, gb, init, kept, rows_tok
+    )
+    w_all = jnp.concatenate([w_proj, m_gate], axis=0)
+    d_normed_part = after(mm(d_x, w_all).astype(BF16), g_ffn, ffn_out)
+
+    def proj_work(since):
+        *got["heads"], got["rates"], got["gain"] = proj_grads(
+            d_x, after(normed, since), w_all, local, head_dim
+        )
+        return got["heads"][:1]
+
+    def heads_work(since):
+        if not plan.mixed:
+            return []
+        block = heads_block(plan, got["heads"])
+        got["corner"] = start_scatter(block)
+        got["across"] = cross_scatter(block, got["corner"])
+        return [got["corner"]]
+
+    d_normed = ring_scatter(by_distance(d_normed_part), seq, [proj_work, heads_work])
+    summed = end_scatter(heads_block(plan, got["heads"]), got["across"]) if plan.mixed else None
+    g_heads = scatter_heads(plan, got["heads"], summed, 4)
+    g_out = exchange(after(g_out, d_normed_part).reshape(-1, seq, width // seq).transpose(1, 0, 2))
+    g_out = g_out.reshape(-1, width // seq)
+    if not plan.mixed:
+        g_out = lax.psum_scatter(g_out, "grp", scatter_dimension=0, tiled=True)
     own_inv = lax.rsqrt(jnp.mean(own_rows * own_rows, -1, keepdims=True) + EPS)
     own_unit = own_rows * own_inv
     first_scaled = d_normed * prenorm_gain
@@ -814,34 +1159,33 @@
         * (first_scaled - own_unit * jnp.mean(first_scaled * own_unit, -1, keepdims=True))
     )[None]
 
-    g_rate_cols = trans_dot(d_logits, normed)
-    g_rate_shift = jnp.sum(d_logits.astype(F32), 0)
+    d_logits = d_x[:, packed : packed + local].astype(F32)
     parts = [item.reshape(local, -1) for item in chain_param_grads(d_gb, d_init, local)]
     parts += [item.reshape(local, head_dim) for item in (g_post_gain, g_post_bias)]
-    parts += [g_rate_cols, g_rate_shift[:, None]]
+    parts += [got["rates"][:local], jnp.sum(d_logits, 0)[:, None]]
     sizes = [item.shape[1] for item in parts]
-    packed = jnp.concatenate(parts, axis=1)
-    packed = jnp.pad(packed, ((0, 0), (0, -packed.shape[1] % 1024)))
-    flat = jnp.concatenate([packed.reshape(-1), g_pre_gain, g_ffn_gain]).reshape(-1, 1024)
-    flat = pairwise_sum(flat, "grp", groups)
-    count = packed.size // 1024
-    gains = pairwise_sum(flat[count:], "seq", seq).reshape(2, width)
-    blocks = jnp.stack(sum(ring_gather(flat[:count], seq), ()))
-    blocks = jnp.take(blocks, slot_of_member, axis=0)
-    packed = plan.order(blocks.reshape(seq, local, -1))
+    flat = jnp.concatenate(parts, axis=1)
+    flat = plan.turn(jnp.pad(flat, ((0, 0), (0, -flat.shape[1] % 1024))), grp_index)
+    count = flat.size
+    flat = jnp.concatenate([flat.reshape(-1), got["gain"][0] / prenorm_gain, g_ffn_gain])
+    flat = pairwise_sum(flat.reshape(-1, 1024), "grp", groups)
+    flat = lax.all_gather(flat, "seq", axis=0).reshape(seq, -1)
+    gains = jnp.sum(flat[:, count:], 0).reshape(2, width)
+    flat = plan.order(flat[:, :count].reshape(seq, local, -1))
     small = []
     offset = 0
     for size in sizes:
-        small.append(packed[:, offset : offset + size])
+        small.append(flat[:, offset : offset + size])
         offset += size
+    g_ffn = join_features(g_ffn, w_down.shape[0], (True, True, False))
     return (
         out_tokens,
         grad_tokens,
         gains[0],
-        g_proj[0].T,
-        g_proj[1].T,
-        g_proj[2].T,
-        g_side[0].T,
+        g_heads[0],
+        g_heads[1],
+        g_heads[2],
+        g_heads[3],
         small[6].T,
         small[7][:, 0],
         small[0].reshape(heads, head_dim, head_dim),
@@ -850,10 +1194,10 @@
         small[3],
         small[4].reshape(width),
         small[5].reshape(width),
-        g_side[1],
+        g_out.astype(F32),
         gains[1],
-        g_ffn[0].T,
-        g_ffn[1].T,
+        g_ffn[0],
+        g_ffn[1],
         g_ffn[2],
     )
 

time: 889 us -> 818 us (0.920)
  the two profiles are of different devices: /device:TPU:14 before, /device:TPU:0 now
where the time goes in v3:
time: 818 us; the launch traced here: 810 us
  waiting for transfers between devices  296 us (36%)
  local copies, waits for them, and re-layouts  149 us (18%)
  Pallas kernels  144 us (18%)
  starting transfers between devices  100 us (12%)
  other arithmetic  61.4 us (8%)
  matrix products  42.8 us (5%)
  between operations  15.8 us (2%)
    ppermute x12, waiting for transfers between devices, ring_scatter(): ahead = lax.ppermute(ahead, 'seq', ring_pairs(size, 1))  118 us
    unnamed x342, local copies, waits for them, and re-layouts  107 us
    ppermute x12, waiting for transfers between devices, ring_gather(): ahead = lax.ppermute(ahead, 'seq', ring_pairs(size, 1))  67.6 us
    pallas_call x5, Pallas kernels, ffn_step(): pl.pallas_call(partial(ffn_kernel, count, len(weights), len(kept)), grid_...  56.1 us
    ppermute x9, waiting for transfers between devices, ring_gather(): back = lax.ppermute(back, 'seq', ring_pairs(size, -1))  43.1 us
    pallas_call x1, Pallas kernels, chain_backward(): pl.pallas_call(partial(backward_kernel, heads), grid_spec=pltpu.PrefetchS...  34.5 us
    all_to_all x6, starting transfers between devices, exchange(): return lax.all_to_all(block, 'seq', 0, 0, tiled=True)  30.7 us
    all_to_all x6, waiting for transfers between devices, exchange(): return lax.all_to_all(block, 'seq', 0, 0, tiled=True)  25.7 us
  transfers between devices with their start and end apart: 75, of which 38 were waited for; matrix products, arithmetic and copies ran while one was open for 21% of the time, Pallas kernels for 15%

profile of v3, /device:TPU:0, one launch (start us, length us, event | category | flops | bytes accessed | tf_op | source)
XLA Modules:
  0.0 809.6 jit_solution(6984697707863859662)
XLA Ops:
  14.3 6.4 all-to-all-start.1
  45.7 5.8 collective-permute-start.2
  57.5 4.7 collective-permute-done.2
  66.8 8.7 %collective-permute-done.3.refs_1_ = bf16[128,2048]{1,0:T(8,128)(2,1)S(1)} collective-permute-done((bf16[128,2048]{1,0:T(8,128)(2,1)S(1)}, bf16[128,2048]{1,0:T(8,128)(2,1)S(1)}, u32[]{:S(2)}, u32[]{:S(2)}) %collective-permute-start.3) | collective-permute-done | bytes 524320 | tf_op jit(solution)/shard_map/ppermute | solution.py:752
  76.4 4.3 all-to-all-start
  97.4 3.5 fusion.56
  105.2 4.7 fusion.122
  112.2 6.1 all-to-all-start.2
  131.7 22.5 %chain_forward.1 = (f32[1024,256]{1,0:T(8,128)S(1)}, f32[64,4096]{1,0:T(8,128)S(1)}, f32[64,4096]{1,0:T(8,128)S(1)}, f32[64,4096]{1,0:T(8,128)S(1)}, f32[8,4096]{1,0:T(8,128)S(1)}, /*index=5*/f32[8,64,384]{2,1,0:T(8,128)S(1)}) custom-call(s32[8]{0:T(128)S(1)} %compare_select_fusion.7.idx_ref, bf16[1024,768]{1,0:T(8,128)(2,1)S(1)} %fusion.50.x_ref, ...), custom_call_target="tpu_custom_call" | custom-call | flops 1 | bytes 1 | tf_op jit(solution)/shard_map/chain_forward/pallas_call | solution.py:351
  160.9 7.7 all-to-all-done.2.refs_2_.refs_1_
  183.6 4.8 multiply_convert_fusion.1
  192.6 21.6 %collective-permute-done.16 = bf16[128,2048]{1,0:T(8,128)(2,1)S(1)} collective-permute-done((bf16[128,2048]{1,0:T(8,128)(2,1)S(1)}, bf16[128,2048]{1,0:T(8,128)(2,1)S(1)}, u32[]{:S(2)}, u32[]{:S(2)}) %collective-permute-start.16) | collective-permute-done | bytes 524320 | tf_op jit(solution)/shard_map/ppermute | solution.py:770
  214.3 3.6 collective-permute-start.17
  221.3 10.3 %collective-permute-done.17 = bf16[128,2048]{1,0:T(8,128)(2,1)S(1)} collective-permute-done((bf16[128,2048]{1,0:T(8,128)(2,1)S(1)}, bf16[128,2048]{1,0:T(8,128)(2,1)S(1)}, u32[]{:S(2)}, u32[]{:S(2)}) %collective-permute-start.17) | collective-permute-done | bytes 524320 | tf_op jit(solution)/shard_map/ppermute | solution.py:770
  234.6 3.8 collective-permute-start.22
  238.4 20.2 %collective-permute-done.18 = bf16[128,2048]{1,0:T(8,128)(2,1)S(1)} collective-permute-done((bf16[128,2048]{1,0:T(8,128)(2,1)S(1)}, bf16[128,2048]{1,0:T(8,128)(2,1)S(1)}, u32[]{:S(2)}, u32[]{:S(2)}) %collective-permute-start.18) | collective-permute-done | bytes 524320 | tf_op jit(solution)/shard_map/ppermute | solution.py:770
  258.6 17.0 %collective-permute-done.22 = bf16[128,2048]{1,0:T(8,128)(2,1)S(1)} collective-permute-done((bf16[128,2048]{1,0:T(8,128)(2,1)S(1)}, bf16[128,2048]{1,0:T(8,128)(2,1)S(1)}, u32[]{:S(2)}, u32[]{:S(2)}) %collective-permute-start.22) | collective-permute-done | bytes 524320 | tf_op jit(solution)/shard_map/ppermute | solution.py:772
  278.6 7.7 collective-permute-done.19.refs_0_
  290.3 11.4 %collective-permute-done.28.refs_1_ = bf16[128,2048]{1,0:T(8,128)(2,1)S(1)} collective-permute-done((bf16[128,2048]{1,0:T(8,128)(2,1)S(1)}, bf16[128,2048]{1,0:T(8,128)(2,1)S(1)}, u32[]{:S(2)}, u32[]{:S(2)}) %collective-permute-start.28) | collective-permute-done | bytes 524320 | tf_op jit(solution)/shard_map/ppermute | solution.py:756
  305.1 8.6 %collective-permute-done.30.refs_1_ = bf16[128,2048]{1,0:T(8,128)(2,1)S(1)} collective-permute-done((bf16[128,2048]{1,0:T(8,128)(2,1)S(1)}, bf16[128,2048]{1,0:T(8,128)(2,1)S(1)}, u32[]{:S(2)}, u32[]{:S(2)}) %collective-permute-start.30) | collective-permute-done | bytes 524320 | tf_op jit(solution)/shard_map/ppermute | solution.py:756
  314.2 10.1 %ffn_step.5 = (bf16[1024,2048]{1,0:T(8,128)(2,1)}, bf16[1024,2048]{1,0:T(8,128)(2,1)}, bf16[704,1024]{1,0:T(8,128)(2,1)S(1)}, bf16[704,1024]{1,0:T(8,128)(2,1)S(...) custom-call(s32[1]{0:T(128)} %get-tuple-element.372.member_ref, ...), custom_call_target="tpu_custom_call" | custom-call | flops 12000000000 | bytes 1 | tf_op jit(solution)/shard_map/ffn_step/pallas_call | solution.py:592
  336.4 12.0 %ffn_step.6 = (bf16[1024,2048]{1,0:T(8,128)(2,1)}, bf16[1024,2048]{1,0:T(8,128)(2,1)}, bf16[704,1024]{1,0:T(8,128)(2,1)S(1)}, bf16[704,1024]{1,0:T(8,128)(2,1)S(...) custom-call(s32[2]{0:T(128)S(1)} %get-tuple-element.371.member_ref, ...), custom_call_target="tpu_custom_call", output_to_operand_aliasing={{0}: (9, {}), {1}: (10, {}), {2}: (11, {}), {3}: (12, {}), ... | custom-call | flops 12000000000 | bytes 1 | tf_op jit(solution)/shard_map/ffn_step/pallas_call | solution.py:592
  358.3 11.9 %ffn_step.7 = (bf16[1024,2048]{1,0:T(8,128)(2,1)}, bf16[1024,2048]{1,0:T(8,128)(2,1)}, bf16[704,1024]{1,0:T(8,128)(2,1)S(1)}, bf16[704,1024]{1,0:T(8,128)(2,1)S(...) custom-call(s32[2]{0:T(128)S(1)} %get-tuple-element.370.member_ref, ...), custom_call_target="tpu_custom_call", output_to_operand_aliasing={{0}: (9, {}), {1}: (10, {}), {2}: (11, {}), {3}: (12, {}), ... | custom-call | flops 12000000000 | bytes 1 | tf_op jit(solution)/shard_map/ffn_step/pallas_call | solution.py:592
  378.5 11.9 %ffn_step.8 = (bf16[1024,2048]{1,0:T(8,128)(2,1)}, bf16[1024,2048]{1,0:T(8,128)(2,1)}, bf16[704,1024]{1,0:T(8,128)(2,1)S(1)}, bf16[704,1024]{1,0:T(8,128)(2,1)S(...) custom-call(s32[2]{0:T(128)S(1)} %get-tuple-element.369.member_ref, ...), custom_call_target="tpu_custom_call", output_to_operand_aliasing={{0}: (9, {}), {1}: (10, {}), {2}: (11, {}), {3}: (12, {}), ... | custom-call | flops 12000000000 | bytes 1 | tf_op jit(solution)/shard_map/ffn_step/pallas_call | solution.py:592
  399.0 10.1 %ffn_step.9 = (bf16[1024,2048]{1,0:T(8,128)(2,1)}, bf16[1024,2048]{1,0:T(8,128)(2,1)}, bf16[704,1024]{1,0:T(8,128)(2,1)S(1)}, bf16[704,1024]{1,0:T(8,128)(2,1)S(...) custom-call(s32[1]{0:T(128)} %get-tuple-element.373.member_ref, ...), custom_call_target="tpu_custom_call", output_to_operand_aliasing={{0}: (7, {}), {1}: (8, {}), {2}: (9, {}), {3}: (10, {}), {4... | custom-call | flops 12000000000 | bytes 1 | tf_op jit(solution)/shard_map/ffn_step/pallas_call | solution.py:592
  414.9 13.2 %ffn_grads.1 = (bf16[528,2048]{1,0:T(8,128)(2,1)S(1)}, bf16[528,2048]{1,0:T(8,128)(2,1)S(1)}, bf16[528,2048]{1,0:T(8,128)(2,1)S(1)}, bf16[528,2048]{1,0:T(8,128)(2,1)}) custom-call(bf16[704,1024]{1,0:T(8,128)(2,1)S(1)} %get-tuple-element.113.at_ref, bf16[704,1024]{1,0:T(8,128)(2,1)S(1)} %copy-done.76, bf16[704,1024]{1,0:T(8,128)(2,1)S(1)} %copy-done.80, ...), custom_call_target="tpu_custom_call" | custom-call | flops 12000000000 | bytes 1 | tf_op jit(solution)/shard_map/ffn_grads/pallas_call | solution.py:645
  432.4 14.3 %collective-permute-done.33.refs_0_ = bf16[128,2048]{1,0:T(8,128)(2,1)S(1)} collective-permute-done((bf16[128,2048]{1,0:T(8,128)(2,1)S(1)}, bf16[128,2048]{1,0:T(8,128)(2,1)S(1)}, u32[]{:S(2)}, u32[]{:S(2)}) %collective-permute-start.33) | collective-permute-done | bytes 524320 | tf_op jit(solution)/shard_map/ppermute | solution.py:770
  451.6 10.9 %collective-permute-done.34.refs_0_ = bf16[128,2048]{1,0:T(8,128)(2,1)} collective-permute-done((bf16[128,2048]{1,0:T(8,128)(2,1)S(1)}, bf16[128,2048]{1,0:T(8,128)(2,1)}, u32[]{:S(2)}, u32[]{:S(2)}) %collective-permute-start.34) | collective-permute-done | bytes 524320 | tf_op jit(solution)/shard_map/ppermute | solution.py:770
  466.9 10.6 %collective-permute-done.36 = bf16[128,2048]{1,0:T(8,128)(2,1)S(1)} collective-permute-done((bf16[128,2048]{1,0:T(8,128)(2,1)S(1)}, bf16[128,2048]{1,0:T(8,128)(2,1)S(1)}, u32[]{:S(2)}, u32[]{:S(2)}) %collective-permute-start.36) | collective-permute-done | bytes 524320 | tf_op jit(solution)/shard_map/ppermute | solution.py:770
  481.2 9.4 %collective-permute-done.37 = bf16[128,2048]{1,0:T(8,128)(2,1)S(1)} collective-permute-done((bf16[128,2048]{1,0:T(8,128)(2,1)S(1)}, bf16[128,2048]{1,0:T(8,128)(2,1)S(1)}, u32[]{:S(2)}, u32[]{:S(2)}) %collective-permute-start.37) | collective-permute-done | bytes 524320 | tf_op jit(solution)/shard_map/ppermute | solution.py:770
  497.5 20.2 %collective-permute-done.41 = bf16[128,2048]{1,0:T(8,128)(2,1)S(1)} collective-permute-done((bf16[128,2048]{1,0:T(8,128)(2,1)S(1)}, bf16[128,2048]{1,0:T(8,128)(2,1)S(1)}, u32[]{:S(2)}, u32[]{:S(2)}) %collective-permute-start.41) | collective-permute-done | bytes 524320 | tf_op jit(solution)/shard_map/ppermute | solution.py:752
  524.2 4.2 collective-permute-done.45
  529.3 12.8 %collective-permute-done.42 = bf16[128,2048]{1,0:T(8,128)(2,1)S(1)} collective-permute-done((bf16[128,2048]{1,0:T(8,128)(2,1)S(1)}, bf16[128,2048]{1,0:T(8,128)(2,1)S(1)}, u32[]{:S(2)}, u32[]{:S(2)}) %collective-permute-start.42) | collective-permute-done | bytes 524320 | tf_op jit(solution)/shard_map/ppermute | solution.py:752
  544.7 11.2 %collective-permute-done.46 = bf16[128,2048]{1,0:T(8,128)(2,1)S(1)} collective-permute-done((bf16[128,2048]{1,0:T(8,128)(2,1)S(1)}, bf16[128,2048]{1,0:T(8,128)(2,1)S(1)}, u32[]{:S(2)}, u32[]{:S(2)}) %collective-permute-start.46) | collective-permute-done | bytes 524320 | tf_op jit(solution)/shard_map/ppermute | solution.py:756
  555.9 12.2 %collective-permute-done.43 = bf16[128,2048]{1,0:T(8,128)(2,1)S(1)} collective-permute-done((bf16[128,2048]{1,0:T(8,128)(2,1)S(1)}, bf16[128,2048]{1,0:T(8,128)(2,1)S(1)}, u32[]{:S(2)}, u32[]{:S(2)}) %collective-permute-start.43) | collective-permute-done | bytes 524320 | tf_op jit(solution)/shard_map/ppermute | solution.py:752
  568.2 7.2 collective-permute-done.47
  575.5 6.5 collective-permute-done.44.refs_1_
  588.5 3.8 collective-permute-done.48
  603.3 4.5 all-to-all-start.3
  626.1 34.5 %chain_backward.1 = (bf16[1024,1152]{1,0:T(8,128)(2,1)S(1)}, f32[2,64,128]{2,1,0:T(8,128)S(1)}, f32[64,384]{1,0:T(8,128)S(1)}) custom-call(s32[8]{0:T(128)S(1)} %compare_select_fusion.7.idx_ref, bf16[1024,768]{1,0:T(8,128)(2,1)S(1)} %copy-done.5, f32[1024,256]{1,0:T(8,128)S(1)} %subtract_multiply_fusion.d_ref, bf16[1024,256]{1,0:T(8,128)(2,1)S(1)} %copy-done.19, ...), custom_call_target="tpu_custom_call" | custom-call | flops 1 | bytes 1 | tf_op jit(solution)/shard_map/chain_backward/pallas_call | solution.py:385
  667.3 9.5 %convolution_convert_fusion.refs_0_ = bf16[1024,2048]{1,0:T(8,128)(2,1)} fusion(bf16[1024,1152]{1,0:T(8,128)(2,1)} %copy-done.51, bf16[1152,2048]{1,0:T(8,128)(2,1)} %get-tuple-element.318.w_ref), kind=kOutput, calls=%fused_computation.2 | convolution fusion | flops 4833935360 | bytes 11272192 | tf_op jit(solution)/shard_map/dot_general | solution.py:17
  685.0 10.9 %proj_grads.1 = (bf16[256,2048]{1,0:T(8,128)(2,1)S(1)}, bf16[256,2048]{1,0:T(8,128)(2,1)S(1)}, bf16[256,2048]{1,0:T(8,128)(2,1)S(1)}, bf16[256,2048]{1,0:T(8,128...) custom-call(bf16[1024,1152]{1,0:T(8,128)(2,1)S(1)} %copy-done.52, bf16[1024,2048]{1,0:T(8,128)(2,1)} %after.36.x_ref, ...), custom_call_target="tpu_custom_call" | custom-call | flops 8999999488 | bytes 1 | tf_op jit(solution)/shard_map/proj_grads/pallas_call | solution.py:687
  705.1 5.5 collective-permute-done.62
  721.6 4.6 all-to-all-start.5
  736.7 13.4 %collective-permute-done.56 = bf16[128,2048]{1,0:T(8,128)(2,1)S(1)} collective-permute-done((bf16[128,2048]{1,0:T(8,128)(2,1)}, bf16[128,2048]{1,0:T(8,128)(2,1)S(1)}, u32[]{:S(2)}, u32[]{:S(2)}) %collective-permute-start.56) | collective-permute-done | bytes 524320 | tf_op jit(solution)/shard_map/ppermute | solution.py:770
  750.2 4.0 collective-permute-done.59
  771.5 4.8 all-to-all-start.4
  785.1 16.3 %all-to-all-done.4.in_ref = bf16[8,256,256]{2,1,0:T(8,128)(2,1)S(1)} async-done(((bf16[8,256,256]{2,1,0:T(8,128)(2,1)}), bf16[8,256,256]{2,1,0:T(8,128)(2,1)S(1)}, u32[]{:S(2)}, u32[]{:S(2)}) %all-to-all-start.4) | async-done | bytes 1048608 | tf_op jit(solution)/shard_map/all_to_all | solution.py:871
  (686 shorter events, 309.8 us)
Async XLA Ops:
  7.2 21.5 %collective-permute-start = (bf16[128,2048]{1,0:T(8,128)(2,1)}, bf16[128,2048]{1,0:T(8,128)(2,1)}, u32[]{:S(2)}, u32[]{:S(2)}) collective-permute-start(bf16[128,2048]{1,0:T(8,128)(2,1)} %bitcast.282), channel_id=1, source_target_pairs={{0,8},{8,16},{16,24},{24,28},{28,20},{20,12},{12,4},{4,0},{1,9},{9... | collective-permute-start | bytes 1572872 | tf_op jit(solution)/shard_map/ppermute | solution.py:752
  10.3 21.1 %collective-permute-start.4 = (bf16[128,2048]{1,0:T(8,128)(2,1)}, bf16[128,2048]{1,0:T(8,128)(2,1)}, u32[]{:S(2)}, u32[]{:S(2)}) collective-permute-start(bf16[128,2048]{1,0:T(8,128)(2,1)} %bitcast.283), channel_id=1, source_target_pairs={{0,4},{8,0},{16,8},{24,16},{28,24},{20,28},{12,20},{4,12},{1,5},{9... | collective-permute-start | bytes 1572872 | tf_op jit(solution)/shard_map/ppermute | solution.py:756
  14.3 40.3 %all-to-all-start.1 = ((bf16[8,192,256]{2,1,0:T(8,128)(2,1)}), bf16[8,192,256]{2,1,0:T(8,128)(2,1)}, u32[]{:S(2)}, u32[]{:S(2)}) async-start(bf16[8,192,256]{2,1,0:T(8,128)(2,1)} %cut_features.4), calls=%async_computation.1 | async-start | bytes 1572864 | tf_op jit(solution)/shard_map/all_to_all | solution.py:871
  31.4 21.6 %collective-permute-start.5 = (bf16[128,2048]{1,0:T(8,128)(2,1)}, bf16[128,2048]{1,0:T(8,128)(2,1)}, u32[]{:S(2)}, u32[]{:S(2)}) collective-permute-start(bf16[128,2048]{1,0:T(8,128)(2,1)} %collective-permute-done.4), channel_id=1, source_target_pairs={{0,4},{8,0},{16,8},{24,16},{28,24},{20,28},{12,20},{4,12},{1,5},{9... | collective-permute-start | bytes 1572872 | tf_op jit(solution)/shard_map/ppermute | solution.py:756
  55.8 33.3 %collective-permute-start.10 = (bf16[192,2048]{1,0:T(8,128)(2,1)S(1)}, bf16[192,2048]{1,0:T(8,128)(2,1)}, u32[]{:S(2)}, u32[]{:S(2)}) collective-permute-start(bf16[192,2048]{1,0:T(8,128)(2,1)S(1)} %bitcast.295), channel_id=1, source_target_pairs={{0,1},{1,0},{2,3},{3,2},{4,5},{5,4},{6,7},{7,6},{8,9},{9,8},{10,11... | collective-permute-start | bytes 2359304 | tf_op jit(solution)/shard_map/ppermute | solution.py:792
  55.9 30.7 %collective-permute-start.11 = (bf16[192,2048]{1,0:T(8,128)(2,1)S(1)}, bf16[192,2048]{1,0:T(8,128)(2,1)}, u32[]{:S(2)}, u32[]{:S(2)}) collective-permute-start(bf16[192,2048]{1,0:T(8,128)(2,1)S(1)} %bitcast.296), channel_id=1, source_target_pairs={{0,2},{1,3},{2,0},{3,1},{4,6},{5,7},{6,4},{7,5},{8,10},{9,11},{10,... | collective-permute-start | bytes 2359304 | tf_op jit(solution)/shard_map/ppermute | solution.py:792
  76.4 35.8 %all-to-all-start = ((bf16[8,128,256]{2,1,0:T(8,128)(2,1)}), bf16[8,128,256]{2,1,0:T(8,128)(2,1)S(1)}, u32[]{:S(2)}, u32[]{:S(2)}) async-start(bf16[8,128,256]{2,1,0:T(8,128)(2,1)} %after.20), calls=%async_computation | async-start | bytes 1048576 | tf_op jit(solution)/shard_map/all_to_all | solution.py:871
  112.2 56.5 %all-to-all-start.2 = ((bf16[8,528,256]{2,1,0:T(8,128)(2,1)}), bf16[8,528,256]{2,1,0:T(8,128)(2,1)S(1)}, u32[]{:S(2)}, u32[]{:S(2)}) async-start(bf16[8,528,256]{2,1,0:T(8,128)(2,1)} %after.21), calls=%async_computation.2 | async-start | bytes 4325376 | tf_op jit(solution)/shard_map/all_to_all | solution.py:871
  118.3 195.9 %all-gather.5.cloned.1.call-start = ((), (), s32[]{:S(2)}) async-start(), calls=%async_computation.10 | async-start | bytes 4718592 | tf_op jit(solution)/shard_map/all_gather | solution.py:1008
  128.7 44.2 %collective-permute-start.7 = (bf16[128,2048]{1,0:T(8,128)(2,1)}, bf16[128,2048]{1,0:T(8,128)(2,1)}, u32[]{:S(2)}, u32[]{:S(2)}) collective-permute-start(bf16[128,2048]{1,0:T(8,128)(2,1)} %bitcast.131), channel_id=1, source_target_pairs={{0,1},{1,0},{2,3},{3,2},{4,5},{5,4},{6,7},{7,6},{8,9},{9,8},{10,11... | collective-permute-start | bytes 1572872 | tf_op jit(solution)/shard_map/ppermute | solution.py:792
  128.9 32.0 %collective-permute-start.8 = (bf16[128,2048]{1,0:T(8,128)(2,1)}, bf16[128,2048]{1,0:T(8,128)(2,1)}, u32[]{:S(2)}, u32[]{:S(2)}) collective-permute-start(bf16[128,2048]{1,0:T(8,128)(2,1)} %bitcast.131), channel_id=1, source_target_pairs={{0,2},{1,3},{2,0},{3,1},{4,6},{5,7},{6,4},{7,5},{8,10},{9,11},{10,... | collective-permute-start | bytes 1572872 | tf_op jit(solution)/shard_map/ppermute | solution.py:792
  160.9 18.9 %collective-permute-start.9 = (bf16[128,2048]{1,0:T(8,128)(2,1)}, bf16[128,2048]{1,0:T(8,128)(2,1)}, u32[]{:S(2)}, u32[]{:S(2)}) collective-permute-start(bf16[128,2048]{1,0:T(8,128)(2,1)} %collective-permute-done.8), channel_id=1, source_target_pairs={{0,1},{1,0},{2,3},{3,2},{4,5},{5,4},{6,7},{7,6},{8,9},{9,8},{10,11... | collective-permute-start | bytes 1572872 | tf_op jit(solution)/shard_map/ppermute | solution.py:792
  181.8 494.9 %reduce-scatter.3.cloned.1.call-start = ((), (), s32[]{:S(2)}) async-start(), calls=%async_computation.8 | async-start | bytes 4718592 | tf_op jit(solution)/shard_map/reduce_scatter | solution.py:1092
  190.6 23.6 %collective-permute-start.16 = (bf16[128,2048]{1,0:T(8,128)(2,1)S(1)}, bf16[128,2048]{1,0:T(8,128)(2,1)S(1)}, u32[]{:S(2)}, u32[]{:S(2)}) collective-permute-start(bf16[128,2048]{1,0:T(8,128)(2,1)S(1)} %get-tuple-element.288), channel_id=1, source_target_pairs={{0,8},{8,16},{16,24},{24,28},{28,20},{20,12},{12,4},{4,0},{1,9},{9... | collective-permute-start | bytes 1572872 | tf_op jit(solution)/shard_map/ppermute | solution.py:770
  191.6 29.7 %collective-permute-start.21 = (bf16[128,2048]{1,0:T(8,128)(2,1)S(1)}, bf16[128,2048]{1,0:T(8,128)(2,1)S(1)}, u32[]{:S(2)}, u32[]{:S(2)}) collective-permute-start(bf16[128,2048]{1,0:T(8,128)(2,1)S(1)} %get-tuple-element.289), channel_id=1, source_target_pairs={{0,4},{8,0},{16,8},{24,16},{28,24},{20,28},{12,20},{4,12},{1,5},{9... | collective-permute-start | bytes 1572872 | tf_op jit(solution)/shard_map/ppermute | solution.py:772
  214.3 17.3 %collective-permute-start.17 = (bf16[128,2048]{1,0:T(8,128)(2,1)S(1)}, bf16[128,2048]{1,0:T(8,128)(2,1)S(1)}, u32[]{:S(2)}, u32[]{:S(2)}) collective-permute-start(bf16[128,2048]{1,0:T(8,128)(2,1)S(1)} %add_convert_fusion.19), channel_id=1, source_target_pairs={{0,8},{8,16},{16,24},{24,28},{28,20},{20,12},{12,4},{4,0},{1,9},{9... | collective-permute-start | bytes 1572872 | tf_op jit(solution)/shard_map/ppermute | solution.py:770
  219.6 58.4 %collective-permute-start.20 = (bf16[528,2048]{1,0:T(8,128)(2,1)}, bf16[528,2048]{1,0:T(8,128)(2,1)}, u32[]{:S(2)}, u32[]{:S(2)}) collective-permute-start(bf16[528,2048]{1,0:T(8,128)(2,1)} %bitcast.137.refs_2_.refs_4_), channel_id=1, source_target_pairs={{0,2},{1,3},{2,0},{3,1},{4,6},{5,7},{6,4},{7,5},{8,10},{9,11},{10,... | collective-permute-start | bytes 6488072 | tf_op jit(solution)/shard_map/ppermute | solution.py:792
  232.1 26.5 %collective-permute-start.18 = (bf16[128,2048]{1,0:T(8,128)(2,1)S(1)}, bf16[128,2048]{1,0:T(8,128)(2,1)S(1)}, u32[]{:S(2)}, u32[]{:S(2)}) collective-permute-start(bf16[128,2048]{1,0:T(8,128)(2,1)S(1)} %get-tuple-element.286), channel_id=1, source_target_pairs={{0,8},{8,16},{16,24},{24,28},{28,20},{20,12},{12,4},{4,0},{1,9},{9... | collective-permute-start | bytes 1572872 | tf_op jit(solution)/shard_map/ppermute | solution.py:770
  234.6 41.0 %collective-permute-start.22 = (bf16[128,2048]{1,0:T(8,128)(2,1)S(1)}, bf16[128,2048]{1,0:T(8,128)(2,1)S(1)}, u32[]{:S(2)}, u32[]{:S(2)}) collective-permute-start(bf16[128,2048]{1,0:T(8,128)(2,1)S(1)} %get-tuple-element.287), channel_id=1, source_target_pairs={{0,4},{8,0},{16,8},{24,16},{28,24},{20,28},{12,20},{4,12},{1,5},{9... | collective-permute-start | bytes 1572872 | tf_op jit(solution)/shard_map/ppermute | solution.py:772
  278.0 36.2 %collective-permute-start.25 = (bf16[528,2048]{1,0:T(8,128)(2,1)}, bf16[528,2048]{1,0:T(8,128)(2,1)}, u32[]{:S(2)}, u32[]{:S(2)}) collective-permute-start(bf16[528,2048]{1,0:T(8,128)(2,1)} %bitcast.137.refs_2_.refs_4_), channel_id=1, source_target_pairs={{0,1},{1,0},{2,3},{3,2},{4,5},{5,4},{6,7},{7,6},{8,9},{9,8},{10,11... | collective-permute-start | bytes 6488072 | tf_op jit(solution)/shard_map/ppermute | solution.py:792
  278.1 36.2 %collective-permute-start.26 = (bf16[528,2048]{1,0:T(8,128)(2,1)}, bf16[528,2048]{1,0:T(8,128)(2,1)}, u32[]{:S(2)}, u32[]{:S(2)}) collective-permute-start(bf16[528,2048]{1,0:T(8,128)(2,1)} %collective-permute-done.20.refs_1_.refs_4_.refs_6_), channel_id=1, source_target_pairs={{0,1},{1,0},{2,3},{3,2},{4,5},{5,4},{6,7},{7,6},{8,9},{9,8},{10,11... | collective-permute-start | bytes 6488072 | tf_op jit(solution)/shard_map/ppermute | solution.py:792
  303.6 25.0 %collective-permute-start.24 = (bf16[128,2048]{1,0:T(8,128)(2,1)S(1)}, bf16[128,2048]{1,0:T(8,128)(2,1)S(1)}, u32[]{:S(2)}, u32[]{:S(2)}) collective-permute-start(bf16[128,2048]{1,0:T(8,128)(2,1)S(1)} %multiply_convert_fusion.refs_0_), channel_id=1, source_target_pairs={{0,8},{8,16},{16,24},{24,28},{28,20},{20,12},{12,4},{4,0},{1,9},{9... | collective-permute-start | bytes 1572872 | tf_op jit(solution)/shard_map/ppermute | solution.py:752
  313.7 60.9 %collective-permute-start.32 = (bf16[128,2048]{1,0:T(8,128)(2,1)S(1)}, bf16[128,2048]{1,0:T(8,128)(2,1)S(1)}, u32[]{:S(2)}, u32[]{:S(2)}) collective-permute-start(bf16[128,2048]{1,0:T(8,128)(2,1)S(1)} %collective-permute-done.30.refs_1_), channel_id=1, source_target_pairs={{0,4},{8,0},{16,8},{24,16},{28,24},{20,28},{12,20},{4,12},{1,5},{9... | collective-permute-start | bytes 1572872 | tf_op jit(solution)/shard_map/ppermute | solution.py:756
  329.4 22.3 %collective-permute-start.27 = (bf16[128,2048]{1,0:T(8,128)(2,1)}, bf16[128,2048]{1,0:T(8,128)(2,1)S(1)}, u32[]{:S(2)}, u32[]{:S(2)}) collective-permute-start(bf16[128,2048]{1,0:T(8,128)(2,1)} %after.25.refs_0_), channel_id=1, source_target_pairs={{0,8},{8,16},{16,24},{24,28},{28,20},{20,12},{12,4},{4,0},{1,9},{9... | collective-permute-start | bytes 1572872 | tf_op jit(solution)/shard_map/ppermute | solution.py:752
  352.5 21.0 %collective-permute-start.29 = (bf16[128,2048]{1,0:T(8,128)(2,1)}, bf16[128,2048]{1,0:T(8,128)(2,1)S(1)}, u32[]{:S(2)}, u32[]{:S(2)}) collective-permute-start(bf16[128,2048]{1,0:T(8,128)(2,1)} %after.26.refs_0_), channel_id=1, source_target_pairs={{0,8},{8,16},{16,24},{24,28},{28,20},{20,12},{12,4},{4,0},{1,9},{9... | collective-permute-start | bytes 1572872 | tf_op jit(solution)/shard_map/ppermute | solution.py:752
  374.3 19.4 %collective-permute-start.31 = (bf16[128,2048]{1,0:T(8,128)(2,1)}, bf16[128,2048]{1,0:T(8,128)(2,1)S(1)}, u32[]{:S(2)}, u32[]{:S(2)}) collective-permute-start(bf16[128,2048]{1,0:T(8,128)(2,1)} %after.27.refs_0_), channel_id=1, source_target_pairs={{0,8},{8,16},{16,24},{24,28},{28,20},{20,12},{12,4},{4,0},{1,9},{9... | collective-permute-start | bytes 1572872 | tf_op jit(solution)/shard_map/ppermute | solution.py:752
  432.2 30.2 %collective-permute-start.35 = (bf16[528,2048]{1,0:T(8,128)(2,1)}, bf16[528,2048]{1,0:T(8,128)(2,1)}, u32[]{:S(2)}, u32[]{:S(2)}) collective-permute-start(bf16[528,2048]{1,0:T(8,128)(2,1)} %get-tuple-element.119), channel_id=1, source_target_pairs={{0,1},{1,0},{2,3},{3,2},{4,5},{5,4},{6,7},{7,6},{8,9},{9,8},{10,11... | collective-permute-start | bytes 6488072 | tf_op jit(solution)/shard_map/ppermute | solution.py:792
  495.5 22.3 %collective-permute-start.41 = (bf16[128,2048]{1,0:T(8,128)(2,1)S(1)}, bf16[128,2048]{1,0:T(8,128)(2,1)S(1)}, u32[]{:S(2)}, u32[]{:S(2)}) collective-permute-start(bf16[128,2048]{1,0:T(8,128)(2,1)S(1)} %fusion.126), channel_id=1, source_target_pairs={{0,8},{8,16},{16,24},{24,28},{28,20},{20,12},{12,4},{4,0},{1,9},{9... | collective-permute-start | bytes 1572872 | tf_op jit(solution)/shard_map/ppermute | solution.py:752
  496.6 100.3 %collective-permute-start.51 = (bf16[528,2048]{1,0:T(8,128)(2,1)S(1)}, bf16[528,2048]{1,0:T(8,128)(2,1)S(1)}, u32[]{:S(2)}, u32[]{:S(2)}) collective-permute-start(bf16[528,2048]{1,0:T(8,128)(2,1)S(1)} %copy-done.54), channel_id=1, source_target_pairs={{0,1},{1,0},{2,3},{3,2},{4,5},{5,4},{6,7},{7,6},{8,9},{9,8},{10,11... | collective-permute-start | bytes 6488072 | tf_op jit(solution)/shard_map/ppermute | solution.py:792
  496.6 31.8 %collective-permute-start.45 = (bf16[128,2048]{1,0:T(8,128)(2,1)S(1)}, bf16[128,2048]{1,0:T(8,128)(2,1)S(1)}, u32[]{:S(2)}, u32[]{:S(2)}) collective-permute-start(bf16[128,2048]{1,0:T(8,128)(2,1)S(1)} %fusion.126), channel_id=1, source_target_pairs={{0,4},{8,0},{16,8},{24,16},{28,24},{20,28},{12,20},{4,12},{1,5},{9... | collective-permute-start | bytes 1572872 | tf_op jit(solution)/shard_map/ppermute | solution.py:756
  517.8 24.3 %collective-permute-start.42 = (bf16[128,2048]{1,0:T(8,128)(2,1)S(1)}, bf16[128,2048]{1,0:T(8,128)(2,1)S(1)}, u32[]{:S(2)}, u32[]{:S(2)}) collective-permute-start(bf16[128,2048]{1,0:T(8,128)(2,1)S(1)} %collective-permute-done.41), channel_id=1, source_target_pairs={{0,8},{8,16},{16,24},{24,28},{28,20},{20,12},{12,4},{4,0},{1,9},{9... | collective-permute-start | bytes 1572872 | tf_op jit(solution)/shard_map/ppermute | solution.py:752
  522.8 74.0 %collective-permute-start.52 = (bf16[528,2048]{1,0:T(8,128)(2,1)S(1)}, bf16[528,2048]{1,0:T(8,128)(2,1)S(1)}, u32[]{:S(2)}, u32[]{:S(2)}) collective-permute-start(bf16[528,2048]{1,0:T(8,128)(2,1)S(1)} %add_convert_fusion.1), channel_id=1, source_target_pairs={{0,2},{1,3},{2,0},{3,1},{4,6},{5,7},{6,4},{7,5},{8,10},{9,11},{10,... | collective-permute-start | bytes 6488072 | tf_op jit(solution)/shard_map/ppermute | solution.py:792
  528.4 27.5 %collective-permute-start.46 = (bf16[128,2048]{1,0:T(8,128)(2,1)S(1)}, bf16[128,2048]{1,0:T(8,128)(2,1)S(1)}, u32[]{:S(2)}, u32[]{:S(2)}) collective-permute-start(bf16[128,2048]{1,0:T(8,128)(2,1)S(1)} %collective-permute-done.45), channel_id=1, source_target_pairs={{0,4},{8,0},{16,8},{24,16},{28,24},{20,28},{12,20},{4,12},{1,5},{9... | collective-permute-start | bytes 1572872 | tf_op jit(solution)/shard_map/ppermute | solution.py:756
  542.1 26.0 %collective-permute-start.43 = (bf16[128,2048]{1,0:T(8,128)(2,1)S(1)}, bf16[128,2048]{1,0:T(8,128)(2,1)S(1)}, u32[]{:S(2)}, u32[]{:S(2)}) collective-permute-start(bf16[128,2048]{1,0:T(8,128)(2,1)S(1)} %collective-permute-done.42), channel_id=1, source_target_pairs={{0,8},{8,16},{16,24},{24,28},{28,20},{20,12},{12,4},{4,0},{1,9},{9... | collective-permute-start | bytes 1572872 | tf_op jit(solution)/shard_map/ppermute | solution.py:752
  555.8 19.6 %collective-permute-start.47 = (bf16[128,2048]{1,0:T(8,128)(2,1)S(1)}, bf16[128,2048]{1,0:T(8,128)(2,1)S(1)}, u32[]{:S(2)}, u32[]{:S(2)}) collective-permute-start(bf16[128,2048]{1,0:T(8,128)(2,1)S(1)} %collective-permute-done.46), channel_id=1, source_target_pairs={{0,4},{8,0},{16,8},{24,16},{28,24},{20,28},{12,20},{4,12},{1,5},{9... | collective-permute-start | bytes 1572872 | tf_op jit(solution)/shard_map/ppermute | solution.py:756
  603.3 73.5 %all-to-all-start.3 = ((bf16[8,528,256]{2,1,0:T(8,128)(2,1)}), bf16[8,528,256]{2,1,0:T(8,128)(2,1)S(1)}, u32[]{:S(2)}, u32[]{:S(2)}) async-start(bf16[8,528,256]{2,1,0:T(8,128)(2,1)} %after.34), calls=%async_computation.4 | async-start | bytes 4325376 | tf_op jit(solution)/shard_map/all_to_all | solution.py:871
  607.8 112.0 %reduce-scatter.5.cloned.1.call-start = ((), (), s32[]{:S(2)}) async-start(), calls=%async_computation.9 | async-start | bytes 1310720 | tf_op jit(solution)/shard_map/reduce_scatter | solution.py:1124
  619.0 139.8 %all-gather.7.cloned.1.call-start = ((), (), s32[]{:S(2)}) async-start(), calls=%async_computation.11 | async-start | bytes 1179648 | tf_op jit(solution)/shard_map/all_gather | solution.py:1172
  697.9 28.3 %collective-permute-start.55 = (bf16[256,2048]{1,0:T(8,128)(2,1)}, bf16[256,2048]{1,0:T(8,128)(2,1)}, u32[]{:S(2)}, u32[]{:S(2)}) collective-permute-start(bf16[256,2048]{1,0:T(8,128)(2,1)} %get-tuple-element.128), channel_id=1, source_target_pairs={{0,1},{1,0},{2,3},{3,2},{4,5},{5,4},{6,7},{7,6},{8,9},{9,8},{10,11... | collective-permute-start | bytes 3145736 | tf_op jit(solution)/shard_map/ppermute | solution.py:792
  698.4 27.9 %collective-permute-start.58 = (bf16[128,2048]{1,0:T(8,128)(2,1)}, bf16[128,2048]{1,0:T(8,128)(2,1)}, u32[]{:S(2)}, u32[]{:S(2)}) collective-permute-start(bf16[128,2048]{1,0:T(8,128)(2,1)} %get-tuple-element.283), channel_id=1, source_target_pairs={{0,4},{8,0},{16,8},{24,16},{28,24},{20,28},{12,20},{4,12},{1,5},{9... | collective-permute-start | bytes 1572872 | tf_op jit(solution)/shard_map/ppermute | solution.py:772
  701.6 24.7 %collective-permute-start.54 = (bf16[128,2048]{1,0:T(8,128)(2,1)}, bf16[128,2048]{1,0:T(8,128)(2,1)}, u32[]{:S(2)}, u32[]{:S(2)}) collective-permute-start(bf16[128,2048]{1,0:T(8,128)(2,1)} %add_convert_fusion.8), channel_id=1, source_target_pairs={{0,8},{8,16},{16,24},{24,28},{28,20},{20,12},{12,4},{4,0},{1,9},{9... | collective-permute-start | bytes 1572872 | tf_op jit(solution)/shard_map/ppermute | solution.py:770
  726.2 41.3 %collective-permute-start.63 = (bf16[256,2048]{1,0:T(8,128)(2,1)S(1)}, bf16[256,2048]{1,0:T(8,128)(2,1)}, u32[]{:S(2)}, u32[]{:S(2)}) collective-permute-start(bf16[256,2048]{1,0:T(8,128)(2,1)S(1)} %copy-done.56), channel_id=1, source_target_pairs={{0,1},{1,0},{2,3},{3,2},{4,5},{5,4},{6,7},{7,6},{8,9},{9,8},{10,11... | collective-permute-start | bytes 3145736 | tf_op jit(solution)/shard_map/ppermute | solution.py:792
  729.2 21.0 %collective-permute-start.56 = (bf16[128,2048]{1,0:T(8,128)(2,1)}, bf16[128,2048]{1,0:T(8,128)(2,1)S(1)}, u32[]{:S(2)}, u32[]{:S(2)}) collective-permute-start(bf16[128,2048]{1,0:T(8,128)(2,1)} %get-tuple-element.280), channel_id=1, source_target_pairs={{0,8},{8,16},{16,24},{24,28},{28,20},{20,12},{12,4},{4,0},{1,9},{9... | collective-permute-start | bytes 1572872 | tf_op jit(solution)/shard_map/ppermute | solution.py:770
  731.2 23.0 %collective-permute-start.59 = (bf16[128,2048]{1,0:T(8,128)(2,1)}, bf16[128,2048]{1,0:T(8,128)(2,1)}, u32[]{:S(2)}, u32[]{:S(2)}) collective-permute-start(bf16[128,2048]{1,0:T(8,128)(2,1)} %get-tuple-element.281), channel_id=1, source_target_pairs={{0,4},{8,0},{16,8},{24,16},{28,24},{20,28},{12,20},{4,12},{1,5},{9... | collective-permute-start | bytes 1572872 | tf_op jit(solution)/shard_map/ppermute | solution.py:772
  734.0 33.5 %collective-permute-start.64 = (bf16[256,2048]{1,0:T(8,128)(2,1)}, bf16[256,2048]{1,0:T(8,128)(2,1)}, u32[]{:S(2)}, u32[]{:S(2)}) collective-permute-start(bf16[256,2048]{1,0:T(8,128)(2,1)} %add_convert_fusion.3), channel_id=1, source_target_pairs={{0,2},{1,3},{2,0},{3,1},{4,6},{5,7},{6,4},{7,5},{8,10},{9,11},{10,... | collective-permute-start | bytes 3145736 | tf_op jit(solution)/shard_map/ppermute | solution.py:792
  756.8 23.3 %collective-permute-start.57 = (bf16[128,2048]{1,0:T(8,128)(2,1)}, bf16[128,2048]{1,0:T(8,128)(2,1)}, u32[]{:S(2)}, u32[]{:S(2)}) collective-permute-start(bf16[128,2048]{1,0:T(8,128)(2,1)} %get-tuple-element.278), channel_id=1, source_target_pairs={{0,8},{8,16},{16,24},{24,28},{28,20},{20,12},{12,4},{4,0},{1,9},{9... | collective-permute-start | bytes 1572872 | tf_op jit(solution)/shard_map/ppermute | solution.py:770
  756.9 23.3 %collective-permute-start.60 = (bf16[128,2048]{1,0:T(8,128)(2,1)}, bf16[128,2048]{1,0:T(8,128)(2,1)}, u32[]{:S(2)}, u32[]{:S(2)}) collective-permute-start(bf16[128,2048]{1,0:T(8,128)(2,1)} %get-tuple-element.279), channel_id=1, source_target_pairs={{0,4},{8,0},{16,8},{24,16},{28,24},{20,28},{12,20},{4,12},{1,5},{9... | collective-permute-start | bytes 1572872 | tf_op jit(solution)/shard_map/ppermute | solution.py:772
  771.5 30.0 %all-to-all-start.4 = ((bf16[8,256,256]{2,1,0:T(8,128)(2,1)}), bf16[8,256,256]{2,1,0:T(8,128)(2,1)S(1)}, u32[]{:S(2)}, u32[]{:S(2)}) async-start(bf16[8,256,256]{2,1,0:T(8,128)(2,1)} %bitcast.289), calls=%async_computation.5 | async-start | bytes 2097152 | tf_op jit(solution)/shard_map/all_to_all | solution.py:871
  (183 other events, 1370.0 us)
Sparse Core Ops, SparseCore 0:
  182.0 99.3 all-gather.4
  492.9 116.8 reduce-scatter.2
  619.2 29.6 reduce-scatter.4
  711.5 45.1 all-gather.6

commit v4 on v3

--- a/solution.py
+++ b/solution.py
@@ -10,6 +10,7 @@
 MB = 16
 EPS = 1e-06
 F32 = jnp.float32
+VMEM_ASKED = 58 * 1024 * 1024
 BF16 = jnp.bfloat16
 
 
@@ -50,6 +51,43 @@
     columns = jnp.transpose(info)
     same = ((row % step) // MB == (col % step) // MB) & (columns[:, 1:2] == info[1:2, :])
     return row // step, col // step, row % MB, col % MB, same, columns
+
+
+def chunk_info(docs_ref, logits, heads, head_dim, chunk):
+    tokens = logits.shape[0]
+    count = heads * tokens
+    step = MB * heads
+    docs = docs_ref.shape[0] - 1
+    pieces = [logits[m * MB : (m + 1) * MB] for m in range(tokens // MB) for _ in range(heads)]
+    spread = jnp.concatenate(pieces, axis=0)
+    lane = lax.broadcasted_iota(jnp.int32, spread.shape, 1)
+    own = (lax.broadcasted_iota(jnp.int32, spread.shape, 0) % step) // MB
+    logit = jnp.sum(jnp.transpose(jnp.where(lane == own, spread, 0.0)), axis=0, keepdims=True)
+    start = chunk * tokens
+    col = lax.broadcasted_iota(jnp.int32, (1, count), 1)
+    block_at = start + (col // step) * MB
+    doc = jnp.zeros((1, count), jnp.int32)
+    before = end = jnp.int32(0)
+    for d in range(docs):
+        doc = doc + (block_at >= docs_ref[d]).astype(jnp.int32)
+        before = before + (docs_ref[d] < start).astype(jnp.int32)
+        end = end + (docs_ref[d] < start + tokens).astype(jnp.int32)
+    live = (block_at + col % MB < docs_ref[docs]).astype(F32)
+    sig = jax.nn.sigmoid(logit)
+    zero = jnp.zeros((1, count), F32)
+    return jnp.concatenate(
+        [
+            sig / head_dim * live,
+            doc.astype(F32),
+            (doc > before).astype(F32),
+            (doc == end).astype(F32),
+            zero + (end > before).astype(F32),
+            live * sig * (1.0 - sig) / head_dim,
+            zero,
+            zero,
+        ],
+        axis=0,
+    )
 
 
 def augment(rows, heads, head_dim, wide):
@@ -69,7 +107,7 @@
 
 
 def forward_kernel(
-    heads, idx_ref, x_ref, info_ref, gb_ref, init_ref, out_ref, n_ref, r_ref, nb_ref, stat_ref, w_ref, state
+    heads, idx_ref, docs_ref, x_ref, logit_ref, gb_ref, init_ref, out_ref, n_ref, r_ref, nb_ref, stat_ref, w_ref, state
 ):
     head_dim = gb_ref.shape[1]
     tokens = x_ref.shape[0]
@@ -83,7 +121,7 @@
 
     carried = state[...]
     w_ref[0] = carried
-    info = info_ref[...]
+    info = chunk_info(docs_ref, logit_ref[...], heads, head_dim, pl.program_id(0))
     x = x_ref[...]
     q_rows = chunk_rows(x, heads, 0, 3 * head_dim, head_dim)
     k_rows = chunk_rows(x, heads, head_dim, 3 * head_dim, head_dim)
@@ -160,10 +198,11 @@
 def backward_kernel(
     heads,
     idx_ref,
+    docs_ref,
     x_ref,
     d_ref,
     gate_ref,
-    info_ref,
+    logit_ref,
     gb_ref,
     init_ref,
     n_ref,
@@ -191,7 +230,8 @@
     d_end = state[...]
     carried = w_ref[0]
     init = init_ref[...]
-    info = info_ref[...]
+    chunk = pl.num_programs(0) - 1 - pl.program_id(0)
+    info = chunk_info(docs_ref, logit_ref[...], heads, head_dim, chunk)
     x = x_ref[...]
     q_rows = chunk_rows(x, heads, 0, 3 * head_dim, head_dim)
     k_rows = chunk_rows(x, heads, head_dim, 3 * head_dim, head_dim)
@@ -328,19 +368,19 @@
 def chain_specs(heads, tokens, head_dim, full, at):
     count = heads * tokens
     return dict(
-        x=pl.BlockSpec((tokens, heads * 3 * head_dim), lambda i, idx: (idx[at(i)], 0)),
-        dx=pl.BlockSpec((tokens, heads * 4 * head_dim + 128), lambda i, idx: (idx[at(i)], 0)),
-        rows=pl.BlockSpec((tokens, heads * head_dim), lambda i, idx: (idx[at(i)], 0)),
-        info=pl.BlockSpec((8, count), lambda i, idx: (0, idx[at(i)])),
-        gb=pl.BlockSpec((2, head_dim, 128), lambda i, idx: (0, 0, 0)),
-        init=pl.BlockSpec((head_dim, full), lambda i, idx: (0, 0)),
-        tall=pl.BlockSpec((head_dim, count), lambda i, idx: (0, at(i))),
-        stat=pl.BlockSpec((8, count), lambda i, idx: (0, at(i))),
-        weight=pl.BlockSpec((1, head_dim, full), lambda i, idx: (at(i), 0, 0)),
-    )
-
-
-def chain_forward(idx, x3, info, gb, init, tokens):
+        x=pl.BlockSpec((tokens, heads * 3 * head_dim), lambda i, idx, docs: (idx[at(i)], 0)),
+        dx=pl.BlockSpec((tokens, heads * 4 * head_dim + 128), lambda i, idx, docs: (idx[at(i)], 0)),
+        rows=pl.BlockSpec((tokens, heads * head_dim), lambda i, idx, docs: (idx[at(i)], 0)),
+        logit=pl.BlockSpec((tokens, 128), lambda i, idx, docs: (idx[at(i)], 0)),
+        gb=pl.BlockSpec((2, head_dim, 128), lambda i, idx, docs: (0, 0, 0)),
+        init=pl.BlockSpec((head_dim, full), lambda i, idx, docs: (0, 0)),
+        tall=pl.BlockSpec((head_dim, count), lambda i, idx, docs: (0, at(i))),
+        stat=pl.BlockSpec((8, count), lambda i, idx, docs: (0, at(i))),
+        weight=pl.BlockSpec((1, head_dim, full), lambda i, idx, docs: (at(i), 0, 0)),
+    )
+
+
+def chain_forward(idx, docs, x3, logits, gb, init, tokens):
     total = x3.shape[0]
     head_dim = gb.shape[1]
     heads = x3.shape[1] // (3 * head_dim)
@@ -351,9 +391,9 @@
     return pl.pallas_call(
         partial(forward_kernel, heads),
         grid_spec=pltpu.PrefetchScalarGridSpec(
-            num_scalar_prefetch=1,
+            num_scalar_prefetch=2,
             grid=(chunks,),
-            in_specs=[s["x"], s["info"], s["gb"], s["init"]],
+            in_specs=[s["x"], s["logit"], s["gb"], s["init"]],
             out_specs=[s["rows"], s["tall"], s["tall"], s["tall"], s["stat"], s["weight"]],
             scratch_shapes=[pltpu.VMEM((head_dim, full), F32)],
         ),
@@ -366,16 +406,14 @@
             jax.ShapeDtypeStruct((chunks, head_dim, full), F32),
         ],
         compiler_params=pltpu.CompilerParams(
-            dimension_semantics=("arbitrary",), vmem_limit_bytes=32 * 1024 * 1024
+            dimension_semantics=("arbitrary",), vmem_limit_bytes=VMEM_ASKED
         ),
-        cost_estimate=pl.CostEstimate(
-            flops=1, bytes_accessed=1, transcendentals=0
-        ),
+        cost_estimate=pl.CostEstimate(flops=1, bytes_accessed=1, transcendentals=0),
         name="chain_forward",
-    )(idx, x3, info, gb, init)
-
-
-def chain_backward(idx, x3, d_inner, d_gate, info, gb, init, kept, tokens):
+    )(idx, docs, x3, logits, gb, init)
+
+
+def chain_backward(idx, docs, x3, d_inner, d_gate, logits, gb, init, kept, tokens):
     total = x3.shape[0]
     head_dim = gb.shape[1]
     heads = x3.shape[1] // (3 * head_dim)
@@ -385,13 +423,13 @@
     return pl.pallas_call(
         partial(backward_kernel, heads),
         grid_spec=pltpu.PrefetchScalarGridSpec(
-            num_scalar_prefetch=1,
+            num_scalar_prefetch=2,
             grid=(chunks,),
             in_specs=[
                 s["x"],
                 s["rows"],
                 s["rows"],
-                s["info"],
+                s["logit"],
                 s["gb"],
                 s["init"],
                 s["tall"],
@@ -409,37 +447,11 @@
             jax.ShapeDtypeStruct(init.shape, F32),
         ],
         compiler_params=pltpu.CompilerParams(
-            dimension_semantics=("arbitrary",), vmem_limit_bytes=40 * 1024 * 1024
+            dimension_semantics=("arbitrary",), vmem_limit_bytes=VMEM_ASKED
         ),
-        cost_estimate=pl.CostEstimate(
-            flops=1, bytes_accessed=1, transcendentals=0
-        ),
+        cost_estimate=pl.CostEstimate(flops=1, bytes_accessed=1, transcendentals=0),
         name="chain_backward",
-    )(idx, x3, d_inner, d_gate, info, gb, init, *kept)
-
-
-def chain_info(starts, chunk_start, rates, factors, heads, tokens):
-    blocks = tokens // MB
-    chunks = chunk_start.shape[0]
-
-    def begun(limit):
-        return jnp.sum((starts < limit[..., None]).astype(jnp.int32), -1)
-
-    at = chunk_start[:, None] + jnp.arange(blocks, dtype=jnp.int32) * MB
-    doc = begun(at + 1)
-    before = begun(chunk_start)[:, None]
-    end = begun(chunk_start + tokens)[:, None]
-    fresh = jnp.broadcast_to(end > before, doc.shape)
-    spread = jnp.stack(
-        [item.astype(F32) for item in (doc, doc > before, doc == end, fresh)]
-    ).reshape(4, chunks * blocks, 1)
-    spread = jnp.broadcast_to(spread, (4, chunks * blocks, heads * MB)).reshape(4, -1)
-
-    def as_row(item):
-        return jnp.swapaxes(item.reshape(-1, MB, heads), 1, 2).reshape(1, -1)
-
-    rows = [as_row(rates), spread, as_row(factors)]
-    return jnp.concatenate(rows + [jnp.zeros((2, spread.shape[1]), F32)], axis=0)
+    )(idx, docs, x3, d_inner, d_gate, logits, gb, init, *kept)
 
 
 def chain_params(init_weight, init_bias, inner_gain, inner_bias):
@@ -472,31 +484,32 @@
     return d_w, d_b, both[0].T, both[1].T
 
 
-def cut_kernel(turned, share, padded, *refs):
+def cut_kernel(turned, shares, *refs):
     mats, out_ref, held = refs[: len(turned)], refs[-2], refs[-1]
-    for i, mat in enumerate(mats):
+    at = 0
+    for mat, turn, share in zip(mats, turned, shares):
+        padded = share + -share % MB
         value = mat[...].astype(F32)
-        held[...] = jnp.transpose(value) if turned[i] else value
+        held[: value.shape[1] if turn else value.shape[0]] = jnp.transpose(value) if turn else value
         for s in range(out_ref.shape[0]):
-            out_ref[s, i * padded : i * padded + share] = held[
-                s * share : (s + 1) * share
-            ].astype(BF16)
+            out_ref[s, at : at + share] = held[s * share : (s + 1) * share].astype(BF16)
             if padded > share:
-                out_ref[s, i * padded + share : (i + 1) * padded] = jnp.zeros(
+                out_ref[s, at + share : at + padded] = jnp.zeros(
                     (padded - share, out_ref.shape[2]), BF16
                 )
+        at += padded
 
 
 def cut_features(seq, mats, turned):
-    features = mats[0].shape[1] if turned[0] else mats[0].shape[0]
+    features = [m.shape[1] if turn else m.shape[0] for m, turn in zip(mats, turned)]
     cols = mats[0].shape[0] if turned[0] else mats[0].shape[1]
-    share = features // seq
-    padded = share + -share % MB
+    shares = [count // seq for count in features]
+    rows = sum(share + -share % MB for share in shares)
     return pl.pallas_call(
-        partial(cut_kernel, turned, share, padded),
-        out_shape=jax.ShapeDtypeStruct((seq, len(mats) * padded, cols), BF16),
-        scratch_shapes=[pltpu.VMEM((features, cols), F32)],
-        compiler_params=pltpu.CompilerParams(vmem_limit_bytes=24 * 1024 * 1024),
+        partial(cut_kernel, turned, shares),
+        out_shape=jax.ShapeDtypeStruct((seq, rows, cols), BF16),
+        scratch_shapes=[pltpu.VMEM((max(features), cols), F32)],
+        compiler_params=pltpu.CompilerParams(vmem_limit_bytes=VMEM_ASKED),
         cost_estimate=pl.CostEstimate(flops=1, bytes_accessed=1, transcendentals=0),
         name="cut_features",
     )(*mats)
@@ -519,7 +532,7 @@
         partial(join_kernel, turned, features // seq, rows // len(turned)),
         out_shape=[jax.ShapeDtypeStruct(shape, F32) for shape in shapes],
         scratch_shapes=[pltpu.VMEM((features, cols), F32)],
-        compiler_params=pltpu.CompilerParams(vmem_limit_bytes=24 * 1024 * 1024),
+        compiler_params=pltpu.CompilerParams(vmem_limit_bytes=VMEM_ASKED),
         cost_estimate=pl.CostEstimate(flops=1, bytes_accessed=1, transcendentals=0),
         name="join_features",
     )(block)
@@ -530,7 +543,7 @@
     grad_refs = refs[count : 2 * count]
     weights = refs[2 * count : 2 * count + parts]
     outs = refs[2 * count + parts + kept :]
-    (x_ref, g_ref, at_ref, ut_ref, ht_ref, y_ref, d_ref, a_t, u_t, h_t, y_all, d_all) = outs
+    (at_ref, ut_ref, ht_ref, y_ref, d_ref, a_t, u_t, h_t, y_all, d_all) = outs
     step = pl.program_id(0)
     size = rows_refs[0].shape[0]
 
@@ -542,7 +555,7 @@
             for i in range(3)
         )
         rows = jnp.concatenate([ref[...] for ref in rows_refs], axis=0)
-        grad = jnp.concatenate([ref[0] for ref in grad_refs], axis=0)
+        grad = jnp.concatenate([ref[...] for ref in grad_refs], axis=0)
         act_a = mm_nt(rows, swish)
         act_u = mm_nt(rows, up)
         d_hidden = mm_nt(grad, down)
@@ -564,8 +577,6 @@
         @pl.when(step == i)
         def _(i=i):
             part = slice(i * size, (i + 1) * size)
-            x_ref[...] = rows_refs[i][...]
-            g_ref[...] = grad_refs[i][0]
             at_ref[...] = a_t[:, part]
             ut_ref[...] = u_t[:, part]
             ht_ref[...] = h_t[:, part]
@@ -573,33 +584,24 @@
             d_ref[...] = d_all[part]
 
 
-def ffn_step(members, slot, rows, grad_all, weights, kept):
+def ffn_step(members, seq, slot, rows, grads, weights, kept):
     count = len(rows)
     size, width = rows[0].shape
-    seq = grad_all.shape[0]
     total = seq * size
     features = sum(w.shape[0] for w in weights) // 3
     whole = pl.BlockSpec(memory_space=pltpu.VMEM)
 
-    def grad_spec(i):
-        return pl.BlockSpec((1, size, width), lambda s, member: (member[i], 0, 0))
-
-    row_spec = pl.BlockSpec((size, width), lambda s, member: (slot + s, 0))
     turned_spec = pl.BlockSpec((features, size), lambda s, member: (0, slot + s))
     turned = jax.ShapeDtypeStruct((features, total), BF16)
-    tall = jax.ShapeDtypeStruct((total, width), BF16)
     first = 1 + 2 * count + len(weights)
     out = pl.pallas_call(
         partial(ffn_kernel, count, len(weights), len(kept)),
         grid_spec=pltpu.PrefetchScalarGridSpec(
             num_scalar_prefetch=1,
             grid=(count,),
-            in_specs=[whole] * count
-            + [grad_spec(i) for i in range(count)]
-            + [whole] * len(weights)
+            in_specs=[whole] * (2 * count + len(weights))
             + [pl.BlockSpec(memory_space=pl.ANY)] * len(kept),
-            out_specs=[row_spec, row_spec]
-            + [turned_spec] * 3
+            out_specs=[turned_spec] * 3
             + [
                 pl.BlockSpec((1, size, width), lambda s, member: (member[s], 0, 0)),
                 pl.BlockSpec((size, width), lambda s, member: (s, 0)),
@@ -607,99 +609,153 @@
             scratch_shapes=[pltpu.VMEM((features, count * size), BF16)] * 3
             + [pltpu.VMEM((count * size, width), BF16)] * 2,
         ),
-        out_shape=[tall, tall, turned, turned, turned]
+        out_shape=[turned] * 3
         + [
             jax.ShapeDtypeStruct((seq, size, width), BF16),
             jax.ShapeDtypeStruct((count * size, width), BF16),
         ],
         input_output_aliases={first + i: i for i in range(len(kept))},
         compiler_params=pltpu.CompilerParams(
-            dimension_semantics=("arbitrary",), vmem_limit_bytes=48 * 1024 * 1024
+            dimension_semantics=("arbitrary",), vmem_limit_bytes=VMEM_ASKED
         ),
-        cost_estimate=pl.CostEstimate(
-            flops=12_000_000_000, bytes_accessed=1, transcendentals=0
-        ),
+        cost_estimate=pl.CostEstimate(flops=1, bytes_accessed=1, transcendentals=0),
         name="ffn_step",
-    )(members, *rows, *([grad_all] * count), *weights, *kept)
+    )(members, *rows, *grads, *weights, *kept)
     return out[:-1], out[-1]
 
 
-def ffn_grad_kernel(parts, at_ref, ut_ref, ht_ref, x_ref, g_ref, *outs):
-    x = x_ref[...]
-    g = g_ref[...]
+def ffn_grad_kernel(parts, count, at_ref, ut_ref, ht_ref, *refs):
+    x = jnp.concatenate([ref[...] for ref in refs[:count]], axis=0)
+    g = jnp.concatenate([ref[...] for ref in refs[count : 2 * count]], axis=0)
     padded = at_ref.shape[0] // parts
-    for i, out in enumerate(outs):
+    for i, out in enumerate(refs[2 * count :]):
         own = slice(i * padded, (i + 1) * padded)
         out[:padded] = mm(at_ref[own], x).astype(BF16)
         out[padded : 2 * padded] = mm(ut_ref[own], x).astype(BF16)
         out[2 * padded :] = mm(ht_ref[own], g).astype(BF16)
 
 
-def ffn_grads(parts, kept):
-    x, g, a_t, u_t, h_t = kept
-    total, width = x.shape
-    features = a_t.shape[0]
-    wide = pl.BlockSpec((total, 256), lambda i: (0, i))
-    whole = pl.BlockSpec((features, total), lambda i: (0, 0))
-    rows = 3 * features // parts
+def ffn_grads(parts, turned, rows, grads):
+    size, width = rows[0].shape
+    count = len(rows)
+    features = turned[0].shape[0]
+    wide = pl.BlockSpec((size, 256), lambda i: (0, i))
+    whole = pl.BlockSpec((features, count * size), lambda i: (0, 0))
+    each = 3 * features // parts
     return pl.pallas_call(
-        partial(ffn_grad_kernel, parts),
+        partial(ffn_grad_kernel, parts, count),
         grid=(width // 256,),
-        in_specs=[whole] * 3 + [wide] * 2,
-        out_specs=[pl.BlockSpec((rows, 256), lambda i: (0, i))] * parts,
-        out_shape=[jax.ShapeDtypeStruct((rows, width), BF16)] * parts,
+        in_specs=[whole] * 3 + [wide] * (2 * count),
+        out_specs=[pl.BlockSpec((each, 256), lambda i: (0, i))] * parts,
+        out_shape=[jax.ShapeDtypeStruct((each, width), BF16)] * parts,
         compiler_params=pltpu.CompilerParams(
-            dimension_semantics=("arbitrary",), vmem_limit_bytes=40 * 1024 * 1024
+            dimension_semantics=("arbitrary",), vmem_limit_bytes=VMEM_ASKED
         ),
-        cost_estimate=pl.CostEstimate(
-            flops=12_000_000_000, bytes_accessed=1, transcendentals=0
-        ),
+        cost_estimate=pl.CostEstimate(flops=1, bytes_accessed=1, transcendentals=0),
         name="ffn_grads",
-    )(a_t, u_t, h_t, x, g)
-
-
-def proj_grad_kernel(heads, head_dim, d_ref, x_ref, w_ref, *refs):
-    outs, rate_ref, gain_ref, turned = refs[:heads], refs[heads], refs[heads + 1], refs[heads + 2]
+    )(*turned, *rows, *grads)
+
+
+def proj_grad_kernel(heads, head_dim, d_ref, x_ref, w_ref, gated_ref, *refs):
+    count = len(refs) - heads - 4
+    mix = refs[:count]
+    outs, rate_ref, gain_ref = refs[count : count + heads], refs[-4], refs[-3]
+    turned, gated_turned = refs[-2:]
     each = 3 * head_dim
 
     @pl.when(pl.program_id(0) == 0)
     def _():
         turned[...] = jnp.transpose(d_ref[...].astype(F32)).astype(BF16)
+        gated_turned[...] = jnp.transpose(gated_ref[...].astype(F32)).astype(BF16)
 
     grad = mm(turned[...], x_ref[...])
+    grad_out = mm(gated_turned[...], jnp.concatenate([ref[...] for ref in mix], axis=0))
     gain_ref[...] = jnp.broadcast_to(
         jnp.sum(grad * w_ref[...].astype(F32), axis=0, keepdims=True), gain_ref.shape
     )
     gate = heads * each + 128
     for h, out in enumerate(outs):
+        own = slice(h * head_dim, (h + 1) * head_dim)
         out[:each] = grad[h * each : (h + 1) * each].astype(BF16)
-        out[each:] = grad[gate + h * head_dim : gate + (h + 1) * head_dim].astype(BF16)
+        out[each : each + head_dim] = grad[gate + h * head_dim : gate + (h + 1) * head_dim].astype(
+            BF16
+        )
+        out[each + head_dim :] = grad_out[own].astype(BF16)
     rate_ref[...] = grad[heads * each : heads * each + 8]
 
 
-def proj_grads(d_x, normed, weight, heads, head_dim):
+def proj_grads(d_x, normed, weight, gated, mix, heads, head_dim):
     total, packed = d_x.shape
     width = normed.shape[1]
 
     def wide(rows):
         return pl.BlockSpec((rows, 256), lambda i: (0, i))
+
+    def whole(array):
+        return pl.BlockSpec(array.shape, lambda i: (0, 0))
 
     return pl.pallas_call(
         partial(proj_grad_kernel, heads, head_dim),
         grid=(width // 256,),
-        in_specs=[pl.BlockSpec((total, packed), lambda i: (0, 0)), wide(total), wide(packed)],
-        out_specs=[wide(4 * head_dim)] * heads + [wide(8)] * 2,
-        out_shape=[jax.ShapeDtypeStruct((4 * head_dim, width), BF16)] * heads
+        in_specs=[whole(d_x), wide(total), wide(packed), whole(gated)]
+        + [wide(block.shape[0]) for block in mix],
+        out_specs=[wide(5 * head_dim)] * heads + [wide(8)] * 2,
+        out_shape=[jax.ShapeDtypeStruct((5 * head_dim, width), BF16)] * heads
         + [jax.ShapeDtypeStruct((8, width), F32)] * 2,
-        scratch_shapes=[pltpu.VMEM((packed, total), BF16)],
+        scratch_shapes=[pltpu.VMEM((packed, total), BF16), pltpu.VMEM(gated.shape[::-1], BF16)],
         compiler_params=pltpu.CompilerParams(
-            dimension_semantics=("arbitrary",), vmem_limit_bytes=40 * 1024 * 1024
+            dimension_semantics=("arbitrary",), vmem_limit_bytes=VMEM_ASKED
         ),
-        cost_estimate=pl.CostEstimate(
-            flops=9_000_000_000, bytes_accessed=1, transcendentals=0
+        cost_estimate=pl.CostEstimate(flops=1, bytes_accessed=1, transcendentals=0),
+        name="proj_grads",
+    )(d_x, normed, weight, gated, *mix)
+
+
+def project_kernel(count, parts, *refs):
+    blocks = refs[:count]
+    weights = refs[count : count + parts]
+    rate_ref, bias_ref, gain_ref, normed_ref, x_ref, logit_ref = refs[count + parts :]
+    size = blocks[0].shape[0]
+    packed = x_ref.shape[1]
+    for i in range(0, count, 2):
+
+        @pl.when(pl.program_id(0) == i // 2)
+        def _(i=i):
+            rows = jnp.concatenate([ref[...] for ref in blocks[i : i + 2]], axis=0).astype(F32)
+            inv = lax.rsqrt(jnp.mean(rows * rows, -1, keepdims=True) + EPS)
+            normed = (rows * inv * gain_ref[...]).astype(BF16)
+            normed_ref[...] = normed
+            weight = jnp.concatenate([ref[...] for ref in weights] + [rate_ref[...]], axis=0)
+            out = mm_nt(normed, weight)
+            x_ref[...] = out[:, :packed].astype(BF16)
+            logit_ref[...] = out[:, packed:] + bias_ref[...]
+
+
+def project(blocks, weights, rate_rows, bias, gain):
+    size, width = blocks[0].shape
+    count = len(blocks)
+    total = count * size
+    packed = sum(w.shape[0] for w in weights)
+
+    def rows(lanes):
+        return pl.BlockSpec((2 * size, lanes), lambda i: (i, 0))
+
+    return pl.pallas_call(
+        partial(project_kernel, count, len(weights)),
+        grid=(count // 2,),
+        in_specs=[pl.BlockSpec(memory_space=pltpu.VMEM)] * (count + len(weights) + 3),
+        out_specs=[rows(width), rows(packed), rows(128)],
+        out_shape=[
+            jax.ShapeDtypeStruct((total, width), BF16),
+            jax.ShapeDtypeStruct((total, packed), BF16),
+            jax.ShapeDtypeStruct((total, 128), F32),
+        ],
+        compiler_params=pltpu.CompilerParams(
+            dimension_semantics=("arbitrary",), vmem_limit_bytes=VMEM_ASKED
         ),
-        name="proj_grads",
-    )(d_x, normed, weight)
+        cost_estimate=pl.CostEstimate(flops=1, bytes_accessed=1, transcendentals=0),
+        name="project",
+    )(*blocks, *weights, rate_rows, bias, gain)
 
 
 def trans_dot(left, right):
@@ -744,21 +800,33 @@
     return [arrived[0], arrived[-1]] + list(arrived[1:-1])
 
 
-def ring_gather(block, size, work=None):
+def ring_gather(block, size, work=None, beside=None):
     arrived = [(block,)]
+    others = [(beside,)]
     ahead = back = block
+    ahead_too = back_too = beside
+
+    def move(value, step):
+        return None if value is None else lax.ppermute(value, "seq", ring_pairs(size, step))
+
+    def do_work(s):
+        if not work:
+            return []
+        return list(work(s, arrived[s], others[s]) if beside is not None else work(s, arrived[s]))
+
     for s in range(1, size // 2 + 1):
-        done = work(s - 1, arrived[-1]) if work else []
-        ahead = lax.ppermute(ahead, "seq", ring_pairs(size, 1))
+        last = s == size // 2
+        done = do_work(s - 1)
+        ahead, ahead_too = move(ahead, 1), move(ahead_too, 1)
+        if not last:
+            back, back_too = move(back, -1), move(back_too, -1)
+            done += [back, back_too]
+        done = [item for item in done + [ahead_too] if item is not None]
         if done:
             ahead = after(ahead, *done)
-        if s < size // 2:
-            back = lax.ppermute(back, "seq", ring_pairs(size, -1))
-            arrived.append((ahead, back))
-        else:
-            arrived.append((ahead,))
-    if work:
-        work(size // 2, arrived[-1])
+        arrived.append((ahead,) if last else (ahead, back))
+        others.append((ahead_too,) if last else (ahead_too, back_too))
+    do_work(size // 2)
     return arrived
 
 
@@ -770,8 +838,11 @@
         ahead = lax.ppermute(ahead, "seq", ring_pairs(size, 1))
         if s < half:
             back = lax.ppermute(back, "seq", ring_pairs(size, -1))
+            done = list(done) + [back]
         if done:
             ahead = after(ahead, *done)
+        if s < half:
+            back = after(back, ahead)
         ahead = ahead.astype(F32)
         if s < half:
             ahead = (ahead + part(half - s)).astype(BF16)
@@ -886,10 +957,14 @@
     return block.reshape(seq, -1, cols)
 
 
-def gather_heads(plan, block, count, head_dim):
+def start_heads(plan, block):
     seq, _, cols = block.shape
     block = block.transpose(1, 0, 2).reshape(-1, seq * cols)
-    parts = end_gather(start_gather(block)) if plan.mixed else [block]
+    return start_gather(block) if plan.mixed else [block]
+
+
+def end_heads(plan, parts, count, head_dim):
+    parts = end_gather(parts) if plan.mixed else parts
     size = count * head_dim
     return [part[i : i + size] for part in parts for i in range(0, part.shape[0], size)]
 
@@ -899,8 +974,9 @@
     return lambda k: jnp.concatenate(grads[k * each : (k + 1) * each], axis=0)
 
 
-def scatter_heads(plan, grads, block, count):
+def scatter_heads(plan, grads, block, turned):
     packed, width = grads[0].shape
+    count = len(turned)
     seq = plan.seq
     cols = width // seq
     head_dim = packed // count
@@ -908,16 +984,16 @@
         each = plan.each
         block = exchange(block.reshape(-1, seq, cols).transpose(1, 0, 2))
         if each == 1:
-            return join_features(block, seq * head_dim, (True,) * count)
+            return join_features(block, seq * head_dim, turned)
         block = block.reshape(seq, each, count, head_dim, cols)
         block = block.transpose(2, 0, 1, 3, 4).reshape(count, -1, cols).astype(F32)
-        return [part.T for part in block]
+        return [part.T if turn else part for part, turn in zip(block, turned)]
     block = jnp.concatenate(grads, axis=0).astype(BF16)
     block = block.reshape(-1, seq, cols).transpose(1, 0, 2)
     block = exchange(block).reshape(seq, plan.local, count, head_dim, cols)
     block = block.transpose(2, 0, 1, 3, 4).reshape(count, -1, cols)
     block = lax.psum_scatter(block, "grp", scatter_dimension=1, tiled=True).astype(F32)
-    return [part.T for part in block]
+    return [part.T if turn else part for part, turn in zip(block, turned)]
 
 
 def body(
@@ -986,47 +1062,52 @@
     own_lengths = lax.dynamic_index_in_dim(lengths, grp_index, 0, keepdims=False)
     ends = jnp.cumsum(own_lengths)
     starts = ends - own_lengths
-    chunk_start = member_of_slot * rows_tok
-    positions = (chunk_start[:, None] + jnp.arange(rows_tok, dtype=jnp.int32)).reshape(stream, 1)
-    live = (positions < ends[-1]).astype(F32)
+    docs = jnp.concatenate([starts, ends[-1:]])
 
     proj_block = exchange(
         cut_heads(plan, (w_query, w_key, w_value), (True, True, True), head_dim)
     )
     padded = w_down.shape[0] // seq
     padded += -padded % MB
-    token_steps = ring_gather(tokens[0], seq)
-    last_tokens = token_steps[-1][0]
     rate_rows = jnp.pad(pick(rate_weight.T), ((0, 128 - local), (0, 0)))
-    w_proj = jnp.concatenate(gather_heads(plan, proj_block, 3, head_dim) + [rate_rows], axis=0)
-    packed = w_proj.shape[0] - 128
-    side_block = cut_heads(plan, (w_gate, w_out), (True, False), head_dim)
-    side_block = exchange(after(side_block, last_tokens))
-    ffn_block = cut_features(seq, (w_swish, w_up, w_down), (True, True, False))
-    ffn_block = exchange(after(ffn_block, last_tokens))
+    gb, init = chain_params(*(pick(i) for i in (init_weight, init_bias, inner_gain, inner_bias)))
+    own = {}
+
+    bias = jnp.pad(pick(rate_bias), (0, 128 - local))[None]
+
+    def token_work(s, arrived):
+        if s == 1:
+            own["parts"] = start_heads(plan, after(proj_block, arrived[0]))
+            return [gb, init]
+        if s == seq // 2 - 2:
+            mats = (w_swish.T, w_up.T, w_down)
+            if plan.each == 1:
+                turned = (True, False, False, False, False)
+                own["rest"] = cut_features(seq, (w_gate, w_out) + mats, turned)
+            else:
+                side = cut_heads(plan, (w_gate, w_out), (True, False), head_dim)
+                own["rest"] = jnp.concatenate(
+                    [side, cut_features(seq, mats, (False,) * 3)], axis=1
+                )
+            return [own["rest"]]
+        if s == seq // 2 - 1:
+            own["parts"] = end_heads(plan, own["parts"], 3, head_dim)
+            return own["parts"][-1:]
+        return []
+
+    token_steps = ring_gather(tokens[0], seq, token_work)
+    normed, x3, logits = project(
+        sum(by_slots(token_steps), ()), own["parts"], rate_rows, bias, prenorm_gain[None]
+    )
+    rest_block = exchange(after(own["rest"], logits))
     grad_own = cotangent[0]
-    grad_all = lax.all_gather(after(grad_own, ffn_block), "seq", axis=0)
-
-    kept_first = []
-    for arrived in token_steps:
-        rows = jnp.concatenate(arrived, axis=0).astype(F32)
-        inv = lax.rsqrt(jnp.mean(rows * rows, -1, keepdims=True) + EPS)
-        unit_gain = (rows * inv * prenorm_gain).astype(BF16)
-        out = mm_nt(unit_gain, w_proj)
-        kept_first.append((unit_gain, out[:, :packed].astype(BF16), out[:, packed:]))
-    normed, x3, logits = (
-        jnp.concatenate(items, axis=0) for items in zip(*by_slots(kept_first))
-    )
-    logits = logits[:, :local] + pick(rate_bias)
-    rate_sig = jax.nn.sigmoid(logits)
-    rates = rate_sig / head_dim * live
-    factors = live * rate_sig * (1.0 - rate_sig) / head_dim
-    gb, init = chain_params(*(pick(i) for i in (init_weight, init_bias, inner_gain, inner_bias)))
-    info = chain_info(starts, chunk_start, rates, factors, local, rows_tok)
-    inner, *kept = chain_forward(slot_of_member, x3, info, gb, init, rows_tok)
-    kept_stat = after(kept[3], side_block, ffn_block)
-
-    sides = gather_heads(plan, side_block, 2, head_dim)
+
+    inner, *kept = chain_forward(slot_of_member, docs, x3, logits, gb, init, rows_tok)
+    kept_stat = after(kept[3], rest_block)
+    side_rows = rest_block.shape[1] - 3 * padded
+    side_block, ffn_block = rest_block[:, :side_rows], rest_block[:, side_rows:]
+
+    sides = end_heads(plan, start_heads(plan, side_block), 2, head_dim)
     m_gate = jnp.concatenate([side[:head_dim] for side in sides], axis=0)
     m_out = jnp.concatenate([side[head_dim:] for side in sides], axis=0)
     gate_pre = mm_nt(normed, m_gate)
@@ -1045,41 +1126,52 @@
     gated = (gelu_val * post).astype(BF16)
     ffn = {}
 
+
+    def ffn_corner(since):
+        ffn["parts"] = end_gather(ffn_parts)
+        return ffn["parts"][-1:]
+
     mixing = ring_scatter(
         by_distance(mm(gated, m_out).astype(BF16)),
         seq,
-        [lambda since: [], lambda since: [], lambda since: [], lambda since: ffn_parts[2:3]],
-    )
-    ffn["parts"] = end_gather(ffn_parts)
+        [lambda since: [], lambda since: [], lambda since: [], ffn_corner],
+    )
     own_rows = tokens[0].astype(F32)
     resid = own_rows + mixing
     inv_second = lax.rsqrt(jnp.mean(resid * resid, -1, keepdims=True) + EPS)
     unit_second = resid * inv_second
     ffn_in = (unit_second * feedforward_norm_gain).astype(BF16)
 
-    got = {"kept": ()}
+    got = {"kept": (), "rows": [], "grads": []}
     d_parts = {}
 
-    def step_work(s, arrived):
+    def step_work(s, arrived, grads):
         slot = 2 * s if s < seq // 2 else 1
         members = lax.slice_in_dim(member_of_slot, slot, slot + len(arrived))
         got["kept"], d_in = ffn_step(
-            members, slot, arrived, grad_all, ffn["parts"], got["kept"]
+            members, seq, slot, arrived, grads, ffn["parts"], got["kept"]
         )
+        got["rows"].append(arrived)
+        got["grads"].append(grads)
         for i in range(len(arrived)):
             d_parts[steps[slot + i]] = d_in[i * rows_tok : (i + 1) * rows_tok]
         return [d_in]
 
-    ring_gather(ffn_in, seq, step_work)
+    ring_gather(ffn_in, seq, step_work, grad_own)
     kept_ffn = got["kept"]
 
     def ffn_work(since):
-        rows, *others = kept_ffn[:5]
-        got["ffn"] = ffn_grads(groups, [after(rows, since)] + others)
+        first, *others = kept_ffn[:3]
+        got["ffn"] = ffn_grads(
+            groups,
+            [after(first, since)] + others,
+            sum(by_slots(got["rows"]), ()),
+            sum(by_slots(got["grads"]), ()),
+        )
         return got["ffn"][:1]
 
-    def ffn_corner(since):
-        got["corner"] = start_scatter(ffn_grad)
+    def ffn_corner_work(since):
+        got["corner"] = start_scatter(lambda k: after(got["ffn"][k], since))
         got["across"] = cross_scatter(ffn_grad, got["corner"])
         return [got["corner"]]
 
@@ -1087,27 +1179,25 @@
         return got["ffn"][k]
 
     d_ffn = ring_scatter(
-        lambda k: d_parts[k if k < seq // 2 else k - seq], seq, [ffn_work, ffn_corner]
-    )
-    ffn_out = lax.psum_scatter(
-        after(kept_ffn[5], d_ffn), "seq", scatter_dimension=0, tiled=False
-    )
-    out_tokens = (resid + ffn_out.astype(F32)).astype(BF16)[None]
+        lambda k: d_parts[k if k < seq // 2 else k - seq], seq, [ffn_work, ffn_corner_work]
+    )
     second_scaled = d_ffn * feedforward_norm_gain
     g_ffn_gain = jnp.sum(d_ffn * unit_second, 0)
     d_resid = grad_own.astype(F32) + inv_second * (
         second_scaled - unit_second * jnp.mean(second_scaled * unit_second, -1, keepdims=True)
     )
-    mix_steps = ring_gather(d_resid.astype(BF16), seq)
+
+    def mix_work(s, arrived):
+        return [got["across"]] if s == seq // 2 - 2 else []
+
+    mix_steps = ring_gather(d_resid.astype(BF16), seq, mix_work)
+    ffn_out = lax.psum_scatter(
+        after(kept_ffn[3], d_ffn), "seq", scatter_dimension=0, tiled=False
+    )
+    out_tokens = (resid + ffn_out.astype(F32)).astype(BF16)[None]
     g_ffn = end_scatter(ffn_grad, got["across"])
     g_ffn = after(g_ffn.reshape(3 * padded, seq, -1).transpose(1, 0, 2), mix_steps[-1][0])
-    d_gated = []
-    g_out = 0.0
-    for s, arrived in enumerate(mix_steps):
-        rows = jnp.concatenate(arrived, axis=0)
-        first = (2 * s if s < seq // 2 else 1) * rows_tok
-        d_gated.append(mm_nt(rows, m_out))
-        g_out = g_out + trans_dot(gated[first : first + rows.shape[0]], rows)
+    d_gated = [mm_nt(jnp.concatenate(arrived, axis=0), m_out) for arrived in mix_steps]
     d_gated = jnp.concatenate(by_slots(d_gated), axis=0)
     d_post = d_gated * gelu_val
     d_gate_pre = gelu_pull(d_gated * post)[0].astype(BF16)
@@ -1118,38 +1208,48 @@
     sums = in_slots(pairwise_sum(in_order(sums), "seq", seq)) / width
     g_ffn = exchange(after(g_ffn, sums))
     d_inner = inv_o * (d_ohat - sums[0][:, None] - o_hat * sums[1][:, None])
-    g_out = g_out.astype(BF16).reshape(local, head_dim, width)
-    if plan.mixed:
-        g_out = plan.turn(g_out, grp_index).reshape(groups, plan.each * head_dim, width)
-        g_out = lax.psum_scatter(g_out, "grp", scatter_dimension=0, tiled=False)
-        g_out = g_out.reshape(plan.each, head_dim, width)
     d_x, d_gb, d_init = chain_backward(
-        slot_of_member, x3, d_inner, d_gate_pre, info, gb, init, kept, rows_tok
-    )
-    w_all = jnp.concatenate([w_proj, m_gate], axis=0)
-    d_normed_part = after(mm(d_x, w_all).astype(BF16), g_ffn, ffn_out)
-
-    def proj_work(since):
-        *got["heads"], got["rates"], got["gain"] = proj_grads(
-            d_x, after(normed, since), w_all, local, head_dim
-        )
-        return got["heads"][:1]
-
-    def heads_work(since):
+        slot_of_member, docs, x3, d_inner, d_gate_pre, logits, gb, init, kept, rows_tok
+    )
+    w_all = jnp.concatenate(own["parts"] + [rate_rows, m_gate], axis=0)
+    d_x = after(d_x, g_ffn, ffn_out)
+    *head_rows_grads, g_rates, g_gain = proj_grads(
+        d_x, normed, w_all, gated, sum(by_slots(mix_steps), ()), local, head_dim
+    )
+    d_logits = d_x[:, 3 * features : 3 * features + local].astype(F32)
+    parts = [item.reshape(local, -1) for item in chain_param_grads(d_gb, d_init, local)]
+    parts += [item.reshape(local, head_dim) for item in (g_post_gain, g_post_bias)]
+    parts += [g_rates[:local], jnp.sum(d_logits, 0)[:, None]]
+    sizes = [item.shape[1] for item in parts]
+    flat = jnp.concatenate(parts, axis=1)
+    flat = plan.turn(jnp.pad(flat, ((0, 0), (0, -flat.shape[1] % 1024))), grp_index)
+    count = flat.size
+    flat = jnp.concatenate([flat.reshape(-1), g_gain[0] / prenorm_gain, g_ffn_gain])
+    flat = pairwise_sum(flat.reshape(-1, 1024), "grp", groups)
+    flat_all = lax.all_gather(flat, "seq", axis=0)
+    d_x = after(d_x, g_gain)
+    d_normed_part = mm(d_x, w_all).astype(BF16)
+
+    def corner_work(since):
         if not plan.mixed:
             return []
-        block = heads_block(plan, got["heads"])
+        block = heads_block(plan, head_rows_grads)
         got["corner"] = start_scatter(block)
-        got["across"] = cross_scatter(block, got["corner"])
+        got["across"] = cross_scatter(block, after(got["corner"], flat))
         return [got["corner"]]
 
-    d_normed = ring_scatter(by_distance(d_normed_part), seq, [proj_work, heads_work])
-    summed = end_scatter(heads_block(plan, got["heads"]), got["across"]) if plan.mixed else None
-    g_heads = scatter_heads(plan, got["heads"], summed, 4)
-    g_out = exchange(after(g_out, d_normed_part).reshape(-1, seq, width // seq).transpose(1, 0, 2))
-    g_out = g_out.reshape(-1, width // seq)
-    if not plan.mixed:
-        g_out = lax.psum_scatter(g_out, "grp", scatter_dimension=0, tiled=True)
+    def join_work(since):
+        got["join"] = join_features(after(g_ffn, since), w_down.shape[0], (False,) * 3)
+        return got["join"][:1]
+
+    def across_work(since):
+        return [got["across"]] if plan.mixed else []
+
+    d_normed = ring_scatter(
+        by_distance(d_normed_part), seq, [corner_work, join_work, across_work]
+    )
+    summed = end_scatter(heads_block(plan, head_rows_grads), got["across"]) if plan.mixed else None
+    g_heads = scatter_heads(plan, head_rows_grads, summed, (True,) * 4 + (False,))
     own_inv = lax.rsqrt(jnp.mean(own_rows * own_rows, -1, keepdims=True) + EPS)
     own_unit = own_rows * own_inv
     first_scaled = d_normed * prenorm_gain
@@ -1159,17 +1259,7 @@
         * (first_scaled - own_unit * jnp.mean(first_scaled * own_unit, -1, keepdims=True))
     )[None]
 
-    d_logits = d_x[:, packed : packed + local].astype(F32)
-    parts = [item.reshape(local, -1) for item in chain_param_grads(d_gb, d_init, local)]
-    parts += [item.reshape(local, head_dim) for item in (g_post_gain, g_post_bias)]
-    parts += [got["rates"][:local], jnp.sum(d_logits, 0)[:, None]]
-    sizes = [item.shape[1] for item in parts]
-    flat = jnp.concatenate(parts, axis=1)
-    flat = plan.turn(jnp.pad(flat, ((0, 0), (0, -flat.shape[1] % 1024))), grp_index)
-    count = flat.size
-    flat = jnp.concatenate([flat.reshape(-1), got["gain"][0] / prenorm_gain, g_ffn_gain])
-    flat = pairwise_sum(flat.reshape(-1, 1024), "grp", groups)
-    flat = lax.all_gather(flat, "seq", axis=0).reshape(seq, -1)
+    flat = after(flat_all, d_normed).reshape(seq, -1)
     gains = jnp.sum(flat[:, count:], 0).reshape(2, width)
     flat = plan.order(flat[:, :count].reshape(seq, local, -1))
     small = []
@@ -1177,7 +1267,7 @@
     for size in sizes:
         small.append(flat[:, offset : offset + size])
         offset += size
-    g_ffn = join_features(g_ffn, w_down.shape[0], (True, True, False))
+    g_ffn = got["join"]
     return (
         out_tokens,
         grad_tokens,
@@ -1194,10 +1284,10 @@
         small[3],
         small[4].reshape(width),
         small[5].reshape(width),
-        g_out.astype(F32),
+        g_heads[4],
         gains[1],
-        g_ffn[0],
-        g_ffn[1],
+        g_ffn[0].T,
+        g_ffn[1].T,
         g_ffn[2],
     )
 

time: 818 us -> 757 us (0.925)
  local copies, waits for them, and re-layouts: 149 us -> 70.7 us
  Pallas kernels: 144 us -> 171 us
  matrix products: 42.8 us -> 20.2 us
  waiting for transfers between devices: 296 us -> 307 us
    unnamed x342 -> x162, local copies, waits for them, and re-layouts: 107 us -> 37.8 us
    ppermute x12, waiting for transfers between devices: 118 us -> 73.3 us  [ring_scatter(): ahead = lax.ppermute(ahead, 'seq', ring_pairs(size, 1))]
    ppermute x15, waiting for transfers between devices: 0.04 us -> 22 us  [swap(): return lax.ppermute(value, 'grp', [(i, i ^ bit) for i in range(4)])]
    pallas_call x4, Pallas kernels: 16.5 us -> 31 us  [the longest x1 14.5 us: ffn_grads(): pl.pallas_call(partial(ffn_grad_kernel, parts, count), grid=(width // 256...]
    ppermute x21 -> x28, waiting for transfers between devices: 111 us -> 124 us  [move(): lax.ppermute(value, 'seq', ring_pairs(size, step))]
    ppermute x21 -> x28, starting transfers between devices: 29.2 us -> 42.6 us  [move(): lax.ppermute(value, 'seq', ring_pairs(size, step))]
    dot_general x11 -> x6, matrix products: 21.8 us -> 8.72 us  [mm_nt(): lax.dot_general(left, right, (((1,), (1,)), ((), ())), preferred_element_...]
    all_to_all x6 -> x4, waiting for transfers between devices: 25.7 us -> 36.3 us  [exchange(): return lax.all_to_all(block, 'seq', 0, 0, tiled=True)]
  transfers between devices with their start and end apart: 75 -> 78, of which waited for: 38 -> 42; matrix products, arithmetic and copies ran while one was open for 21% -> 14% of each run, Pallas kernels for 15% -> 19%
where the time goes in v4:
time: 757 us; the launch traced here: 746 us
  waiting for transfers between devices  307 us (41%)
  Pallas kernels  171 us (23%)
  starting transfers between devices  101 us (13%)
  local copies, waits for them, and re-layouts  70.7 us (9%)
  other arithmetic  61.4 us (8%)
  matrix products  20.2 us (3%)
  between operations  15.3 us (2%)
    ppermute x28, waiting for transfers between devices, move(): lax.ppermute(value, 'seq', ring_pairs(size, step))  124 us
    ppermute x12, waiting for transfers between devices, ring_scatter(): ahead = lax.ppermute(ahead, 'seq', ring_pairs(size, 1))  73.3 us
    pallas_call x5, Pallas kernels, ffn_step(): pl.pallas_call(partial(ffn_kernel, count, len(weights), len(kept)), grid_...  57.1 us
    ppermute x28, starting transfers between devices, move(): lax.ppermute(value, 'seq', ring_pairs(size, step))  42.6 us
    unnamed x162, local copies, waits for them, and re-layouts  37.8 us
    pallas_call x1, Pallas kernels, chain_backward(): pl.pallas_call(partial(backward_kernel, heads), grid_spec=pltpu.PrefetchS...  37.5 us
    all_to_all x4, waiting for transfers between devices, exchange(): return lax.all_to_all(block, 'seq', 0, 0, tiled=True)  36.3 us
    ppermute x9, waiting for transfers between devices, ring_scatter(): back = lax.ppermute(back, 'seq', ring_pairs(size, -1))  29.3 us
  transfers between devices with their start and end apart: 78, of which 42 were waited for; matrix products, arithmetic and copies ran while one was open for 14% of the time, Pallas kernels for 19%

profile of v4, /device:TPU:0, one launch (start us, length us, event | category | flops | bytes accessed | tf_op | source)
XLA Modules:
  0.0 745.7 jit_solution(13613403001699966383)
XLA Ops:
  9.5 7.3 all-to-all-start
  20.7 22.3 %collective-permute-done.1.refs_1_.refs_3_ = bf16[128,2048]{1,0:T(8,128)(2,1)S(1)} collective-permute-done((bf16[128,2048]{1,0:T(8,128)(2,1)S(1)}, bf16[128,2048]{1,0:T(8,128)(2,1)S(1)}, u32[]{:S(2)}, u32[]{:S(2)}) %collective-permute-start.1) | collective-permute-done | bytes 524320 | tf_op jit(solution)/shard_map/ppermute | solution.py:810
  44.7 5.7 collective-permute-start.2
  57.5 5.3 collective-permute-done.3.refs_3_.refs_5_
  66.5 3.9 collective-permute-done.7.refs_10_
  73.6 3.6 cut_features.2.refs_1_.refs_0_
  84.1 8.8 %collective-permute-done.6.refs_0_ = bf16[128,2048]{1,0:T(8,128)(2,1)} collective-permute-done((bf16[128,2048]{1,0:T(8,128)(2,1)}, bf16[128,2048]{1,0:T(8,128)(2,1)}, u32[]{:S(2)}, u32[]{:S(2)}) %collective-permute-start.6) | collective-permute-done | bytes 524320 | tf_op jit(solution)/shard_map/ppermute | solution.py:810
  92.9 10.6 %project.1 = (bf16[1024,2048]{1,0:T(8,128)(2,1)}, bf16[1024,768]{1,0:T(8,128)(2,1)}, f32[1024,128]{1,0:T(8,128)}) custom-call(bf16[128,2048]{1,0:T(8,128)(2,1)} %bitcast.237, bf16[128,2048]{1,0:T(8,128)(2,1)} %after.47.refs_1_, bf16[128,2048]{1,0:T(8,128)(2,1)} %after.43.refs_1_.refs_2_, bf16[128,2048]{1,0:T(8,128)(2,1)} %copy-done.47, ...), custom_call_target="tpu_custom_call" | custom-call | flops 1 | bytes 1 | tf_op jit(solution)/shard_map/project/pallas_call | solution.py:743
  103.5 5.3 all-to-all-start.1
  112.0 24.5 %chain_forward.1 = (f32[1024,256]{1,0:T(8,128)}, f32[64,4096]{1,0:T(8,128)}, f32[64,4096]{1,0:T(8,128)}, f32[64,4096]{1,0:T(8,128)}, f32[8,4096]{1,0:T(8,128)}, /*index=5*/f32[8,64,384]{2,1,0:T(8,128)}) custom-call(s32[8]{0:T(128)} %compare_select_fusion.7.idx_ref, s32[5]{0:T(128)} %pad_add_fusion.docs_ref, bf16[1024,768]{1,0:T(8,128)(2,1)} %get-tuple-element.77.x_ref, ...), custom_call_target="tpu_custom_call" | custom-call | flops 1 | bytes 1 | tf_op jit(solution)/shard_map/chain_forward/pallas_call | solution.py:391
  138.1 31.5 %all-to-all-done.1.refs_1_ = bf16[8,656,256]{2,1,0:T(8,128)(2,1)S(1)} async-done(((bf16[8,656,256]{2,1,0:T(8,128)(2,1)}), bf16[8,656,256]{2,1,0:T(8,128)(2,1)S(1)}, u32[]{:S(2)}, u32[]{:S(2)}) %all-to-all-start.1) | async-done | bytes 2687008 | tf_op jit(solution)/shard_map/all_to_all | solution.py:942
  196.4 12.3 %collective-permute-done.16.refs_0_ = bf16[128,2048]{1,0:T(8,128)(2,1)S(1)} collective-permute-done((bf16[128,2048]{1,0:T(8,128)(2,1)S(1)}, bf16[128,2048]{1,0:T(8,128)(2,1)S(1)}, u32[]{:S(2)}, u32[]{:S(2)}) %collective-permute-start.16) | collective-permute-done | bytes 524320 | tf_op jit(solution)/shard_map/ppermute | solution.py:838
  214.2 15.5 %collective-permute-done.23.refs_4_.refs_6_ = bf16[528,2048]{1,0:T(8,128)(2,1)} collective-permute-done((bf16[528,2048]{1,0:T(8,128)(2,1)}, bf16[528,2048]{1,0:T(8,128)(2,1)}, u32[]{:S(2)}, u32[]{:S(2)}) %collective-permute-start.23) | collective-permute-done | bytes 2162720 | tf_op jit(solution)/shard_map/ppermute | solution.py:863
  235.5 12.3 %collective-permute-done.20.refs_0_ = bf16[128,2048]{1,0:T(8,128)(2,1)S(1)} collective-permute-done((bf16[128,2048]{1,0:T(8,128)(2,1)S(1)}, bf16[128,2048]{1,0:T(8,128)(2,1)S(1)}, u32[]{:S(2)}, u32[]{:S(2)}) %collective-permute-start.20) | collective-permute-done | bytes 524320 | tf_op jit(solution)/shard_map/ppermute | solution.py:838
  254.7 10.9 %collective-permute-done.22.refs_0_ = bf16[128,2048]{1,0:T(8,128)(2,1)S(1)} collective-permute-done((bf16[128,2048]{1,0:T(8,128)(2,1)S(1)}, bf16[128,2048]{1,0:T(8,128)(2,1)S(1)}, u32[]{:S(2)}, u32[]{:S(2)}) %collective-permute-start.22) | collective-permute-done | bytes 524320 | tf_op jit(solution)/shard_map/ppermute | solution.py:838
  272.0 4.9 collective-permute-done.29.refs_4_.refs_2_.refs_10_
  280.1 10.2 %ffn_step.5 = (bf16[704,1024]{1,0:T(8,128)(2,1)}, bf16[704,1024]{1,0:T(8,128)(2,1)}, bf16[704,1024]{1,0:T(8,128)(2,1)}, bf16[8,128,2048]{2,1,0:T(8,128)(2,1)}, bf16[128,2048]{1,0:T(8,128)(2,1)}) custom-call(s32[1]{0:T(128)} %get-tuple-element.223.member_ref, bf16[128,2048]{1,0:T(8,128)(2,1)} %copy-done.26, bf16[128,2048]{1,0:T(8,128)(2,1)} %bitcast.73.refs_1_.refs_8_, ...), custom_call_target="tpu_custom_call" | custom-call | flops 1 | bytes 1 | tf_op jit(solution)/shard_map/ffn_step/pallas_call | solution.py:597
  293.7 5.7 collective-permute-done.33.refs_4_.refs_2_.refs_12_
  301.4 12.3 %ffn_step.6 = (bf16[704,1024]{1,0:T(8,128)(2,1)}, bf16[704,1024]{1,0:T(8,128)(2,1)}, bf16[704,1024]{1,0:T(8,128)(2,1)}, bf16[8,128,2048]{2,1,0:T(8,128)(2,1)}, bf16[256,2048]{1,0:T(8,128)(2,1)}) custom-call(s32[2]{0:T(128)} %get-tuple-element.222.member_ref, ...), custom_call_target="tpu_custom_call", output_to_operand_aliasing={{0}: (9, {}), {1}: (10, {}), {2}: (11, {}), {3}: (12, {})} | custom-call | flops 1 | bytes 1 | tf_op jit(solution)/shard_map/ffn_step/pallas_call | solution.py:597
  316.3 5.5 collective-permute-done.37.refs_4_.refs_2_.refs_14_
  323.8 12.3 %ffn_step.7 = (bf16[704,1024]{1,0:T(8,128)(2,1)}, bf16[704,1024]{1,0:T(8,128)(2,1)}, bf16[704,1024]{1,0:T(8,128)(2,1)}, bf16[8,128,2048]{2,1,0:T(8,128)(2,1)}, bf16[256,2048]{1,0:T(8,128)(2,1)}) custom-call(s32[2]{0:T(128)} %get-tuple-element.221.member_ref, ...), custom_call_target="tpu_custom_call", output_to_operand_aliasing={{0}: (9, {}), {1}: (10, {}), {2}: (11, {}), {3}: (12, {})} | custom-call | flops 1 | bytes 1 | tf_op jit(solution)/shard_map/ffn_step/pallas_call | solution.py:597
  338.0 12.2 %ffn_step.8 = (bf16[704,1024]{1,0:T(8,128)(2,1)}, bf16[704,1024]{1,0:T(8,128)(2,1)}, bf16[704,1024]{1,0:T(8,128)(2,1)}, bf16[8,128,2048]{2,1,0:T(8,128)(2,1)}, bf16[256,2048]{1,0:T(8,128)(2,1)}) custom-call(s32[2]{0:T(128)} %get-tuple-element.220.member_ref, ...), custom_call_target="tpu_custom_call", output_to_operand_aliasing={{0}: (9, {}), {1}: (10, {}), {2}: (11, {}), {3}: (12, {})} | custom-call | flops 1 | bytes 1 | tf_op jit(solution)/shard_map/ffn_step/pallas_call | solution.py:597
  355.2 10.2 %ffn_step.9 = (bf16[704,1024]{1,0:T(8,128)(2,1)}, bf16[704,1024]{1,0:T(8,128)(2,1)}, bf16[704,1024]{1,0:T(8,128)(2,1)}, bf16[8,128,2048]{2,1,0:T(8,128)(2,1)}, bf16[128,2048]{1,0:T(8,128)(2,1)}) custom-call(s32[1]{0:T(128)} %get-tuple-element.224.member_ref, ...), custom_call_target="tpu_custom_call", output_to_operand_aliasing={{0}: (7, {}), {1}: (8, {}), {2}: (9, {}), {3}: (10, {})} | custom-call | flops 1 | bytes 1 | tf_op jit(solution)/shard_map/ffn_step/pallas_call | solution.py:597
  367.1 14.5 %ffn_grads.1 = (bf16[528,2048]{1,0:T(8,128)(2,1)}, bf16[528,2048]{1,0:T(8,128)(2,1)}, bf16[528,2048]{1,0:T(8,128)(2,1)}, bf16[528,2048]{1,0:T(8,128)(2,1)}) custom-call(bf16[704,1024]{1,0:T(8,128)(2,1)} %after.61.at_ref, bf16[704,1024]{1,0:T(8,128)(2,1)} %get-tuple-element.103.ut_ref, bf16[704,1024]{1,0:T(8,128)(2,1)} %get-tuple-element.104.ht_ref, ...), custom_call_target="tpu_custom_call" | custom-call | flops 1 | bytes 1 | tf_op jit(solution)/shard_map/ffn_grads/pallas_call | solution.py:645
  388.6 12.3 %collective-permute-done.44.refs_2_.refs_0_ = bf16[128,2048]{1,0:T(8,128)(2,1)S(1)} collective-permute-done((bf16[128,2048]{1,0:T(8,128)(2,1)S(1)}, bf16[128,2048]{1,0:T(8,128)(2,1)S(1)}, u32[]{:S(2)}, u32[]{:S(2)}) %collective-permute-start.44) | collective-permute-done | bytes 524320 | tf_op jit(solution)/shard_map/ppermute | solution.py:840
  409.5 11.6 %collective-permute-done.46.refs_1_.refs_0_ = bf16[128,2048]{1,0:T(8,128)(2,1)} collective-permute-done((bf16[128,2048]{1,0:T(8,128)(2,1)S(1)}, bf16[128,2048]{1,0:T(8,128)(2,1)}, u32[]{:S(2)}, u32[]{:S(2)}) %collective-permute-start.46) | collective-permute-done | bytes 524320 | tf_op jit(solution)/shard_map/ppermute | solution.py:840
  425.3 3.8 add_convert_fusion.1
  430.6 5.8 collective-permute-done.47
  442.7 12.7 %collective-permute-done.49.refs_1_.refs_3_ = bf16[128,2048]{1,0:T(8,128)(2,1)S(1)} collective-permute-done((bf16[128,2048]{1,0:T(8,128)(2,1)}, bf16[128,2048]{1,0:T(8,128)(2,1)S(1)}, u32[]{:S(2)}, u32[]{:S(2)}) %collective-permute-start.49) | collective-permute-done | bytes 524320 | tf_op jit(solution)/shard_map/ppermute | solution.py:810
  460.6 23.3 %collective-permute-done.51.refs_1_.refs_5_ = bf16[128,2048]{1,0:T(8,128)(2,1)} collective-permute-done((bf16[128,2048]{1,0:T(8,128)(2,1)S(1)}, bf16[128,2048]{1,0:T(8,128)(2,1)}, u32[]{:S(2)}, u32[]{:S(2)}) %collective-permute-start.51) | collective-permute-done | bytes 524320 | tf_op jit(solution)/shard_map/ppermute | solution.py:810
  484.7 4.9 collective-permute-start.52
  489.6 18.6 %collective-permute-done.54.refs_2_.refs_7_ = bf16[128,2048]{1,0:T(8,128)(2,1)} collective-permute-done((bf16[128,2048]{1,0:T(8,128)(2,1)}, bf16[128,2048]{1,0:T(8,128)(2,1)}, u32[]{:S(2)}, u32[]{:S(2)}) %collective-permute-start.54) | collective-permute-done | bytes 524320 | tf_op jit(solution)/shard_map/ppermute | solution.py:810
  513.9 14.0 %collective-permute-done.55.refs_1_ = bf16[128,2048]{1,0:T(8,128)(2,1)S(1)} collective-permute-done((bf16[128,2048]{1,0:T(8,128)(2,1)}, bf16[128,2048]{1,0:T(8,128)(2,1)S(1)}, u32[]{:S(2)}, u32[]{:S(2)}) %collective-permute-start.55) | collective-permute-done | bytes 524320 | tf_op jit(solution)/shard_map/ppermute | solution.py:810
  536.7 3.6 collective-permute-done.56
  540.4 3.8 collective-permute-done.57
  550.2 5.2 all-to-all-start.2
  558.9 37.5 %chain_backward.1 = (bf16[1024,1152]{1,0:T(8,128)(2,1)}, f32[2,64,128]{2,1,0:T(8,128)}, f32[64,384]{1,0:T(8,128)}) custom-call(s32[8]{0:T(128)} %compare_select_fusion.7.idx_ref, s32[5]{0:T(128)} %pad_add_fusion.docs_ref, bf16[1024,768]{1,0:T(8,128)(2,1)} %get-tuple-element.77.x_ref, f32[1024,256]{1,0:T(8,128)} %subtract_multiply_fusion.d_ref, ...), custom_call_target="tpu_custom_call" | custom-call | flops 1 | bytes 1 | tf_op jit(solution)/shard_map/chain_backward/pallas_call | solution.py:423
  599.2 4.2 all-to-all-done.2.refs_1_.refs_0_
  605.9 14.0 %proj_grads.1 = (bf16[320,2048]{1,0:T(8,128)(2,1)}, bf16[320,2048]{1,0:T(8,128)(2,1)}, bf16[320,2048]{1,0:T(8,128)(2,1)}, bf16[320,2048]{1,0:T(8,128)(2,1)}, f32[8,2048]{1,0:T(8,128)}, /*index=5*/f32[8,2048]{1,0:T(8,128)}) custom-call(bf16[1024,1152]{1,0:T(8,128)(2,1)} %after.75.d_ref.refs_0_, bf16[1024,2048]{1,0:T(8,128)(2,1)} %get-tuple-element.75.x_ref, ...), custom_call_target="tpu_custom_call" | custom-call | flops 1 | bytes 1 | tf_op jit(solution)/shard_map/proj_grads/pallas_call | solution.py:697
  620.7 9.6 %convolution_convert_fusion = bf16[1024,2048]{1,0:T(8,128)(2,1)} fusion(bf16[1024,1152]{1,0:T(8,128)(2,1)} %after.76, bf16[1152,2048]{1,0:T(8,128)(2,1)} %get-tuple-element.168.w_ref), kind=kOutput, calls=%fused_computation.2 | convolution fusion | flops 4833935360 | bytes 11272192 | tf_op jit(solution)/shard_map/dot_general | solution.py:18
  638.1 4.2 collective-permute-done.67
  643.0 4.7 collective-permute-done.60.refs_0_
  658.7 4.0 join_features.2
  662.7 3.6 collective-permute-done.64.refs_2_.refs_0_
  672.4 12.1 %collective-permute-done.65.refs_0_ = bf16[128,2048]{1,0:T(8,128)(2,1)S(1)} collective-permute-done((bf16[128,2048]{1,0:T(8,128)(2,1)}, bf16[128,2048]{1,0:T(8,128)(2,1)S(1)}, u32[]{:S(2)}, u32[]{:S(2)}) %collective-permute-start.65) | collective-permute-done | bytes 524320 | tf_op jit(solution)/shard_map/ppermute | solution.py:838
  694.3 4.4 all-to-all-start.3
  698.7 13.4 %collective-permute-done.70 = bf16[128,2048]{1,0:T(8,128)(2,1)S(1)} collective-permute-done((bf16[128,2048]{1,0:T(8,128)(2,1)S(1)}, bf16[128,2048]{1,0:T(8,128)(2,1)S(1)}, u32[]{:S(2)}, u32[]{:S(2)}) %collective-permute-start.70) | collective-permute-done | bytes 524320 | tf_op jit(solution)/shard_map/ppermute | solution.py:838
  714.7 4.2 all-gather.3.cloned.1.call-done
  (464 shorter events, 227.3 us)
Async XLA Ops:
  9.5 40.8 %all-to-all-start = ((bf16[8,192,256]{2,1,0:T(8,128)(2,1)}), bf16[8,192,256]{2,1,0:T(8,128)(2,1)S(1)}, u32[]{:S(2)}, u32[]{:S(2)}) async-start(bf16[8,192,256]{2,1,0:T(8,128)(2,1)} %cut_features.3), calls=%async_computation | async-start | bytes 1572864 | tf_op jit(solution)/shard_map/all_to_all | solution.py:942
  16.8 26.3 %collective-permute-start.1 = (bf16[128,2048]{1,0:T(8,128)(2,1)S(1)}, bf16[128,2048]{1,0:T(8,128)(2,1)S(1)}, u32[]{:S(2)}, u32[]{:S(2)}) collective-permute-start(bf16[128,2048]{1,0:T(8,128)(2,1)S(1)} %bitcast.238), channel_id=1, source_target_pairs={{0,4},{8,0},{16,8},{24,16},{28,24},{20,28},{12,20},{4,12},{1,5},{9... | collective-permute-start | bytes 1572872 | tf_op jit(solution)/shard_map/ppermute | solution.py:810
  18.8 24.3 %collective-permute-start = (bf16[128,2048]{1,0:T(8,128)(2,1)S(1)}, bf16[128,2048]{1,0:T(8,128)(2,1)S(1)}, u32[]{:S(2)}, u32[]{:S(2)}) collective-permute-start(bf16[128,2048]{1,0:T(8,128)(2,1)S(1)} %bitcast.239), channel_id=1, source_target_pairs={{0,8},{8,16},{16,24},{24,28},{28,20},{20,12},{12,4},{4,0},{1,9},{9... | collective-permute-start | bytes 1572872 | tf_op jit(solution)/shard_map/ppermute | solution.py:810
  44.7 18.2 %collective-permute-start.2 = (bf16[128,2048]{1,0:T(8,128)(2,1)}, bf16[128,2048]{1,0:T(8,128)(2,1)}, u32[]{:S(2)}, u32[]{:S(2)}) collective-permute-start(bf16[128,2048]{1,0:T(8,128)(2,1)} %after.43.refs_1_.refs_2_), channel_id=1, source_target_pairs={{0,8},{8,16},{16,24},{24,28},{28,20},{20,12},{12,4},{4,0},{1,9},{9... | collective-permute-start | bytes 1572872 | tf_op jit(solution)/shard_map/ppermute | solution.py:810
  52.5 18.0 %collective-permute-start.7 = (bf16[192,2048]{1,0:T(8,128)(2,1)S(1)}, bf16[192,2048]{1,0:T(8,128)(2,1)S(1)}, u32[]{:S(2)}, u32[]{:S(2)}) collective-permute-start(bf16[192,2048]{1,0:T(8,128)(2,1)S(1)} %bitcast.240), channel_id=1, source_target_pairs={{0,2},{1,3},{2,0},{3,1},{4,6},{5,7},{6,4},{7,5},{8,10},{9,11},{10,... | collective-permute-start | bytes 2359304 | tf_op jit(solution)/shard_map/ppermute | solution.py:863
  56.2 23.7 %collective-permute-start.9 = (bf16[192,2048]{1,0:T(8,128)(2,1)S(1)}, bf16[192,2048]{1,0:T(8,128)(2,1)S(1)}, u32[]{:S(2)}, u32[]{:S(2)}) collective-permute-start(bf16[192,2048]{1,0:T(8,128)(2,1)S(1)} %bitcast.241), channel_id=1, source_target_pairs={{0,1},{1,0},{2,3},{3,2},{4,5},{5,4},{6,7},{7,6},{8,9},{9,8},{10,11... | collective-permute-start | bytes 2359304 | tf_op jit(solution)/shard_map/ppermute | solution.py:863
  103.5 66.1 %all-to-all-start.1 = ((bf16[8,656,256]{2,1,0:T(8,128)(2,1)}), bf16[8,656,256]{2,1,0:T(8,128)(2,1)S(1)}, u32[]{:S(2)}, u32[]{:S(2)}) async-start(bf16[8,656,256]{2,1,0:T(8,128)(2,1)} %after.48), calls=%async_computation.1 | async-start | bytes 5373952 | tf_op jit(solution)/shard_map/all_to_all | solution.py:942
  108.8 494.7 %reduce-scatter.2.cloned.1.call-start = ((), (), s32[]{:S(2)}) async-start(), calls=%async_computation.5 | async-start | bytes 4718592 | tf_op jit(solution)/shard_map/reduce_scatter | solution.py:1194
  170.7 15.1 %collective-permute-start.11 = (bf16[128,2048]{1,0:T(8,128)(2,1)}, bf16[128,2048]{1,0:T(8,128)(2,1)}, u32[]{:S(2)}, u32[]{:S(2)}) collective-permute-start(bf16[128,2048]{1,0:T(8,128)(2,1)} %bitcast.120), channel_id=1, source_target_pairs={{0,2},{1,3},{2,0},{3,1},{4,6},{5,7},{6,4},{7,5},{8,10},{9,11},{10,... | collective-permute-start | bytes 1572872 | tf_op jit(solution)/shard_map/ppermute | solution.py:863
  179.1 50.6 %collective-permute-start.23 = (bf16[528,2048]{1,0:T(8,128)(2,1)}, bf16[528,2048]{1,0:T(8,128)(2,1)}, u32[]{:S(2)}, u32[]{:S(2)}) collective-permute-start(bf16[528,2048]{1,0:T(8,128)(2,1)} %bitcast.124.refs_2_.refs_4_), channel_id=1, source_target_pairs={{0,2},{1,3},{2,0},{3,1},{4,6},{5,7},{6,4},{7,5},{8,10},{9,11},{10,... | collective-permute-start | bytes 6488072 | tf_op jit(solution)/shard_map/ppermute | solution.py:863
  212.1 17.6 %collective-permute-start.18 = (bf16[128,2048]{1,0:T(8,128)(2,1)S(1)}, bf16[128,2048]{1,0:T(8,128)(2,1)S(1)}, u32[]{:S(2)}, u32[]{:S(2)}) collective-permute-start(bf16[128,2048]{1,0:T(8,128)(2,1)S(1)} %get-tuple-element.150), channel_id=1, source_target_pairs={{0,8},{8,16},{16,24},{24,28},{28,20},{20,12},{12,4},{4,0},{1,9},{9... | collective-permute-start | bytes 1572872 | tf_op jit(solution)/shard_map/ppermute | solution.py:838
  213.3 16.4 %collective-permute-start.19 = (bf16[128,2048]{1,0:T(8,128)(2,1)S(1)}, bf16[128,2048]{1,0:T(8,128)(2,1)S(1)}, u32[]{:S(2)}, u32[]{:S(2)}) collective-permute-start(bf16[128,2048]{1,0:T(8,128)(2,1)S(1)} %get-tuple-element.151), channel_id=1, source_target_pairs={{0,4},{8,0},{16,8},{24,16},{28,24},{20,28},{12,20},{4,12},{1,5},{9... | collective-permute-start | bytes 1572872 | tf_op jit(solution)/shard_map/ppermute | solution.py:840
  229.8 35.9 %collective-permute-start.24 = (bf16[528,2048]{1,0:T(8,128)(2,1)}, bf16[528,2048]{1,0:T(8,128)(2,1)S(1)}, u32[]{:S(2)}, u32[]{:S(2)}) collective-permute-start(bf16[528,2048]{1,0:T(8,128)(2,1)} %collective-permute-done.23.refs_4_.refs_6_), channel_id=1, source_target_pairs={{0,1},{1,0},{2,3},{3,2},{4,5},{5,4},{6,7},{7,6},{8,9},{9,8},{10,11... | collective-permute-start | bytes 6488072 | tf_op jit(solution)/shard_map/ppermute | solution.py:863
  235.3 44.7 %collective-permute-start.26 = (bf16[528,2048]{1,0:T(8,128)(2,1)}, bf16[528,2048]{1,0:T(8,128)(2,1)}, u32[]{:S(2)}, u32[]{:S(2)}) collective-permute-start(bf16[528,2048]{1,0:T(8,128)(2,1)} %bitcast.124.refs_2_.refs_4_), channel_id=1, source_target_pairs={{0,1},{1,0},{2,3},{3,2},{4,5},{5,4},{6,7},{7,6},{8,9},{9,8},{10,11... | collective-permute-start | bytes 6488072 | tf_op jit(solution)/shard_map/ppermute | solution.py:863
  250.8 14.9 %collective-permute-start.22 = (bf16[128,2048]{1,0:T(8,128)(2,1)S(1)}, bf16[128,2048]{1,0:T(8,128)(2,1)S(1)}, u32[]{:S(2)}, u32[]{:S(2)}) collective-permute-start(bf16[128,2048]{1,0:T(8,128)(2,1)S(1)} %add_convert_fusion.15), channel_id=1, source_target_pairs={{0,8},{8,16},{16,24},{24,28},{28,20},{20,12},{12,4},{4,0},{1,9},{9... | collective-permute-start | bytes 1572872 | tf_op jit(solution)/shard_map/ppermute | solution.py:838
  252.7 24.3 %collective-permute-start.29 = (bf16[128,2048]{1,0:T(8,128)(2,1)}, bf16[128,2048]{1,0:T(8,128)(2,1)}, u32[]{:S(2)}, u32[]{:S(2)}) collective-permute-start(bf16[128,2048]{1,0:T(8,128)(2,1)} %bitcast.73.refs_1_.refs_8_), channel_id=1, source_target_pairs={{0,8},{8,16},{16,24},{24,28},{28,20},{20,12},{12,4},{4,0},{1,9},{9... | collective-permute-start | bytes 1572872 | tf_op jit(solution)/shard_map/ppermute | solution.py:810
  254.4 24.4 %collective-permute-start.28 = (bf16[128,2048]{1,0:T(8,128)(2,1)}, bf16[128,2048]{1,0:T(8,128)(2,1)}, u32[]{:S(2)}, u32[]{:S(2)}) collective-permute-start(bf16[128,2048]{1,0:T(8,128)(2,1)} %bitcast.73.refs_1_.refs_8_), channel_id=1, source_target_pairs={{0,4},{8,0},{16,8},{24,16},{28,24},{20,28},{12,20},{4,12},{1,5},{9... | collective-permute-start | bytes 1572872 | tf_op jit(solution)/shard_map/ppermute | solution.py:810
  270.0 20.3 %collective-permute-start.27 = (bf16[128,2048]{1,0:T(8,128)(2,1)S(1)}, bf16[128,2048]{1,0:T(8,128)(2,1)}, u32[]{:S(2)}, u32[]{:S(2)}) collective-permute-start(bf16[128,2048]{1,0:T(8,128)(2,1)S(1)} %multiply_convert_fusion.refs_0_), channel_id=1, source_target_pairs={{0,4},{8,0},{16,8},{24,16},{28,24},{20,28},{12,20},{4,12},{1,5},{9... | collective-permute-start | bytes 1572872 | tf_op jit(solution)/shard_map/ppermute | solution.py:810
  271.8 20.3 %collective-permute-start.25 = (bf16[128,2048]{1,0:T(8,128)(2,1)S(1)}, bf16[128,2048]{1,0:T(8,128)(2,1)S(1)}, u32[]{:S(2)}, u32[]{:S(2)}) collective-permute-start(bf16[128,2048]{1,0:T(8,128)(2,1)S(1)} %multiply_convert_fusion.refs_0_), channel_id=1, source_target_pairs={{0,8},{8,16},{16,24},{24,28},{28,20},{20,12},{12,4},{4,0},{1,9},{9... | collective-permute-start | bytes 1572872 | tf_op jit(solution)/shard_map/ppermute | solution.py:810
  277.0 22.4 %collective-permute-start.33 = (bf16[128,2048]{1,0:T(8,128)(2,1)}, bf16[128,2048]{1,0:T(8,128)(2,1)S(1)}, u32[]{:S(2)}, u32[]{:S(2)}) collective-permute-start(bf16[128,2048]{1,0:T(8,128)(2,1)} %collective-permute-done.29.refs_4_.refs_2_.refs_10_), channel_id=1, source_target_pairs={{0,8},{8,16},{16,24},{24,28},{28,20},{20,12},{12,4},{4,0},{1,9},{9... | collective-permute-start | bytes 1572872 | tf_op jit(solution)/shard_map/ppermute | solution.py:810
  278.8 22.4 %collective-permute-start.32 = (bf16[128,2048]{1,0:T(8,128)(2,1)}, bf16[128,2048]{1,0:T(8,128)(2,1)S(1)}, u32[]{:S(2)}, u32[]{:S(2)}) collective-permute-start(bf16[128,2048]{1,0:T(8,128)(2,1)} %collective-permute-done.28.refs_3_.refs_11_), channel_id=1, source_target_pairs={{0,4},{8,0},{16,8},{24,16},{28,24},{20,28},{12,20},{4,12},{1,5},{9... | collective-permute-start | bytes 1572872 | tf_op jit(solution)/shard_map/ppermute | solution.py:810
  290.3 23.4 %collective-permute-start.31 = (bf16[128,2048]{1,0:T(8,128)(2,1)}, bf16[128,2048]{1,0:T(8,128)(2,1)S(1)}, u32[]{:S(2)}, u32[]{:S(2)}) collective-permute-start(bf16[128,2048]{1,0:T(8,128)(2,1)} %collective-permute-done.27.refs_2_.refs_1_.refs_3_), channel_id=1, source_target_pairs={{0,4},{8,0},{16,8},{24,16},{28,24},{20,28},{12,20},{4,12},{1,5},{9... | collective-permute-start | bytes 1572872 | tf_op jit(solution)/shard_map/ppermute | solution.py:810
  292.8 22.7 %collective-permute-start.30 = (bf16[128,2048]{1,0:T(8,128)(2,1)}, bf16[128,2048]{1,0:T(8,128)(2,1)}, u32[]{:S(2)}, u32[]{:S(2)}) collective-permute-start(bf16[128,2048]{1,0:T(8,128)(2,1)} %after.57.refs_0_.refs_2_), channel_id=1, source_target_pairs={{0,8},{8,16},{16,24},{24,28},{28,20},{20,12},{12,4},{4,0},{1,9},{9... | collective-permute-start | bytes 1572872 | tf_op jit(solution)/shard_map/ppermute | solution.py:810
  299.3 22.5 %collective-permute-start.37 = (bf16[128,2048]{1,0:T(8,128)(2,1)S(1)}, bf16[128,2048]{1,0:T(8,128)(2,1)S(1)}, u32[]{:S(2)}, u32[]{:S(2)}) collective-permute-start(bf16[128,2048]{1,0:T(8,128)(2,1)S(1)} %collective-permute-done.33.refs_4_.refs_2_.refs_12_), channel_id=1, source_target_pairs={{0,8},{8,16},{16,24},{24,28},{28,20},{20,12},{12,4},{4,0},{1,9},{9... | collective-permute-start | bytes 1572872 | tf_op jit(solution)/shard_map/ppermute | solution.py:810
  301.2 34.9 %collective-permute-start.36 = (bf16[128,2048]{1,0:T(8,128)(2,1)S(1)}, bf16[128,2048]{1,0:T(8,128)(2,1)}, u32[]{:S(2)}, u32[]{:S(2)}) collective-permute-start(bf16[128,2048]{1,0:T(8,128)(2,1)S(1)} %collective-permute-done.32.refs_3_.refs_13_), channel_id=1, source_target_pairs={{0,4},{8,0},{16,8},{24,16},{28,24},{20,28},{12,20},{4,12},{1,5},{9... | collective-permute-start | bytes 1572872 | tf_op jit(solution)/shard_map/ppermute | solution.py:810
  313.7 22.4 %collective-permute-start.35 = (bf16[128,2048]{1,0:T(8,128)(2,1)S(1)}, bf16[128,2048]{1,0:T(8,128)(2,1)}, u32[]{:S(2)}, u32[]{:S(2)}) collective-permute-start(bf16[128,2048]{1,0:T(8,128)(2,1)S(1)} %collective-permute-done.31.refs_2_.refs_1_.refs_5_), channel_id=1, source_target_pairs={{0,4},{8,0},{16,8},{24,16},{28,24},{20,28},{12,20},{4,12},{1,5},{9... | collective-permute-start | bytes 1572872 | tf_op jit(solution)/shard_map/ppermute | solution.py:810
  315.5 20.6 %collective-permute-start.34 = (bf16[128,2048]{1,0:T(8,128)(2,1)}, bf16[128,2048]{1,0:T(8,128)(2,1)}, u32[]{:S(2)}, u32[]{:S(2)}) collective-permute-start(bf16[128,2048]{1,0:T(8,128)(2,1)} %after.58.refs_0_.refs_4_), channel_id=1, source_target_pairs={{0,8},{8,16},{16,24},{24,28},{28,20},{20,12},{12,4},{4,0},{1,9},{9... | collective-permute-start | bytes 1572872 | tf_op jit(solution)/shard_map/ppermute | solution.py:810
  321.8 30.7 %collective-permute-start.39 = (bf16[128,2048]{1,0:T(8,128)(2,1)S(1)}, bf16[128,2048]{1,0:T(8,128)(2,1)}, u32[]{:S(2)}, u32[]{:S(2)}) collective-permute-start(bf16[128,2048]{1,0:T(8,128)(2,1)S(1)} %collective-permute-done.37.refs_4_.refs_2_.refs_14_), channel_id=1, source_target_pairs={{0,8},{8,16},{16,24},{24,28},{28,20},{20,12},{12,4},{4,0},{1,9},{9... | collective-permute-start | bytes 1572872 | tf_op jit(solution)/shard_map/ppermute | solution.py:810
  336.1 18.2 %collective-permute-start.38 = (bf16[128,2048]{1,0:T(8,128)(2,1)}, bf16[128,2048]{1,0:T(8,128)(2,1)S(1)}, u32[]{:S(2)}, u32[]{:S(2)}) collective-permute-start(bf16[128,2048]{1,0:T(8,128)(2,1)} %after.59.refs_0_.refs_6_), channel_id=1, source_target_pairs={{0,8},{8,16},{16,24},{24,28},{28,20},{20,12},{12,4},{4,0},{1,9},{9... | collective-permute-start | bytes 1572872 | tf_op jit(solution)/shard_map/ppermute | solution.py:810
  352.1 29.5 %collective-permute-start.41 = (bf16[128,2048]{1,0:T(8,128)(2,1)}, bf16[128,2048]{1,0:T(8,128)(2,1)S(1)}, u32[]{:S(2)}, u32[]{:S(2)}) collective-permute-start(bf16[128,2048]{1,0:T(8,128)(2,1)} %slice.231), channel_id=1, source_target_pairs={{0,4},{8,0},{16,8},{24,16},{28,24},{20,28},{12,20},{4,12},{1,5},{9... | collective-permute-start | bytes 1572872 | tf_op jit(solution)/shard_map/ppermute | solution.py:840
  365.4 16.3 %collective-permute-start.40 = (bf16[128,2048]{1,0:T(8,128)(2,1)}, bf16[128,2048]{1,0:T(8,128)(2,1)S(1)}, u32[]{:S(2)}, u32[]{:S(2)}) collective-permute-start(bf16[128,2048]{1,0:T(8,128)(2,1)} %get-tuple-element.101.refs_1_), channel_id=1, source_target_pairs={{0,8},{8,16},{16,24},{24,28},{28,20},{20,12},{12,4},{4,0},{1,9},{9... | collective-permute-start | bytes 1572872 | tf_op jit(solution)/shard_map/ppermute | solution.py:838
  385.2 17.3 %collective-permute-start.43 = (bf16[528,2048]{1,0:T(8,128)(2,1)}, bf16[528,2048]{1,0:T(8,128)(2,1)S(1)}, u32[]{:S(2)}, u32[]{:S(2)}) collective-permute-start(bf16[528,2048]{1,0:T(8,128)(2,1)} %after.63), channel_id=1, source_target_pairs={{0,1},{1,0},{2,3},{3,2},{4,5},{5,4},{6,7},{7,6},{8,9},{9,8},{10,11... | collective-permute-start | bytes 6488072 | tf_op jit(solution)/shard_map/ppermute | solution.py:863
  386.8 14.8 %collective-permute-start.42 = (bf16[128,2048]{1,0:T(8,128)(2,1)}, bf16[128,2048]{1,0:T(8,128)(2,1)S(1)}, u32[]{:S(2)}, u32[]{:S(2)}) collective-permute-start(bf16[128,2048]{1,0:T(8,128)(2,1)} %add_convert_fusion.14.refs_1_), channel_id=1, source_target_pairs={{0,8},{8,16},{16,24},{24,28},{28,20},{20,12},{12,4},{4,0},{1,9},{9... | collective-permute-start | bytes 1572872 | tf_op jit(solution)/shard_map/ppermute | solution.py:838
  429.1 60.5 %collective-permute-start.53 = (bf16[528,2048]{1,0:T(8,128)(2,1)}, bf16[528,2048]{1,0:T(8,128)(2,1)}, u32[]{:S(2)}, u32[]{:S(2)}) collective-permute-start(bf16[528,2048]{1,0:T(8,128)(2,1)} %add_convert_fusion.1), channel_id=1, source_target_pairs={{0,2},{1,3},{2,0},{3,1},{4,6},{5,7},{6,4},{7,5},{8,10},{9,11},{10,... | collective-permute-start | bytes 6488072 | tf_op jit(solution)/shard_map/ppermute | solution.py:863
  442.2 15.6 %collective-permute-start.48 = (bf16[128,2048]{1,0:T(8,128)(2,1)}, bf16[128,2048]{1,0:T(8,128)(2,1)S(1)}, u32[]{:S(2)}, u32[]{:S(2)}) collective-permute-start(bf16[128,2048]{1,0:T(8,128)(2,1)} %fusion.95.refs_0_), channel_id=1, source_target_pairs={{0,8},{8,16},{16,24},{24,28},{28,20},{20,12},{12,4},{4,0},{1,9},{9... | collective-permute-start | bytes 1572872 | tf_op jit(solution)/shard_map/ppermute | solution.py:810
  455.4 28.5 %collective-permute-start.51 = (bf16[128,2048]{1,0:T(8,128)(2,1)S(1)}, bf16[128,2048]{1,0:T(8,128)(2,1)}, u32[]{:S(2)}, u32[]{:S(2)}) collective-permute-start(bf16[128,2048]{1,0:T(8,128)(2,1)S(1)} %collective-permute-done.49.refs_1_.refs_3_), channel_id=1, source_target_pairs={{0,4},{8,0},{16,8},{24,16},{28,24},{20,28},{12,20},{4,12},{1,5},{9... | collective-permute-start | bytes 1572872 | tf_op jit(solution)/shard_map/ppermute | solution.py:810
  458.6 25.3 %collective-permute-start.50 = (bf16[128,2048]{1,0:T(8,128)(2,1)}, bf16[128,2048]{1,0:T(8,128)(2,1)S(1)}, u32[]{:S(2)}, u32[]{:S(2)}) collective-permute-start(bf16[128,2048]{1,0:T(8,128)(2,1)} %after.70.refs_2_), channel_id=1, source_target_pairs={{0,8},{8,16},{16,24},{24,28},{28,20},{20,12},{12,4},{4,0},{1,9},{9... | collective-permute-start | bytes 1572872 | tf_op jit(solution)/shard_map/ppermute | solution.py:810
  483.9 24.3 %collective-permute-start.54 = (bf16[128,2048]{1,0:T(8,128)(2,1)}, bf16[128,2048]{1,0:T(8,128)(2,1)}, u32[]{:S(2)}, u32[]{:S(2)}) collective-permute-start(bf16[128,2048]{1,0:T(8,128)(2,1)} %collective-permute-done.51.refs_1_.refs_5_), channel_id=1, source_target_pairs={{0,4},{8,0},{16,8},{24,16},{28,24},{20,28},{12,20},{4,12},{1,5},{9... | collective-permute-start | bytes 1572872 | tf_op jit(solution)/shard_map/ppermute | solution.py:810
  484.7 24.8 %collective-permute-start.52 = (bf16[128,2048]{1,0:T(8,128)(2,1)}, bf16[128,2048]{1,0:T(8,128)(2,1)}, u32[]{:S(2)}, u32[]{:S(2)}) collective-permute-start(bf16[128,2048]{1,0:T(8,128)(2,1)} %after.71.refs_4_), channel_id=1, source_target_pairs={{0,8},{8,16},{16,24},{24,28},{28,20},{20,12},{12,4},{4,0},{1,9},{9... | collective-permute-start | bytes 1572872 | tf_op jit(solution)/shard_map/ppermute | solution.py:810
  489.6 55.4 %collective-permute-start.59 = (bf16[528,2048]{1,0:T(8,128)(2,1)}, bf16[528,2048]{1,0:T(8,128)(2,1)S(1)}, u32[]{:S(2)}, u32[]{:S(2)}) collective-permute-start(bf16[528,2048]{1,0:T(8,128)(2,1)} %get-tuple-element.113), channel_id=1, source_target_pairs={{0,1},{1,0},{2,3},{3,2},{4,5},{5,4},{6,7},{7,6},{8,9},{9,8},{10,11... | collective-permute-start | bytes 6488072 | tf_op jit(solution)/shard_map/ppermute | solution.py:863
  509.6 18.3 %collective-permute-start.55 = (bf16[128,2048]{1,0:T(8,128)(2,1)}, bf16[128,2048]{1,0:T(8,128)(2,1)S(1)}, u32[]{:S(2)}, u32[]{:S(2)}) collective-permute-start(bf16[128,2048]{1,0:T(8,128)(2,1)} %after.72.refs_6_), channel_id=1, source_target_pairs={{0,8},{8,16},{16,24},{24,28},{28,20},{20,12},{12,4},{4,0},{1,9},{9... | collective-permute-start | bytes 1572872 | tf_op jit(solution)/shard_map/ppermute | solution.py:810
  550.2 53.3 %all-to-all-start.2 = ((bf16[8,528,256]{2,1,0:T(8,128)(2,1)}), bf16[8,528,256]{2,1,0:T(8,128)(2,1)S(1)}, u32[]{:S(2)}, u32[]{:S(2)}) async-start(bf16[8,528,256]{2,1,0:T(8,128)(2,1)} %after.74), calls=%async_computation.3 | async-start | bytes 4325376 | tf_op jit(solution)/shard_map/all_to_all | solution.py:942
  555.4 163.5 %all-gather.3.cloned.1.call-start = ((), (), s32[]{:S(2)}) async-start(), calls=%async_computation.6 | async-start | bytes 1179648 | tf_op jit(solution)/shard_map/all_gather | solution.py:1229
  630.7 17.1 %collective-permute-start.61 = (bf16[320,2048]{1,0:T(8,128)(2,1)}, bf16[320,2048]{1,0:T(8,128)(2,1)S(1)}, u32[]{:S(2)}, u32[]{:S(2)}) collective-permute-start(bf16[320,2048]{1,0:T(8,128)(2,1)} %get-tuple-element.115), channel_id=1, source_target_pairs={{0,1},{1,0},{2,3},{3,2},{4,5},{5,4},{6,7},{7,6},{8,9},{9,8},{10,11... | collective-permute-start | bytes 3932168 | tf_op jit(solution)/shard_map/ppermute | solution.py:863
  657.4 30.1 %collective-permute-start.68 = (bf16[320,2048]{1,0:T(8,128)(2,1)}, bf16[320,2048]{1,0:T(8,128)(2,1)S(1)}, u32[]{:S(2)}, u32[]{:S(2)}) collective-permute-start(bf16[320,2048]{1,0:T(8,128)(2,1)} %add_convert_fusion.3), channel_id=1, source_target_pairs={{0,2},{1,3},{2,0},{3,1},{4,6},{5,7},{6,4},{7,5},{8,10},{9,11},{10,... | collective-permute-start | bytes 3932168 | tf_op jit(solution)/shard_map/ppermute | solution.py:863
  658.7 32.1 %collective-permute-start.71 = (bf16[320,2048]{1,0:T(8,128)(2,1)}, bf16[320,2048]{1,0:T(8,128)(2,1)}, u32[]{:S(2)}, u32[]{:S(2)}) collective-permute-start(bf16[320,2048]{1,0:T(8,128)(2,1)} %get-tuple-element.122), channel_id=1, source_target_pairs={{0,1},{1,0},{2,3},{3,2},{4,5},{5,4},{6,7},{7,6},{8,9},{9,8},{10,11... | collective-permute-start | bytes 3932168 | tf_op jit(solution)/shard_map/ppermute | solution.py:863
  690.1 22.1 %collective-permute-start.70 = (bf16[128,2048]{1,0:T(8,128)(2,1)S(1)}, bf16[128,2048]{1,0:T(8,128)(2,1)S(1)}, u32[]{:S(2)}, u32[]{:S(2)}) collective-permute-start(bf16[128,2048]{1,0:T(8,128)(2,1)S(1)} %add_convert_fusion.4), channel_id=1, source_target_pairs={{0,8},{8,16},{16,24},{24,28},{28,20},{20,12},{12,4},{4,0},{1,9},{9... | collective-permute-start | bytes 1572872 | tf_op jit(solution)/shard_map/ppermute | solution.py:838
  694.3 41.4 %all-to-all-start.3 = ((bf16[8,320,256]{2,1,0:T(8,128)(2,1)}), bf16[8,320,256]{2,1,0:T(8,128)(2,1)}, u32[]{:S(2)}, u32[]{:S(2)}) async-start(bf16[8,320,256]{2,1,0:T(8,128)(2,1)} %bitcast.232), calls=%async_computation.4 | async-start | bytes 2621440 | tf_op jit(solution)/shard_map/all_to_all | solution.py:942
  (104 other events, 768.7 us)
Sparse Core Ops, SparseCore 0:
  442.9 115.0 reduce-scatter.1
  672.5 46.3 all-gather.2

commit v5 on v4

--- a/solution.py
+++ b/solution.py
@@ -1099,7 +1099,7 @@
     normed, x3, logits = project(
         sum(by_slots(token_steps), ()), own["parts"], rate_rows, bias, prenorm_gain[None]
     )
-    rest_block = exchange(after(own["rest"], logits))
+    rest_block = exchange(after(own["rest"], token_steps[-1][0]))
     grad_own = cotangent[0]
 
     inner, *kept = chain_forward(slot_of_member, docs, x3, logits, gb, init, rows_tok)
@@ -1128,7 +1128,7 @@
 
 
     def ffn_corner(since):
-        ffn["parts"] = end_gather(ffn_parts)
+        ffn["parts"] = end_gather(ffn_parts[:-1] + [after(ffn_parts[-1], since)])
         return ffn["parts"][-1:]
 
     mixing = ring_scatter(
@@ -1188,15 +1188,19 @@
     )
 
     def mix_work(s, arrived):
-        return [got["across"]] if s == seq // 2 - 2 else []
+        if s == seq // 2 - 2:
+            return [got["across"]]
+        if s == seq // 2 - 1:
+            summed = end_scatter(ffn_grad, after(got["across"], arrived[0]))
+            got["summed"] = summed.reshape(3 * padded, seq, -1).transpose(1, 0, 2)
+            return [got["summed"]]
+        return []
 
     mix_steps = ring_gather(d_resid.astype(BF16), seq, mix_work)
     ffn_out = lax.psum_scatter(
-        after(kept_ffn[3], d_ffn), "seq", scatter_dimension=0, tiled=False
+        after(kept_ffn[3], mix_steps[seq // 2 - 2][0]), "seq", scatter_dimension=0, tiled=False
     )
     out_tokens = (resid + ffn_out.astype(F32)).astype(BF16)[None]
-    g_ffn = end_scatter(ffn_grad, got["across"])
-    g_ffn = after(g_ffn.reshape(3 * padded, seq, -1).transpose(1, 0, 2), mix_steps[-1][0])
     d_gated = [mm_nt(jnp.concatenate(arrived, axis=0), m_out) for arrived in mix_steps]
     d_gated = jnp.concatenate(by_slots(d_gated), axis=0)
     d_post = d_gated * gelu_val
@@ -1206,13 +1210,12 @@
     d_ohat = d_post * post_g
     sums = jnp.stack([jnp.sum(d_ohat, -1), jnp.sum(d_ohat * o_hat, -1)])
     sums = in_slots(pairwise_sum(in_order(sums), "seq", seq)) / width
-    g_ffn = exchange(after(g_ffn, sums))
+    g_ffn = exchange(after(got["summed"], sums))
     d_inner = inv_o * (d_ohat - sums[0][:, None] - o_hat * sums[1][:, None])
     d_x, d_gb, d_init = chain_backward(
         slot_of_member, docs, x3, d_inner, d_gate_pre, logits, gb, init, kept, rows_tok
     )
     w_all = jnp.concatenate(own["parts"] + [rate_rows, m_gate], axis=0)
-    d_x = after(d_x, g_ffn, ffn_out)
     *head_rows_grads, g_rates, g_gain = proj_grads(
         d_x, normed, w_all, gated, sum(by_slots(mix_steps), ()), local, head_dim
     )
@@ -1227,7 +1230,7 @@
     flat = jnp.concatenate([flat.reshape(-1), g_gain[0] / prenorm_gain, g_ffn_gain])
     flat = pairwise_sum(flat.reshape(-1, 1024), "grp", groups)
     flat_all = lax.all_gather(flat, "seq", axis=0)
-    d_x = after(d_x, g_gain)
+    d_x = after(d_x, g_gain, g_ffn)
     d_normed_part = mm(d_x, w_all).astype(BF16)
 
     def corner_work(since):
@@ -1243,7 +1246,7 @@
         return got["join"][:1]
 
     def across_work(since):
-        return [got["across"]] if plan.mixed else []
+        return [ffn_out] + ([got["across"]] if plan.mixed else [])
 
     d_normed = ring_scatter(
         by_distance(d_normed_part), seq, [corner_work, join_work, across_work]

time: 757 us -> 727 us (0.960)
  waiting for transfers between devices: 307 us -> 281 us
  starting transfers between devices: 101 us -> 90.1 us
    ppermute x28, waiting for transfers between devices: 124 us -> 88.8 us  [move(): lax.ppermute(value, 'seq', ring_pairs(size, step))]
    all_gather x1, waiting for transfers between devices: 4.22 us -> 21.3 us  [body(): flat_all = lax.all_gather(flat, 'seq', axis=0)]
    ppermute x9, waiting for transfers between devices: 29.3 us -> 45.1 us  [ring_scatter(): back = lax.ppermute(back, 'seq', ring_pairs(size, -1))]
    ppermute x28, starting transfers between devices: 42.6 us -> 30.8 us  [move(): lax.ppermute(value, 'seq', ring_pairs(size, step))]
    all_to_all x4, waiting for transfers between devices: 36.3 us -> 25.1 us  [exchange(): return lax.all_to_all(block, 'seq', 0, 0, tiled=True)]
    ppermute x12, waiting for transfers between devices: 73.3 us -> 64.9 us  [ring_scatter(): ahead = lax.ppermute(ahead, 'seq', ring_pairs(size, 1))]
    unnamed x162 -> x182, local copies, waits for them, and re-layouts: 37.8 us -> 42 us
  transfers between devices with their start and end apart: 78 -> 78, of which waited for: 42 -> 46; matrix products, arithmetic and copies ran while one was open for 14% -> 14% of each run, Pallas kernels for 19% -> 23%
where the time goes in v5:
time: 727 us; the launch traced here: 714 us
  waiting for transfers between devices  281 us (39%)
  Pallas kernels  172 us (24%)
  starting transfers between devices  90.1 us (12%)
  local copies, waits for them, and re-layouts  70.3 us (10%)
  other arithmetic  64.2 us (9%)
  matrix products  21.7 us (3%)
  between operations  15.6 us (2%)
    ppermute x28, waiting for transfers between devices, move(): lax.ppermute(value, 'seq', ring_pairs(size, step))  88.8 us
    ppermute x12, waiting for transfers between devices, ring_scatter(): ahead = lax.ppermute(ahead, 'seq', ring_pairs(size, 1))  64.9 us
    pallas_call x5, Pallas kernels, ffn_step(): pl.pallas_call(partial(ffn_kernel, count, len(weights), len(kept)), grid_...  57.4 us
    ppermute x9, waiting for transfers between devices, ring_scatter(): back = lax.ppermute(back, 'seq', ring_pairs(size, -1))  45.1 us
    unnamed x182, local copies, waits for them, and re-layouts  42 us
    pallas_call x1, Pallas kernels, chain_backward(): pl.pallas_call(partial(backward_kernel, heads), grid_spec=pltpu.PrefetchS...  37.5 us
    ppermute x28, starting transfers between devices, move(): lax.ppermute(value, 'seq', ring_pairs(size, step))  30.8 us
    all_to_all x4, waiting for transfers between devices, exchange(): return lax.all_to_all(block, 'seq', 0, 0, tiled=True)  25.1 us
  transfers between devices with their start and end apart: 78, of which 46 were waited for; matrix products, arithmetic and copies ran while one was open for 14% of the time, Pallas kernels for 23%

profile of v5, /device:TPU:0, one launch (start us, length us, event | category | flops | bytes accessed | tf_op | source)
XLA Modules:
  0.0 714.1 jit_solution(14777999102893622456)
XLA Ops:
  9.5 7.3 %all-to-all-start = ((bf16[8,192,256]{2,1,0:T(8,128)(2,1)}), bf16[8,192,256]{2,1,0:T(8,128)(2,1)S(1)}, u32[]{:S(2)}, u32[]{:S(2)}) async-start(bf16[8,192,256]{2,1,0:T(8,128)(2,1)} %cut_features.3), calls=%async_computation | async-start | bytes 1572864 | tf_op jit(solution)/shard_map/all_to_all | solution.py:942
  20.6 22.4 %collective-permute-done.1.refs_1_.refs_3_ = bf16[128,2048]{1,0:T(8,128)(2,1)S(1)} collective-permute-done((bf16[128,2048]{1,0:T(8,128)(2,1)S(1)}, bf16[128,2048]{1,0:T(8,128)(2,1)S(1)}, u32[]{:S(2)}, u32[]{:S(2)}) %collective-permute-start.1) | collective-permute-done | bytes 524320 | tf_op jit(solution)/shard_map/ppermute | solution.py:810
  44.6 5.7 collective-permute-start.2
  56.9 6.0 collective-permute-done.3.refs_3_.refs_5_
  65.7 4.8 collective-permute-done.7.refs_10_
  70.4 3.8 cut_features.2.refs_1_.refs_0_
  77.7 11.6 %collective-permute-done.6.refs_0_ = bf16[128,2048]{1,0:T(8,128)(2,1)S(1)} collective-permute-done((bf16[128,2048]{1,0:T(8,128)(2,1)}, bf16[128,2048]{1,0:T(8,128)(2,1)S(1)}, u32[]{:S(2)}, u32[]{:S(2)}) %collective-permute-start.6) | collective-permute-done | bytes 524320 | tf_op jit(solution)/shard_map/ppermute | solution.py:810
  91.0 5.9 all-to-all-start.1
  109.6 10.5 %project.1 = (bf16[1024,2048]{1,0:T(8,128)(2,1)}, bf16[1024,768]{1,0:T(8,128)(2,1)}, f32[1024,128]{1,0:T(8,128)}) custom-call(bf16[128,2048]{1,0:T(8,128)(2,1)} %bitcast.235, bf16[128,2048]{1,0:T(8,128)(2,1)} %after.48.refs_1_, bf16[128,2048]{1,0:T(8,128)(2,1)} %after.44.refs_1_.refs_2_, bf16[128,2048]{1,0:T(8,128)(2,1)} %copy-done.60, ...), custom_call_target="tpu_custom_call" | custom-call | flops 1 | bytes 1 | tf_op jit(solution)/shard_map/project/pallas_call | solution.py:743
  120.1 24.7 %chain_forward.1 = (f32[1024,256]{1,0:T(8,128)}, f32[64,4096]{1,0:T(8,128)}, f32[64,4096]{1,0:T(8,128)}, f32[64,4096]{1,0:T(8,128)}, f32[8,4096]{1,0:T(8,128)}, /*index=5*/f32[8,64,384]{2,1,0:T(8,128)}) custom-call(s32[8]{0:T(128)} %compare_select_fusion.7.idx_ref, s32[5]{0:T(128)} %pad_add_fusion.docs_ref, bf16[1024,768]{1,0:T(8,128)(2,1)} %get-tuple-element.76.x_ref, ...), custom_call_target="tpu_custom_call" | custom-call | flops 1 | bytes 1 | tf_op jit(solution)/shard_map/chain_forward/pallas_call | solution.py:391
  146.4 8.9 %all-to-all-done.1.refs_1_ = bf16[8,656,256]{2,1,0:T(8,128)(2,1)S(1)} async-done(((bf16[8,656,256]{2,1,0:T(8,128)(2,1)}), bf16[8,656,256]{2,1,0:T(8,128)(2,1)S(1)}, u32[]{:S(2)}, u32[]{:S(2)}) %all-to-all-start.1) | async-done | bytes 2687008 | tf_op jit(solution)/shard_map/all_to_all | solution.py:942
  162.4 3.6 collective-permute-done.14
  166.7 3.8 collective-permute-done.15
  185.3 8.7 %collective-permute-done.16.refs_0_ = bf16[128,2048]{1,0:T(8,128)(2,1)S(1)} collective-permute-done((bf16[128,2048]{1,0:T(8,128)(2,1)S(1)}, bf16[128,2048]{1,0:T(8,128)(2,1)S(1)}, u32[]{:S(2)}, u32[]{:S(2)}) %collective-permute-start.16) | collective-permute-done | bytes 524320 | tf_op jit(solution)/shard_map/ppermute | solution.py:838
  199.6 11.2 %collective-permute-done.18.refs_0_ = bf16[128,2048]{1,0:T(8,128)(2,1)S(1)} collective-permute-done((bf16[128,2048]{1,0:T(8,128)(2,1)S(1)}, bf16[128,2048]{1,0:T(8,128)(2,1)S(1)}, u32[]{:S(2)}, u32[]{:S(2)}) %collective-permute-start.18) | collective-permute-done | bytes 524320 | tf_op jit(solution)/shard_map/ppermute | solution.py:838
  216.4 10.2 %collective-permute-done.20.refs_0_ = bf16[128,2048]{1,0:T(8,128)(2,1)S(1)} collective-permute-done((bf16[128,2048]{1,0:T(8,128)(2,1)S(1)}, bf16[128,2048]{1,0:T(8,128)(2,1)S(1)}, u32[]{:S(2)}, u32[]{:S(2)}) %collective-permute-start.20) | collective-permute-done | bytes 524320 | tf_op jit(solution)/shard_map/ppermute | solution.py:838
  236.9 12.9 %collective-permute-done.22.refs_0_ = bf16[128,2048]{1,0:T(8,128)(2,1)} collective-permute-done((bf16[128,2048]{1,0:T(8,128)(2,1)}, bf16[128,2048]{1,0:T(8,128)(2,1)}, u32[]{:S(2)}, u32[]{:S(2)}) %collective-permute-start.22) | collective-permute-done | bytes 524320 | tf_op jit(solution)/shard_map/ppermute | solution.py:838
  255.2 5.7 collective-permute-done.29.refs_4_.refs_2_.refs_10_
  263.5 10.2 %ffn_step.5 = (bf16[704,1024]{1,0:T(8,128)(2,1)}, bf16[704,1024]{1,0:T(8,128)(2,1)}, bf16[704,1024]{1,0:T(8,128)(2,1)}, bf16[8,128,2048]{2,1,0:T(8,128)(2,1)}, bf16[128,2048]{1,0:T(8,128)(2,1)}) custom-call(s32[1]{0:T(128)} %get-tuple-element.222.member_ref, bf16[128,2048]{1,0:T(8,128)(2,1)} %copy-done.31, bf16[128,2048]{1,0:T(8,128)(2,1)} %bitcast.247, ...), custom_call_target="tpu_custom_call" | custom-call | flops 1 | bytes 1 | tf_op jit(solution)/shard_map/ffn_step/pallas_call | solution.py:597
  277.2 6.2 collective-permute-done.33.refs_4_.refs_2_.refs_12_
  285.8 12.3 %ffn_step.6 = (bf16[704,1024]{1,0:T(8,128)(2,1)}, bf16[704,1024]{1,0:T(8,128)(2,1)}, bf16[704,1024]{1,0:T(8,128)(2,1)}, bf16[8,128,2048]{2,1,0:T(8,128)(2,1)}, bf16[256,2048]{1,0:T(8,128)(2,1)}) custom-call(s32[2]{0:T(128)} %get-tuple-element.221.member_ref, ...), custom_call_target="tpu_custom_call", output_to_operand_aliasing={{0}: (9, {}), {1}: (10, {}), {2}: (11, {}), {3}: (12, {})} | custom-call | flops 1 | bytes 1 | tf_op jit(solution)/shard_map/ffn_step/pallas_call | solution.py:597
  300.2 5.7 collective-permute-done.37.refs_4_.refs_2_.refs_14_
  306.0 12.3 %ffn_step.7 = (bf16[704,1024]{1,0:T(8,128)(2,1)}, bf16[704,1024]{1,0:T(8,128)(2,1)}, bf16[704,1024]{1,0:T(8,128)(2,1)}, bf16[8,128,2048]{2,1,0:T(8,128)(2,1)}, bf16[256,2048]{1,0:T(8,128)(2,1)}) custom-call(s32[2]{0:T(128)} %get-tuple-element.220.member_ref, ...), custom_call_target="tpu_custom_call", output_to_operand_aliasing={{0}: (9, {}), {1}: (10, {}), {2}: (11, {}), {3}: (12, {})} | custom-call | flops 1 | bytes 1 | tf_op jit(solution)/shard_map/ffn_step/pallas_call | solution.py:597
  320.1 12.3 %ffn_step.8 = (bf16[704,1024]{1,0:T(8,128)(2,1)}, bf16[704,1024]{1,0:T(8,128)(2,1)}, bf16[704,1024]{1,0:T(8,128)(2,1)}, bf16[8,128,2048]{2,1,0:T(8,128)(2,1)}, bf16[256,2048]{1,0:T(8,128)(2,1)}) custom-call(s32[2]{0:T(128)} %get-tuple-element.219.member_ref, ...), custom_call_target="tpu_custom_call", output_to_operand_aliasing={{0}: (9, {}), {1}: (10, {}), {2}: (11, {}), {3}: (12, {})} | custom-call | flops 1 | bytes 1 | tf_op jit(solution)/shard_map/ffn_step/pallas_call | solution.py:597
  334.8 3.8 collective-permute-done.38.refs_0_
  339.4 10.2 %ffn_step.9 = (bf16[704,1024]{1,0:T(8,128)(2,1)}, bf16[704,1024]{1,0:T(8,128)(2,1)}, bf16[704,1024]{1,0:T(8,128)(2,1)}, bf16[8,128,2048]{2,1,0:T(8,128)(2,1)}, bf16[128,2048]{1,0:T(8,128)(2,1)}) custom-call(s32[1]{0:T(128)} %get-tuple-element.223.member_ref, ...), custom_call_target="tpu_custom_call", output_to_operand_aliasing={{0}: (7, {}), {1}: (8, {}), {2}: (9, {}), {3}: (10, {})} | custom-call | flops 1 | bytes 1 | tf_op jit(solution)/shard_map/ffn_step/pallas_call | solution.py:597
  349.9 14.5 %ffn_grads.1 = (bf16[528,2048]{1,0:T(8,128)(2,1)}, bf16[528,2048]{1,0:T(8,128)(2,1)}, bf16[528,2048]{1,0:T(8,128)(2,1)}, bf16[528,2048]{1,0:T(8,128)(2,1)}) custom-call(bf16[704,1024]{1,0:T(8,128)(2,1)} %after.63.at_ref, bf16[704,1024]{1,0:T(8,128)(2,1)} %get-tuple-element.103.ut_ref, bf16[704,1024]{1,0:T(8,128)(2,1)} %get-tuple-element.104.ht_ref, ...), custom_call_target="tpu_custom_call" | custom-call | flops 1 | bytes 1 | tf_op jit(solution)/shard_map/ffn_grads/pallas_call | solution.py:645
  371.4 12.3 %collective-permute-done.44.refs_2_.refs_0_ = bf16[128,2048]{1,0:T(8,128)(2,1)S(1)} collective-permute-done((bf16[128,2048]{1,0:T(8,128)(2,1)S(1)}, bf16[128,2048]{1,0:T(8,128)(2,1)S(1)}, u32[]{:S(2)}, u32[]{:S(2)}) %collective-permute-start.44) | collective-permute-done | bytes 524320 | tf_op jit(solution)/shard_map/ppermute | solution.py:840
  393.3 11.3 %collective-permute-done.46.refs_1_.refs_0_ = bf16[128,2048]{1,0:T(8,128)(2,1)} collective-permute-done((bf16[128,2048]{1,0:T(8,128)(2,1)S(1)}, bf16[128,2048]{1,0:T(8,128)(2,1)}, u32[]{:S(2)}, u32[]{:S(2)}) %collective-permute-start.46) | collective-permute-done | bytes 524320 | tf_op jit(solution)/shard_map/ppermute | solution.py:840
  408.8 3.7 add_convert_fusion.1
  414.1 6.6 collective-permute-done.47
  427.3 9.8 %collective-permute-done.49.refs_1_.refs_3_ = bf16[128,2048]{1,0:T(8,128)(2,1)} collective-permute-done((bf16[128,2048]{1,0:T(8,128)(2,1)S(1)}, bf16[128,2048]{1,0:T(8,128)(2,1)}, u32[]{:S(2)}, u32[]{:S(2)}) %collective-permute-start.49) | collective-permute-done | bytes 524320 | tf_op jit(solution)/shard_map/ppermute | solution.py:810
  439.1 10.1 %collective-permute-done.51.refs_1_.refs_5_ = bf16[128,2048]{1,0:T(8,128)(2,1)} collective-permute-done((bf16[128,2048]{1,0:T(8,128)(2,1)}, bf16[128,2048]{1,0:T(8,128)(2,1)}, u32[]{:S(2)}, u32[]{:S(2)}) %collective-permute-start.51) | collective-permute-done | bytes 524320 | tf_op jit(solution)/shard_map/ppermute | solution.py:810
  453.6 6.0 collective-permute-done.53.refs_1_.refs_0_
  462.7 3.5 add_convert_fusion
  467.7 4.7 collective-permute-done.55.refs_0_
  494.8 4.2 all-to-all-start.2
  503.0 37.5 %chain_backward.1 = (bf16[1024,1152]{1,0:T(8,128)(2,1)}, f32[2,64,128]{2,1,0:T(8,128)}, f32[64,384]{1,0:T(8,128)}) custom-call(s32[8]{0:T(128)} %compare_select_fusion.7.idx_ref, s32[5]{0:T(128)} %pad_add_fusion.docs_ref, bf16[1024,768]{1,0:T(8,128)(2,1)} %get-tuple-element.76.x_ref, f32[1024,256]{1,0:T(8,128)} %subtract_multiply_fusion.d_ref, ...), custom_call_target="tpu_custom_call" | custom-call | flops 1 | bytes 1 | tf_op jit(solution)/shard_map/chain_backward/pallas_call | solution.py:423
  540.5 14.2 %proj_grads.1 = (bf16[320,2048]{1,0:T(8,128)(2,1)}, bf16[320,2048]{1,0:T(8,128)(2,1)}, bf16[320,2048]{1,0:T(8,128)(2,1)}, bf16[320,2048]{1,0:T(8,128)(2,1)}, f32[8,2048]{1,0:T(8,128)}, /*index=5*/f32[8,2048]{1,0:T(8,128)}) custom-call(bf16[1024,1152]{1,0:T(8,128)(2,1)} %get-tuple-element.113.d_ref.refs_0_, bf16[1024,2048]{1,0:T(8,128)(2,1)} %get-tuple-element.75.x_ref, ...), custom_call_target="tpu_custom_call" | custom-call | flops 1 | bytes 1 | tf_op jit(solution)/shard_map/proj_grads/pallas_call | solution.py:697
  559.4 16.2 %all-to-all-done.2.refs_2_.refs_0_ = bf16[8,528,256]{2,1,0:T(8,128)(2,1)S(1)} async-done(((bf16[8,528,256]{2,1,0:T(8,128)(2,1)}), bf16[8,528,256]{2,1,0:T(8,128)(2,1)S(1)}, u32[]{:S(2)}, u32[]{:S(2)}) %all-to-all-start.2) | async-done | bytes 2162720 | tf_op jit(solution)/shard_map/all_to_all | solution.py:942
  576.9 8.2 %convolution_convert_fusion = bf16[1024,2048]{1,0:T(8,128)(2,1)S(1)} fusion(bf16[1024,1152]{1,0:T(8,128)(2,1)} %after.78, bf16[1152,2048]{1,0:T(8,128)(2,1)} %get-tuple-element.167.w_ref), kind=kOutput, calls=%fused_computation.2 | convolution fusion | flops 4833935360 | bytes 11272192 | tf_op jit(solution)/shard_map/dot_general | solution.py:18
  591.5 4.0 collective-permute-done.67
  608.5 4.0 join_features.2
  612.5 18.8 %collective-permute-done.64.refs_2_.refs_0_ = bf16[128,2048]{1,0:T(8,128)(2,1)S(1)} collective-permute-done((bf16[128,2048]{1,0:T(8,128)(2,1)}, bf16[128,2048]{1,0:T(8,128)(2,1)S(1)}, u32[]{:S(2)}, u32[]{:S(2)}) %collective-permute-start.64) | collective-permute-done | bytes 524320 | tf_op jit(solution)/shard_map/ppermute | solution.py:840
  637.2 8.8 %collective-permute-done.65.refs_0_ = bf16[128,2048]{1,0:T(8,128)(2,1)S(1)} collective-permute-done((bf16[128,2048]{1,0:T(8,128)(2,1)}, bf16[128,2048]{1,0:T(8,128)(2,1)S(1)}, u32[]{:S(2)}, u32[]{:S(2)}) %collective-permute-start.65) | collective-permute-done | bytes 524320 | tf_op jit(solution)/shard_map/ppermute | solution.py:838
  653.6 5.3 all-to-all-start.3
  659.8 4.5 collective-permute-done.70
  666.9 21.3 %all-gather.3.cloned.1.call-done = f32[256,1024]{1,0:T(8,128)} async-done(((f32[32,1024]{1,0:T(8,128)}), f32[256,1024]{1,0:T(8,128)}) %all-gather.3.cloned.1.call-update) | async-done | bytes 1048592 | tf_op jit(solution)/shard_map/all_gather | solution.py:1232
  (486 shorter events, 228.5 us)
Async XLA Ops:
  9.5 40.8 %all-to-all-start = ((bf16[8,192,256]{2,1,0:T(8,128)(2,1)}), bf16[8,192,256]{2,1,0:T(8,128)(2,1)S(1)}, u32[]{:S(2)}, u32[]{:S(2)}) async-start(bf16[8,192,256]{2,1,0:T(8,128)(2,1)} %cut_features.3), calls=%async_computation | async-start | bytes 1572864 | tf_op jit(solution)/shard_map/all_to_all | solution.py:942
  16.8 26.3 %collective-permute-start.1 = (bf16[128,2048]{1,0:T(8,128)(2,1)S(1)}, bf16[128,2048]{1,0:T(8,128)(2,1)S(1)}, u32[]{:S(2)}, u32[]{:S(2)}) collective-permute-start(bf16[128,2048]{1,0:T(8,128)(2,1)S(1)} %bitcast.236), channel_id=1, source_target_pairs={{0,4},{8,0},{16,8},{24,16},{28,24},{20,28},{12,20},{4,12},{1,5},{9... | collective-permute-start | bytes 1572872 | tf_op jit(solution)/shard_map/ppermute | solution.py:810
  18.8 24.3 %collective-permute-start = (bf16[128,2048]{1,0:T(8,128)(2,1)S(1)}, bf16[128,2048]{1,0:T(8,128)(2,1)S(1)}, u32[]{:S(2)}, u32[]{:S(2)}) collective-permute-start(bf16[128,2048]{1,0:T(8,128)(2,1)S(1)} %bitcast.237), channel_id=1, source_target_pairs={{0,8},{8,16},{16,24},{24,28},{28,20},{20,12},{12,4},{4,0},{1,9},{9... | collective-permute-start | bytes 1572872 | tf_op jit(solution)/shard_map/ppermute | solution.py:810
  44.6 18.5 %collective-permute-start.2 = (bf16[128,2048]{1,0:T(8,128)(2,1)}, bf16[128,2048]{1,0:T(8,128)(2,1)S(1)}, u32[]{:S(2)}, u32[]{:S(2)}) collective-permute-start(bf16[128,2048]{1,0:T(8,128)(2,1)} %after.44.refs_1_.refs_2_), channel_id=1, source_target_pairs={{0,8},{8,16},{16,24},{24,28},{28,20},{20,12},{12,4},{4,0},{1,9},{9... | collective-permute-start | bytes 1572872 | tf_op jit(solution)/shard_map/ppermute | solution.py:810
  52.5 18.0 %collective-permute-start.7 = (bf16[192,2048]{1,0:T(8,128)(2,1)S(1)}, bf16[192,2048]{1,0:T(8,128)(2,1)S(1)}, u32[]{:S(2)}, u32[]{:S(2)}) collective-permute-start(bf16[192,2048]{1,0:T(8,128)(2,1)S(1)} %bitcast.238), channel_id=1, source_target_pairs={{0,2},{1,3},{2,0},{3,1},{4,6},{5,7},{6,4},{7,5},{8,10},{9,11},{10,... | collective-permute-start | bytes 2359304 | tf_op jit(solution)/shard_map/ppermute | solution.py:863
  70.4 18.9 %collective-permute-start.8 = (bf16[192,2048]{1,0:T(8,128)(2,1)S(1)}, bf16[192,2048]{1,0:T(8,128)(2,1)S(1)}, u32[]{:S(2)}, u32[]{:S(2)}) collective-permute-start(bf16[192,2048]{1,0:T(8,128)(2,1)S(1)} %collective-permute-done.7.refs_10_), channel_id=1, source_target_pairs={{0,1},{1,0},{2,3},{3,2},{4,5},{5,4},{6,7},{7,6},{8,9},{9,8},{10,11... | collective-permute-start | bytes 2359304 | tf_op jit(solution)/shard_map/ppermute | solution.py:863
  91.0 64.3 %all-to-all-start.1 = ((bf16[8,656,256]{2,1,0:T(8,128)(2,1)}), bf16[8,656,256]{2,1,0:T(8,128)(2,1)S(1)}, u32[]{:S(2)}, u32[]{:S(2)}) async-start(bf16[8,656,256]{2,1,0:T(8,128)(2,1)} %after.49), calls=%async_computation.1 | async-start | bytes 5373952 | tf_op jit(solution)/shard_map/all_to_all | solution.py:942
  180.0 14.1 %collective-permute-start.16 = (bf16[128,2048]{1,0:T(8,128)(2,1)S(1)}, bf16[128,2048]{1,0:T(8,128)(2,1)S(1)}, u32[]{:S(2)}, u32[]{:S(2)}) collective-permute-start(bf16[128,2048]{1,0:T(8,128)(2,1)S(1)} %get-tuple-element.153), channel_id=1, source_target_pairs={{0,8},{8,16},{16,24},{24,28},{28,20},{20,12},{12,4},{4,0},{1,9},{9... | collective-permute-start | bytes 1572872 | tf_op jit(solution)/shard_map/ppermute | solution.py:838
  180.1 14.1 %collective-permute-start.17 = (bf16[128,2048]{1,0:T(8,128)(2,1)S(1)}, bf16[128,2048]{1,0:T(8,128)(2,1)S(1)}, u32[]{:S(2)}, u32[]{:S(2)}) collective-permute-start(bf16[128,2048]{1,0:T(8,128)(2,1)S(1)} %get-tuple-element.154), channel_id=1, source_target_pairs={{0,4},{8,0},{16,8},{24,16},{28,24},{20,28},{12,20},{4,12},{1,5},{9... | collective-permute-start | bytes 1572872 | tf_op jit(solution)/shard_map/ppermute | solution.py:840
  183.8 49.0 %collective-permute-start.23 = (bf16[528,2048]{1,0:T(8,128)(2,1)}, bf16[528,2048]{1,0:T(8,128)(2,1)S(1)}, u32[]{:S(2)}, u32[]{:S(2)}) collective-permute-start(bf16[528,2048]{1,0:T(8,128)(2,1)} %bitcast.124.refs_2_.refs_4_), channel_id=1, source_target_pairs={{0,2},{1,3},{2,0},{3,1},{4,6},{5,7},{6,4},{7,5},{8,10},{9,11},{10,... | collective-permute-start | bytes 6488072 | tf_op jit(solution)/shard_map/ppermute | solution.py:863
  197.6 13.2 %collective-permute-start.18 = (bf16[128,2048]{1,0:T(8,128)(2,1)S(1)}, bf16[128,2048]{1,0:T(8,128)(2,1)S(1)}, u32[]{:S(2)}, u32[]{:S(2)}) collective-permute-start(bf16[128,2048]{1,0:T(8,128)(2,1)S(1)} %get-tuple-element.151), channel_id=1, source_target_pairs={{0,8},{8,16},{16,24},{24,28},{28,20},{20,12},{12,4},{4,0},{1,9},{9... | collective-permute-start | bytes 1572872 | tf_op jit(solution)/shard_map/ppermute | solution.py:838
  198.4 12.9 %collective-permute-start.19 = (bf16[128,2048]{1,0:T(8,128)(2,1)S(1)}, bf16[128,2048]{1,0:T(8,128)(2,1)S(1)}, u32[]{:S(2)}, u32[]{:S(2)}) collective-permute-start(bf16[128,2048]{1,0:T(8,128)(2,1)S(1)} %get-tuple-element.152), channel_id=1, source_target_pairs={{0,4},{8,0},{16,8},{24,16},{28,24},{20,28},{12,20},{4,12},{1,5},{9... | collective-permute-start | bytes 1572872 | tf_op jit(solution)/shard_map/ppermute | solution.py:840
  234.2 15.6 %collective-permute-start.24 = (bf16[528,2048]{1,0:T(8,128)(2,1)}, bf16[528,2048]{1,0:T(8,128)(2,1)S(1)}, u32[]{:S(2)}, u32[]{:S(2)}) collective-permute-start(bf16[528,2048]{1,0:T(8,128)(2,1)} %after.56.refs_4_.refs_6_), channel_id=1, source_target_pairs={{0,1},{1,0},{2,3},{3,2},{4,5},{5,4},{6,7},{7,6},{8,9},{9,8},{10,11... | collective-permute-start | bytes 6488072 | tf_op jit(solution)/shard_map/ppermute | solution.py:863
  234.2 29.4 %collective-permute-start.26 = (bf16[528,2048]{1,0:T(8,128)(2,1)}, bf16[528,2048]{1,0:T(8,128)(2,1)}, u32[]{:S(2)}, u32[]{:S(2)}) collective-permute-start(bf16[528,2048]{1,0:T(8,128)(2,1)} %bitcast.124.refs_2_.refs_4_), channel_id=1, source_target_pairs={{0,1},{1,0},{2,3},{3,2},{4,5},{5,4},{6,7},{7,6},{8,9},{9,8},{10,11... | collective-permute-start | bytes 6488072 | tf_op jit(solution)/shard_map/ppermute | solution.py:863
  234.7 15.1 %collective-permute-start.22 = (bf16[128,2048]{1,0:T(8,128)(2,1)}, bf16[128,2048]{1,0:T(8,128)(2,1)}, u32[]{:S(2)}, u32[]{:S(2)}) collective-permute-start(bf16[128,2048]{1,0:T(8,128)(2,1)} %add_convert_fusion.15.refs_1_), channel_id=1, source_target_pairs={{0,8},{8,16},{16,24},{24,28},{28,20},{20,12},{12,4},{4,0},{1,9},{9... | collective-permute-start | bytes 1572872 | tf_op jit(solution)/shard_map/ppermute | solution.py:838
  234.8 26.1 %collective-permute-start.29 = (bf16[128,2048]{1,0:T(8,128)(2,1)}, bf16[128,2048]{1,0:T(8,128)(2,1)S(1)}, u32[]{:S(2)}, u32[]{:S(2)}) collective-permute-start(bf16[128,2048]{1,0:T(8,128)(2,1)} %bitcast.245), channel_id=1, source_target_pairs={{0,8},{8,16},{16,24},{24,28},{28,20},{20,12},{12,4},{4,0},{1,9},{9... | collective-permute-start | bytes 1572872 | tf_op jit(solution)/shard_map/ppermute | solution.py:810
  236.3 24.7 %collective-permute-start.28 = (bf16[128,2048]{1,0:T(8,128)(2,1)}, bf16[128,2048]{1,0:T(8,128)(2,1)}, u32[]{:S(2)}, u32[]{:S(2)}) collective-permute-start(bf16[128,2048]{1,0:T(8,128)(2,1)} %bitcast.246), channel_id=1, source_target_pairs={{0,4},{8,0},{16,8},{24,16},{28,24},{20,28},{12,20},{4,12},{1,5},{9... | collective-permute-start | bytes 1572872 | tf_op jit(solution)/shard_map/ppermute | solution.py:810
  253.1 20.6 %collective-permute-start.27 = (bf16[128,2048]{1,0:T(8,128)(2,1)S(1)}, bf16[128,2048]{1,0:T(8,128)(2,1)}, u32[]{:S(2)}, u32[]{:S(2)}) collective-permute-start(bf16[128,2048]{1,0:T(8,128)(2,1)S(1)} %multiply_convert_fusion.refs_0_), channel_id=1, source_target_pairs={{0,4},{8,0},{16,8},{24,16},{28,24},{20,28},{12,20},{4,12},{1,5},{9... | collective-permute-start | bytes 1572872 | tf_op jit(solution)/shard_map/ppermute | solution.py:810
  253.5 20.6 %collective-permute-start.25 = (bf16[128,2048]{1,0:T(8,128)(2,1)S(1)}, bf16[128,2048]{1,0:T(8,128)(2,1)S(1)}, u32[]{:S(2)}, u32[]{:S(2)}) collective-permute-start(bf16[128,2048]{1,0:T(8,128)(2,1)S(1)} %multiply_convert_fusion.refs_0_), channel_id=1, source_target_pairs={{0,8},{8,16},{16,24},{24,28},{28,20},{20,12},{12,4},{4,0},{1,9},{9... | collective-permute-start | bytes 1572872 | tf_op jit(solution)/shard_map/ppermute | solution.py:810
  260.9 22.5 %collective-permute-start.33 = (bf16[128,2048]{1,0:T(8,128)(2,1)S(1)}, bf16[128,2048]{1,0:T(8,128)(2,1)S(1)}, u32[]{:S(2)}, u32[]{:S(2)}) collective-permute-start(bf16[128,2048]{1,0:T(8,128)(2,1)S(1)} %collective-permute-done.29.refs_4_.refs_2_.refs_10_), channel_id=1, source_target_pairs={{0,8},{8,16},{16,24},{24,28},{28,20},{20,12},{12,4},{4,0},{1,9},{9... | collective-permute-start | bytes 1572872 | tf_op jit(solution)/shard_map/ppermute | solution.py:810
  261.1 22.5 %collective-permute-start.32 = (bf16[128,2048]{1,0:T(8,128)(2,1)}, bf16[128,2048]{1,0:T(8,128)(2,1)S(1)}, u32[]{:S(2)}, u32[]{:S(2)}) collective-permute-start(bf16[128,2048]{1,0:T(8,128)(2,1)} %collective-permute-done.28.refs_3_.refs_11_), channel_id=1, source_target_pairs={{0,4},{8,0},{16,8},{24,16},{28,24},{20,28},{12,20},{4,12},{1,5},{9... | collective-permute-start | bytes 1572872 | tf_op jit(solution)/shard_map/ppermute | solution.py:810
  273.7 24.4 %collective-permute-start.31 = (bf16[128,2048]{1,0:T(8,128)(2,1)}, bf16[128,2048]{1,0:T(8,128)(2,1)S(1)}, u32[]{:S(2)}, u32[]{:S(2)}) collective-permute-start(bf16[128,2048]{1,0:T(8,128)(2,1)} %collective-permute-done.27.refs_2_.refs_1_.refs_3_), channel_id=1, source_target_pairs={{0,4},{8,0},{16,8},{24,16},{28,24},{20,28},{12,20},{4,12},{1,5},{9... | collective-permute-start | bytes 1572872 | tf_op jit(solution)/shard_map/ppermute | solution.py:810
  274.9 23.6 %collective-permute-start.30 = (bf16[128,2048]{1,0:T(8,128)(2,1)}, bf16[128,2048]{1,0:T(8,128)(2,1)}, u32[]{:S(2)}, u32[]{:S(2)}) collective-permute-start(bf16[128,2048]{1,0:T(8,128)(2,1)} %after.59.refs_0_.refs_2_), channel_id=1, source_target_pairs={{0,8},{8,16},{16,24},{24,28},{28,20},{20,12},{12,4},{4,0},{1,9},{9... | collective-permute-start | bytes 1572872 | tf_op jit(solution)/shard_map/ppermute | solution.py:810
  283.4 22.5 %collective-permute-start.37 = (bf16[128,2048]{1,0:T(8,128)(2,1)S(1)}, bf16[128,2048]{1,0:T(8,128)(2,1)S(1)}, u32[]{:S(2)}, u32[]{:S(2)}) collective-permute-start(bf16[128,2048]{1,0:T(8,128)(2,1)S(1)} %collective-permute-done.33.refs_4_.refs_2_.refs_12_), channel_id=1, source_target_pairs={{0,8},{8,16},{16,24},{24,28},{28,20},{20,12},{12,4},{4,0},{1,9},{9... | collective-permute-start | bytes 1572872 | tf_op jit(solution)/shard_map/ppermute | solution.py:810
  283.5 34.8 %collective-permute-start.36 = (bf16[128,2048]{1,0:T(8,128)(2,1)S(1)}, bf16[128,2048]{1,0:T(8,128)(2,1)}, u32[]{:S(2)}, u32[]{:S(2)}) collective-permute-start(bf16[128,2048]{1,0:T(8,128)(2,1)S(1)} %collective-permute-done.32.refs_3_.refs_13_), channel_id=1, source_target_pairs={{0,4},{8,0},{16,8},{24,16},{28,24},{20,28},{12,20},{4,12},{1,5},{9... | collective-permute-start | bytes 1572872 | tf_op jit(solution)/shard_map/ppermute | solution.py:810
  298.1 20.2 %collective-permute-start.35 = (bf16[128,2048]{1,0:T(8,128)(2,1)S(1)}, bf16[128,2048]{1,0:T(8,128)(2,1)}, u32[]{:S(2)}, u32[]{:S(2)}) collective-permute-start(bf16[128,2048]{1,0:T(8,128)(2,1)S(1)} %collective-permute-done.31.refs_2_.refs_1_.refs_5_), channel_id=1, source_target_pairs={{0,4},{8,0},{16,8},{24,16},{28,24},{20,28},{12,20},{4,12},{1,5},{9... | collective-permute-start | bytes 1572872 | tf_op jit(solution)/shard_map/ppermute | solution.py:810
  298.9 19.5 %collective-permute-start.34 = (bf16[128,2048]{1,0:T(8,128)(2,1)}, bf16[128,2048]{1,0:T(8,128)(2,1)}, u32[]{:S(2)}, u32[]{:S(2)}) collective-permute-start(bf16[128,2048]{1,0:T(8,128)(2,1)} %after.60.refs_0_.refs_4_), channel_id=1, source_target_pairs={{0,8},{8,16},{16,24},{24,28},{28,20},{20,12},{12,4},{4,0},{1,9},{9... | collective-permute-start | bytes 1572872 | tf_op jit(solution)/shard_map/ppermute | solution.py:810
  305.9 28.9 %collective-permute-start.39 = (bf16[128,2048]{1,0:T(8,128)(2,1)S(1)}, bf16[128,2048]{1,0:T(8,128)(2,1)}, u32[]{:S(2)}, u32[]{:S(2)}) collective-permute-start(bf16[128,2048]{1,0:T(8,128)(2,1)S(1)} %collective-permute-done.37.refs_4_.refs_2_.refs_14_), channel_id=1, source_target_pairs={{0,8},{8,16},{16,24},{24,28},{28,20},{20,12},{12,4},{4,0},{1,9},{9... | collective-permute-start | bytes 1572872 | tf_op jit(solution)/shard_map/ppermute | solution.py:810
  318.4 20.2 %collective-permute-start.38 = (bf16[128,2048]{1,0:T(8,128)(2,1)}, bf16[128,2048]{1,0:T(8,128)(2,1)S(1)}, u32[]{:S(2)}, u32[]{:S(2)}) collective-permute-start(bf16[128,2048]{1,0:T(8,128)(2,1)} %after.61.refs_0_.refs_6_), channel_id=1, source_target_pairs={{0,8},{8,16},{16,24},{24,28},{28,20},{20,12},{12,4},{4,0},{1,9},{9... | collective-permute-start | bytes 1572872 | tf_op jit(solution)/shard_map/ppermute | solution.py:810
  334.2 30.2 %collective-permute-start.41 = (bf16[128,2048]{1,0:T(8,128)(2,1)}, bf16[128,2048]{1,0:T(8,128)(2,1)S(1)}, u32[]{:S(2)}, u32[]{:S(2)}) collective-permute-start(bf16[128,2048]{1,0:T(8,128)(2,1)} %slice.231), channel_id=1, source_target_pairs={{0,4},{8,0},{16,8},{24,16},{28,24},{20,28},{12,20},{4,12},{1,5},{9... | collective-permute-start | bytes 1572872 | tf_op jit(solution)/shard_map/ppermute | solution.py:840
  349.7 14.8 %collective-permute-start.40 = (bf16[128,2048]{1,0:T(8,128)(2,1)}, bf16[128,2048]{1,0:T(8,128)(2,1)S(1)}, u32[]{:S(2)}, u32[]{:S(2)}) collective-permute-start(bf16[128,2048]{1,0:T(8,128)(2,1)} %get-tuple-element.101.refs_1_), channel_id=1, source_target_pairs={{0,8},{8,16},{16,24},{24,28},{28,20},{20,12},{12,4},{4,0},{1,9},{9... | collective-permute-start | bytes 1572872 | tf_op jit(solution)/shard_map/ppermute | solution.py:838
  368.0 18.2 %collective-permute-start.43 = (bf16[528,2048]{1,0:T(8,128)(2,1)}, bf16[528,2048]{1,0:T(8,128)(2,1)S(1)}, u32[]{:S(2)}, u32[]{:S(2)}) collective-permute-start(bf16[528,2048]{1,0:T(8,128)(2,1)} %after.65), channel_id=1, source_target_pairs={{0,1},{1,0},{2,3},{3,2},{4,5},{5,4},{6,7},{7,6},{8,9},{9,8},{10,11... | collective-permute-start | bytes 6488072 | tf_op jit(solution)/shard_map/ppermute | solution.py:863
  369.3 14.4 %collective-permute-start.44 = (bf16[128,2048]{1,0:T(8,128)(2,1)S(1)}, bf16[128,2048]{1,0:T(8,128)(2,1)S(1)}, u32[]{:S(2)}, u32[]{:S(2)}) collective-permute-start(bf16[128,2048]{1,0:T(8,128)(2,1)S(1)} %add_convert_fusion.13), channel_id=1, source_target_pairs={{0,4},{8,0},{16,8},{24,16},{28,24},{20,28},{12,20},{4,12},{1,5},{9... | collective-permute-start | bytes 1572872 | tf_op jit(solution)/shard_map/ppermute | solution.py:840
  371.2 14.3 %collective-permute-start.42 = (bf16[128,2048]{1,0:T(8,128)(2,1)}, bf16[128,2048]{1,0:T(8,128)(2,1)S(1)}, u32[]{:S(2)}, u32[]{:S(2)}) collective-permute-start(bf16[128,2048]{1,0:T(8,128)(2,1)} %add_convert_fusion.14.refs_1_), channel_id=1, source_target_pairs={{0,8},{8,16},{16,24},{24,28},{28,20},{20,12},{12,4},{4,0},{1,9},{9... | collective-permute-start | bytes 1572872 | tf_op jit(solution)/shard_map/ppermute | solution.py:838
  391.2 13.4 %collective-permute-start.46 = (bf16[128,2048]{1,0:T(8,128)(2,1)S(1)}, bf16[128,2048]{1,0:T(8,128)(2,1)}, u32[]{:S(2)}, u32[]{:S(2)}) collective-permute-start(bf16[128,2048]{1,0:T(8,128)(2,1)S(1)} %add_convert_fusion.11), channel_id=1, source_target_pairs={{0,4},{8,0},{16,8},{24,16},{28,24},{20,28},{12,20},{4,12},{1,5},{9... | collective-permute-start | bytes 1572872 | tf_op jit(solution)/shard_map/ppermute | solution.py:840
  392.1 13.6 %collective-permute-start.45 = (bf16[128,2048]{1,0:T(8,128)(2,1)}, bf16[128,2048]{1,0:T(8,128)(2,1)}, u32[]{:S(2)}, u32[]{:S(2)}) collective-permute-start(bf16[128,2048]{1,0:T(8,128)(2,1)} %add_convert_fusion.12), channel_id=1, source_target_pairs={{0,8},{8,16},{16,24},{24,28},{28,20},{20,12},{12,4},{4,0},{1,9},{9... | collective-permute-start | bytes 1572872 | tf_op jit(solution)/shard_map/ppermute | solution.py:838
  393.3 69.3 %collective-permute-start.56 = (bf16[528,2048]{1,0:T(8,128)(2,1)}, bf16[528,2048]{1,0:T(8,128)(2,1)}, u32[]{:S(2)}, u32[]{:S(2)}) collective-permute-start(bf16[528,2048]{1,0:T(8,128)(2,1)} %get-tuple-element.108), channel_id=1, source_target_pairs={{0,1},{1,0},{2,3},{3,2},{4,5},{5,4},{6,7},{7,6},{8,9},{9,8},{10,11... | collective-permute-start | bytes 6488072 | tf_op jit(solution)/shard_map/ppermute | solution.py:863
  412.6 47.1 %collective-permute-start.53 = (bf16[528,2048]{1,0:T(8,128)(2,1)}, bf16[528,2048]{1,0:T(8,128)(2,1)S(1)}, u32[]{:S(2)}, u32[]{:S(2)}) collective-permute-start(bf16[528,2048]{1,0:T(8,128)(2,1)} %add_convert_fusion.1), channel_id=1, source_target_pairs={{0,2},{1,3},{2,0},{3,1},{4,6},{5,7},{6,4},{7,5},{8,10},{9,11},{10,... | collective-permute-start | bytes 6488072 | tf_op jit(solution)/shard_map/ppermute | solution.py:863
  494.8 80.7 %all-to-all-start.2 = ((bf16[8,528,256]{2,1,0:T(8,128)(2,1)}), bf16[8,528,256]{2,1,0:T(8,128)(2,1)S(1)}, u32[]{:S(2)}, u32[]{:S(2)}) async-start(bf16[8,528,256]{2,1,0:T(8,128)(2,1)} %after.77), calls=%async_computation.3 | async-start | bytes 4325376 | tf_op jit(solution)/shard_map/all_to_all | solution.py:942
  499.0 147.1 %reduce-scatter.2.cloned.1.call-start = ((), (), s32[]{:S(2)}) async-start(), calls=%async_computation.5 | async-start | bytes 4718592 | tf_op jit(solution)/shard_map/reduce_scatter | solution.py:1200
  499.7 188.5 %all-gather.3.cloned.1.call-start = ((), (), s32[]{:S(2)}) async-start(), calls=%async_computation.6 | async-start | bytes 1179648 | tf_op jit(solution)/shard_map/all_gather | solution.py:1232
  559.3 37.0 %collective-permute-start.61 = (bf16[320,2048]{1,0:T(8,128)(2,1)}, bf16[320,2048]{1,0:T(8,128)(2,1)}, u32[]{:S(2)}, u32[]{:S(2)}) collective-permute-start(bf16[320,2048]{1,0:T(8,128)(2,1)} %get-tuple-element.115), channel_id=1, source_target_pairs={{0,1},{1,0},{2,3},{3,2},{4,5},{5,4},{6,7},{7,6},{8,9},{9,8},{10,11... | collective-permute-start | bytes 3932168 | tf_op jit(solution)/shard_map/ppermute | solution.py:863
  601.6 29.6 %collective-permute-start.64 = (bf16[128,2048]{1,0:T(8,128)(2,1)}, bf16[128,2048]{1,0:T(8,128)(2,1)S(1)}, u32[]{:S(2)}, u32[]{:S(2)}) collective-permute-start(bf16[128,2048]{1,0:T(8,128)(2,1)} %get-tuple-element.146), channel_id=1, source_target_pairs={{0,4},{8,0},{16,8},{24,16},{28,24},{20,28},{12,20},{4,12},{1,5},{9... | collective-permute-start | bytes 1572872 | tf_op jit(solution)/shard_map/ppermute | solution.py:840
  604.1 27.2 %collective-permute-start.63 = (bf16[128,2048]{1,0:T(8,128)(2,1)}, bf16[128,2048]{1,0:T(8,128)(2,1)S(1)}, u32[]{:S(2)}, u32[]{:S(2)}) collective-permute-start(bf16[128,2048]{1,0:T(8,128)(2,1)} %get-tuple-element.145.refs_1_), channel_id=1, source_target_pairs={{0,8},{8,16},{16,24},{24,28},{28,20},{20,12},{12,4},{4,0},{1,9},{9... | collective-permute-start | bytes 1572872 | tf_op jit(solution)/shard_map/ppermute | solution.py:838
  607.0 39.0 %collective-permute-start.68 = (bf16[320,2048]{1,0:T(8,128)(2,1)}, bf16[320,2048]{1,0:T(8,128)(2,1)S(1)}, u32[]{:S(2)}, u32[]{:S(2)}) collective-permute-start(bf16[320,2048]{1,0:T(8,128)(2,1)} %add_convert_fusion.3), channel_id=1, source_target_pairs={{0,2},{1,3},{2,0},{3,1},{4,6},{5,7},{6,4},{7,5},{8,10},{9,11},{10,... | collective-permute-start | bytes 3932168 | tf_op jit(solution)/shard_map/ppermute | solution.py:863
  608.5 41.4 %collective-permute-start.71 = (bf16[320,2048]{1,0:T(8,128)(2,1)}, bf16[320,2048]{1,0:T(8,128)(2,1)}, u32[]{:S(2)}, u32[]{:S(2)}) collective-permute-start(bf16[320,2048]{1,0:T(8,128)(2,1)} %get-tuple-element.122), channel_id=1, source_target_pairs={{0,1},{1,0},{2,3},{3,2},{4,5},{5,4},{6,7},{7,6},{8,9},{9,8},{10,11... | collective-permute-start | bytes 3932168 | tf_op jit(solution)/shard_map/ppermute | solution.py:863
  649.6 14.6 %collective-permute-start.70 = (bf16[128,2048]{1,0:T(8,128)(2,1)}, bf16[128,2048]{1,0:T(8,128)(2,1)}, u32[]{:S(2)}, u32[]{:S(2)}) collective-permute-start(bf16[128,2048]{1,0:T(8,128)(2,1)} %add_convert_fusion.4), channel_id=1, source_target_pairs={{0,8},{8,16},{16,24},{24,28},{28,20},{20,12},{12,4},{4,0},{1,9},{9... | collective-permute-start | bytes 1572872 | tf_op jit(solution)/shard_map/ppermute | solution.py:838
  653.6 49.2 %all-to-all-start.3 = ((bf16[8,320,256]{2,1,0:T(8,128)(2,1)}), bf16[8,320,256]{2,1,0:T(8,128)(2,1)S(1)}, u32[]{:S(2)}, u32[]{:S(2)}) async-start(bf16[8,320,256]{2,1,0:T(8,128)(2,1)} %bitcast.244), calls=%async_computation.4 | async-start | bytes 2621440 | tf_op jit(solution)/shard_map/all_to_all | solution.py:942
  (114 other events, 663.8 us)
Sparse Core Ops, SparseCore 0:
  503.4 128.8 reduce-scatter.1
  637.3 50.8 all-gather.2

commit v6 on v5

--- a/solution.py
+++ b/solution.py
@@ -1078,7 +1078,7 @@
     def token_work(s, arrived):
         if s == 1:
             own["parts"] = start_heads(plan, after(proj_block, arrived[0]))
-            return [gb, init]
+            return [gb, init, rate_rows, bias, docs, slot_of_member, member_of_slot]
         if s == seq // 2 - 2:
             mats = (w_swish.T, w_up.T, w_down)
             if plan.each == 1:
@@ -1103,7 +1103,6 @@
     grad_own = cotangent[0]
 
     inner, *kept = chain_forward(slot_of_member, docs, x3, logits, gb, init, rows_tok)
-    kept_stat = after(kept[3], rest_block)
     side_rows = rest_block.shape[1] - 3 * padded
     side_block, ffn_block = rest_block[:, :side_rows], rest_block[:, side_rows:]
 
@@ -1114,8 +1113,9 @@
     ffn_block = ffn_block.transpose(1, 0, 2).reshape(3 * padded, width)
     ffn_parts = start_gather(ffn_block)
 
-    sums = jnp.sum(kept_stat[2:4].reshape(2, stream // MB, local, MB), axis=2).reshape(2, stream)
-    sums = in_slots(pairwise_sum(sums, "seq", seq)) / width
+    sums = jnp.sum(kept[3][2:4].reshape(2, stream // MB, local, MB), axis=2).reshape(2, stream)
+    sums = after(pairwise_sum(sums, "seq", seq), rest_block)
+    sums = in_slots(sums) / width
     mean_o = sums[0][:, None]
     inv_o = lax.rsqrt(sums[1][:, None] - mean_o * mean_o + EPS)
     o_hat = (inner - mean_o) * inv_o
@@ -1188,6 +1188,10 @@
     )
 
     def mix_work(s, arrived):
+        if s == 0:
+            late = [after(own["parts"][0], arrived[0])] + own["parts"][1:]
+            got["w_all"] = jnp.concatenate(late + [rate_rows, m_gate], axis=0)
+            return [got["w_all"]]
         if s == seq // 2 - 2:
             return [got["across"]]
         if s == seq // 2 - 1:
@@ -1215,9 +1219,8 @@
     d_x, d_gb, d_init = chain_backward(
         slot_of_member, docs, x3, d_inner, d_gate_pre, logits, gb, init, kept, rows_tok
     )
-    w_all = jnp.concatenate(own["parts"] + [rate_rows, m_gate], axis=0)
     *head_rows_grads, g_rates, g_gain = proj_grads(
-        d_x, normed, w_all, gated, sum(by_slots(mix_steps), ()), local, head_dim
+        d_x, normed, got["w_all"], gated, sum(by_slots(mix_steps), ()), local, head_dim
     )
     d_logits = d_x[:, 3 * features : 3 * features + local].astype(F32)
     parts = [item.reshape(local, -1) for item in chain_param_grads(d_gb, d_init, local)]
@@ -1231,7 +1234,7 @@
     flat = pairwise_sum(flat.reshape(-1, 1024), "grp", groups)
     flat_all = lax.all_gather(flat, "seq", axis=0)
     d_x = after(d_x, g_gain, g_ffn)
-    d_normed_part = mm(d_x, w_all).astype(BF16)
+    d_normed_part = mm(d_x, got["w_all"]).astype(BF16)
 
     def corner_work(since):
         if not plan.mixed:

time: 727 us -> 718 us (0.988)
  waiting for transfers between devices: 281 us -> 265 us
    ppermute x28, waiting for transfers between devices: 88.8 us -> 49.8 us  [move(): lax.ppermute(value, 'seq', ring_pairs(size, step))]
    ppermute x8, waiting for transfers between devices: 18.3 us -> 29.1 us  [pairwise_sum(): lax.ppermute(value, axis, [(i, i ^ bit) for i in range(size)])]
    ppermute x12, waiting for transfers between devices: 64.9 us -> 73.2 us  [ring_scatter(): ahead = lax.ppermute(ahead, 'seq', ring_pairs(size, 1))]
    ppermute x15, waiting for transfers between devices: 16.2 us -> 24.4 us  [swap(): return lax.ppermute(value, 'grp', [(i, i ^ bit) for i in range(4)])]
    unnamed x182 -> x175, local copies, waits for them, and re-layouts: 42 us -> 39.5 us
  transfers between devices with their start and end apart: 78 -> 78, of which waited for: 46 -> 43; matrix products, arithmetic and copies ran while one was open for 14% -> 16% of each run, Pallas kernels for 23% -> 24%
where the time goes in v6:
time: 718 us; the launch traced here: 708 us
  waiting for transfers between devices  265 us (37%)
  Pallas kernels  172 us (24%)
  starting transfers between devices  96.6 us (13%)
  local copies, waits for them, and re-layouts  71.6 us (10%)
  other arithmetic  64.7 us (9%)
  matrix products  22.4 us (3%)
  between operations  15.6 us (2%)
    ppermute x12, waiting for transfers between devices, ring_scatter(): ahead = lax.ppermute(ahead, 'seq', ring_pairs(size, 1))  73.2 us
    pallas_call x5, Pallas kernels, ffn_step(): pl.pallas_call(partial(ffn_kernel, count, len(weights), len(kept)), grid_...  57.3 us
    ppermute x28, waiting for transfers between devices, move(): lax.ppermute(value, 'seq', ring_pairs(size, step))  49.8 us
    ppermute x9, waiting for transfers between devices, ring_scatter(): back = lax.ppermute(back, 'seq', ring_pairs(size, -1))  47.4 us
    unnamed x175, local copies, waits for them, and re-layouts  39.5 us
    pallas_call x1, Pallas kernels, chain_backward(): pl.pallas_call(partial(backward_kernel, heads), grid_spec=pltpu.PrefetchS...  37.5 us
    ppermute x28, starting transfers between devices, move(): lax.ppermute(value, 'seq', ring_pairs(size, step))  31.7 us
    ppermute x8, waiting for transfers between devices, pairwise_sum(): lax.ppermute(value, axis, [(i, i ^ bit) for i in range(size)])  29.1 us
  transfers between devices with their start and end apart: 78, of which 43 were waited for; matrix products, arithmetic and copies ran while one was open for 16% of the time, Pallas kernels for 24%

profile of v6, /device:TPU:0, one launch (start us, length us, event | category | flops | bytes accessed | tf_op | source)
XLA Modules:
  0.0 707.6 jit_solution(13266375357825318866)
XLA Ops:
  12.6 6.2 all-to-all-start
  30.3 11.3 %all-to-all-done.refs_0_ = bf16[8,192,256]{2,1,0:T(8,128)(2,1)S(1)} async-done(((bf16[8,192,256]{2,1,0:T(8,128)(2,1)}), bf16[8,192,256]{2,1,0:T(8,128)(2,1)S(1)}, u32[]{:S(2)}, u32[]{:S(2)}) %all-to-all-start) | async-done | bytes 786464 | tf_op jit(solution)/shard_map/all_to_all | solution.py:942
  45.3 3.2 fusion.87.refs_4_.refs_13_
  50.2 3.1 collective-permute-start.5
  54.1 6.7 collective-permute-done.7.refs_10_
  60.9 3.9 cut_features.2.refs_1_.refs_0_
  67.0 13.4 %collective-permute-done.6.refs_0_ = bf16[128,2048]{1,0:T(8,128)(2,1)S(1)} collective-permute-done((bf16[128,2048]{1,0:T(8,128)(2,1)}, bf16[128,2048]{1,0:T(8,128)(2,1)S(1)}, u32[]{:S(2)}, u32[]{:S(2)}) %collective-permute-start.6) | collective-permute-done | bytes 524320 | tf_op jit(solution)/shard_map/ppermute | solution.py:810
  82.1 4.4 all-to-all-start.1
  89.0 10.6 %project.1 = (bf16[1024,2048]{1,0:T(8,128)(2,1)}, bf16[1024,768]{1,0:T(8,128)(2,1)}, f32[1024,128]{1,0:T(8,128)}) custom-call(bf16[128,2048]{1,0:T(8,128)(2,1)} %bitcast.240, bf16[128,2048]{1,0:T(8,128)(2,1)} %after.49.refs_1_, bf16[128,2048]{1,0:T(8,128)(2,1)} %after.45.refs_1_.refs_2_, bf16[128,2048]{1,0:T(8,128)(2,1)} %copy-done.49, ...), custom_call_target="tpu_custom_call" | custom-call | flops 1 | bytes 1 | tf_op jit(solution)/shard_map/project/pallas_call | solution.py:743
  99.5 24.7 %chain_forward.1 = (f32[1024,256]{1,0:T(8,128)}, f32[64,4096]{1,0:T(8,128)}, f32[64,4096]{1,0:T(8,128)}, f32[64,4096]{1,0:T(8,128)}, f32[8,4096]{1,0:T(8,128)}, /*index=5*/f32[8,64,384]{2,1,0:T(8,128)}) custom-call(s32[8]{0:T(128)} %get-tuple-element.222.refs_6_.idx_ref, s32[5]{0:T(128)} %pad_add_fusion.refs_5_.docs_ref, ...), custom_call_target="tpu_custom_call" | custom-call | flops 1 | bytes 1 | tf_op jit(solution)/shard_map/chain_forward/pallas_call | solution.py:391
  136.0 11.2 %collective-permute-done.15 = f32[2,1024]{1,0:T(2,128)S(1)} collective-permute-done((f32[2,1024]{1,0:T(2,128)S(1)}, f32[2,1024]{1,0:T(2,128)S(1)}, u32[]{:S(2)}, u32[]{:S(2)}) %collective-permute-start.15) | collective-permute-done | bytes 8224 | tf_op jit(solution)/shard_map/ppermute | solution.py:857
  151.6 9.8 %collective-permute-done.11 = bf16[128,2048]{1,0:T(8,128)(2,1)} collective-permute-done((bf16[128,2048]{1,0:T(8,128)(2,1)}, bf16[128,2048]{1,0:T(8,128)(2,1)}, u32[]{:S(2)}, u32[]{:S(2)}) %collective-permute-start.11) | collective-permute-done | bytes 524320 | tf_op jit(solution)/shard_map/ppermute | solution.py:863
  174.3 9.2 %collective-permute-done.16.refs_0_ = bf16[128,2048]{1,0:T(8,128)(2,1)S(1)} collective-permute-done((bf16[128,2048]{1,0:T(8,128)(2,1)S(1)}, bf16[128,2048]{1,0:T(8,128)(2,1)S(1)}, u32[]{:S(2)}, u32[]{:S(2)}) %collective-permute-start.16) | collective-permute-done | bytes 524320 | tf_op jit(solution)/shard_map/ppermute | solution.py:838
  189.1 11.7 %collective-permute-done.18.refs_0_ = bf16[128,2048]{1,0:T(8,128)(2,1)S(1)} collective-permute-done((bf16[128,2048]{1,0:T(8,128)(2,1)S(1)}, bf16[128,2048]{1,0:T(8,128)(2,1)S(1)}, u32[]{:S(2)}, u32[]{:S(2)}) %collective-permute-start.18) | collective-permute-done | bytes 524320 | tf_op jit(solution)/shard_map/ppermute | solution.py:838
  207.0 10.3 %collective-permute-done.20.refs_0_ = bf16[128,2048]{1,0:T(8,128)(2,1)S(1)} collective-permute-done((bf16[128,2048]{1,0:T(8,128)(2,1)S(1)}, bf16[128,2048]{1,0:T(8,128)(2,1)S(1)}, u32[]{:S(2)}, u32[]{:S(2)}) %collective-permute-start.20) | collective-permute-done | bytes 524320 | tf_op jit(solution)/shard_map/ppermute | solution.py:838
  227.0 11.8 %collective-permute-done.22.refs_0_ = bf16[128,2048]{1,0:T(8,128)(2,1)S(1)} collective-permute-done((bf16[128,2048]{1,0:T(8,128)(2,1)S(1)}, bf16[128,2048]{1,0:T(8,128)(2,1)S(1)}, u32[]{:S(2)}, u32[]{:S(2)}) %collective-permute-start.22) | collective-permute-done | bytes 524320 | tf_op jit(solution)/shard_map/ppermute | solution.py:838
  245.8 4.4 collective-permute-done.29.refs_4_.refs_2_.refs_10_
  252.8 10.2 %ffn_step.5 = (bf16[704,1024]{1,0:T(8,128)(2,1)}, bf16[704,1024]{1,0:T(8,128)(2,1)}, bf16[704,1024]{1,0:T(8,128)(2,1)}, bf16[8,128,2048]{2,1,0:T(8,128)(2,1)}, bf16[128,2048]{1,0:T(8,128)(2,1)}) custom-call(s32[1]{0:T(128)} %get-tuple-element.217.member_ref, bf16[128,2048]{1,0:T(8,128)(2,1)} %copy-done.27, bf16[128,2048]{1,0:T(8,128)(2,1)} %bitcast.73.refs_1_.refs_8_, ...), custom_call_target="tpu_custom_call" | custom-call | flops 1 | bytes 1 | tf_op jit(solution)/shard_map/ffn_step/pallas_call | solution.py:597
  266.4 6.2 collective-permute-done.33.refs_4_.refs_2_.refs_12_
  275.0 12.4 %ffn_step.6 = (bf16[704,1024]{1,0:T(8,128)(2,1)}, bf16[704,1024]{1,0:T(8,128)(2,1)}, bf16[704,1024]{1,0:T(8,128)(2,1)}, bf16[8,128,2048]{2,1,0:T(8,128)(2,1)}, bf16[256,2048]{1,0:T(8,128)(2,1)}) custom-call(s32[2]{0:T(128)} %get-tuple-element.216.member_ref, ...), custom_call_target="tpu_custom_call", output_to_operand_aliasing={{0}: (9, {}), {1}: (10, {}), {2}: (11, {}), {3}: (12, {})} | custom-call | flops 1 | bytes 1 | tf_op jit(solution)/shard_map/ffn_step/pallas_call | solution.py:597
  289.5 5.6 collective-permute-done.37.refs_4_.refs_2_.refs_14_
  296.0 12.3 %ffn_step.7 = (bf16[704,1024]{1,0:T(8,128)(2,1)}, bf16[704,1024]{1,0:T(8,128)(2,1)}, bf16[704,1024]{1,0:T(8,128)(2,1)}, bf16[8,128,2048]{2,1,0:T(8,128)(2,1)}, bf16[256,2048]{1,0:T(8,128)(2,1)}) custom-call(s32[2]{0:T(128)} %get-tuple-element.215.member_ref, ...), custom_call_target="tpu_custom_call", output_to_operand_aliasing={{0}: (9, {}), {1}: (10, {}), {2}: (11, {}), {3}: (12, {})} | custom-call | flops 1 | bytes 1 | tf_op jit(solution)/shard_map/ffn_step/pallas_call | solution.py:597
  310.5 12.3 %ffn_step.8 = (bf16[704,1024]{1,0:T(8,128)(2,1)}, bf16[704,1024]{1,0:T(8,128)(2,1)}, bf16[704,1024]{1,0:T(8,128)(2,1)}, bf16[8,128,2048]{2,1,0:T(8,128)(2,1)}, bf16[256,2048]{1,0:T(8,128)(2,1)}) custom-call(s32[2]{0:T(128)} %get-tuple-element.214.member_ref, ...), custom_call_target="tpu_custom_call", output_to_operand_aliasing={{0}: (9, {}), {1}: (10, {}), {2}: (11, {}), {3}: (12, {})} | custom-call | flops 1 | bytes 1 | tf_op jit(solution)/shard_map/ffn_step/pallas_call | solution.py:597
  324.7 3.2 collective-permute-done.38.refs_0_
  328.8 10.2 %ffn_step.9 = (bf16[704,1024]{1,0:T(8,128)(2,1)}, bf16[704,1024]{1,0:T(8,128)(2,1)}, bf16[704,1024]{1,0:T(8,128)(2,1)}, bf16[8,128,2048]{2,1,0:T(8,128)(2,1)}, bf16[128,2048]{1,0:T(8,128)(2,1)}) custom-call(s32[1]{0:T(128)} %get-tuple-element.218.member_ref, ...), custom_call_target="tpu_custom_call", output_to_operand_aliasing={{0}: (7, {}), {1}: (8, {}), {2}: (9, {}), {3}: (10, {})} | custom-call | flops 1 | bytes 1 | tf_op jit(solution)/shard_map/ffn_step/pallas_call | solution.py:597
  339.8 14.5 %ffn_grads.1 = (bf16[528,2048]{1,0:T(8,128)(2,1)}, bf16[528,2048]{1,0:T(8,128)(2,1)}, bf16[528,2048]{1,0:T(8,128)(2,1)}, bf16[528,2048]{1,0:T(8,128)(2,1)}) custom-call(bf16[704,1024]{1,0:T(8,128)(2,1)} %after.64.at_ref, bf16[704,1024]{1,0:T(8,128)(2,1)} %get-tuple-element.103.ut_ref, bf16[704,1024]{1,0:T(8,128)(2,1)} %get-tuple-element.104.ht_ref, ...), custom_call_target="tpu_custom_call" | custom-call | flops 1 | bytes 1 | tf_op jit(solution)/shard_map/ffn_grads/pallas_call | solution.py:645
  361.2 12.5 %collective-permute-done.44.refs_2_.refs_0_ = bf16[128,2048]{1,0:T(8,128)(2,1)S(1)} collective-permute-done((bf16[128,2048]{1,0:T(8,128)(2,1)S(1)}, bf16[128,2048]{1,0:T(8,128)(2,1)S(1)}, u32[]{:S(2)}, u32[]{:S(2)}) %collective-permute-start.44) | collective-permute-done | bytes 524320 | tf_op jit(solution)/shard_map/ppermute | solution.py:840
  382.6 11.8 %collective-permute-done.46.refs_1_.refs_0_ = bf16[128,2048]{1,0:T(8,128)(2,1)} collective-permute-done((bf16[128,2048]{1,0:T(8,128)(2,1)S(1)}, bf16[128,2048]{1,0:T(8,128)(2,1)}, u32[]{:S(2)}, u32[]{:S(2)}) %collective-permute-start.46) | collective-permute-done | bytes 524320 | tf_op jit(solution)/shard_map/ppermute | solution.py:840
  398.7 3.8 add_convert_fusion.1
  404.0 6.2 collective-permute-done.47
  431.0 9.9 %collective-permute-done.51.refs_1_.refs_5_ = bf16[128,2048]{1,0:T(8,128)(2,1)} collective-permute-done((bf16[128,2048]{1,0:T(8,128)(2,1)}, bf16[128,2048]{1,0:T(8,128)(2,1)}, u32[]{:S(2)}, u32[]{:S(2)}) %collective-permute-start.51) | collective-permute-done | bytes 524320 | tf_op jit(solution)/shard_map/ppermute | solution.py:810
  445.3 4.8 collective-permute-done.53.refs_1_.refs_0_
  454.8 3.5 add_convert_fusion
  459.8 4.1 collective-permute-done.55.refs_0_
  473.9 3.3 collective-permute-done.57
  482.5 3.0 collective-permute-done.59
  486.4 10.0 %all-to-all-start.2 = ((bf16[8,528,256]{2,1,0:T(8,128)(2,1)}), bf16[8,528,256]{2,1,0:T(8,128)(2,1)S(1)}, u32[]{:S(2)}, u32[]{:S(2)}) async-start(bf16[8,528,256]{2,1,0:T(8,128)(2,1)} %after.79), calls=%async_computation.3 | async-start | bytes 4325376 | tf_op jit(solution)/shard_map/all_to_all | solution.py:942
  500.5 37.5 %chain_backward.1 = (bf16[1024,1152]{1,0:T(8,128)(2,1)}, f32[2,64,128]{2,1,0:T(8,128)}, f32[64,384]{1,0:T(8,128)}) custom-call(s32[8]{0:T(128)} %get-tuple-element.222.refs_6_.idx_ref, s32[5]{0:T(128)} %pad_add_fusion.refs_5_.docs_ref, bf16[1024,768]{1,0:T(8,128)(2,1)} %get-tuple-element.76.x_ref, f32[1024,256]{1,0:T(8,128)} %subtract_multiply_fusion.d_ref, ...), custom_call_target="tpu_custom_call" | custom-call | flops 1 | bytes 1 | tf_op jit(solution)/shard_map/chain_backward/pallas_call | solution.py:423
  538.0 14.1 %proj_grads.1 = (bf16[320,2048]{1,0:T(8,128)(2,1)}, bf16[320,2048]{1,0:T(8,128)(2,1)}, bf16[320,2048]{1,0:T(8,128)(2,1)}, bf16[320,2048]{1,0:T(8,128)(2,1)}, f32[8,2048]{1,0:T(8,128)}, /*index=5*/f32[8,2048]{1,0:T(8,128)}) custom-call(bf16[1024,1152]{1,0:T(8,128)(2,1)} %get-tuple-element.113.d_ref.refs_0_, bf16[1024,2048]{1,0:T(8,128)(2,1)} %get-tuple-element.75.x_ref, ...), custom_call_target="tpu_custom_call" | custom-call | flops 1 | bytes 1 | tf_op jit(solution)/shard_map/proj_grads/pallas_call | solution.py:697
  555.9 10.2 %all-to-all-done.2.refs_2_.refs_0_ = bf16[8,528,256]{2,1,0:T(8,128)(2,1)S(1)} async-done(((bf16[8,528,256]{2,1,0:T(8,128)(2,1)}), bf16[8,528,256]{2,1,0:T(8,128)(2,1)S(1)}, u32[]{:S(2)}, u32[]{:S(2)}) %all-to-all-start.2) | async-done | bytes 2162720 | tf_op jit(solution)/shard_map/all_to_all | solution.py:942
  567.5 8.2 %convolution_convert_fusion = bf16[1024,2048]{1,0:T(8,128)(2,1)S(1)} fusion(bf16[1024,1152]{1,0:T(8,128)(2,1)} %after.80, bf16[1152,2048]{1,0:T(8,128)(2,1)} %constant_dynamic-update-slice_fusion.refs_1_.w_ref), kind=kOutput, calls=%fused_computation.2 | convolution fusion | flops 4833935360 | bytes 11272192 | tf_op jit(solution)/shard_map/dot_general | solution.py:18
  582.0 4.1 collective-permute-done.67
  597.8 4.0 join_features.2
  601.8 19.8 %collective-permute-done.64.refs_2_.refs_0_ = bf16[128,2048]{1,0:T(8,128)(2,1)S(1)} collective-permute-done((bf16[128,2048]{1,0:T(8,128)(2,1)}, bf16[128,2048]{1,0:T(8,128)(2,1)S(1)}, u32[]{:S(2)}, u32[]{:S(2)}) %collective-permute-start.64) | collective-permute-done | bytes 524320 | tf_op jit(solution)/shard_map/ppermute | solution.py:840
  627.3 13.0 %collective-permute-done.65.refs_0_ = bf16[128,2048]{1,0:T(8,128)(2,1)S(1)} collective-permute-done((bf16[128,2048]{1,0:T(8,128)(2,1)}, bf16[128,2048]{1,0:T(8,128)(2,1)S(1)}, u32[]{:S(2)}, u32[]{:S(2)}) %collective-permute-start.65) | collective-permute-done | bytes 524320 | tf_op jit(solution)/shard_map/ppermute | solution.py:838
  648.0 4.3 all-to-all-start.3
  653.2 9.3 %collective-permute-done.70 = bf16[128,2048]{1,0:T(8,128)(2,1)S(1)} collective-permute-done((bf16[128,2048]{1,0:T(8,128)(2,1)S(1)}, bf16[128,2048]{1,0:T(8,128)(2,1)S(1)}, u32[]{:S(2)}, u32[]{:S(2)}) %collective-permute-start.70) | collective-permute-done | bytes 524320 | tf_op jit(solution)/shard_map/ppermute | solution.py:838
  665.0 18.9 %all-gather.3.cloned.1.call-done = f32[256,1024]{1,0:T(8,128)} async-done(((f32[32,1024]{1,0:T(8,128)}), f32[256,1024]{1,0:T(8,128)}) %all-gather.3.cloned.1.call-update) | async-done | bytes 1048592 | tf_op jit(solution)/shard_map/all_gather | solution.py:1235
  (483 shorter events, 233.1 us)
Async XLA Ops:
  7.2 19.4 %collective-permute-start.1 = (bf16[128,2048]{1,0:T(8,128)(2,1)}, bf16[128,2048]{1,0:T(8,128)(2,1)S(1)}, u32[]{:S(2)}, u32[]{:S(2)}) collective-permute-start(bf16[128,2048]{1,0:T(8,128)(2,1)} %bitcast.238), channel_id=1, source_target_pairs={{0,4},{8,0},{16,8},{24,16},{28,24},{20,28},{12,20},{4,12},{1,5},{9... | collective-permute-start | bytes 1572872 | tf_op jit(solution)/shard_map/ppermute | solution.py:810
  10.2 16.4 %collective-permute-start = (bf16[128,2048]{1,0:T(8,128)(2,1)}, bf16[128,2048]{1,0:T(8,128)(2,1)S(1)}, u32[]{:S(2)}, u32[]{:S(2)}) collective-permute-start(bf16[128,2048]{1,0:T(8,128)(2,1)} %bitcast.239), channel_id=1, source_target_pairs={{0,8},{8,16},{16,24},{24,28},{28,20},{20,12},{12,4},{4,0},{1,9},{9... | collective-permute-start | bytes 1572872 | tf_op jit(solution)/shard_map/ppermute | solution.py:810
  12.6 29.0 %all-to-all-start = ((bf16[8,192,256]{2,1,0:T(8,128)(2,1)}), bf16[8,192,256]{2,1,0:T(8,128)(2,1)S(1)}, u32[]{:S(2)}, u32[]{:S(2)}) async-start(bf16[8,192,256]{2,1,0:T(8,128)(2,1)} %cut_features.3), calls=%async_computation | async-start | bytes 1572864 | tf_op jit(solution)/shard_map/all_to_all | solution.py:942
  28.2 25.1 %collective-permute-start.2 = (bf16[128,2048]{1,0:T(8,128)(2,1)}, bf16[128,2048]{1,0:T(8,128)(2,1)S(1)}, u32[]{:S(2)}, u32[]{:S(2)}) collective-permute-start(bf16[128,2048]{1,0:T(8,128)(2,1)} %after.45.refs_1_.refs_2_), channel_id=1, source_target_pairs={{0,8},{8,16},{16,24},{24,28},{28,20},{20,12},{12,4},{4,0},{1,9},{9... | collective-permute-start | bytes 1572872 | tf_op jit(solution)/shard_map/ppermute | solution.py:810
  30.3 20.0 %collective-permute-start.3 = (bf16[128,2048]{1,0:T(8,128)(2,1)}, bf16[128,2048]{1,0:T(8,128)(2,1)S(1)}, u32[]{:S(2)}, u32[]{:S(2)}) collective-permute-start(bf16[128,2048]{1,0:T(8,128)(2,1)} %copy-done.49), channel_id=1, source_target_pairs={{0,4},{8,0},{16,8},{24,16},{28,24},{20,28},{12,20},{4,12},{1,5},{9... | collective-permute-start | bytes 1572872 | tf_op jit(solution)/shard_map/ppermute | solution.py:810
  43.7 17.1 %collective-permute-start.7 = (bf16[192,2048]{1,0:T(8,128)(2,1)S(1)}, bf16[192,2048]{1,0:T(8,128)(2,1)S(1)}, u32[]{:S(2)}, u32[]{:S(2)}) collective-permute-start(bf16[192,2048]{1,0:T(8,128)(2,1)S(1)} %bitcast.233), channel_id=1, source_target_pairs={{0,2},{1,3},{2,0},{3,1},{4,6},{5,7},{6,4},{7,5},{8,10},{9,11},{10,... | collective-permute-start | bytes 2359304 | tf_op jit(solution)/shard_map/ppermute | solution.py:863
  50.2 14.5 %collective-permute-start.5 = (bf16[128,2048]{1,0:T(8,128)(2,1)S(1)}, bf16[128,2048]{1,0:T(8,128)(2,1)}, u32[]{:S(2)}, u32[]{:S(2)}) collective-permute-start(bf16[128,2048]{1,0:T(8,128)(2,1)S(1)} %collective-permute-done.3.refs_8_.refs_5_), channel_id=1, source_target_pairs={{0,4},{8,0},{16,8},{24,16},{28,24},{20,28},{12,20},{4,12},{1,5},{9... | collective-permute-start | bytes 1572872 | tf_op jit(solution)/shard_map/ppermute | solution.py:810
  60.9 19.6 %collective-permute-start.8 = (bf16[192,2048]{1,0:T(8,128)(2,1)S(1)}, bf16[192,2048]{1,0:T(8,128)(2,1)S(1)}, u32[]{:S(2)}, u32[]{:S(2)}) collective-permute-start(bf16[192,2048]{1,0:T(8,128)(2,1)S(1)} %collective-permute-done.7.refs_10_), channel_id=1, source_target_pairs={{0,1},{1,0},{2,3},{3,2},{4,5},{5,4},{6,7},{7,6},{8,9},{9,8},{10,11... | collective-permute-start | bytes 2359304 | tf_op jit(solution)/shard_map/ppermute | solution.py:863
  65.5 14.9 %collective-permute-start.6 = (bf16[128,2048]{1,0:T(8,128)(2,1)}, bf16[128,2048]{1,0:T(8,128)(2,1)S(1)}, u32[]{:S(2)}, u32[]{:S(2)}) collective-permute-start(bf16[128,2048]{1,0:T(8,128)(2,1)} %after.47.refs_6_), channel_id=1, source_target_pairs={{0,8},{8,16},{16,24},{24,28},{28,20},{20,12},{12,4},{4,0},{1,9},{9... | collective-permute-start | bytes 1572872 | tf_op jit(solution)/shard_map/ppermute | solution.py:810
  82.1 65.8 %all-to-all-start.1 = ((bf16[8,656,256]{2,1,0:T(8,128)(2,1)}), bf16[8,656,256]{2,1,0:T(8,128)(2,1)S(1)}, u32[]{:S(2)}, u32[]{:S(2)}) async-start(bf16[8,656,256]{2,1,0:T(8,128)(2,1)} %after.50), calls=%async_computation.1 | async-start | bytes 5373952 | tf_op jit(solution)/shard_map/all_to_all | solution.py:942
  133.0 14.3 %collective-permute-start.15 = (f32[2,1024]{1,0:T(2,128)S(1)}, f32[2,1024]{1,0:T(2,128)S(1)}, u32[]{:S(2)}, u32[]{:S(2)}) collective-permute-start(f32[2,1024]{1,0:T(2,128)S(1)} %add.416), channel_id=1, source_target_pairs={{0,16},{4,20},{8,24},{12,28},{16,0},{20,4},{24,8},{28,12},{1,17},{... | collective-permute-start | bytes 24584 | tf_op jit(solution)/shard_map/ppermute | solution.py:857
  168.6 14.9 %collective-permute-start.16 = (bf16[128,2048]{1,0:T(8,128)(2,1)S(1)}, bf16[128,2048]{1,0:T(8,128)(2,1)S(1)}, u32[]{:S(2)}, u32[]{:S(2)}) collective-permute-start(bf16[128,2048]{1,0:T(8,128)(2,1)S(1)} %get-tuple-element.153), channel_id=1, source_target_pairs={{0,8},{8,16},{16,24},{24,28},{28,20},{20,12},{12,4},{4,0},{1,9},{9... | collective-permute-start | bytes 1572872 | tf_op jit(solution)/shard_map/ppermute | solution.py:838
  172.8 49.4 %collective-permute-start.23 = (bf16[528,2048]{1,0:T(8,128)(2,1)}, bf16[528,2048]{1,0:T(8,128)(2,1)S(1)}, u32[]{:S(2)}, u32[]{:S(2)}) collective-permute-start(bf16[528,2048]{1,0:T(8,128)(2,1)} %bitcast.124.refs_2_.refs_4_), channel_id=1, source_target_pairs={{0,2},{1,3},{2,0},{3,1},{4,6},{5,7},{6,4},{7,5},{8,10},{9,11},{10,... | collective-permute-start | bytes 6488072 | tf_op jit(solution)/shard_map/ppermute | solution.py:863
  223.6 15.3 %collective-permute-start.24 = (bf16[528,2048]{1,0:T(8,128)(2,1)}, bf16[528,2048]{1,0:T(8,128)(2,1)S(1)}, u32[]{:S(2)}, u32[]{:S(2)}) collective-permute-start(bf16[528,2048]{1,0:T(8,128)(2,1)} %after.57.refs_4_.refs_6_), channel_id=1, source_target_pairs={{0,1},{1,0},{2,3},{3,2},{4,5},{5,4},{6,7},{7,6},{8,9},{9,8},{10,11... | collective-permute-start | bytes 6488072 | tf_op jit(solution)/shard_map/ppermute | solution.py:863
  223.6 29.2 %collective-permute-start.26 = (bf16[528,2048]{1,0:T(8,128)(2,1)}, bf16[528,2048]{1,0:T(8,128)(2,1)}, u32[]{:S(2)}, u32[]{:S(2)}) collective-permute-start(bf16[528,2048]{1,0:T(8,128)(2,1)} %bitcast.124.refs_2_.refs_4_), channel_id=1, source_target_pairs={{0,1},{1,0},{2,3},{3,2},{4,5},{5,4},{6,7},{7,6},{8,9},{9,8},{10,11... | collective-permute-start | bytes 6488072 | tf_op jit(solution)/shard_map/ppermute | solution.py:863
  224.1 14.8 %collective-permute-start.22 = (bf16[128,2048]{1,0:T(8,128)(2,1)S(1)}, bf16[128,2048]{1,0:T(8,128)(2,1)S(1)}, u32[]{:S(2)}, u32[]{:S(2)}) collective-permute-start(bf16[128,2048]{1,0:T(8,128)(2,1)S(1)} %copy-done.52), channel_id=1, source_target_pairs={{0,8},{8,16},{16,24},{24,28},{28,20},{20,12},{12,4},{4,0},{1,9},{9... | collective-permute-start | bytes 1572872 | tf_op jit(solution)/shard_map/ppermute | solution.py:838
  225.0 25.2 %collective-permute-start.29 = (bf16[128,2048]{1,0:T(8,128)(2,1)}, bf16[128,2048]{1,0:T(8,128)(2,1)}, u32[]{:S(2)}, u32[]{:S(2)}) collective-permute-start(bf16[128,2048]{1,0:T(8,128)(2,1)} %bitcast.73.refs_1_.refs_8_), channel_id=1, source_target_pairs={{0,8},{8,16},{16,24},{24,28},{28,20},{20,12},{12,4},{4,0},{1,9},{9... | collective-permute-start | bytes 1572872 | tf_op jit(solution)/shard_map/ppermute | solution.py:810
  227.0 24.1 %collective-permute-start.28 = (bf16[128,2048]{1,0:T(8,128)(2,1)}, bf16[128,2048]{1,0:T(8,128)(2,1)}, u32[]{:S(2)}, u32[]{:S(2)}) collective-permute-start(bf16[128,2048]{1,0:T(8,128)(2,1)} %bitcast.73.refs_1_.refs_8_), channel_id=1, source_target_pairs={{0,4},{8,0},{16,8},{24,16},{28,24},{20,28},{12,20},{4,12},{1,5},{9... | collective-permute-start | bytes 1572872 | tf_op jit(solution)/shard_map/ppermute | solution.py:810
  243.7 19.3 %collective-permute-start.27 = (bf16[128,2048]{1,0:T(8,128)(2,1)S(1)}, bf16[128,2048]{1,0:T(8,128)(2,1)}, u32[]{:S(2)}, u32[]{:S(2)}) collective-permute-start(bf16[128,2048]{1,0:T(8,128)(2,1)S(1)} %multiply_convert_fusion.refs_0_), channel_id=1, source_target_pairs={{0,4},{8,0},{16,8},{24,16},{28,24},{20,28},{12,20},{4,12},{1,5},{9... | collective-permute-start | bytes 1572872 | tf_op jit(solution)/shard_map/ppermute | solution.py:810
  245.7 19.2 %collective-permute-start.25 = (bf16[128,2048]{1,0:T(8,128)(2,1)S(1)}, bf16[128,2048]{1,0:T(8,128)(2,1)S(1)}, u32[]{:S(2)}, u32[]{:S(2)}) collective-permute-start(bf16[128,2048]{1,0:T(8,128)(2,1)S(1)} %multiply_convert_fusion.refs_0_), channel_id=1, source_target_pairs={{0,8},{8,16},{16,24},{24,28},{28,20},{20,12},{12,4},{4,0},{1,9},{9... | collective-permute-start | bytes 1572872 | tf_op jit(solution)/shard_map/ppermute | solution.py:810
  250.2 22.4 %collective-permute-start.33 = (bf16[128,2048]{1,0:T(8,128)(2,1)}, bf16[128,2048]{1,0:T(8,128)(2,1)S(1)}, u32[]{:S(2)}, u32[]{:S(2)}) collective-permute-start(bf16[128,2048]{1,0:T(8,128)(2,1)} %collective-permute-done.29.refs_4_.refs_2_.refs_10_), channel_id=1, source_target_pairs={{0,8},{8,16},{16,24},{24,28},{28,20},{20,12},{12,4},{4,0},{1,9},{9... | collective-permute-start | bytes 1572872 | tf_op jit(solution)/shard_map/ppermute | solution.py:810
  251.1 22.4 %collective-permute-start.32 = (bf16[128,2048]{1,0:T(8,128)(2,1)}, bf16[128,2048]{1,0:T(8,128)(2,1)S(1)}, u32[]{:S(2)}, u32[]{:S(2)}) collective-permute-start(bf16[128,2048]{1,0:T(8,128)(2,1)} %collective-permute-done.28.refs_3_.refs_11_), channel_id=1, source_target_pairs={{0,4},{8,0},{16,8},{24,16},{28,24},{20,28},{12,20},{4,12},{1,5},{9... | collective-permute-start | bytes 1572872 | tf_op jit(solution)/shard_map/ppermute | solution.py:810
  263.0 24.4 %collective-permute-start.31 = (bf16[128,2048]{1,0:T(8,128)(2,1)}, bf16[128,2048]{1,0:T(8,128)(2,1)S(1)}, u32[]{:S(2)}, u32[]{:S(2)}) collective-permute-start(bf16[128,2048]{1,0:T(8,128)(2,1)} %collective-permute-done.27.refs_2_.refs_1_.refs_3_), channel_id=1, source_target_pairs={{0,4},{8,0},{16,8},{24,16},{28,24},{20,28},{12,20},{4,12},{1,5},{9... | collective-permute-start | bytes 1572872 | tf_op jit(solution)/shard_map/ppermute | solution.py:810
  265.7 23.5 %collective-permute-start.30 = (bf16[128,2048]{1,0:T(8,128)(2,1)}, bf16[128,2048]{1,0:T(8,128)(2,1)}, u32[]{:S(2)}, u32[]{:S(2)}) collective-permute-start(bf16[128,2048]{1,0:T(8,128)(2,1)} %after.60.refs_0_.refs_2_), channel_id=1, source_target_pairs={{0,8},{8,16},{16,24},{24,28},{28,20},{20,12},{12,4},{4,0},{1,9},{9... | collective-permute-start | bytes 1572872 | tf_op jit(solution)/shard_map/ppermute | solution.py:810
  272.6 22.5 %collective-permute-start.37 = (bf16[128,2048]{1,0:T(8,128)(2,1)S(1)}, bf16[128,2048]{1,0:T(8,128)(2,1)S(1)}, u32[]{:S(2)}, u32[]{:S(2)}) collective-permute-start(bf16[128,2048]{1,0:T(8,128)(2,1)S(1)} %collective-permute-done.33.refs_4_.refs_2_.refs_12_), channel_id=1, source_target_pairs={{0,8},{8,16},{16,24},{24,28},{28,20},{20,12},{12,4},{4,0},{1,9},{9... | collective-permute-start | bytes 1572872 | tf_op jit(solution)/shard_map/ppermute | solution.py:810
  273.5 34.8 %collective-permute-start.36 = (bf16[128,2048]{1,0:T(8,128)(2,1)S(1)}, bf16[128,2048]{1,0:T(8,128)(2,1)}, u32[]{:S(2)}, u32[]{:S(2)}) collective-permute-start(bf16[128,2048]{1,0:T(8,128)(2,1)S(1)} %collective-permute-done.32.refs_3_.refs_13_), channel_id=1, source_target_pairs={{0,4},{8,0},{16,8},{24,16},{28,24},{20,28},{12,20},{4,12},{1,5},{9... | collective-permute-start | bytes 1572872 | tf_op jit(solution)/shard_map/ppermute | solution.py:810
  287.4 20.9 %collective-permute-start.35 = (bf16[128,2048]{1,0:T(8,128)(2,1)S(1)}, bf16[128,2048]{1,0:T(8,128)(2,1)}, u32[]{:S(2)}, u32[]{:S(2)}) collective-permute-start(bf16[128,2048]{1,0:T(8,128)(2,1)S(1)} %collective-permute-done.31.refs_2_.refs_1_.refs_5_), channel_id=1, source_target_pairs={{0,4},{8,0},{16,8},{24,16},{28,24},{20,28},{12,20},{4,12},{1,5},{9... | collective-permute-start | bytes 1572872 | tf_op jit(solution)/shard_map/ppermute | solution.py:810
  289.2 19.0 %collective-permute-start.34 = (bf16[128,2048]{1,0:T(8,128)(2,1)}, bf16[128,2048]{1,0:T(8,128)(2,1)}, u32[]{:S(2)}, u32[]{:S(2)}) collective-permute-start(bf16[128,2048]{1,0:T(8,128)(2,1)} %after.61.refs_0_.refs_4_), channel_id=1, source_target_pairs={{0,8},{8,16},{16,24},{24,28},{28,20},{20,12},{12,4},{4,0},{1,9},{9... | collective-permute-start | bytes 1572872 | tf_op jit(solution)/shard_map/ppermute | solution.py:810
  295.0 29.7 %collective-permute-start.39 = (bf16[128,2048]{1,0:T(8,128)(2,1)S(1)}, bf16[128,2048]{1,0:T(8,128)(2,1)}, u32[]{:S(2)}, u32[]{:S(2)}) collective-permute-start(bf16[128,2048]{1,0:T(8,128)(2,1)S(1)} %collective-permute-done.37.refs_4_.refs_2_.refs_14_), channel_id=1, source_target_pairs={{0,8},{8,16},{16,24},{24,28},{28,20},{20,12},{12,4},{4,0},{1,9},{9... | collective-permute-start | bytes 1572872 | tf_op jit(solution)/shard_map/ppermute | solution.py:810
  308.3 19.7 %collective-permute-start.38 = (bf16[128,2048]{1,0:T(8,128)(2,1)}, bf16[128,2048]{1,0:T(8,128)(2,1)S(1)}, u32[]{:S(2)}, u32[]{:S(2)}) collective-permute-start(bf16[128,2048]{1,0:T(8,128)(2,1)} %after.62.refs_0_.refs_6_), channel_id=1, source_target_pairs={{0,8},{8,16},{16,24},{24,28},{28,20},{20,12},{12,4},{4,0},{1,9},{9... | collective-permute-start | bytes 1572872 | tf_op jit(solution)/shard_map/ppermute | solution.py:810
  324.7 29.6 %collective-permute-start.41 = (bf16[128,2048]{1,0:T(8,128)(2,1)}, bf16[128,2048]{1,0:T(8,128)(2,1)S(1)}, u32[]{:S(2)}, u32[]{:S(2)}) collective-permute-start(bf16[128,2048]{1,0:T(8,128)(2,1)} %slice.231), channel_id=1, source_target_pairs={{0,4},{8,0},{16,8},{24,16},{28,24},{20,28},{12,20},{4,12},{1,5},{9... | collective-permute-start | bytes 1572872 | tf_op jit(solution)/shard_map/ppermute | solution.py:840
  339.0 15.2 %collective-permute-start.40 = (bf16[128,2048]{1,0:T(8,128)(2,1)}, bf16[128,2048]{1,0:T(8,128)(2,1)S(1)}, u32[]{:S(2)}, u32[]{:S(2)}) collective-permute-start(bf16[128,2048]{1,0:T(8,128)(2,1)} %get-tuple-element.101.refs_1_), channel_id=1, source_target_pairs={{0,8},{8,16},{16,24},{24,28},{28,20},{20,12},{12,4},{4,0},{1,9},{9... | collective-permute-start | bytes 1572872 | tf_op jit(solution)/shard_map/ppermute | solution.py:838
  357.8 17.7 %collective-permute-start.43 = (bf16[528,2048]{1,0:T(8,128)(2,1)}, bf16[528,2048]{1,0:T(8,128)(2,1)S(1)}, u32[]{:S(2)}, u32[]{:S(2)}) collective-permute-start(bf16[528,2048]{1,0:T(8,128)(2,1)} %after.66), channel_id=1, source_target_pairs={{0,1},{1,0},{2,3},{3,2},{4,5},{5,4},{6,7},{7,6},{8,9},{9,8},{10,11... | collective-permute-start | bytes 6488072 | tf_op jit(solution)/shard_map/ppermute | solution.py:863
  359.1 14.6 %collective-permute-start.44 = (bf16[128,2048]{1,0:T(8,128)(2,1)S(1)}, bf16[128,2048]{1,0:T(8,128)(2,1)S(1)}, u32[]{:S(2)}, u32[]{:S(2)}) collective-permute-start(bf16[128,2048]{1,0:T(8,128)(2,1)S(1)} %add_convert_fusion.13), channel_id=1, source_target_pairs={{0,4},{8,0},{16,8},{24,16},{28,24},{20,28},{12,20},{4,12},{1,5},{9... | collective-permute-start | bytes 1572872 | tf_op jit(solution)/shard_map/ppermute | solution.py:840
  382.5 70.6 %collective-permute-start.56 = (bf16[528,2048]{1,0:T(8,128)(2,1)}, bf16[528,2048]{1,0:T(8,128)(2,1)}, u32[]{:S(2)}, u32[]{:S(2)}) collective-permute-start(bf16[528,2048]{1,0:T(8,128)(2,1)} %get-tuple-element.108), channel_id=1, source_target_pairs={{0,1},{1,0},{2,3},{3,2},{4,5},{5,4},{6,7},{7,6},{8,9},{9,8},{10,11... | collective-permute-start | bytes 6488072 | tf_op jit(solution)/shard_map/ppermute | solution.py:863
  402.5 47.7 %collective-permute-start.53 = (bf16[528,2048]{1,0:T(8,128)(2,1)}, bf16[528,2048]{1,0:T(8,128)(2,1)S(1)}, u32[]{:S(2)}, u32[]{:S(2)}) collective-permute-start(bf16[528,2048]{1,0:T(8,128)(2,1)} %add_convert_fusion.1), channel_id=1, source_target_pairs={{0,2},{1,3},{2,0},{3,1},{4,6},{5,7},{6,4},{7,5},{8,10},{9,11},{10,... | collective-permute-start | bytes 6488072 | tf_op jit(solution)/shard_map/ppermute | solution.py:863
  486.4 79.7 %all-to-all-start.2 = ((bf16[8,528,256]{2,1,0:T(8,128)(2,1)}), bf16[8,528,256]{2,1,0:T(8,128)(2,1)S(1)}, u32[]{:S(2)}, u32[]{:S(2)}) async-start(bf16[8,528,256]{2,1,0:T(8,128)(2,1)} %after.79), calls=%async_computation.3 | async-start | bytes 4325376 | tf_op jit(solution)/shard_map/all_to_all | solution.py:942
  496.4 144.0 %reduce-scatter.2.cloned.1.call-start = ((), (), s32[]{:S(2)}) async-start(), calls=%async_computation.5 | async-start | bytes 4718592 | tf_op jit(solution)/shard_map/reduce_scatter | solution.py:1204
  497.1 186.8 %all-gather.3.cloned.1.call-start = ((), (), s32[]{:S(2)}) async-start(), calls=%async_computation.6 | async-start | bytes 1179648 | tf_op jit(solution)/shard_map/all_gather | solution.py:1235
  555.9 31.0 %collective-permute-start.61 = (bf16[320,2048]{1,0:T(8,128)(2,1)}, bf16[320,2048]{1,0:T(8,128)(2,1)}, u32[]{:S(2)}, u32[]{:S(2)}) collective-permute-start(bf16[320,2048]{1,0:T(8,128)(2,1)} %get-tuple-element.115), channel_id=1, source_target_pairs={{0,1},{1,0},{2,3},{3,2},{4,5},{5,4},{6,7},{7,6},{8,9},{9,8},{10,11... | collective-permute-start | bytes 3932168 | tf_op jit(solution)/shard_map/ppermute | solution.py:863
  591.5 30.1 %collective-permute-start.64 = (bf16[128,2048]{1,0:T(8,128)(2,1)}, bf16[128,2048]{1,0:T(8,128)(2,1)S(1)}, u32[]{:S(2)}, u32[]{:S(2)}) collective-permute-start(bf16[128,2048]{1,0:T(8,128)(2,1)} %get-tuple-element.146), channel_id=1, source_target_pairs={{0,4},{8,0},{16,8},{24,16},{28,24},{20,28},{12,20},{4,12},{1,5},{9... | collective-permute-start | bytes 1572872 | tf_op jit(solution)/shard_map/ppermute | solution.py:840
  593.4 28.1 %collective-permute-start.63 = (bf16[128,2048]{1,0:T(8,128)(2,1)}, bf16[128,2048]{1,0:T(8,128)(2,1)}, u32[]{:S(2)}, u32[]{:S(2)}) collective-permute-start(bf16[128,2048]{1,0:T(8,128)(2,1)} %get-tuple-element.145.refs_1_), channel_id=1, source_target_pairs={{0,8},{8,16},{16,24},{24,28},{28,20},{20,12},{12,4},{4,0},{1,9},{9... | collective-permute-start | bytes 1572872 | tf_op jit(solution)/shard_map/ppermute | solution.py:838
  596.4 44.0 %collective-permute-start.68 = (bf16[320,2048]{1,0:T(8,128)(2,1)}, bf16[320,2048]{1,0:T(8,128)(2,1)S(1)}, u32[]{:S(2)}, u32[]{:S(2)}) collective-permute-start(bf16[320,2048]{1,0:T(8,128)(2,1)} %add_convert_fusion.3), channel_id=1, source_target_pairs={{0,2},{1,3},{2,0},{3,1},{4,6},{5,7},{6,4},{7,5},{8,10},{9,11},{10,... | collective-permute-start | bytes 3932168 | tf_op jit(solution)/shard_map/ppermute | solution.py:863
  597.8 46.6 %collective-permute-start.71 = (bf16[320,2048]{1,0:T(8,128)(2,1)}, bf16[320,2048]{1,0:T(8,128)(2,1)}, u32[]{:S(2)}, u32[]{:S(2)}) collective-permute-start(bf16[320,2048]{1,0:T(8,128)(2,1)} %get-tuple-element.122), channel_id=1, source_target_pairs={{0,1},{1,0},{2,3},{3,2},{4,5},{5,4},{6,7},{7,6},{8,9},{9,8},{10,11... | collective-permute-start | bytes 3932168 | tf_op jit(solution)/shard_map/ppermute | solution.py:863
  625.2 15.0 %collective-permute-start.65 = (bf16[128,2048]{1,0:T(8,128)(2,1)}, bf16[128,2048]{1,0:T(8,128)(2,1)S(1)}, u32[]{:S(2)}, u32[]{:S(2)}) collective-permute-start(bf16[128,2048]{1,0:T(8,128)(2,1)} %get-tuple-element.143), channel_id=1, source_target_pairs={{0,8},{8,16},{16,24},{24,28},{28,20},{20,12},{12,4},{4,0},{1,9},{9... | collective-permute-start | bytes 1572872 | tf_op jit(solution)/shard_map/ppermute | solution.py:838
  626.0 14.4 %collective-permute-start.69 = (bf16[128,2048]{1,0:T(8,128)(2,1)}, bf16[128,2048]{1,0:T(8,128)(2,1)}, u32[]{:S(2)}, u32[]{:S(2)}) collective-permute-start(bf16[128,2048]{1,0:T(8,128)(2,1)} %get-tuple-element.144), channel_id=1, source_target_pairs={{0,4},{8,0},{16,8},{24,16},{28,24},{20,28},{12,20},{4,12},{1,5},{9... | collective-permute-start | bytes 1572872 | tf_op jit(solution)/shard_map/ppermute | solution.py:840
  643.0 19.5 %collective-permute-start.70 = (bf16[128,2048]{1,0:T(8,128)(2,1)S(1)}, bf16[128,2048]{1,0:T(8,128)(2,1)S(1)}, u32[]{:S(2)}, u32[]{:S(2)}) collective-permute-start(bf16[128,2048]{1,0:T(8,128)(2,1)S(1)} %add_convert_fusion.4), channel_id=1, source_target_pairs={{0,8},{8,16},{16,24},{24,28},{28,20},{20,12},{12,4},{4,0},{1,9},{9... | collective-permute-start | bytes 1572872 | tf_op jit(solution)/shard_map/ppermute | solution.py:838
  648.0 49.4 %all-to-all-start.3 = ((bf16[8,320,256]{2,1,0:T(8,128)(2,1)}), bf16[8,320,256]{2,1,0:T(8,128)(2,1)}, u32[]{:S(2)}, u32[]{:S(2)}) async-start(bf16[8,320,256]{2,1,0:T(8,128)(2,1)} %bitcast.228), calls=%async_computation.4 | async-start | bytes 2621440 | tf_op jit(solution)/shard_map/all_to_all | solution.py:942
  (111 other events, 718.9 us)
Sparse Core Ops, SparseCore 0:
  500.9 121.2 reduce-scatter.1
  627.4 56.4 all-gather.2

commit v7 on v6

--- a/solution.py
+++ b/solution.py
@@ -800,32 +800,31 @@
     return [arrived[0], arrived[-1]] + list(arrived[1:-1])
 
 
+def ring_step(blocks, s, size):
+    ahead = lax.ppermute(blocks[0], "seq", ring_pairs(size, 1))
+    if s == size // 2:
+        return (ahead,)
+    return ahead, lax.ppermute(blocks[-1], "seq", ring_pairs(size, -1))
+
+
 def ring_gather(block, size, work=None, beside=None):
     arrived = [(block,)]
-    others = [(beside,)]
-    ahead = back = block
-    ahead_too = back_too = beside
-
-    def move(value, step):
-        return None if value is None else lax.ppermute(value, "seq", ring_pairs(size, step))
+    others = list(beside or ())
 
     def do_work(s):
         if not work:
             return []
-        return list(work(s, arrived[s], others[s]) if beside is not None else work(s, arrived[s]))
+        return list(work(s, arrived[s], others[s]) if others else work(s, arrived[s]))
 
     for s in range(1, size // 2 + 1):
-        last = s == size // 2
         done = do_work(s - 1)
-        ahead, ahead_too = move(ahead, 1), move(ahead_too, 1)
-        if not last:
-            back, back_too = move(back, -1), move(back_too, -1)
-            done += [back, back_too]
-        done = [item for item in done + [ahead_too] if item is not None]
-        if done:
-            ahead = after(ahead, *done)
-        arrived.append((ahead,) if last else (ahead, back))
-        others.append((ahead_too,) if last else (ahead_too, back_too))
+        moved = ring_step(arrived[-1], s, size)
+        done += moved[1:]
+        if others and len(others) <= size // 2:
+            others.append(ring_step(others[-1], len(others), size))
+            done += others[-1]
+        ahead = after(moved[0], *done) if done else moved[0]
+        arrived.append((ahead,) + moved[1:])
     do_work(size // 2)
     return arrived
 
@@ -1101,6 +1100,8 @@
     )
     rest_block = exchange(after(own["rest"], token_steps[-1][0]))
     grad_own = cotangent[0]
+    grad_steps = [(after(grad_own, rest_block),)]
+    grad_steps.append(ring_step(grad_steps[0], 1, seq))
 
     inner, *kept = chain_forward(slot_of_member, docs, x3, logits, gb, init, rows_tok)
     side_rows = rest_block.shape[1] - 3 * padded
@@ -1132,7 +1133,7 @@
         return ffn["parts"][-1:]
 
     mixing = ring_scatter(
-        by_distance(mm(gated, m_out).astype(BF16)),
+        by_distance(after(mm(gated, m_out).astype(BF16), *grad_steps[1])),
         seq,
         [lambda since: [], lambda since: [], lambda since: [], ffn_corner],
     )
@@ -1157,7 +1158,7 @@
             d_parts[steps[slot + i]] = d_in[i * rows_tok : (i + 1) * rows_tok]
         return [d_in]
 
-    ring_gather(ffn_in, seq, step_work, grad_own)
+    ring_gather(ffn_in, seq, step_work, grad_steps)
     kept_ffn = got["kept"]
 
     def ffn_work(since):
@@ -1238,18 +1239,18 @@
 
     def corner_work(since):
         if not plan.mixed:
-            return []
+            return [ffn_out]
         block = heads_block(plan, head_rows_grads)
         got["corner"] = start_scatter(block)
         got["across"] = cross_scatter(block, after(got["corner"], flat))
-        return [got["corner"]]
+        return [got["corner"], ffn_out]
 
     def join_work(since):
         got["join"] = join_features(after(g_ffn, since), w_down.shape[0], (False,) * 3)
         return got["join"][:1]
 
     def across_work(since):
-        return [ffn_out] + ([got["across"]] if plan.mixed else [])
+        return [got["across"]] if plan.mixed else []
 
     d_normed = ring_scatter(
         by_distance(d_normed_part), seq, [corner_work, join_work, across_work]

time: 718 us -> 711 us (level)
  waiting for transfers between devices: 265 us -> 241 us
  starting transfers between devices: 96.6 us -> 111 us
    ppermute x9, waiting for transfers between devices: 47.4 us -> 32.5 us  [ring_scatter(): back = lax.ppermute(back, 'seq', ring_pairs(size, -1))]
    ppermute x8, starting transfers between devices: 11.4 us -> 23.8 us  [pairwise_sum(): lax.ppermute(value, axis, [(i, i ^ bit) for i in range(size)])]
    all_gather x1, waiting for transfers between devices: 18.9 us -> 10.6 us  [body(): flat_all = lax.all_gather(flat, 'seq', axis=0)]
    all_to_all x4, waiting for transfers between devices: 21.5 us -> 13.7 us  [exchange(): return lax.all_to_all(block, 'seq', 0, 0, tiled=True)]
    ppermute x15, waiting for transfers between devices: 24.4 us -> 31.8 us  [swap(): return lax.ppermute(value, 'grp', [(i, i ^ bit) for i in range(4)])]
    unnamed x175 -> x194, local copies, waits for them, and re-layouts: 39.5 us -> 37.2 us
  transfers between devices with their start and end apart: 78 -> 78, of which waited for: 43 -> 43; matrix products, arithmetic and copies ran while one was open for 16% -> 18% of each run, Pallas kernels for 24% -> 24%
where the time goes in v7:
time: 711 us; the launch traced here: 698 us
  waiting for transfers between devices  241 us (34%)
  Pallas kernels  172 us (24%)
  starting transfers between devices  111 us (16%)
  local copies, waits for them, and re-layouts  70.6 us (10%)
  other arithmetic  64.5 us (9%)
  matrix products  24.5 us (3%)
  between operations  15.6 us (2%)
    ppermute x12, waiting for transfers between devices, ring_scatter(): ahead = lax.ppermute(ahead, 'seq', ring_pairs(size, 1))  72.6 us
    pallas_call x5, Pallas kernels, ffn_step(): pl.pallas_call(partial(ffn_kernel, count, len(weights), len(kept)), grid_...  57.4 us
    ppermute x16, waiting for transfers between devices, ring_step(): ahead = lax.ppermute(blocks[0], 'seq', ring_pairs(size, 1))  45.7 us
    pallas_call x1, Pallas kernels, chain_backward(): pl.pallas_call(partial(backward_kernel, heads), grid_spec=pltpu.PrefetchS...  37.5 us
    unnamed x194, local copies, waits for them, and re-layouts  37.2 us
    ppermute x9, waiting for transfers between devices, ring_scatter(): back = lax.ppermute(back, 'seq', ring_pairs(size, -1))  32.5 us
    ppermute x15, waiting for transfers between devices, swap(): return lax.ppermute(value, 'grp', [(i, i ^ bit) for i in range(4)])  31.8 us
    pallas_call x1, Pallas kernels, chain_forward(): pl.pallas_call(partial(forward_kernel, heads), grid_spec=pltpu.PrefetchSc...  24.6 us
  transfers between devices with their start and end apart: 78, of which 43 were waited for; matrix products, arithmetic and copies ran while one was open for 18% of the time, Pallas kernels for 24%

profile of v7, /device:TPU:0, one launch (start us, length us, event | category | flops | bytes accessed | tf_op | source)
XLA Modules:
  0.0 698.1 jit_solution(7524364377997841920)
XLA Ops:
  12.6 6.2 all-to-all-start
  30.3 11.4 %all-to-all-done.refs_0_ = bf16[8,192,256]{2,1,0:T(8,128)(2,1)S(1)} async-done(((bf16[8,192,256]{2,1,0:T(8,128)(2,1)}), bf16[8,192,256]{2,1,0:T(8,128)(2,1)S(1)}, u32[]{:S(2)}, u32[]{:S(2)}) %all-to-all-start) | async-done | bytes 786464 | tf_op jit(solution)/shard_map/all_to_all | solution.py:941
  45.3 3.2 fusion.87.refs_4_.refs_13_
  50.2 3.1 collective-permute-start.5
  54.1 6.7 collective-permute-done.7.refs_10_
  60.9 3.8 cut_features.2.refs_1_.refs_0_
  67.0 13.4 %collective-permute-done.6.refs_0_ = bf16[128,2048]{1,0:T(8,128)(2,1)S(1)} collective-permute-done((bf16[128,2048]{1,0:T(8,128)(2,1)}, bf16[128,2048]{1,0:T(8,128)(2,1)S(1)}, u32[]{:S(2)}, u32[]{:S(2)}) %collective-permute-start.6) | collective-permute-done | bytes 524320 | tf_op jit(solution)/shard_map/ppermute | solution.py:804
  82.1 4.4 all-to-all-start.1
  89.1 10.5 %project.1 = (bf16[1024,2048]{1,0:T(8,128)(2,1)}, bf16[1024,768]{1,0:T(8,128)(2,1)}, f32[1024,128]{1,0:T(8,128)}) custom-call(bf16[128,2048]{1,0:T(8,128)(2,1)} %bitcast.240, bf16[128,2048]{1,0:T(8,128)(2,1)} %after.51.refs_1_, bf16[128,2048]{1,0:T(8,128)(2,1)} %after.47.refs_1_.refs_2_, bf16[128,2048]{1,0:T(8,128)(2,1)} %copy-done.48, ...), custom_call_target="tpu_custom_call" | custom-call | flops 1 | bytes 1 | tf_op jit(solution)/shard_map/project/pallas_call | solution.py:743
  99.6 24.6 %chain_forward.1 = (f32[1024,256]{1,0:T(8,128)}, f32[64,4096]{1,0:T(8,128)}, f32[64,4096]{1,0:T(8,128)}, f32[64,4096]{1,0:T(8,128)}, f32[8,4096]{1,0:T(8,128)}, /*index=5*/f32[8,64,384]{2,1,0:T(8,128)}) custom-call(s32[8]{0:T(128)} %get-tuple-element.222.refs_6_.idx_ref, s32[5]{0:T(128)} %pad_add_fusion.refs_5_.docs_ref, ...), custom_call_target="tpu_custom_call" | custom-call | flops 1 | bytes 1 | tf_op jit(solution)/shard_map/chain_forward/pallas_call | solution.py:391
  136.9 10.5 %collective-permute-done.15 = f32[2,1024]{1,0:T(2,128)S(1)} collective-permute-done((f32[2,1024]{1,0:T(2,128)S(1)}, f32[2,1024]{1,0:T(2,128)S(1)}, u32[]{:S(2)}, u32[]{:S(2)}) %collective-permute-start.15) | collective-permute-done | bytes 8224 | tf_op jit(solution)/shard_map/ppermute | solution.py:856
  155.6 9.5 %collective-permute-done.11 = bf16[128,2048]{1,0:T(8,128)(2,1)S(1)} collective-permute-done((bf16[128,2048]{1,0:T(8,128)(2,1)S(1)}, bf16[128,2048]{1,0:T(8,128)(2,1)S(1)}, u32[]{:S(2)}, u32[]{:S(2)}) %collective-permute-start.11) | collective-permute-done | bytes 524320 | tf_op jit(solution)/shard_map/ppermute | solution.py:862
  170.4 3.3 convolution_convert_fusion.1.refs_0_
  180.6 8.6 %collective-permute-done.18.refs_0_ = bf16[128,2048]{1,0:T(8,128)(2,1)S(1)} collective-permute-done((bf16[128,2048]{1,0:T(8,128)(2,1)S(1)}, bf16[128,2048]{1,0:T(8,128)(2,1)S(1)}, u32[]{:S(2)}, u32[]{:S(2)}) %collective-permute-start.18) | collective-permute-done | bytes 524320 | tf_op jit(solution)/shard_map/ppermute | solution.py:837
  194.2 11.1 %collective-permute-done.20.refs_0_ = bf16[128,2048]{1,0:T(8,128)(2,1)S(1)} collective-permute-done((bf16[128,2048]{1,0:T(8,128)(2,1)S(1)}, bf16[128,2048]{1,0:T(8,128)(2,1)S(1)}, u32[]{:S(2)}, u32[]{:S(2)}) %collective-permute-start.20) | collective-permute-done | bytes 524320 | tf_op jit(solution)/shard_map/ppermute | solution.py:837
  211.3 9.8 %collective-permute-done.22.refs_0_ = bf16[128,2048]{1,0:T(8,128)(2,1)S(1)} collective-permute-done((bf16[128,2048]{1,0:T(8,128)(2,1)S(1)}, bf16[128,2048]{1,0:T(8,128)(2,1)S(1)}, u32[]{:S(2)}, u32[]{:S(2)}) %collective-permute-start.22) | collective-permute-done | bytes 524320 | tf_op jit(solution)/shard_map/ppermute | solution.py:837
  233.0 11.6 %collective-permute-done.24.refs_0_ = bf16[128,2048]{1,0:T(8,128)(2,1)S(1)} collective-permute-done((bf16[128,2048]{1,0:T(8,128)(2,1)S(1)}, bf16[128,2048]{1,0:T(8,128)(2,1)S(1)}, u32[]{:S(2)}, u32[]{:S(2)}) %collective-permute-start.24) | collective-permute-done | bytes 524320 | tf_op jit(solution)/shard_map/ppermute | solution.py:837
  252.1 3.9 collective-permute-done.30.refs_3_.refs_2_.refs_12_
  258.0 10.2 %ffn_step.5 = (bf16[704,1024]{1,0:T(8,128)(2,1)}, bf16[704,1024]{1,0:T(8,128)(2,1)}, bf16[704,1024]{1,0:T(8,128)(2,1)}, bf16[8,128,2048]{2,1,0:T(8,128)(2,1)}, bf16[128,2048]{1,0:T(8,128)(2,1)}) custom-call(s32[1]{0:T(128)} %get-tuple-element.217.member_ref, bf16[128,2048]{1,0:T(8,128)(2,1)} %copy-done.27, bf16[128,2048]{1,0:T(8,128)(2,1)} %after.54.refs_1_.refs_8_, ...), custom_call_target="tpu_custom_call" | custom-call | flops 1 | bytes 1 | tf_op jit(solution)/shard_map/ffn_step/pallas_call | solution.py:597
  271.6 6.7 collective-permute-done.34.refs_3_.refs_2_.refs_14_
  279.9 12.3 %ffn_step.6 = (bf16[704,1024]{1,0:T(8,128)(2,1)}, bf16[704,1024]{1,0:T(8,128)(2,1)}, bf16[704,1024]{1,0:T(8,128)(2,1)}, bf16[8,128,2048]{2,1,0:T(8,128)(2,1)}, bf16[256,2048]{1,0:T(8,128)(2,1)}) custom-call(s32[2]{0:T(128)} %get-tuple-element.216.member_ref, ...), custom_call_target="tpu_custom_call", output_to_operand_aliasing={{0}: (9, {}), {1}: (10, {}), {2}: (11, {}), {3}: (12, {})} | custom-call | flops 1 | bytes 1 | tf_op jit(solution)/shard_map/ffn_step/pallas_call | solution.py:597
  295.2 12.4 %ffn_step.7 = (bf16[704,1024]{1,0:T(8,128)(2,1)}, bf16[704,1024]{1,0:T(8,128)(2,1)}, bf16[704,1024]{1,0:T(8,128)(2,1)}, bf16[8,128,2048]{2,1,0:T(8,128)(2,1)}, bf16[256,2048]{1,0:T(8,128)(2,1)}) custom-call(s32[2]{0:T(128)} %get-tuple-element.215.member_ref, ...), custom_call_target="tpu_custom_call", output_to_operand_aliasing={{0}: (9, {}), {1}: (10, {}), {2}: (11, {}), {3}: (12, {})} | custom-call | flops 1 | bytes 1 | tf_op jit(solution)/shard_map/ffn_step/pallas_call | solution.py:597
  307.6 3.5 collective-permute-done.36.refs_0_
  313.2 12.3 %ffn_step.8 = (bf16[704,1024]{1,0:T(8,128)(2,1)}, bf16[704,1024]{1,0:T(8,128)(2,1)}, bf16[704,1024]{1,0:T(8,128)(2,1)}, bf16[8,128,2048]{2,1,0:T(8,128)(2,1)}, bf16[256,2048]{1,0:T(8,128)(2,1)}) custom-call(s32[2]{0:T(128)} %get-tuple-element.214.member_ref, ...), custom_call_target="tpu_custom_call", output_to_operand_aliasing={{0}: (9, {}), {1}: (10, {}), {2}: (11, {}), {3}: (12, {})} | custom-call | flops 1 | bytes 1 | tf_op jit(solution)/shard_map/ffn_step/pallas_call | solution.py:597
  329.1 10.3 %ffn_step.9 = (bf16[704,1024]{1,0:T(8,128)(2,1)}, bf16[704,1024]{1,0:T(8,128)(2,1)}, bf16[704,1024]{1,0:T(8,128)(2,1)}, bf16[8,128,2048]{2,1,0:T(8,128)(2,1)}, bf16[128,2048]{1,0:T(8,128)(2,1)}) custom-call(s32[1]{0:T(128)} %get-tuple-element.218.member_ref, ...), custom_call_target="tpu_custom_call", output_to_operand_aliasing={{0}: (7, {}), {1}: (8, {}), {2}: (9, {}), {3}: (10, {})} | custom-call | flops 1 | bytes 1 | tf_op jit(solution)/shard_map/ffn_step/pallas_call | solution.py:597
  340.4 14.5 %ffn_grads.1 = (bf16[528,2048]{1,0:T(8,128)(2,1)}, bf16[528,2048]{1,0:T(8,128)(2,1)}, bf16[528,2048]{1,0:T(8,128)(2,1)}, bf16[528,2048]{1,0:T(8,128)(2,1)}) custom-call(bf16[704,1024]{1,0:T(8,128)(2,1)} %after.68.at_ref, bf16[704,1024]{1,0:T(8,128)(2,1)} %get-tuple-element.103.ut_ref, bf16[704,1024]{1,0:T(8,128)(2,1)} %get-tuple-element.104.ht_ref, ...), custom_call_target="tpu_custom_call" | custom-call | flops 1 | bytes 1 | tf_op jit(solution)/shard_map/ffn_grads/pallas_call | solution.py:645
  361.9 12.3 %collective-permute-done.44.refs_2_.refs_0_ = bf16[128,2048]{1,0:T(8,128)(2,1)S(1)} collective-permute-done((bf16[128,2048]{1,0:T(8,128)(2,1)S(1)}, bf16[128,2048]{1,0:T(8,128)(2,1)S(1)}, u32[]{:S(2)}, u32[]{:S(2)}) %collective-permute-start.44) | collective-permute-done | bytes 524320 | tf_op jit(solution)/shard_map/ppermute | solution.py:839
  382.9 11.7 %collective-permute-done.46.refs_1_.refs_0_ = bf16[128,2048]{1,0:T(8,128)(2,1)} collective-permute-done((bf16[128,2048]{1,0:T(8,128)(2,1)S(1)}, bf16[128,2048]{1,0:T(8,128)(2,1)}, u32[]{:S(2)}, u32[]{:S(2)}) %collective-permute-start.46) | collective-permute-done | bytes 524320 | tf_op jit(solution)/shard_map/ppermute | solution.py:839
  399.0 3.8 add_convert_fusion.1
  404.2 6.3 collective-permute-done.47
  429.3 9.8 %collective-permute-done.51.refs_1_.refs_5_ = bf16[128,2048]{1,0:T(8,128)(2,1)} collective-permute-done((bf16[128,2048]{1,0:T(8,128)(2,1)}, bf16[128,2048]{1,0:T(8,128)(2,1)}, u32[]{:S(2)}, u32[]{:S(2)}) %collective-permute-start.51) | collective-permute-done | bytes 524320 | tf_op jit(solution)/shard_map/ppermute | solution.py:807
  443.5 6.8 collective-permute-done.53.refs_1_.refs_0_
  453.2 3.5 add_convert_fusion
  458.3 17.6 %collective-permute-done.55.refs_0_ = bf16[128,2048]{1,0:T(8,128)(2,1)} collective-permute-done((bf16[128,2048]{1,0:T(8,128)(2,1)}, bf16[128,2048]{1,0:T(8,128)(2,1)}, u32[]{:S(2)}, u32[]{:S(2)}) %collective-permute-start.55) | collective-permute-done | bytes 524320 | tf_op jit(solution)/shard_map/ppermute | solution.py:804
  485.5 9.6 %collective-permute-start.57 = (f32[2,1024]{1,0:T(2,128)S(1)}, f32[2,1024]{1,0:T(2,128)S(1)}, u32[]{:S(2)}, u32[]{:S(2)}) collective-permute-start(f32[2,1024]{1,0:T(2,128)S(1)} %bitcast.284), channel_id=1, source_target_pairs={{0,4},{4,0},{8,12},{12,8},{16,20},{20,16},{24,28},{28,24},{1,5},{5... | collective-permute-start | bytes 24584 | tf_op jit(solution)/shard_map/ppermute | solution.py:856
  496.8 3.1 collective-permute-start.58
  506.9 6.6 all-to-all-start.2
  516.8 37.5 %chain_backward.1 = (bf16[1024,1152]{1,0:T(8,128)(2,1)}, f32[2,64,128]{2,1,0:T(8,128)}, f32[64,384]{1,0:T(8,128)}) custom-call(s32[8]{0:T(128)} %get-tuple-element.222.refs_6_.idx_ref, s32[5]{0:T(128)} %pad_add_fusion.refs_5_.docs_ref, bf16[1024,768]{1,0:T(8,128)(2,1)} %get-tuple-element.76.x_ref, f32[1024,256]{1,0:T(8,128)} %subtract_multiply_fusion.d_ref, ...), custom_call_target="tpu_custom_call" | custom-call | flops 1 | bytes 1 | tf_op jit(solution)/shard_map/chain_backward/pallas_call | solution.py:423
  554.4 14.1 %proj_grads.1 = (bf16[320,2048]{1,0:T(8,128)(2,1)}, bf16[320,2048]{1,0:T(8,128)(2,1)}, bf16[320,2048]{1,0:T(8,128)(2,1)}, bf16[320,2048]{1,0:T(8,128)(2,1)}, f32[8,2048]{1,0:T(8,128)}, /*index=5*/f32[8,2048]{1,0:T(8,128)}) custom-call(bf16[1024,1152]{1,0:T(8,128)(2,1)} %get-tuple-element.113.d_ref.refs_0_, bf16[1024,2048]{1,0:T(8,128)(2,1)} %get-tuple-element.75.x_ref, ...), custom_call_target="tpu_custom_call" | custom-call | flops 1 | bytes 1 | tf_op jit(solution)/shard_map/proj_grads/pallas_call | solution.py:697
  573.7 8.2 %convolution_convert_fusion = bf16[1024,2048]{1,0:T(8,128)(2,1)S(1)} fusion(bf16[1024,1152]{1,0:T(8,128)(2,1)} %after.84, bf16[1152,2048]{1,0:T(8,128)(2,1)} %constant_dynamic-update-slice_fusion.refs_1_.w_ref), kind=kOutput, calls=%fused_computation.2 | convolution fusion | flops 4833935360 | bytes 11272192 | tf_op jit(solution)/shard_map/dot_general | solution.py:18
  589.0 4.1 collective-permute-done.67
  593.8 3.8 collective-permute-done.60.refs_0_
  608.9 4.0 join_features.2
  622.5 10.5 %collective-permute-done.65.refs_0_ = bf16[128,2048]{1,0:T(8,128)(2,1)S(1)} collective-permute-done((bf16[128,2048]{1,0:T(8,128)(2,1)}, bf16[128,2048]{1,0:T(8,128)(2,1)S(1)}, u32[]{:S(2)}, u32[]{:S(2)}) %collective-permute-start.65) | collective-permute-done | bytes 524320 | tf_op jit(solution)/shard_map/ppermute | solution.py:837
  633.8 3.4 collective-permute-done.68.refs_1_
  645.1 4.8 all-to-all-start.3
  650.9 8.1 %collective-permute-done.70 = bf16[128,2048]{1,0:T(8,128)(2,1)S(1)} collective-permute-done((bf16[128,2048]{1,0:T(8,128)(2,1)S(1)}, bf16[128,2048]{1,0:T(8,128)(2,1)S(1)}, u32[]{:S(2)}, u32[]{:S(2)}) %collective-permute-start.70) | collective-permute-done | bytes 524320 | tf_op jit(solution)/shard_map/ppermute | solution.py:837
  661.4 10.6 %all-gather.3.cloned.1.call-done = f32[256,1024]{1,0:T(8,128)} async-done(((f32[32,1024]{1,0:T(8,128)}), f32[256,1024]{1,0:T(8,128)}) %all-gather.3.cloned.1.call-update) | async-done | bytes 1048592 | tf_op jit(solution)/shard_map/all_gather | solution.py:1236
  (504 shorter events, 244.7 us)
Async XLA Ops:
  7.2 19.4 %collective-permute-start.1 = (bf16[128,2048]{1,0:T(8,128)(2,1)}, bf16[128,2048]{1,0:T(8,128)(2,1)S(1)}, u32[]{:S(2)}, u32[]{:S(2)}) collective-permute-start(bf16[128,2048]{1,0:T(8,128)(2,1)} %bitcast.238), channel_id=1, source_target_pairs={{0,4},{8,0},{16,8},{24,16},{28,24},{20,28},{12,20},{4,12},{1,5},{9... | collective-permute-start | bytes 1572872 | tf_op jit(solution)/shard_map/ppermute | solution.py:807
  10.2 16.4 %collective-permute-start = (bf16[128,2048]{1,0:T(8,128)(2,1)}, bf16[128,2048]{1,0:T(8,128)(2,1)S(1)}, u32[]{:S(2)}, u32[]{:S(2)}) collective-permute-start(bf16[128,2048]{1,0:T(8,128)(2,1)} %bitcast.239), channel_id=1, source_target_pairs={{0,8},{8,16},{16,24},{24,28},{28,20},{20,12},{12,4},{4,0},{1,9},{9... | collective-permute-start | bytes 1572872 | tf_op jit(solution)/shard_map/ppermute | solution.py:804
  12.6 29.0 %all-to-all-start = ((bf16[8,192,256]{2,1,0:T(8,128)(2,1)}), bf16[8,192,256]{2,1,0:T(8,128)(2,1)S(1)}, u32[]{:S(2)}, u32[]{:S(2)}) async-start(bf16[8,192,256]{2,1,0:T(8,128)(2,1)} %cut_features.3), calls=%async_computation | async-start | bytes 1572864 | tf_op jit(solution)/shard_map/all_to_all | solution.py:941
  28.2 25.1 %collective-permute-start.2 = (bf16[128,2048]{1,0:T(8,128)(2,1)}, bf16[128,2048]{1,0:T(8,128)(2,1)S(1)}, u32[]{:S(2)}, u32[]{:S(2)}) collective-permute-start(bf16[128,2048]{1,0:T(8,128)(2,1)} %after.47.refs_1_.refs_2_), channel_id=1, source_target_pairs={{0,8},{8,16},{16,24},{24,28},{28,20},{20,12},{12,4},{4,0},{1,9},{9... | collective-permute-start | bytes 1572872 | tf_op jit(solution)/shard_map/ppermute | solution.py:804
  30.2 20.0 %collective-permute-start.3 = (bf16[128,2048]{1,0:T(8,128)(2,1)}, bf16[128,2048]{1,0:T(8,128)(2,1)S(1)}, u32[]{:S(2)}, u32[]{:S(2)}) collective-permute-start(bf16[128,2048]{1,0:T(8,128)(2,1)} %copy-done.48), channel_id=1, source_target_pairs={{0,4},{8,0},{16,8},{24,16},{28,24},{20,28},{12,20},{4,12},{1,5},{9... | collective-permute-start | bytes 1572872 | tf_op jit(solution)/shard_map/ppermute | solution.py:807
  43.7 17.1 %collective-permute-start.7 = (bf16[192,2048]{1,0:T(8,128)(2,1)S(1)}, bf16[192,2048]{1,0:T(8,128)(2,1)S(1)}, u32[]{:S(2)}, u32[]{:S(2)}) collective-permute-start(bf16[192,2048]{1,0:T(8,128)(2,1)S(1)} %bitcast.233), channel_id=1, source_target_pairs={{0,2},{1,3},{2,0},{3,1},{4,6},{5,7},{6,4},{7,5},{8,10},{9,11},{10,... | collective-permute-start | bytes 2359304 | tf_op jit(solution)/shard_map/ppermute | solution.py:862
  50.2 14.5 %collective-permute-start.5 = (bf16[128,2048]{1,0:T(8,128)(2,1)S(1)}, bf16[128,2048]{1,0:T(8,128)(2,1)}, u32[]{:S(2)}, u32[]{:S(2)}) collective-permute-start(bf16[128,2048]{1,0:T(8,128)(2,1)S(1)} %collective-permute-done.3.refs_8_.refs_5_), channel_id=1, source_target_pairs={{0,4},{8,0},{16,8},{24,16},{28,24},{20,28},{12,20},{4,12},{1,5},{9... | collective-permute-start | bytes 1572872 | tf_op jit(solution)/shard_map/ppermute | solution.py:807
  60.9 19.6 %collective-permute-start.8 = (bf16[192,2048]{1,0:T(8,128)(2,1)S(1)}, bf16[192,2048]{1,0:T(8,128)(2,1)S(1)}, u32[]{:S(2)}, u32[]{:S(2)}) collective-permute-start(bf16[192,2048]{1,0:T(8,128)(2,1)S(1)} %collective-permute-done.7.refs_10_), channel_id=1, source_target_pairs={{0,1},{1,0},{2,3},{3,2},{4,5},{5,4},{6,7},{7,6},{8,9},{9,8},{10,11... | collective-permute-start | bytes 2359304 | tf_op jit(solution)/shard_map/ppermute | solution.py:862
  65.5 14.9 %collective-permute-start.6 = (bf16[128,2048]{1,0:T(8,128)(2,1)}, bf16[128,2048]{1,0:T(8,128)(2,1)S(1)}, u32[]{:S(2)}, u32[]{:S(2)}) collective-permute-start(bf16[128,2048]{1,0:T(8,128)(2,1)} %after.49.refs_6_), channel_id=1, source_target_pairs={{0,8},{8,16},{16,24},{24,28},{28,20},{20,12},{12,4},{4,0},{1,9},{9... | collective-permute-start | bytes 1572872 | tf_op jit(solution)/shard_map/ppermute | solution.py:804
  82.1 65.8 %all-to-all-start.1 = ((bf16[8,656,256]{2,1,0:T(8,128)(2,1)}), bf16[8,656,256]{2,1,0:T(8,128)(2,1)S(1)}, u32[]{:S(2)}, u32[]{:S(2)}) async-start(bf16[8,656,256]{2,1,0:T(8,128)(2,1)} %after.52), calls=%async_computation.1 | async-start | bytes 5373952 | tf_op jit(solution)/shard_map/all_to_all | solution.py:941
  86.5 512.3 %reduce-scatter.2.cloned.1.call-start = ((), (), s32[]{:S(2)}) async-start(), calls=%async_computation.5 | async-start | bytes 4718592 | tf_op jit(solution)/shard_map/reduce_scatter | solution.py:1205
  133.0 14.3 %collective-permute-start.15 = (f32[2,1024]{1,0:T(2,128)S(1)}, f32[2,1024]{1,0:T(2,128)S(1)}, u32[]{:S(2)}, u32[]{:S(2)}) collective-permute-start(f32[2,1024]{1,0:T(2,128)S(1)} %add.416), channel_id=1, source_target_pairs={{0,16},{4,20},{8,24},{12,28},{16,0},{20,4},{24,8},{28,12},{1,17},{... | collective-permute-start | bytes 24584 | tf_op jit(solution)/shard_map/ppermute | solution.py:856
  149.5 24.3 %collective-permute-start.17 = (bf16[128,2048]{1,0:T(8,128)(2,1)}, bf16[128,2048]{1,0:T(8,128)(2,1)}, u32[]{:S(2)}, u32[]{:S(2)}) collective-permute-start(bf16[128,2048]{1,0:T(8,128)(2,1)} %after.54.refs_1_.refs_8_), channel_id=1, source_target_pairs={{0,4},{8,0},{16,8},{24,16},{28,24},{20,28},{12,20},{4,12},{1,5},{9... | collective-permute-start | bytes 1572872 | tf_op jit(solution)/shard_map/ppermute | solution.py:807
  150.9 22.8 %collective-permute-start.16 = (bf16[128,2048]{1,0:T(8,128)(2,1)}, bf16[128,2048]{1,0:T(8,128)(2,1)}, u32[]{:S(2)}, u32[]{:S(2)}) collective-permute-start(bf16[128,2048]{1,0:T(8,128)(2,1)} %after.54.refs_1_.refs_8_), channel_id=1, source_target_pairs={{0,8},{8,16},{16,24},{24,28},{28,20},{20,12},{12,4},{4,0},{1,9},{9... | collective-permute-start | bytes 1572872 | tf_op jit(solution)/shard_map/ppermute | solution.py:804
  176.0 14.3 %collective-permute-start.19 = (bf16[128,2048]{1,0:T(8,128)(2,1)S(1)}, bf16[128,2048]{1,0:T(8,128)(2,1)}, u32[]{:S(2)}, u32[]{:S(2)}) collective-permute-start(bf16[128,2048]{1,0:T(8,128)(2,1)S(1)} %get-tuple-element.154), channel_id=1, source_target_pairs={{0,4},{8,0},{16,8},{24,16},{28,24},{20,28},{12,20},{4,12},{1,5},{9... | collective-permute-start | bytes 1572872 | tf_op jit(solution)/shard_map/ppermute | solution.py:839
  179.1 48.8 %collective-permute-start.25 = (bf16[528,2048]{1,0:T(8,128)(2,1)}, bf16[528,2048]{1,0:T(8,128)(2,1)S(1)}, u32[]{:S(2)}, u32[]{:S(2)}) collective-permute-start(bf16[528,2048]{1,0:T(8,128)(2,1)} %bitcast.124.refs_2_.refs_4_), channel_id=1, source_target_pairs={{0,2},{1,3},{2,0},{3,1},{4,6},{5,7},{6,4},{7,5},{8,10},{9,11},{10,... | collective-permute-start | bytes 6488072 | tf_op jit(solution)/shard_map/ppermute | solution.py:862
  229.3 15.3 %collective-permute-start.26 = (bf16[528,2048]{1,0:T(8,128)(2,1)}, bf16[528,2048]{1,0:T(8,128)(2,1)S(1)}, u32[]{:S(2)}, u32[]{:S(2)}) collective-permute-start(bf16[528,2048]{1,0:T(8,128)(2,1)} %after.61.refs_4_.refs_6_), channel_id=1, source_target_pairs={{0,1},{1,0},{2,3},{3,2},{4,5},{5,4},{6,7},{7,6},{8,9},{9,8},{10,11... | collective-permute-start | bytes 6488072 | tf_op jit(solution)/shard_map/ppermute | solution.py:862
  229.3 28.7 %collective-permute-start.28 = (bf16[528,2048]{1,0:T(8,128)(2,1)}, bf16[528,2048]{1,0:T(8,128)(2,1)}, u32[]{:S(2)}, u32[]{:S(2)}) collective-permute-start(bf16[528,2048]{1,0:T(8,128)(2,1)} %bitcast.124.refs_2_.refs_4_), channel_id=1, source_target_pairs={{0,1},{1,0},{2,3},{3,2},{4,5},{5,4},{6,7},{7,6},{8,9},{9,8},{10,11... | collective-permute-start | bytes 6488072 | tf_op jit(solution)/shard_map/ppermute | solution.py:862
  229.8 14.8 %collective-permute-start.24 = (bf16[128,2048]{1,0:T(8,128)(2,1)S(1)}, bf16[128,2048]{1,0:T(8,128)(2,1)S(1)}, u32[]{:S(2)}, u32[]{:S(2)}) collective-permute-start(bf16[128,2048]{1,0:T(8,128)(2,1)S(1)} %copy-done.51), channel_id=1, source_target_pairs={{0,8},{8,16},{16,24},{24,28},{28,20},{20,12},{12,4},{4,0},{1,9},{9... | collective-permute-start | bytes 1572872 | tf_op jit(solution)/shard_map/ppermute | solution.py:837
  231.0 26.1 %collective-permute-start.31 = (bf16[128,2048]{1,0:T(8,128)(2,1)}, bf16[128,2048]{1,0:T(8,128)(2,1)}, u32[]{:S(2)}, u32[]{:S(2)}) collective-permute-start(bf16[128,2048]{1,0:T(8,128)(2,1)} %collective-permute-done.17.refs_2_.refs_3_.refs_11_), channel_id=1, source_target_pairs={{0,4},{8,0},{16,8},{24,16},{28,24},{20,28},{12,20},{4,12},{1,5},{9... | collective-permute-start | bytes 1572872 | tf_op jit(solution)/shard_map/ppermute | solution.py:807
  231.9 24.1 %collective-permute-start.30 = (bf16[128,2048]{1,0:T(8,128)(2,1)}, bf16[128,2048]{1,0:T(8,128)(2,1)}, u32[]{:S(2)}, u32[]{:S(2)}) collective-permute-start(bf16[128,2048]{1,0:T(8,128)(2,1)} %collective-permute-done.16.refs_1_.refs_2_.refs_10_), channel_id=1, source_target_pairs={{0,8},{8,16},{16,24},{24,28},{28,20},{20,12},{12,4},{4,0},{1,9},{9... | collective-permute-start | bytes 1572872 | tf_op jit(solution)/shard_map/ppermute | solution.py:804
  249.4 18.7 %collective-permute-start.29 = (bf16[128,2048]{1,0:T(8,128)(2,1)S(1)}, bf16[128,2048]{1,0:T(8,128)(2,1)}, u32[]{:S(2)}, u32[]{:S(2)}) collective-permute-start(bf16[128,2048]{1,0:T(8,128)(2,1)S(1)} %multiply_convert_fusion.refs_0_), channel_id=1, source_target_pairs={{0,4},{8,0},{16,8},{24,16},{28,24},{20,28},{12,20},{4,12},{1,5},{9... | collective-permute-start | bytes 1572872 | tf_op jit(solution)/shard_map/ppermute | solution.py:807
  251.2 18.7 %collective-permute-start.27 = (bf16[128,2048]{1,0:T(8,128)(2,1)S(1)}, bf16[128,2048]{1,0:T(8,128)(2,1)S(1)}, u32[]{:S(2)}, u32[]{:S(2)}) collective-permute-start(bf16[128,2048]{1,0:T(8,128)(2,1)S(1)} %multiply_convert_fusion.refs_0_), channel_id=1, source_target_pairs={{0,8},{8,16},{16,24},{24,28},{28,20},{20,12},{12,4},{4,0},{1,9},{9... | collective-permute-start | bytes 1572872 | tf_op jit(solution)/shard_map/ppermute | solution.py:804
  256.0 22.4 %collective-permute-start.34 = (bf16[128,2048]{1,0:T(8,128)(2,1)}, bf16[128,2048]{1,0:T(8,128)(2,1)S(1)}, u32[]{:S(2)}, u32[]{:S(2)}) collective-permute-start(bf16[128,2048]{1,0:T(8,128)(2,1)} %collective-permute-done.30.refs_3_.refs_2_.refs_12_), channel_id=1, source_target_pairs={{0,8},{8,16},{16,24},{24,28},{28,20},{20,12},{12,4},{4,0},{1,9},{9... | collective-permute-start | bytes 1572872 | tf_op jit(solution)/shard_map/ppermute | solution.py:804
  257.1 36.1 %collective-permute-start.35 = (bf16[128,2048]{1,0:T(8,128)(2,1)}, bf16[128,2048]{1,0:T(8,128)(2,1)S(1)}, u32[]{:S(2)}, u32[]{:S(2)}) collective-permute-start(bf16[128,2048]{1,0:T(8,128)(2,1)} %collective-permute-done.31.refs_4_.refs_3_.refs_13_), channel_id=1, source_target_pairs={{0,4},{8,0},{16,8},{24,16},{28,24},{20,28},{12,20},{4,12},{1,5},{9... | collective-permute-start | bytes 1572872 | tf_op jit(solution)/shard_map/ppermute | solution.py:807
  268.2 23.9 %collective-permute-start.33 = (bf16[128,2048]{1,0:T(8,128)(2,1)}, bf16[128,2048]{1,0:T(8,128)(2,1)S(1)}, u32[]{:S(2)}, u32[]{:S(2)}) collective-permute-start(bf16[128,2048]{1,0:T(8,128)(2,1)} %collective-permute-done.29.refs_2_.refs_1_.refs_3_), channel_id=1, source_target_pairs={{0,4},{8,0},{16,8},{24,16},{28,24},{20,28},{12,20},{4,12},{1,5},{9... | collective-permute-start | bytes 1572872 | tf_op jit(solution)/shard_map/ppermute | solution.py:807
  270.6 22.5 %collective-permute-start.32 = (bf16[128,2048]{1,0:T(8,128)(2,1)}, bf16[128,2048]{1,0:T(8,128)(2,1)S(1)}, u32[]{:S(2)}, u32[]{:S(2)}) collective-permute-start(bf16[128,2048]{1,0:T(8,128)(2,1)} %after.64.refs_0_.refs_2_), channel_id=1, source_target_pairs={{0,8},{8,16},{16,24},{24,28},{28,20},{20,12},{12,4},{4,0},{1,9},{9... | collective-permute-start | bytes 1572872 | tf_op jit(solution)/shard_map/ppermute | solution.py:804
  278.3 29.2 %collective-permute-start.38 = (bf16[128,2048]{1,0:T(8,128)(2,1)S(1)}, bf16[128,2048]{1,0:T(8,128)(2,1)}, u32[]{:S(2)}, u32[]{:S(2)}) collective-permute-start(bf16[128,2048]{1,0:T(8,128)(2,1)S(1)} %collective-permute-done.34.refs_3_.refs_2_.refs_14_), channel_id=1, source_target_pairs={{0,8},{8,16},{16,24},{24,28},{28,20},{20,12},{12,4},{4,0},{1,9},{9... | collective-permute-start | bytes 1572872 | tf_op jit(solution)/shard_map/ppermute | solution.py:804
  292.1 15.4 %collective-permute-start.37 = (bf16[128,2048]{1,0:T(8,128)(2,1)S(1)}, bf16[128,2048]{1,0:T(8,128)(2,1)}, u32[]{:S(2)}, u32[]{:S(2)}) collective-permute-start(bf16[128,2048]{1,0:T(8,128)(2,1)S(1)} %collective-permute-done.33.refs_2_.refs_1_.refs_5_), channel_id=1, source_target_pairs={{0,4},{8,0},{16,8},{24,16},{28,24},{20,28},{12,20},{4,12},{1,5},{9... | collective-permute-start | bytes 1572872 | tf_op jit(solution)/shard_map/ppermute | solution.py:807
  294.1 16.9 %collective-permute-start.36 = (bf16[128,2048]{1,0:T(8,128)(2,1)}, bf16[128,2048]{1,0:T(8,128)(2,1)S(1)}, u32[]{:S(2)}, u32[]{:S(2)}) collective-permute-start(bf16[128,2048]{1,0:T(8,128)(2,1)} %after.65.refs_0_.refs_4_), channel_id=1, source_target_pairs={{0,8},{8,16},{16,24},{24,28},{28,20},{20,12},{12,4},{4,0},{1,9},{9... | collective-permute-start | bytes 1572872 | tf_op jit(solution)/shard_map/ppermute | solution.py:804
  311.9 16.4 %collective-permute-start.39 = (bf16[128,2048]{1,0:T(8,128)(2,1)}, bf16[128,2048]{1,0:T(8,128)(2,1)S(1)}, u32[]{:S(2)}, u32[]{:S(2)}) collective-permute-start(bf16[128,2048]{1,0:T(8,128)(2,1)} %after.66.refs_0_.refs_6_), channel_id=1, source_target_pairs={{0,8},{8,16},{16,24},{24,28},{28,20},{20,12},{12,4},{4,0},{1,9},{9... | collective-permute-start | bytes 1572872 | tf_op jit(solution)/shard_map/ppermute | solution.py:804
  327.4 27.6 %collective-permute-start.41 = (bf16[128,2048]{1,0:T(8,128)(2,1)}, bf16[128,2048]{1,0:T(8,128)(2,1)S(1)}, u32[]{:S(2)}, u32[]{:S(2)}) collective-permute-start(bf16[128,2048]{1,0:T(8,128)(2,1)} %slice.231), channel_id=1, source_target_pairs={{0,4},{8,0},{16,8},{24,16},{28,24},{20,28},{12,20},{4,12},{1,5},{9... | collective-permute-start | bytes 1572872 | tf_op jit(solution)/shard_map/ppermute | solution.py:839
  339.3 15.6 %collective-permute-start.40 = (bf16[128,2048]{1,0:T(8,128)(2,1)}, bf16[128,2048]{1,0:T(8,128)(2,1)S(1)}, u32[]{:S(2)}, u32[]{:S(2)}) collective-permute-start(bf16[128,2048]{1,0:T(8,128)(2,1)} %get-tuple-element.101.refs_1_), channel_id=1, source_target_pairs={{0,8},{8,16},{16,24},{24,28},{28,20},{20,12},{12,4},{4,0},{1,9},{9... | collective-permute-start | bytes 1572872 | tf_op jit(solution)/shard_map/ppermute | solution.py:837
  358.5 17.4 %collective-permute-start.43 = (bf16[528,2048]{1,0:T(8,128)(2,1)}, bf16[528,2048]{1,0:T(8,128)(2,1)S(1)}, u32[]{:S(2)}, u32[]{:S(2)}) collective-permute-start(bf16[528,2048]{1,0:T(8,128)(2,1)} %after.70), channel_id=1, source_target_pairs={{0,1},{1,0},{2,3},{3,2},{4,5},{5,4},{6,7},{7,6},{8,9},{9,8},{10,11... | collective-permute-start | bytes 6488072 | tf_op jit(solution)/shard_map/ppermute | solution.py:862
  359.8 14.4 %collective-permute-start.44 = (bf16[128,2048]{1,0:T(8,128)(2,1)S(1)}, bf16[128,2048]{1,0:T(8,128)(2,1)S(1)}, u32[]{:S(2)}, u32[]{:S(2)}) collective-permute-start(bf16[128,2048]{1,0:T(8,128)(2,1)S(1)} %add_convert_fusion.13), channel_id=1, source_target_pairs={{0,4},{8,0},{16,8},{24,16},{28,24},{20,28},{12,20},{4,12},{1,5},{9... | collective-permute-start | bytes 1572872 | tf_op jit(solution)/shard_map/ppermute | solution.py:839
  360.8 14.3 %collective-permute-start.42 = (bf16[128,2048]{1,0:T(8,128)(2,1)}, bf16[128,2048]{1,0:T(8,128)(2,1)S(1)}, u32[]{:S(2)}, u32[]{:S(2)}) collective-permute-start(bf16[128,2048]{1,0:T(8,128)(2,1)} %add_convert_fusion.14.refs_1_), channel_id=1, source_target_pairs={{0,8},{8,16},{16,24},{24,28},{28,20},{20,12},{12,4},{4,0},{1,9},{9... | collective-permute-start | bytes 1572872 | tf_op jit(solution)/shard_map/ppermute | solution.py:837
  382.9 70.3 %collective-permute-start.56 = (bf16[528,2048]{1,0:T(8,128)(2,1)}, bf16[528,2048]{1,0:T(8,128)(2,1)}, u32[]{:S(2)}, u32[]{:S(2)}) collective-permute-start(bf16[528,2048]{1,0:T(8,128)(2,1)} %get-tuple-element.108), channel_id=1, source_target_pairs={{0,1},{1,0},{2,3},{3,2},{4,5},{5,4},{6,7},{7,6},{8,9},{9,8},{10,11... | collective-permute-start | bytes 6488072 | tf_op jit(solution)/shard_map/ppermute | solution.py:862
  402.7 47.5 %collective-permute-start.53 = (bf16[528,2048]{1,0:T(8,128)(2,1)}, bf16[528,2048]{1,0:T(8,128)(2,1)S(1)}, u32[]{:S(2)}, u32[]{:S(2)}) collective-permute-start(bf16[528,2048]{1,0:T(8,128)(2,1)} %add_convert_fusion.1), channel_id=1, source_target_pairs={{0,2},{1,3},{2,0},{3,1},{4,6},{5,7},{6,4},{7,5},{8,10},{9,11},{10,... | collective-permute-start | bytes 6488072 | tf_op jit(solution)/shard_map/ppermute | solution.py:862
  451.6 24.3 %collective-permute-start.55 = (bf16[128,2048]{1,0:T(8,128)(2,1)}, bf16[128,2048]{1,0:T(8,128)(2,1)}, u32[]{:S(2)}, u32[]{:S(2)}) collective-permute-start(bf16[128,2048]{1,0:T(8,128)(2,1)} %after.80.refs_1_.refs_6_), channel_id=1, source_target_pairs={{0,8},{8,16},{16,24},{24,28},{28,20},{20,12},{12,4},{4,0},{1,9},{9... | collective-permute-start | bytes 1572872 | tf_op jit(solution)/shard_map/ppermute | solution.py:804
  506.9 65.4 %all-to-all-start.2 = ((bf16[8,528,256]{2,1,0:T(8,128)(2,1)}), bf16[8,528,256]{2,1,0:T(8,128)(2,1)S(1)}, u32[]{:S(2)}, u32[]{:S(2)}) async-start(bf16[8,528,256]{2,1,0:T(8,128)(2,1)} %after.83), calls=%async_computation.3 | async-start | bytes 4325376 | tf_op jit(solution)/shard_map/all_to_all | solution.py:941
  513.5 158.5 %all-gather.3.cloned.1.call-start = ((), (), s32[]{:S(2)}) async-start(), calls=%async_computation.6 | async-start | bytes 1179648 | tf_op jit(solution)/shard_map/all_gather | solution.py:1236
  572.2 21.6 %collective-permute-start.61 = (bf16[320,2048]{1,0:T(8,128)(2,1)}, bf16[320,2048]{1,0:T(8,128)(2,1)}, u32[]{:S(2)}, u32[]{:S(2)}) collective-permute-start(bf16[320,2048]{1,0:T(8,128)(2,1)} %get-tuple-element.115), channel_id=1, source_target_pairs={{0,1},{1,0},{2,3},{3,2},{4,5},{5,4},{6,7},{7,6},{8,9},{9,8},{10,11... | collective-permute-start | bytes 3932168 | tf_op jit(solution)/shard_map/ppermute | solution.py:862
  582.9 14.8 %collective-permute-start.60 = (bf16[128,2048]{1,0:T(8,128)(2,1)}, bf16[128,2048]{1,0:T(8,128)(2,1)S(1)}, u32[]{:S(2)}, u32[]{:S(2)}) collective-permute-start(bf16[128,2048]{1,0:T(8,128)(2,1)} %get-tuple-element.147), channel_id=1, source_target_pairs={{0,8},{8,16},{16,24},{24,28},{28,20},{20,12},{12,4},{4,0},{1,9},{9... | collective-permute-start | bytes 1572872 | tf_op jit(solution)/shard_map/ppermute | solution.py:837
  584.8 14.0 %collective-permute-start.62 = (bf16[128,2048]{1,0:T(8,128)(2,1)S(1)}, bf16[128,2048]{1,0:T(8,128)(2,1)S(1)}, u32[]{:S(2)}, u32[]{:S(2)}) collective-permute-start(bf16[128,2048]{1,0:T(8,128)(2,1)S(1)} %get-tuple-element.148), channel_id=1, source_target_pairs={{0,4},{8,0},{16,8},{24,16},{28,24},{20,28},{12,20},{4,12},{1,5},{9... | collective-permute-start | bytes 1572872 | tf_op jit(solution)/shard_map/ppermute | solution.py:839
  607.5 29.8 %collective-permute-start.68 = (bf16[320,2048]{1,0:T(8,128)(2,1)}, bf16[320,2048]{1,0:T(8,128)(2,1)S(1)}, u32[]{:S(2)}, u32[]{:S(2)}) collective-permute-start(bf16[320,2048]{1,0:T(8,128)(2,1)} %add_convert_fusion.3), channel_id=1, source_target_pairs={{0,2},{1,3},{2,0},{3,1},{4,6},{5,7},{6,4},{7,5},{8,10},{9,11},{10,... | collective-permute-start | bytes 3932168 | tf_op jit(solution)/shard_map/ppermute | solution.py:862
  608.9 32.7 %collective-permute-start.71 = (bf16[320,2048]{1,0:T(8,128)(2,1)}, bf16[320,2048]{1,0:T(8,128)(2,1)}, u32[]{:S(2)}, u32[]{:S(2)}) collective-permute-start(bf16[320,2048]{1,0:T(8,128)(2,1)} %get-tuple-element.122), channel_id=1, source_target_pairs={{0,1},{1,0},{2,3},{3,2},{4,5},{5,4},{6,7},{7,6},{8,9},{9,8},{10,11... | collective-permute-start | bytes 3932168 | tf_op jit(solution)/shard_map/ppermute | solution.py:862
  639.8 19.1 %collective-permute-start.70 = (bf16[128,2048]{1,0:T(8,128)(2,1)S(1)}, bf16[128,2048]{1,0:T(8,128)(2,1)S(1)}, u32[]{:S(2)}, u32[]{:S(2)}) collective-permute-start(bf16[128,2048]{1,0:T(8,128)(2,1)S(1)} %add_convert_fusion.4), channel_id=1, source_target_pairs={{0,8},{8,16},{16,24},{24,28},{28,20},{20,12},{12,4},{4,0},{1,9},{9... | collective-permute-start | bytes 1572872 | tf_op jit(solution)/shard_map/ppermute | solution.py:837
  645.1 42.6 %all-to-all-start.3 = ((bf16[8,320,256]{2,1,0:T(8,128)(2,1)}), bf16[8,320,256]{2,1,0:T(8,128)(2,1)}, u32[]{:S(2)}, u32[]{:S(2)}) async-start(bf16[8,320,256]{2,1,0:T(8,128)(2,1)} %bitcast.228), calls=%async_computation.4 | async-start | bytes 2621440 | tf_op jit(solution)/shard_map/all_to_all | solution.py:941
  (120 other events, 890.6 us)
Sparse Core Ops, SparseCore 0:
  443.6 123.5 reduce-scatter.1
  622.7 49.3 all-gather.2

commit v8 on v7

--- a/solution.py
+++ b/solution.py
@@ -1102,6 +1102,7 @@
     grad_own = cotangent[0]
     grad_steps = [(after(grad_own, rest_block),)]
     grad_steps.append(ring_step(grad_steps[0], 1, seq))
+    grad_steps.append(ring_step(grad_steps[1], 2, seq))
 
     inner, *kept = chain_forward(slot_of_member, docs, x3, logits, gb, init, rows_tok)
     side_rows = rest_block.shape[1] - 3 * padded
@@ -1135,7 +1136,7 @@
     mixing = ring_scatter(
         by_distance(after(mm(gated, m_out).astype(BF16), *grad_steps[1])),
         seq,
-        [lambda since: [], lambda since: [], lambda since: [], ffn_corner],
+        [lambda since: [], lambda since: list(grad_steps[2]), lambda since: [], ffn_corner],
     )
     own_rows = tokens[0].astype(F32)
     resid = own_rows + mixing

time: 711 us -> 708 us (level)
    ppermute x12, waiting for transfers between devices: 9.82 us -> 24.6 us  [ring_step(): return (ahead, lax.ppermute(blocks[-1], 'seq', ring_pairs(size, -1)))]
    ppermute x16, waiting for transfers between devices: 45.7 us -> 33.3 us  [ring_step(): ahead = lax.ppermute(blocks[0], 'seq', ring_pairs(size, 1))]
    unnamed x194 -> x196, local copies, waits for them, and re-layouts: 37.2 us -> 38.9 us
  transfers between devices with their start and end apart: 78 -> 78, of which waited for: 43 -> 44; matrix products, arithmetic and copies ran while one was open for 18% -> 18% of each run, Pallas kernels for 24% -> 24%
where the time goes in v8:
time: 708 us; the launch traced here: 695 us
  waiting for transfers between devices  242 us (34%)
  Pallas kernels  172 us (24%)
  starting transfers between devices  105 us (15%)
  local copies, waits for them, and re-layouts  72.3 us (10%)
  other arithmetic  64.5 us (9%)
  matrix products  24.5 us (3%)
  between operations  15.6 us (2%)
    ppermute x12, waiting for transfers between devices, ring_scatter(): ahead = lax.ppermute(ahead, 'seq', ring_pairs(size, 1))  70 us
    pallas_call x5, Pallas kernels, ffn_step(): pl.pallas_call(partial(ffn_kernel, count, len(weights), len(kept)), grid_...  57.4 us
    unnamed x196, local copies, waits for them, and re-layouts  38.9 us
    pallas_call x1, Pallas kernels, chain_backward(): pl.pallas_call(partial(backward_kernel, heads), grid_spec=pltpu.PrefetchS...  37.5 us
    ppermute x9, waiting for transfers between devices, ring_scatter(): back = lax.ppermute(back, 'seq', ring_pairs(size, -1))  34.3 us
    ppermute x16, waiting for transfers between devices, ring_step(): ahead = lax.ppermute(blocks[0], 'seq', ring_pairs(size, 1))  33.3 us
    ppermute x8, waiting for transfers between devices, pairwise_sum(): lax.ppermute(value, axis, [(i, i ^ bit) for i in range(size)])  26.8 us
    ppermute x15, waiting for transfers between devices, swap(): return lax.ppermute(value, 'grp', [(i, i ^ bit) for i in range(4)])  26.8 us
  transfers between devices with their start and end apart: 78, of which 44 were waited for; matrix products, arithmetic and copies ran while one was open for 18% of the time, Pallas kernels for 24%

profile of v8, /device:TPU:0, one launch (start us, length us, event | category | flops | bytes accessed | tf_op | source)
XLA Modules:
  0.0 695.0 jit_solution(13415746473361623991)
XLA Ops:
  12.6 6.2 all-to-all-start
  30.2 11.4 %all-to-all-done.refs_0_ = bf16[8,192,256]{2,1,0:T(8,128)(2,1)S(1)} async-done(((bf16[8,192,256]{2,1,0:T(8,128)(2,1)}), bf16[8,192,256]{2,1,0:T(8,128)(2,1)S(1)}, u32[]{:S(2)}, u32[]{:S(2)}) %all-to-all-start) | async-done | bytes 786464 | tf_op jit(solution)/shard_map/all_to_all | solution.py:941
  45.3 3.2 fusion.87.refs_4_.refs_13_
  50.2 3.1 collective-permute-start.5
  54.1 6.7 collective-permute-done.7.refs_10_
  60.9 3.8 cut_features.2.refs_1_.refs_0_
  67.0 13.4 %collective-permute-done.6.refs_0_ = bf16[128,2048]{1,0:T(8,128)(2,1)S(1)} collective-permute-done((bf16[128,2048]{1,0:T(8,128)(2,1)}, bf16[128,2048]{1,0:T(8,128)(2,1)S(1)}, u32[]{:S(2)}, u32[]{:S(2)}) %collective-permute-start.6) | collective-permute-done | bytes 524320 | tf_op jit(solution)/shard_map/ppermute | solution.py:804
  82.1 4.4 all-to-all-start.1
  89.1 10.5 %project.1 = (bf16[1024,2048]{1,0:T(8,128)(2,1)}, bf16[1024,768]{1,0:T(8,128)(2,1)}, f32[1024,128]{1,0:T(8,128)}) custom-call(bf16[128,2048]{1,0:T(8,128)(2,1)} %bitcast.240, bf16[128,2048]{1,0:T(8,128)(2,1)} %after.51.refs_1_, bf16[128,2048]{1,0:T(8,128)(2,1)} %after.47.refs_1_.refs_2_, bf16[128,2048]{1,0:T(8,128)(2,1)} %copy-done.49, ...), custom_call_target="tpu_custom_call" | custom-call | flops 1 | bytes 1 | tf_op jit(solution)/shard_map/project/pallas_call | solution.py:743
  99.6 24.6 %chain_forward.1 = (f32[1024,256]{1,0:T(8,128)}, f32[64,4096]{1,0:T(8,128)}, f32[64,4096]{1,0:T(8,128)}, f32[64,4096]{1,0:T(8,128)}, f32[8,4096]{1,0:T(8,128)}, /*index=5*/f32[8,64,384]{2,1,0:T(8,128)}) custom-call(s32[8]{0:T(128)} %get-tuple-element.222.refs_6_.idx_ref, s32[5]{0:T(128)} %pad_add_fusion.refs_5_.docs_ref, ...), custom_call_target="tpu_custom_call" | custom-call | flops 1 | bytes 1 | tf_op jit(solution)/shard_map/chain_forward/pallas_call | solution.py:391
  136.9 10.5 %collective-permute-done.15 = f32[2,1024]{1,0:T(2,128)S(1)} collective-permute-done((f32[2,1024]{1,0:T(2,128)S(1)}, f32[2,1024]{1,0:T(2,128)S(1)}, u32[]{:S(2)}, u32[]{:S(2)}) %collective-permute-start.15) | collective-permute-done | bytes 8224 | tf_op jit(solution)/shard_map/ppermute | solution.py:856
  155.6 9.5 %collective-permute-done.11 = bf16[128,2048]{1,0:T(8,128)(2,1)S(1)} collective-permute-done((bf16[128,2048]{1,0:T(8,128)(2,1)S(1)}, bf16[128,2048]{1,0:T(8,128)(2,1)S(1)}, u32[]{:S(2)}, u32[]{:S(2)}) %collective-permute-start.11) | collective-permute-done | bytes 524320 | tf_op jit(solution)/shard_map/ppermute | solution.py:862
  169.7 3.3 convolution_convert_fusion.1.refs_0_
  182.7 7.4 %collective-permute-done.18.refs_0_ = bf16[128,2048]{1,0:T(8,128)(2,1)} collective-permute-done((bf16[128,2048]{1,0:T(8,128)(2,1)S(1)}, bf16[128,2048]{1,0:T(8,128)(2,1)}, u32[]{:S(2)}, u32[]{:S(2)}) %collective-permute-start.18) | collective-permute-done | bytes 524320 | tf_op jit(solution)/shard_map/ppermute | solution.py:837
  195.1 7.1 %collective-permute-done.22.refs_2_.refs_3_.refs_13_ = bf16[128,2048]{1,0:T(8,128)(2,1)S(1)} collective-permute-done((bf16[128,2048]{1,0:T(8,128)(2,1)S(1)}, bf16[128,2048]{1,0:T(8,128)(2,1)S(1)}, u32[]{:S(2)}, u32[]{:S(2)}) %collective-permute-start.22) | collective-permute-done | bytes 524320 | tf_op jit(solution)/shard_map/ppermute | solution.py:807
  202.2 9.6 %collective-permute-done.20.refs_0_ = bf16[128,2048]{1,0:T(8,128)(2,1)} collective-permute-done((bf16[128,2048]{1,0:T(8,128)(2,1)S(1)}, bf16[128,2048]{1,0:T(8,128)(2,1)}, u32[]{:S(2)}, u32[]{:S(2)}) %collective-permute-start.20) | collective-permute-done | bytes 524320 | tf_op jit(solution)/shard_map/ppermute | solution.py:837
  216.7 11.1 %collective-permute-done.24.refs_0_ = bf16[128,2048]{1,0:T(8,128)(2,1)S(1)} collective-permute-done((bf16[128,2048]{1,0:T(8,128)(2,1)S(1)}, bf16[128,2048]{1,0:T(8,128)(2,1)S(1)}, u32[]{:S(2)}, u32[]{:S(2)}) %collective-permute-start.24) | collective-permute-done | bytes 524320 | tf_op jit(solution)/shard_map/ppermute | solution.py:837
  236.6 12.0 %collective-permute-done.26.refs_0_ = bf16[128,2048]{1,0:T(8,128)(2,1)S(1)} collective-permute-done((bf16[128,2048]{1,0:T(8,128)(2,1)S(1)}, bf16[128,2048]{1,0:T(8,128)(2,1)S(1)}, u32[]{:S(2)}, u32[]{:S(2)}) %collective-permute-start.26) | collective-permute-done | bytes 524320 | tf_op jit(solution)/shard_map/ppermute | solution.py:837
  256.8 3.2 collective-permute-done.32.refs_3_.refs_2_.refs_14_
  261.7 10.2 %ffn_step.5 = (bf16[704,1024]{1,0:T(8,128)(2,1)}, bf16[704,1024]{1,0:T(8,128)(2,1)}, bf16[704,1024]{1,0:T(8,128)(2,1)}, bf16[8,128,2048]{2,1,0:T(8,128)(2,1)}, bf16[128,2048]{1,0:T(8,128)(2,1)}) custom-call(s32[1]{0:T(128)} %get-tuple-element.217.member_ref, bf16[128,2048]{1,0:T(8,128)(2,1)} %copy-done.29, bf16[128,2048]{1,0:T(8,128)(2,1)} %after.54.refs_1_.refs_8_, ...), custom_call_target="tpu_custom_call" | custom-call | flops 1 | bytes 1 | tf_op jit(solution)/shard_map/ffn_step/pallas_call | solution.py:597
  272.2 7.4 %collective-permute-done.33.refs_4_.refs_3_.refs_15_ = bf16[128,2048]{1,0:T(8,128)(2,1)S(1)} collective-permute-done((bf16[128,2048]{1,0:T(8,128)(2,1)S(1)}, bf16[128,2048]{1,0:T(8,128)(2,1)S(1)}, u32[]{:S(2)}, u32[]{:S(2)}) %collective-permute-start.33) | collective-permute-done | bytes 524320 | tf_op jit(solution)/shard_map/ppermute | solution.py:807
  283.3 12.3 %ffn_step.6 = (bf16[704,1024]{1,0:T(8,128)(2,1)}, bf16[704,1024]{1,0:T(8,128)(2,1)}, bf16[704,1024]{1,0:T(8,128)(2,1)}, bf16[8,128,2048]{2,1,0:T(8,128)(2,1)}, bf16[256,2048]{1,0:T(8,128)(2,1)}) custom-call(s32[2]{0:T(128)} %get-tuple-element.216.member_ref, ...), custom_call_target="tpu_custom_call", output_to_operand_aliasing={{0}: (9, {}), {1}: (10, {}), {2}: (11, {}), {3}: (12, {})} | custom-call | flops 1 | bytes 1 | tf_op jit(solution)/shard_map/ffn_step/pallas_call | solution.py:597
  298.5 12.4 %ffn_step.7 = (bf16[704,1024]{1,0:T(8,128)(2,1)}, bf16[704,1024]{1,0:T(8,128)(2,1)}, bf16[704,1024]{1,0:T(8,128)(2,1)}, bf16[8,128,2048]{2,1,0:T(8,128)(2,1)}, bf16[256,2048]{1,0:T(8,128)(2,1)}) custom-call(s32[2]{0:T(128)} %get-tuple-element.215.member_ref, ...), custom_call_target="tpu_custom_call", output_to_operand_aliasing={{0}: (9, {}), {1}: (10, {}), {2}: (11, {}), {3}: (12, {})} | custom-call | flops 1 | bytes 1 | tf_op jit(solution)/shard_map/ffn_step/pallas_call | solution.py:597
  313.0 12.2 %ffn_step.8 = (bf16[704,1024]{1,0:T(8,128)(2,1)}, bf16[704,1024]{1,0:T(8,128)(2,1)}, bf16[704,1024]{1,0:T(8,128)(2,1)}, bf16[8,128,2048]{2,1,0:T(8,128)(2,1)}, bf16[256,2048]{1,0:T(8,128)(2,1)}) custom-call(s32[2]{0:T(128)} %get-tuple-element.214.member_ref, ...), custom_call_target="tpu_custom_call", output_to_operand_aliasing={{0}: (9, {}), {1}: (10, {}), {2}: (11, {}), {3}: (12, {})} | custom-call | flops 1 | bytes 1 | tf_op jit(solution)/shard_map/ffn_step/pallas_call | solution.py:597
  329.0 10.3 %ffn_step.9 = (bf16[704,1024]{1,0:T(8,128)(2,1)}, bf16[704,1024]{1,0:T(8,128)(2,1)}, bf16[704,1024]{1,0:T(8,128)(2,1)}, bf16[8,128,2048]{2,1,0:T(8,128)(2,1)}, bf16[128,2048]{1,0:T(8,128)(2,1)}) custom-call(s32[1]{0:T(128)} %get-tuple-element.218.member_ref, ...), custom_call_target="tpu_custom_call", output_to_operand_aliasing={{0}: (7, {}), {1}: (8, {}), {2}: (9, {}), {3}: (10, {})} | custom-call | flops 1 | bytes 1 | tf_op jit(solution)/shard_map/ffn_step/pallas_call | solution.py:597
  340.3 14.5 %ffn_grads.1 = (bf16[528,2048]{1,0:T(8,128)(2,1)}, bf16[528,2048]{1,0:T(8,128)(2,1)}, bf16[528,2048]{1,0:T(8,128)(2,1)}, bf16[528,2048]{1,0:T(8,128)(2,1)}) custom-call(bf16[704,1024]{1,0:T(8,128)(2,1)} %after.68.at_ref, bf16[704,1024]{1,0:T(8,128)(2,1)} %get-tuple-element.103.ut_ref, bf16[704,1024]{1,0:T(8,128)(2,1)} %get-tuple-element.104.ht_ref, ...), custom_call_target="tpu_custom_call" | custom-call | flops 1 | bytes 1 | tf_op jit(solution)/shard_map/ffn_grads/pallas_call | solution.py:645
  361.7 12.3 %collective-permute-done.44.refs_2_.refs_0_ = bf16[128,2048]{1,0:T(8,128)(2,1)S(1)} collective-permute-done((bf16[128,2048]{1,0:T(8,128)(2,1)S(1)}, bf16[128,2048]{1,0:T(8,128)(2,1)S(1)}, u32[]{:S(2)}, u32[]{:S(2)}) %collective-permute-start.44) | collective-permute-done | bytes 524320 | tf_op jit(solution)/shard_map/ppermute | solution.py:839
  382.9 11.4 %collective-permute-done.46.refs_1_.refs_0_ = bf16[128,2048]{1,0:T(8,128)(2,1)} collective-permute-done((bf16[128,2048]{1,0:T(8,128)(2,1)S(1)}, bf16[128,2048]{1,0:T(8,128)(2,1)}, u32[]{:S(2)}, u32[]{:S(2)}) %collective-permute-start.46) | collective-permute-done | bytes 524320 | tf_op jit(solution)/shard_map/ppermute | solution.py:839
  398.6 3.8 add_convert_fusion.1
  403.9 6.4 collective-permute-done.47
  429.1 10.1 %collective-permute-done.51.refs_1_.refs_5_ = bf16[128,2048]{1,0:T(8,128)(2,1)} collective-permute-done((bf16[128,2048]{1,0:T(8,128)(2,1)}, bf16[128,2048]{1,0:T(8,128)(2,1)}, u32[]{:S(2)}, u32[]{:S(2)}) %collective-permute-start.51) | collective-permute-done | bytes 524320 | tf_op jit(solution)/shard_map/ppermute | solution.py:807
  443.6 5.9 collective-permute-done.53.refs_1_.refs_0_
  452.5 3.5 add_convert_fusion
  457.5 16.5 %collective-permute-done.55.refs_0_ = bf16[128,2048]{1,0:T(8,128)(2,1)} collective-permute-done((bf16[128,2048]{1,0:T(8,128)(2,1)}, bf16[128,2048]{1,0:T(8,128)(2,1)}, u32[]{:S(2)}, u32[]{:S(2)}) %collective-permute-start.55) | collective-permute-done | bytes 524320 | tf_op jit(solution)/shard_map/ppermute | solution.py:804
  483.7 12.5 %collective-permute-start.57 = (f32[2,1024]{1,0:T(2,128)S(1)}, f32[2,1024]{1,0:T(2,128)S(1)}, u32[]{:S(2)}, u32[]{:S(2)}) collective-permute-start(f32[2,1024]{1,0:T(2,128)S(1)} %bitcast.284), channel_id=1, source_target_pairs={{0,4},{4,0},{8,12},{12,8},{16,20},{20,16},{24,28},{28,24},{1,5},{5... | collective-permute-start | bytes 24584 | tf_op jit(solution)/shard_map/ppermute | solution.py:856
  497.9 3.6 collective-permute-done.58
  503.0 3.2 collective-permute-done.59
  507.0 4.1 all-to-all-start.2
  514.4 37.5 %chain_backward.1 = (bf16[1024,1152]{1,0:T(8,128)(2,1)}, f32[2,64,128]{2,1,0:T(8,128)}, f32[64,384]{1,0:T(8,128)}) custom-call(s32[8]{0:T(128)} %get-tuple-element.222.refs_6_.idx_ref, s32[5]{0:T(128)} %pad_add_fusion.refs_5_.docs_ref, bf16[1024,768]{1,0:T(8,128)(2,1)} %get-tuple-element.76.x_ref, f32[1024,256]{1,0:T(8,128)} %subtract_multiply_fusion.d_ref, ...), custom_call_target="tpu_custom_call" | custom-call | flops 1 | bytes 1 | tf_op jit(solution)/shard_map/chain_backward/pallas_call | solution.py:423
  551.9 14.1 %proj_grads.1 = (bf16[320,2048]{1,0:T(8,128)(2,1)}, bf16[320,2048]{1,0:T(8,128)(2,1)}, bf16[320,2048]{1,0:T(8,128)(2,1)}, bf16[320,2048]{1,0:T(8,128)(2,1)}, f32[8,2048]{1,0:T(8,128)}, /*index=5*/f32[8,2048]{1,0:T(8,128)}) custom-call(bf16[1024,1152]{1,0:T(8,128)(2,1)} %get-tuple-element.113.d_ref.refs_0_, bf16[1024,2048]{1,0:T(8,128)(2,1)} %get-tuple-element.75.x_ref, ...), custom_call_target="tpu_custom_call" | custom-call | flops 1 | bytes 1 | tf_op jit(solution)/shard_map/proj_grads/pallas_call | solution.py:697
  573.1 8.2 %convolution_convert_fusion = bf16[1024,2048]{1,0:T(8,128)(2,1)S(1)} fusion(bf16[1024,1152]{1,0:T(8,128)(2,1)} %after.84, bf16[1152,2048]{1,0:T(8,128)(2,1)} %constant_dynamic-update-slice_fusion.refs_1_.w_ref), kind=kOutput, calls=%fused_computation.2 | convolution fusion | flops 4833935360 | bytes 11272192 | tf_op jit(solution)/shard_map/dot_general | solution.py:18
  587.8 4.0 collective-permute-done.67
  605.8 4.0 join_features.2
  609.8 3.5 collective-permute-done.64.refs_2_.refs_0_
  619.1 10.7 %collective-permute-done.65.refs_0_ = bf16[128,2048]{1,0:T(8,128)(2,1)S(1)} collective-permute-done((bf16[128,2048]{1,0:T(8,128)(2,1)}, bf16[128,2048]{1,0:T(8,128)(2,1)S(1)}, u32[]{:S(2)}, u32[]{:S(2)}) %collective-permute-start.65) | collective-permute-done | bytes 524320 | tf_op jit(solution)/shard_map/ppermute | solution.py:837
  642.7 4.7 all-to-all-start.3
  648.4 8.1 %collective-permute-done.70 = bf16[128,2048]{1,0:T(8,128)(2,1)S(1)} collective-permute-done((bf16[128,2048]{1,0:T(8,128)(2,1)S(1)}, bf16[128,2048]{1,0:T(8,128)(2,1)S(1)}, u32[]{:S(2)}, u32[]{:S(2)}) %collective-permute-start.70) | collective-permute-done | bytes 524320 | tf_op jit(solution)/shard_map/ppermute | solution.py:837
  659.0 9.8 %all-gather.3.cloned.1.call-done = f32[256,1024]{1,0:T(8,128)} async-done(((f32[32,1024]{1,0:T(8,128)}), f32[256,1024]{1,0:T(8,128)}) %all-gather.3.cloned.1.call-update) | async-done | bytes 1048592 | tf_op jit(solution)/shard_map/all_gather | solution.py:1237
  (506 shorter events, 241.2 us)
Async XLA Ops:
  7.2 19.4 %collective-permute-start.1 = (bf16[128,2048]{1,0:T(8,128)(2,1)}, bf16[128,2048]{1,0:T(8,128)(2,1)S(1)}, u32[]{:S(2)}, u32[]{:S(2)}) collective-permute-start(bf16[128,2048]{1,0:T(8,128)(2,1)} %bitcast.238), channel_id=1, source_target_pairs={{0,4},{8,0},{16,8},{24,16},{28,24},{20,28},{12,20},{4,12},{1,5},{9... | collective-permute-start | bytes 1572872 | tf_op jit(solution)/shard_map/ppermute | solution.py:807
  10.2 16.4 %collective-permute-start = (bf16[128,2048]{1,0:T(8,128)(2,1)}, bf16[128,2048]{1,0:T(8,128)(2,1)S(1)}, u32[]{:S(2)}, u32[]{:S(2)}) collective-permute-start(bf16[128,2048]{1,0:T(8,128)(2,1)} %bitcast.239), channel_id=1, source_target_pairs={{0,8},{8,16},{16,24},{24,28},{28,20},{20,12},{12,4},{4,0},{1,9},{9... | collective-permute-start | bytes 1572872 | tf_op jit(solution)/shard_map/ppermute | solution.py:804
  12.6 29.0 %all-to-all-start = ((bf16[8,192,256]{2,1,0:T(8,128)(2,1)}), bf16[8,192,256]{2,1,0:T(8,128)(2,1)S(1)}, u32[]{:S(2)}, u32[]{:S(2)}) async-start(bf16[8,192,256]{2,1,0:T(8,128)(2,1)} %cut_features.3), calls=%async_computation | async-start | bytes 1572864 | tf_op jit(solution)/shard_map/all_to_all | solution.py:941
  28.2 25.1 %collective-permute-start.2 = (bf16[128,2048]{1,0:T(8,128)(2,1)}, bf16[128,2048]{1,0:T(8,128)(2,1)S(1)}, u32[]{:S(2)}, u32[]{:S(2)}) collective-permute-start(bf16[128,2048]{1,0:T(8,128)(2,1)} %after.47.refs_1_.refs_2_), channel_id=1, source_target_pairs={{0,8},{8,16},{16,24},{24,28},{28,20},{20,12},{12,4},{4,0},{1,9},{9... | collective-permute-start | bytes 1572872 | tf_op jit(solution)/shard_map/ppermute | solution.py:804
  30.2 20.0 %collective-permute-start.3 = (bf16[128,2048]{1,0:T(8,128)(2,1)}, bf16[128,2048]{1,0:T(8,128)(2,1)S(1)}, u32[]{:S(2)}, u32[]{:S(2)}) collective-permute-start(bf16[128,2048]{1,0:T(8,128)(2,1)} %copy-done.49), channel_id=1, source_target_pairs={{0,4},{8,0},{16,8},{24,16},{28,24},{20,28},{12,20},{4,12},{1,5},{9... | collective-permute-start | bytes 1572872 | tf_op jit(solution)/shard_map/ppermute | solution.py:807
  43.7 17.1 %collective-permute-start.7 = (bf16[192,2048]{1,0:T(8,128)(2,1)S(1)}, bf16[192,2048]{1,0:T(8,128)(2,1)S(1)}, u32[]{:S(2)}, u32[]{:S(2)}) collective-permute-start(bf16[192,2048]{1,0:T(8,128)(2,1)S(1)} %bitcast.233), channel_id=1, source_target_pairs={{0,2},{1,3},{2,0},{3,1},{4,6},{5,7},{6,4},{7,5},{8,10},{9,11},{10,... | collective-permute-start | bytes 2359304 | tf_op jit(solution)/shard_map/ppermute | solution.py:862
  50.2 14.5 %collective-permute-start.5 = (bf16[128,2048]{1,0:T(8,128)(2,1)S(1)}, bf16[128,2048]{1,0:T(8,128)(2,1)}, u32[]{:S(2)}, u32[]{:S(2)}) collective-permute-start(bf16[128,2048]{1,0:T(8,128)(2,1)S(1)} %collective-permute-done.3.refs_8_.refs_5_), channel_id=1, source_target_pairs={{0,4},{8,0},{16,8},{24,16},{28,24},{20,28},{12,20},{4,12},{1,5},{9... | collective-permute-start | bytes 1572872 | tf_op jit(solution)/shard_map/ppermute | solution.py:807
  60.9 19.5 %collective-permute-start.8 = (bf16[192,2048]{1,0:T(8,128)(2,1)S(1)}, bf16[192,2048]{1,0:T(8,128)(2,1)S(1)}, u32[]{:S(2)}, u32[]{:S(2)}) collective-permute-start(bf16[192,2048]{1,0:T(8,128)(2,1)S(1)} %collective-permute-done.7.refs_10_), channel_id=1, source_target_pairs={{0,1},{1,0},{2,3},{3,2},{4,5},{5,4},{6,7},{7,6},{8,9},{9,8},{10,11... | collective-permute-start | bytes 2359304 | tf_op jit(solution)/shard_map/ppermute | solution.py:862
  65.5 14.9 %collective-permute-start.6 = (bf16[128,2048]{1,0:T(8,128)(2,1)}, bf16[128,2048]{1,0:T(8,128)(2,1)S(1)}, u32[]{:S(2)}, u32[]{:S(2)}) collective-permute-start(bf16[128,2048]{1,0:T(8,128)(2,1)} %after.49.refs_6_), channel_id=1, source_target_pairs={{0,8},{8,16},{16,24},{24,28},{28,20},{20,12},{12,4},{4,0},{1,9},{9... | collective-permute-start | bytes 1572872 | tf_op jit(solution)/shard_map/ppermute | solution.py:804
  82.1 65.8 %all-to-all-start.1 = ((bf16[8,656,256]{2,1,0:T(8,128)(2,1)}), bf16[8,656,256]{2,1,0:T(8,128)(2,1)S(1)}, u32[]{:S(2)}, u32[]{:S(2)}) async-start(bf16[8,656,256]{2,1,0:T(8,128)(2,1)} %after.52), calls=%async_computation.1 | async-start | bytes 5373952 | tf_op jit(solution)/shard_map/all_to_all | solution.py:941
  86.5 509.9 %reduce-scatter.2.cloned.1.call-start = ((), (), s32[]{:S(2)}) async-start(), calls=%async_computation.5 | async-start | bytes 4718592 | tf_op jit(solution)/shard_map/reduce_scatter | solution.py:1206
  133.0 14.3 %collective-permute-start.15 = (f32[2,1024]{1,0:T(2,128)S(1)}, f32[2,1024]{1,0:T(2,128)S(1)}, u32[]{:S(2)}, u32[]{:S(2)}) collective-permute-start(f32[2,1024]{1,0:T(2,128)S(1)} %add.416), channel_id=1, source_target_pairs={{0,16},{4,20},{8,24},{12,28},{16,0},{20,4},{24,8},{28,12},{1,17},{... | collective-permute-start | bytes 24584 | tf_op jit(solution)/shard_map/ppermute | solution.py:856
  149.5 23.5 %collective-permute-start.17 = (bf16[128,2048]{1,0:T(8,128)(2,1)}, bf16[128,2048]{1,0:T(8,128)(2,1)S(1)}, u32[]{:S(2)}, u32[]{:S(2)}) collective-permute-start(bf16[128,2048]{1,0:T(8,128)(2,1)} %after.54.refs_1_.refs_8_), channel_id=1, source_target_pairs={{0,4},{8,0},{16,8},{24,16},{28,24},{20,28},{12,20},{4,12},{1,5},{9... | collective-permute-start | bytes 1572872 | tf_op jit(solution)/shard_map/ppermute | solution.py:807
  150.9 22.0 %collective-permute-start.16 = (bf16[128,2048]{1,0:T(8,128)(2,1)}, bf16[128,2048]{1,0:T(8,128)(2,1)}, u32[]{:S(2)}, u32[]{:S(2)}) collective-permute-start(bf16[128,2048]{1,0:T(8,128)(2,1)} %after.54.refs_1_.refs_8_), channel_id=1, source_target_pairs={{0,8},{8,16},{16,24},{24,28},{28,20},{20,12},{12,4},{4,0},{1,9},{9... | collective-permute-start | bytes 1572872 | tf_op jit(solution)/shard_map/ppermute | solution.py:804
  175.2 14.9 %collective-permute-start.18 = (bf16[128,2048]{1,0:T(8,128)(2,1)S(1)}, bf16[128,2048]{1,0:T(8,128)(2,1)}, u32[]{:S(2)}, u32[]{:S(2)}) collective-permute-start(bf16[128,2048]{1,0:T(8,128)(2,1)S(1)} %get-tuple-element.153), channel_id=1, source_target_pairs={{0,8},{8,16},{16,24},{24,28},{28,20},{20,12},{12,4},{4,0},{1,9},{9... | collective-permute-start | bytes 1572872 | tf_op jit(solution)/shard_map/ppermute | solution.py:837
  176.0 15.1 %collective-permute-start.19 = (bf16[128,2048]{1,0:T(8,128)(2,1)S(1)}, bf16[128,2048]{1,0:T(8,128)(2,1)}, u32[]{:S(2)}, u32[]{:S(2)}) collective-permute-start(bf16[128,2048]{1,0:T(8,128)(2,1)S(1)} %get-tuple-element.154), channel_id=1, source_target_pairs={{0,4},{8,0},{16,8},{24,16},{28,24},{20,28},{12,20},{4,12},{1,5},{9... | collective-permute-start | bytes 1572872 | tf_op jit(solution)/shard_map/ppermute | solution.py:839
  179.1 52.8 %collective-permute-start.27 = (bf16[528,2048]{1,0:T(8,128)(2,1)}, bf16[528,2048]{1,0:T(8,128)(2,1)S(1)}, u32[]{:S(2)}, u32[]{:S(2)}) collective-permute-start(bf16[528,2048]{1,0:T(8,128)(2,1)} %bitcast.124.refs_2_.refs_4_), channel_id=1, source_target_pairs={{0,2},{1,3},{2,0},{3,1},{4,6},{5,7},{6,4},{7,5},{8,10},{9,11},{10,... | collective-permute-start | bytes 6488072 | tf_op jit(solution)/shard_map/ppermute | solution.py:862
  180.6 21.5 %collective-permute-start.22 = (bf16[128,2048]{1,0:T(8,128)(2,1)S(1)}, bf16[128,2048]{1,0:T(8,128)(2,1)S(1)}, u32[]{:S(2)}, u32[]{:S(2)}) collective-permute-start(bf16[128,2048]{1,0:T(8,128)(2,1)S(1)} %copy-done.18), channel_id=1, source_target_pairs={{0,4},{8,0},{16,8},{24,16},{28,24},{20,28},{12,20},{4,12},{1,5},{9... | collective-permute-start | bytes 1572872 | tf_op jit(solution)/shard_map/ppermute | solution.py:807
  182.4 19.8 %collective-permute-start.21 = (bf16[128,2048]{1,0:T(8,128)(2,1)}, bf16[128,2048]{1,0:T(8,128)(2,1)}, u32[]{:S(2)}, u32[]{:S(2)}) collective-permute-start(bf16[128,2048]{1,0:T(8,128)(2,1)} %collective-permute-done.16.refs_1_.refs_2_.refs_10_), channel_id=1, source_target_pairs={{0,8},{8,16},{16,24},{24,28},{28,20},{20,12},{12,4},{4,0},{1,9},{9... | collective-permute-start | bytes 1572872 | tf_op jit(solution)/shard_map/ppermute | solution.py:804
  192.9 18.9 %collective-permute-start.20 = (bf16[128,2048]{1,0:T(8,128)(2,1)S(1)}, bf16[128,2048]{1,0:T(8,128)(2,1)}, u32[]{:S(2)}, u32[]{:S(2)}) collective-permute-start(bf16[128,2048]{1,0:T(8,128)(2,1)S(1)} %get-tuple-element.151), channel_id=1, source_target_pairs={{0,8},{8,16},{16,24},{24,28},{28,20},{20,12},{12,4},{4,0},{1,9},{9... | collective-permute-start | bytes 1572872 | tf_op jit(solution)/shard_map/ppermute | solution.py:837
  195.0 17.7 %collective-permute-start.23 = (bf16[128,2048]{1,0:T(8,128)(2,1)S(1)}, bf16[128,2048]{1,0:T(8,128)(2,1)}, u32[]{:S(2)}, u32[]{:S(2)}) collective-permute-start(bf16[128,2048]{1,0:T(8,128)(2,1)S(1)} %get-tuple-element.152), channel_id=1, source_target_pairs={{0,4},{8,0},{16,8},{24,16},{28,24},{20,28},{12,20},{4,12},{1,5},{9... | collective-permute-start | bytes 1572872 | tf_op jit(solution)/shard_map/ppermute | solution.py:839
  233.3 15.3 %collective-permute-start.28 = (bf16[528,2048]{1,0:T(8,128)(2,1)}, bf16[528,2048]{1,0:T(8,128)(2,1)S(1)}, u32[]{:S(2)}, u32[]{:S(2)}) collective-permute-start(bf16[528,2048]{1,0:T(8,128)(2,1)} %after.61.refs_4_.refs_6_), channel_id=1, source_target_pairs={{0,1},{1,0},{2,3},{3,2},{4,5},{5,4},{6,7},{7,6},{8,9},{9,8},{10,11... | collective-permute-start | bytes 6488072 | tf_op jit(solution)/shard_map/ppermute | solution.py:862
  233.3 28.4 %collective-permute-start.30 = (bf16[528,2048]{1,0:T(8,128)(2,1)}, bf16[528,2048]{1,0:T(8,128)(2,1)}, u32[]{:S(2)}, u32[]{:S(2)}) collective-permute-start(bf16[528,2048]{1,0:T(8,128)(2,1)} %bitcast.124.refs_2_.refs_4_), channel_id=1, source_target_pairs={{0,1},{1,0},{2,3},{3,2},{4,5},{5,4},{6,7},{7,6},{8,9},{9,8},{10,11... | collective-permute-start | bytes 6488072 | tf_op jit(solution)/shard_map/ppermute | solution.py:862
  233.8 14.8 %collective-permute-start.26 = (bf16[128,2048]{1,0:T(8,128)(2,1)S(1)}, bf16[128,2048]{1,0:T(8,128)(2,1)S(1)}, u32[]{:S(2)}, u32[]{:S(2)}) collective-permute-start(bf16[128,2048]{1,0:T(8,128)(2,1)S(1)} %copy-done.52), channel_id=1, source_target_pairs={{0,8},{8,16},{16,24},{24,28},{28,20},{20,12},{12,4},{4,0},{1,9},{9... | collective-permute-start | bytes 1572872 | tf_op jit(solution)/shard_map/ppermute | solution.py:837
  235.5 24.4 %collective-permute-start.32 = (bf16[128,2048]{1,0:T(8,128)(2,1)}, bf16[128,2048]{1,0:T(8,128)(2,1)}, u32[]{:S(2)}, u32[]{:S(2)}) collective-permute-start(bf16[128,2048]{1,0:T(8,128)(2,1)} %collective-permute-done.21.refs_1_.refs_2_.refs_12_), channel_id=1, source_target_pairs={{0,8},{8,16},{16,24},{24,28},{28,20},{20,12},{12,4},{4,0},{1,9},{9... | collective-permute-start | bytes 1572872 | tf_op jit(solution)/shard_map/ppermute | solution.py:804
  253.5 18.3 %collective-permute-start.31 = (bf16[128,2048]{1,0:T(8,128)(2,1)S(1)}, bf16[128,2048]{1,0:T(8,128)(2,1)S(1)}, u32[]{:S(2)}, u32[]{:S(2)}) collective-permute-start(bf16[128,2048]{1,0:T(8,128)(2,1)S(1)} %multiply_convert_fusion.refs_0_), channel_id=1, source_target_pairs={{0,4},{8,0},{16,8},{24,16},{28,24},{20,28},{12,20},{4,12},{1,5},{9... | collective-permute-start | bytes 1572872 | tf_op jit(solution)/shard_map/ppermute | solution.py:807
  254.1 25.5 %collective-permute-start.33 = (bf16[128,2048]{1,0:T(8,128)(2,1)S(1)}, bf16[128,2048]{1,0:T(8,128)(2,1)S(1)}, u32[]{:S(2)}, u32[]{:S(2)}) collective-permute-start(bf16[128,2048]{1,0:T(8,128)(2,1)S(1)} %copy-done.20), channel_id=1, source_target_pairs={{0,4},{8,0},{16,8},{24,16},{28,24},{20,28},{12,20},{4,12},{1,5},{9... | collective-permute-start | bytes 1572872 | tf_op jit(solution)/shard_map/ppermute | solution.py:807
  255.4 24.2 %collective-permute-start.29 = (bf16[128,2048]{1,0:T(8,128)(2,1)S(1)}, bf16[128,2048]{1,0:T(8,128)(2,1)S(1)}, u32[]{:S(2)}, u32[]{:S(2)}) collective-permute-start(bf16[128,2048]{1,0:T(8,128)(2,1)S(1)} %multiply_convert_fusion.refs_0_), channel_id=1, source_target_pairs={{0,8},{8,16},{16,24},{24,28},{28,20},{20,12},{12,4},{4,0},{1,9},{9... | collective-permute-start | bytes 1572872 | tf_op jit(solution)/shard_map/ppermute | solution.py:804
  260.0 36.1 %collective-permute-start.36 = (bf16[128,2048]{1,0:T(8,128)(2,1)}, bf16[128,2048]{1,0:T(8,128)(2,1)}, u32[]{:S(2)}, u32[]{:S(2)}) collective-permute-start(bf16[128,2048]{1,0:T(8,128)(2,1)} %collective-permute-done.32.refs_3_.refs_2_.refs_14_), channel_id=1, source_target_pairs={{0,8},{8,16},{16,24},{24,28},{28,20},{20,12},{12,4},{4,0},{1,9},{9... | collective-permute-start | bytes 1572872 | tf_op jit(solution)/shard_map/ppermute | solution.py:804
  271.8 23.8 %collective-permute-start.35 = (bf16[128,2048]{1,0:T(8,128)(2,1)S(1)}, bf16[128,2048]{1,0:T(8,128)(2,1)}, u32[]{:S(2)}, u32[]{:S(2)}) collective-permute-start(bf16[128,2048]{1,0:T(8,128)(2,1)S(1)} %collective-permute-done.31.refs_2_.refs_1_.refs_3_), channel_id=1, source_target_pairs={{0,4},{8,0},{16,8},{24,16},{28,24},{20,28},{12,20},{4,12},{1,5},{9... | collective-permute-start | bytes 1572872 | tf_op jit(solution)/shard_map/ppermute | solution.py:807
  280.7 15.4 %collective-permute-start.34 = (bf16[128,2048]{1,0:T(8,128)(2,1)}, bf16[128,2048]{1,0:T(8,128)(2,1)S(1)}, u32[]{:S(2)}, u32[]{:S(2)}) collective-permute-start(bf16[128,2048]{1,0:T(8,128)(2,1)} %after.64.refs_0_.refs_2_), channel_id=1, source_target_pairs={{0,8},{8,16},{16,24},{24,28},{28,20},{20,12},{12,4},{4,0},{1,9},{9... | collective-permute-start | bytes 1572872 | tf_op jit(solution)/shard_map/ppermute | solution.py:804
  295.6 15.3 %collective-permute-start.38 = (bf16[128,2048]{1,0:T(8,128)(2,1)}, bf16[128,2048]{1,0:T(8,128)(2,1)S(1)}, u32[]{:S(2)}, u32[]{:S(2)}) collective-permute-start(bf16[128,2048]{1,0:T(8,128)(2,1)} %collective-permute-done.35.refs_2_.refs_1_.refs_5_), channel_id=1, source_target_pairs={{0,4},{8,0},{16,8},{24,16},{28,24},{20,28},{12,20},{4,12},{1,5},{9... | collective-permute-start | bytes 1572872 | tf_op jit(solution)/shard_map/ppermute | solution.py:807
  311.8 16.4 %collective-permute-start.39 = (bf16[128,2048]{1,0:T(8,128)(2,1)}, bf16[128,2048]{1,0:T(8,128)(2,1)S(1)}, u32[]{:S(2)}, u32[]{:S(2)}) collective-permute-start(bf16[128,2048]{1,0:T(8,128)(2,1)} %after.66.refs_0_.refs_6_), channel_id=1, source_target_pairs={{0,8},{8,16},{16,24},{24,28},{28,20},{20,12},{12,4},{4,0},{1,9},{9... | collective-permute-start | bytes 1572872 | tf_op jit(solution)/shard_map/ppermute | solution.py:804
  327.2 27.6 %collective-permute-start.41 = (bf16[128,2048]{1,0:T(8,128)(2,1)}, bf16[128,2048]{1,0:T(8,128)(2,1)S(1)}, u32[]{:S(2)}, u32[]{:S(2)}) collective-permute-start(bf16[128,2048]{1,0:T(8,128)(2,1)} %slice.231), channel_id=1, source_target_pairs={{0,4},{8,0},{16,8},{24,16},{28,24},{20,28},{12,20},{4,12},{1,5},{9... | collective-permute-start | bytes 1572872 | tf_op jit(solution)/shard_map/ppermute | solution.py:839
  339.3 15.5 %collective-permute-start.40 = (bf16[128,2048]{1,0:T(8,128)(2,1)}, bf16[128,2048]{1,0:T(8,128)(2,1)S(1)}, u32[]{:S(2)}, u32[]{:S(2)}) collective-permute-start(bf16[128,2048]{1,0:T(8,128)(2,1)} %get-tuple-element.101.refs_1_), channel_id=1, source_target_pairs={{0,8},{8,16},{16,24},{24,28},{28,20},{20,12},{12,4},{4,0},{1,9},{9... | collective-permute-start | bytes 1572872 | tf_op jit(solution)/shard_map/ppermute | solution.py:837
  358.3 17.5 %collective-permute-start.43 = (bf16[528,2048]{1,0:T(8,128)(2,1)}, bf16[528,2048]{1,0:T(8,128)(2,1)S(1)}, u32[]{:S(2)}, u32[]{:S(2)}) collective-permute-start(bf16[528,2048]{1,0:T(8,128)(2,1)} %after.70), channel_id=1, source_target_pairs={{0,1},{1,0},{2,3},{3,2},{4,5},{5,4},{6,7},{7,6},{8,9},{9,8},{10,11... | collective-permute-start | bytes 6488072 | tf_op jit(solution)/shard_map/ppermute | solution.py:862
  359.7 14.4 %collective-permute-start.44 = (bf16[128,2048]{1,0:T(8,128)(2,1)S(1)}, bf16[128,2048]{1,0:T(8,128)(2,1)S(1)}, u32[]{:S(2)}, u32[]{:S(2)}) collective-permute-start(bf16[128,2048]{1,0:T(8,128)(2,1)S(1)} %add_convert_fusion.13), channel_id=1, source_target_pairs={{0,4},{8,0},{16,8},{24,16},{28,24},{20,28},{12,20},{4,12},{1,5},{9... | collective-permute-start | bytes 1572872 | tf_op jit(solution)/shard_map/ppermute | solution.py:839
  360.8 14.3 %collective-permute-start.42 = (bf16[128,2048]{1,0:T(8,128)(2,1)}, bf16[128,2048]{1,0:T(8,128)(2,1)S(1)}, u32[]{:S(2)}, u32[]{:S(2)}) collective-permute-start(bf16[128,2048]{1,0:T(8,128)(2,1)} %add_convert_fusion.14.refs_1_), channel_id=1, source_target_pairs={{0,8},{8,16},{16,24},{24,28},{28,20},{20,12},{12,4},{4,0},{1,9},{9... | collective-permute-start | bytes 1572872 | tf_op jit(solution)/shard_map/ppermute | solution.py:837
  382.9 68.7 %collective-permute-start.56 = (bf16[528,2048]{1,0:T(8,128)(2,1)}, bf16[528,2048]{1,0:T(8,128)(2,1)}, u32[]{:S(2)}, u32[]{:S(2)}) collective-permute-start(bf16[528,2048]{1,0:T(8,128)(2,1)} %get-tuple-element.108), channel_id=1, source_target_pairs={{0,1},{1,0},{2,3},{3,2},{4,5},{5,4},{6,7},{7,6},{8,9},{9,8},{10,11... | collective-permute-start | bytes 6488072 | tf_op jit(solution)/shard_map/ppermute | solution.py:862
  402.3 47.2 %collective-permute-start.53 = (bf16[528,2048]{1,0:T(8,128)(2,1)}, bf16[528,2048]{1,0:T(8,128)(2,1)S(1)}, u32[]{:S(2)}, u32[]{:S(2)}) collective-permute-start(bf16[528,2048]{1,0:T(8,128)(2,1)} %add_convert_fusion.1), channel_id=1, source_target_pairs={{0,2},{1,3},{2,0},{3,1},{4,6},{5,7},{6,4},{7,5},{8,10},{9,11},{10,... | collective-permute-start | bytes 6488072 | tf_op jit(solution)/shard_map/ppermute | solution.py:862
  450.9 23.2 %collective-permute-start.55 = (bf16[128,2048]{1,0:T(8,128)(2,1)}, bf16[128,2048]{1,0:T(8,128)(2,1)}, u32[]{:S(2)}, u32[]{:S(2)}) collective-permute-start(bf16[128,2048]{1,0:T(8,128)(2,1)} %after.80.refs_1_.refs_6_), channel_id=1, source_target_pairs={{0,8},{8,16},{16,24},{24,28},{28,20},{20,12},{12,4},{4,0},{1,9},{9... | collective-permute-start | bytes 1572872 | tf_op jit(solution)/shard_map/ppermute | solution.py:804
  507.0 64.7 %all-to-all-start.2 = ((bf16[8,528,256]{2,1,0:T(8,128)(2,1)}), bf16[8,528,256]{2,1,0:T(8,128)(2,1)S(1)}, u32[]{:S(2)}, u32[]{:S(2)}) async-start(bf16[8,528,256]{2,1,0:T(8,128)(2,1)} %after.83), calls=%async_computation.3 | async-start | bytes 4325376 | tf_op jit(solution)/shard_map/all_to_all | solution.py:941
  511.1 157.8 %all-gather.3.cloned.1.call-start = ((), (), s32[]{:S(2)}) async-start(), calls=%async_computation.6 | async-start | bytes 1179648 | tf_op jit(solution)/shard_map/all_gather | solution.py:1237
  569.7 22.8 %collective-permute-start.61 = (bf16[320,2048]{1,0:T(8,128)(2,1)}, bf16[320,2048]{1,0:T(8,128)(2,1)}, u32[]{:S(2)}, u32[]{:S(2)}) collective-permute-start(bf16[320,2048]{1,0:T(8,128)(2,1)} %get-tuple-element.115), channel_id=1, source_target_pairs={{0,1},{1,0},{2,3},{3,2},{4,5},{5,4},{6,7},{7,6},{8,9},{9,8},{10,11... | collective-permute-start | bytes 3932168 | tf_op jit(solution)/shard_map/ppermute | solution.py:862
  605.0 29.5 %collective-permute-start.68 = (bf16[320,2048]{1,0:T(8,128)(2,1)}, bf16[320,2048]{1,0:T(8,128)(2,1)S(1)}, u32[]{:S(2)}, u32[]{:S(2)}) collective-permute-start(bf16[320,2048]{1,0:T(8,128)(2,1)} %add_convert_fusion.3), channel_id=1, source_target_pairs={{0,2},{1,3},{2,0},{3,1},{4,6},{5,7},{6,4},{7,5},{8,10},{9,11},{10,... | collective-permute-start | bytes 3932168 | tf_op jit(solution)/shard_map/ppermute | solution.py:862
  605.8 33.3 %collective-permute-start.71 = (bf16[320,2048]{1,0:T(8,128)(2,1)}, bf16[320,2048]{1,0:T(8,128)(2,1)}, u32[]{:S(2)}, u32[]{:S(2)}) collective-permute-start(bf16[320,2048]{1,0:T(8,128)(2,1)} %get-tuple-element.122), channel_id=1, source_target_pairs={{0,1},{1,0},{2,3},{3,2},{4,5},{5,4},{6,7},{7,6},{8,9},{9,8},{10,11... | collective-permute-start | bytes 3932168 | tf_op jit(solution)/shard_map/ppermute | solution.py:862
  637.1 19.4 %collective-permute-start.70 = (bf16[128,2048]{1,0:T(8,128)(2,1)S(1)}, bf16[128,2048]{1,0:T(8,128)(2,1)S(1)}, u32[]{:S(2)}, u32[]{:S(2)}) collective-permute-start(bf16[128,2048]{1,0:T(8,128)(2,1)S(1)} %add_convert_fusion.4), channel_id=1, source_target_pairs={{0,8},{8,16},{16,24},{24,28},{28,20},{20,12},{12,4},{4,0},{1,9},{9... | collective-permute-start | bytes 1572872 | tf_op jit(solution)/shard_map/ppermute | solution.py:837
  642.7 42.0 %all-to-all-start.3 = ((bf16[8,320,256]{2,1,0:T(8,128)(2,1)}), bf16[8,320,256]{2,1,0:T(8,128)(2,1)}, u32[]{:S(2)}, u32[]{:S(2)}) async-start(bf16[8,320,256]{2,1,0:T(8,128)(2,1)} %bitcast.228), calls=%async_computation.4 | async-start | bytes 2621440 | tf_op jit(solution)/shard_map/all_to_all | solution.py:941
  (121 other events, 893.7 us)
Sparse Core Ops, SparseCore 0:
  443.7 125.7 reduce-scatter.1
  619.3 49.4 all-gather.2
